TPU v7x, 32 devices: a whole 2x2x4 slice. The times are simulated.
32 devices in a mesh: dp: 8 (over z, x), mp: 4 (over y, core).
Axes of the slice: x: 2, y: 2, z: 4, core: 2. Of those that a mesh axis runs over, the one named last changes fastest.
Arguments:
- patches: bfloat16 [128, 196, 768], P(('dp', 'mp')), may hold values from -6 to 6
- keep_mask: int32 [128, 196], P(('dp', 'mp')), may hold values from 0 to 1, as said below
- labels: int32 [128], P(('dp', 'mp')), may hold values from 0 to 999
- stem_weight: float32 [768, 768], replicated, may hold values from -0.21875 to 0.21875
- position_table: float32 [197, 768], replicated, may hold values from -3 to 3
- attend_in: float32 [768, 3, 768], P('dp', None, 'mp'), may hold values from -0.21875 to 0.21875
- attend_out: float32 [768, 768], P('mp', 'dp'), may hold values from -0.875 to 0.875
- expand: float32 [768, 3072], P('dp', 'mp'), may hold values from -0.21875 to 0.21875
- contract: float32 [3072, 768], P('mp', 'dp'), may hold values from -0.109375 to 0.109375
- head_weight: float32 [768, 1000], replicated, may hold values from -0.21875 to 0.21875
- vectors: float32 [12520], replicated, as said below
- stem_rows: float32 [768], replicated, may hold values from 6.009615e-07 to 2.403846e-06
- stem_cols: float32 [768], replicated, may hold values from 6.009615e-07 to 2.403846e-06
- table_rows: float32 [197], replicated, may hold values from 4.6227813e-09 to 1.8491125e-08
- table_cols: float32 [768], replicated, may hold values from 4.6227813e-09 to 1.8491125e-08
- attend_in_rows: float32 [768], replicated, may hold values from 1.2019231e-07 to 3.0048077e-06
- attend_in_cols: float32 [3, 768], replicated, may hold values from 1.5024038e-07 to 6.009615e-07
- attend_out_rows: float32 [768], replicated, may hold values from 1.5024038e-07 to 6.009615e-07
- attend_out_cols: float32 [768], replicated, may hold values from 1.2019231e-07 to 3.0048077e-06
- expand_rows: float32 [768], replicated, may hold values from 1.2019231e-07 to 3.0048077e-06
- expand_cols: float32 [3072], replicated, may hold values from 1.5024038e-07 to 6.009615e-07
- contract_rows: float32 [3072], replicated, may hold values from 1.5024038e-07 to 6.009615e-07
- contract_cols: float32 [768], replicated, may hold values from 1.2019231e-07 to 3.0048077e-06
- head_rows: float32 [768], replicated, may hold values from 7.8125e-06 to 3.125e-05
- head_cols: float32 [1000], replicated, may hold values from 7.8125e-06 to 3.125e-05
- vector_second: float32 [12520], replicated, may hold values from 6.009615e-07 to 2.403846e-06
Outputs:
- loss_sum: float32 [], replicated
- stem_new: float32 [768, 768], replicated
- stem_rows_new: float32 [768], replicated
- stem_cols_new: float32 [768], replicated
- table_new: float32 [197, 768], replicated
- table_rows_new: float32 [197], replicated
- table_cols_new: float32 [768], replicated
- attend_in_new: float32 [768, 3, 768], P('dp', None, 'mp')
- attend_in_copy: bfloat16 [768, 3, 768], P('dp', None, 'mp')
- attend_in_rows_new: float32 [768], replicated
- attend_in_cols_new: float32 [3, 768], replicated
- attend_out_new: float32 [768, 768], P('mp', 'dp')
- attend_out_copy: bfloat16 [768, 768], P('mp', 'dp')
- attend_out_rows_new: float32 [768], replicated
- attend_out_cols_new: float32 [768], replicated
- expand_new: float32 [768, 3072], P('dp', 'mp')
- expand_copy: bfloat16 [768, 3072], P('dp', 'mp')
- expand_rows_new: float32 [768], replicated
- expand_cols_new: float32 [3072], replicated
- contract_new: float32 [3072, 768], P('mp', 'dp')
- contract_copy: bfloat16 [3072, 768], P('mp', 'dp')
- contract_rows_new: float32 [3072], replicated
- contract_cols_new: float32 [768], replicated
- head_new: float32 [768, 1000], replicated
- head_rows_new: float32 [768], replicated
- head_cols_new: float32 [1000], replicated
- vectors_new: float32 [12520], replicated
- vector_grad: float32 [12520], replicated
- vector_second_new: float32 [12520], replicated
Inputs may be any that keep to these rules, and one draw needn't show every extreme that they name: `keep_mask`: each image keeps 64 to 196 of its patches; some image keeps exactly 64 and some keeps all. `vectors`: gains one, two and last lie near 1, all other entries near 0.
All inputs are finite; a program needn't handle non-finite values.
Results may differ from a plain program's by a relative error of at most 0.011.
Values may be sent and summed in bfloat16 or wider, within the bound.
No kernel may reach another device: no remote copies, remote signals or barrier semaphores. Data moves between devices by JAX's collectives and lax.ppermute only.
A program may use at most 256 MiB of HBM per device.

v0:
```python
import jax
import jax.numpy as jnp
from jax import lax
from jax.sharding import PartitionSpec as P

D = 768
HEAD_DIM = 64
FF = 3072
CLASSES = 1000


eps_norm = 1e-06
eps_one = 1e-30
eps_two = 0.001
decay_rate = 0.5
clip_level = 0.3
step_rate = 1.0
smoothing = 0.1


def layer_norm(values, gain, shift):
    centred = values - jnp.mean(values, -1, keepdims=True)
    variance = jnp.mean(centred * centred, -1, keepdims=True)
    return centred * lax.rsqrt(variance + eps_norm) * gain + shift


def pieces_of(vectors):
    widths = [D] * 8 + [FF] + [D] * 3 + [CLASSES]
    pieces = []
    offset = 0
    for extent in widths:
        pieces.append(vectors[offset : offset + extent])
        offset = offset + extent
    return pieces


def place(piece, extent, offset, axis):
    full_shape = list(piece.shape)
    full_shape[axis] = extent
    return lax.dynamic_update_slice_in_dim(jnp.zeros(full_shape, jnp.float32), piece, offset, axis)


def gather_rows(rows, flags):
    return (
        lax.all_gather(rows, "mp", axis=0, tiled=True),
        lax.all_gather(flags, "mp", axis=0, tiled=True),
    )


def scatter_rows(terms):
    return lax.psum_scatter(
        terms.astype(jnp.bfloat16), "mp", scatter_dimension=0, tiled=True
    ).astype(jnp.float32)


def gather_grads(grads):
    return lax.all_gather(grads, "mp", axis=0, tiled=True)


def scatter_grads(terms):
    return lax.psum_scatter(
        terms.astype(jnp.bfloat16), "mp", scatter_dimension=0, tiled=True
    ).astype(jnp.float32)


def fetch_block(attend_in, attend_out, expand, contract):
    return (
        lax.all_gather(attend_in.astype(jnp.bfloat16), "dp", axis=0, tiled=True),
        lax.all_gather(attend_out.astype(jnp.bfloat16), "dp", axis=1, tiled=True),
        lax.all_gather(expand.astype(jnp.bfloat16), "dp", axis=0, tiled=True),
        lax.all_gather(contract.astype(jnp.bfloat16), "dp", axis=1, tiled=True),
    )


def reduce_block(grads):
    return (
        lax.psum_scatter(grads[0], "dp", scatter_dimension=0, tiled=True),
        lax.psum_scatter(grads[1], "dp", scatter_dimension=1, tiled=True),
        lax.psum_scatter(grads[2], "dp", scatter_dimension=0, tiled=True),
        lax.psum_scatter(grads[3], "dp", scatter_dimension=1, tiled=True),
    )


def reduce_shared(grads):
    return lax.psum((grads[0], grads[1], grads[2], grads[3], grads[4]), ("dp", "mp"))


def micro_step(
    pixels, kept_rows, classes, current, stem_low, head_low, position_table, vectors, inverse_count
):
    block_in, block_out, block_expand, block_contract = current
    (
        stem_bias,
        gain_one,
        shift_one,
        query_bias,
        value_bias,
        attend_bias,
        gain_two,
        shift_two,
        expand_bias,
        contract_bias,
        gain_last,
        shift_last,
        head_bias,
    ) = pieces_of(vectors)
    model_index = lax.axis_index("mp")
    head_share = block_in.shape[2]
    hidden_share = block_expand.shape[1]
    query_part = lax.dynamic_slice_in_dim(query_bias, model_index * head_share, head_share)
    value_part = lax.dynamic_slice_in_dim(value_bias, model_index * head_share, head_share)
    expand_part = lax.dynamic_slice_in_dim(expand_bias, model_index * hidden_share, hidden_share)
    batch_count = pixels.shape[0]
    scale_factor = HEAD_DIM ** (-0.5)
    embedded = (
        jnp.einsum("bpi,id->bpd", pixels, stem_low, preferred_element_type=jnp.float32) + stem_bias
    )
    start_rows = jnp.zeros((batch_count, 1, embedded.shape[2]), jnp.float32)
    stream_zero = jnp.concatenate([start_rows, embedded], 1) + position_table
    present = jnp.concatenate(
        [jnp.ones((batch_count, 1), jnp.float32), kept_rows.astype(jnp.float32)], 1
    )
    present_low = present.astype(jnp.bfloat16)
    normed_one, pull_one = jax.vjp(layer_norm, stream_zero, gain_one, shift_one)
    rows_one, present_all = gather_rows(normed_one.astype(jnp.bfloat16), present_low)
    group_count = rows_one.shape[0]
    slot_count = rows_one.shape[1]
    heads_here = head_share // HEAD_DIM
    head_shape = (group_count, slot_count, heads_here, HEAD_DIM)
    projected = jnp.einsum("bsd,dte->bste", rows_one, block_in, preferred_element_type=jnp.float32)
    query_rows = (projected[:, :, 0] + query_part).astype(jnp.bfloat16).reshape(head_shape)
    key_rows = projected[:, :, 1].astype(jnp.bfloat16).reshape(head_shape)
    value_rows = (projected[:, :, 2] + value_part).astype(jnp.bfloat16).reshape(head_shape)
    raw_scores = (
        jnp.einsum("bqhe,bkhe->bhqk", query_rows, key_rows, preferred_element_type=jnp.float32)
        * scale_factor
    )
    visible = present_all[:, None, None, :] > 0.5
    attention = jax.nn.softmax(jnp.where(visible, raw_scores, -1e30), -1)
    attention_low = attention.astype(jnp.bfloat16)
    attended = jnp.einsum(
        "bhqk,bkhe->bqhe", attention_low, value_rows, preferred_element_type=jnp.float32
    )
    attended = attended.astype(jnp.bfloat16).reshape(group_count, slot_count, head_share)
    attend_sum = scatter_rows(
        jnp.einsum("bsm,md->bsd", attended, block_out, preferred_element_type=jnp.float32)
    )
    stream_one = stream_zero + attend_sum + attend_bias
    normed_two, pull_two = jax.vjp(layer_norm, stream_one, gain_two, shift_two)
    rows_two, unused_flags = gather_rows(normed_two.astype(jnp.bfloat16), present_low)
    hidden = (
        jnp.einsum("bsd,df->bsf", rows_two, block_expand, preferred_element_type=jnp.float32)
        + expand_part
    )
    active, gelu_pull = jax.vjp(jax.nn.gelu, hidden)
    active_low = active.astype(jnp.bfloat16)
    mlp_sum = scatter_rows(
        jnp.einsum("bsf,fd->bsd", active_low, block_contract, preferred_element_type=jnp.float32)
    )
    stream_two = stream_one + mlp_sum + contract_bias
    kept_count = jnp.sum(present, 1)
    pooled = jnp.sum(present[:, :, None] * stream_two, 1) / kept_count[:, None]
    final_row, pull_last = jax.vjp(layer_norm, pooled, gain_last, shift_last)
    final_low = final_row.astype(jnp.bfloat16)
    logits = jnp.dot(final_low, head_low, preferred_element_type=jnp.float32) + head_bias
    log_probs = jax.nn.log_softmax(logits, -1)
    target = smoothing / CLASSES + (1.0 - smoothing) * jax.nn.one_hot(
        classes, CLASSES, dtype=jnp.float32
    )
    loss_local = -jnp.sum(target * log_probs)
    d_logits = (jnp.exp(log_probs) - target) * inverse_count
    grad_head_bias = jnp.sum(d_logits, 0)
    d_logits_low = d_logits.astype(jnp.bfloat16)
    grad_head = jnp.einsum("bd,bc->dc", final_low, d_logits_low, preferred_element_type=jnp.float32)
    d_final = jnp.einsum("bc,dc->bd", d_logits_low, head_low, preferred_element_type=jnp.float32)
    d_pooled, grad_gain_last, grad_shift_last = pull_last(d_final)
    d_stream = present[:, :, None] * (d_pooled / kept_count[:, None])[:, None, :]
    grad_contract_bias = jnp.sum(d_stream, (0, 1))
    d_mlp_all = gather_grads(d_stream.astype(jnp.bfloat16))
    grad_contract = jnp.einsum(
        "bsf,bsd->fd", active_low, d_mlp_all, preferred_element_type=jnp.float32
    )
    d_active = jnp.einsum(
        "bsd,fd->bsf", d_mlp_all, block_contract, preferred_element_type=jnp.float32
    )
    (d_hidden,) = gelu_pull(d_active)
    grad_expand_bias = jnp.sum(d_hidden, (0, 1))
    d_hidden_low = d_hidden.astype(jnp.bfloat16)
    grad_expand = jnp.einsum(
        "bsd,bsf->df", rows_two, d_hidden_low, preferred_element_type=jnp.float32
    )
    d_normed_two = scatter_grads(
        jnp.einsum("bsf,df->bsd", d_hidden_low, block_expand, preferred_element_type=jnp.float32)
    )
    d_from_two, grad_gain_two, grad_shift_two = pull_two(d_normed_two)
    d_stream = d_stream + d_from_two
    grad_attend_bias = jnp.sum(d_stream, (0, 1))
    d_attend_all = gather_grads(d_stream.astype(jnp.bfloat16))
    grad_out = jnp.einsum("bsm,bsd->md", attended, d_attend_all, preferred_element_type=jnp.float32)
    d_attended = jnp.einsum(
        "bsd,md->bsm", d_attend_all, block_out, preferred_element_type=jnp.float32
    )
    d_attended = d_attended.astype(jnp.bfloat16).reshape(head_shape)
    d_attention = jnp.einsum(
        "bqhe,bkhe->bhqk", d_attended, value_rows, preferred_element_type=jnp.float32
    )
    d_value = jnp.einsum(
        "bhqk,bqhe->bkhe", attention_low, d_attended, preferred_element_type=jnp.float32
    )
    d_scores = attention * (d_attention - jnp.sum(d_attention * attention, -1, keepdims=True))
    d_scores = d_scores.astype(jnp.bfloat16)
    d_query = (
        jnp.einsum("bhqk,bkhe->bqhe", d_scores, key_rows, preferred_element_type=jnp.float32)
        * scale_factor
    )
    d_key = (
        jnp.einsum("bhqk,bqhe->bkhe", d_scores, query_rows, preferred_element_type=jnp.float32)
        * scale_factor
    )
    grad_query_bias = jnp.sum(d_query, (0, 1)).reshape(head_share)
    grad_value_bias = jnp.sum(d_value, (0, 1)).reshape(head_share)
    d_projected = jnp.stack([d_query, d_key, d_value], 2).reshape(
        group_count, slot_count, 3, head_share
    )
    d_projected = d_projected.astype(jnp.bfloat16)
    grad_in = jnp.einsum("bsd,bste->dte", rows_one, d_projected, preferred_element_type=jnp.float32)
    d_normed_one = scatter_grads(
        jnp.einsum("bste,dte->bsd", d_projected, block_in, preferred_element_type=jnp.float32)
    )
    d_from_one, grad_gain_one, grad_shift_one = pull_one(d_normed_one)
    d_stream = d_stream + d_from_one
    grad_table = jnp.sum(d_stream, 0)
    d_embedded = d_stream[:, 1:]
    grad_stem_bias = jnp.sum(d_embedded, (0, 1))
    grad_stem = jnp.einsum(
        "bpi,bpd->id", pixels, d_embedded.astype(jnp.bfloat16), preferred_element_type=jnp.float32
    )
    width_all = stem_bias.shape[0]
    grad_vector = jnp.concatenate(
        [
            grad_stem_bias,
            grad_gain_one,
            grad_shift_one,
            place(grad_query_bias, width_all, model_index * head_share, 0),
            place(grad_value_bias, width_all, model_index * head_share, 0),
            grad_attend_bias,
            grad_gain_two,
            grad_shift_two,
            place(grad_expand_bias, expand_bias.shape[0], model_index * hidden_share, 0),
            grad_contract_bias,
            grad_gain_last,
            grad_shift_last,
            grad_head_bias,
        ]
    )
    block_local = (grad_in, grad_out, grad_expand, grad_contract)
    shared_local = (grad_stem, grad_table, grad_head, grad_vector, loss_local)
    return (block_local, shared_local)


def factored_step(weight, grad, rows, cols):
    squared = grad * grad + eps_one
    rows_new = decay_rate * rows + (1.0 - decay_rate) * jnp.mean(squared, 1)
    cols_new = decay_rate * cols + (1.0 - decay_rate) * jnp.mean(squared, 0)
    denominator = rows_new[:, None] * cols_new[None, :] / jnp.mean(rows_new)
    update = grad * lax.rsqrt(denominator)
    update = update / jnp.maximum(1.0, jnp.sqrt(jnp.mean(update * update)) / clip_level)
    magnitude = jnp.maximum(eps_two, jnp.sqrt(jnp.mean(weight * weight)))
    return (weight - step_rate * magnitude * update, rows_new, cols_new)


def vector_step(vectors, grad, second):
    second_new = decay_rate * second + (1.0 - decay_rate) * (grad * grad + eps_one)
    update = grad * lax.rsqrt(second_new)
    update = update / jnp.maximum(1.0, jnp.sqrt(jnp.mean(update * update)) / clip_level)
    magnitude = jnp.maximum(eps_two, jnp.sqrt(jnp.mean(vectors * vectors)))
    return (vectors - step_rate * magnitude * update, second_new)


def renewed(state, total, count):
    return decay_rate * state + (1.0 - decay_rate) * (total / count)


def stepped(weight, update, update_total, weight_total, count):
    update = update / jnp.maximum(1.0, jnp.sqrt(update_total / count) / clip_level)
    magnitude = jnp.maximum(eps_two, jnp.sqrt(weight_total / count))
    return weight - step_rate * magnitude * update


def local(
    patches,
    keep_mask,
    labels,
    stem_weight,
    position_table,
    attend_in,
    attend_out,
    expand,
    contract,
    head_weight,
    vectors,
    stem_rows,
    stem_cols,
    table_rows,
    table_cols,
    attend_in_rows,
    attend_in_cols,
    attend_out_rows,
    attend_out_cols,
    expand_rows,
    expand_cols,
    contract_rows,
    contract_cols,
    head_rows,
    head_cols,
    vector_second,
):
    data_size = lax.axis_size("dp")
    model_size = lax.axis_size("mp")
    local_count = patches.shape[0]
    inverse_count = 1.0 / (local_count * data_size * model_size)
    stem_low = stem_weight.astype(jnp.bfloat16)
    head_low = head_weight.astype(jnp.bfloat16)
    block_total = None
    shared_total = None
    for micro in range(local_count):
        current = fetch_block(attend_in, attend_out, expand, contract)
        block_local, shared_local = micro_step(
            patches[micro : micro + 1],
            keep_mask[micro : micro + 1],
            labels[micro : micro + 1],
            current,
            stem_low,
            head_low,
            position_table,
            vectors,
            inverse_count,
        )
        block_local = reduce_block(block_local)
        if micro == 0:
            block_total = block_local
            shared_total = shared_local
        else:
            block_total = jax.tree.map(jnp.add, block_total, block_local)
            shared_total = jax.tree.map(jnp.add, shared_total, shared_local)
    grad_stem, grad_table, grad_head, grad_vector, loss_sum = reduce_shared(shared_total)
    grad_in, grad_out, grad_expand, grad_contract = block_total
    data_index = lax.axis_index("dp")
    model_index = lax.axis_index("mp")
    row_share = attend_in.shape[0]
    head_share = attend_in.shape[2]
    hidden_share = expand.shape[1]
    row_start = data_index * row_share
    head_start = model_index * head_share
    hidden_start = model_index * hidden_share
    squared_in = grad_in * grad_in + eps_one
    squared_out = grad_out * grad_out + eps_one
    squared_expand = grad_expand * grad_expand + eps_one
    squared_contract = grad_contract * grad_contract + eps_one
    sums = lax.psum(
        (
            place(jnp.sum(squared_in, (1, 2)), D, row_start, 0),
            place(jnp.sum(squared_in, 0), D, head_start, 1),
            place(jnp.sum(squared_out, 1), D, head_start, 0),
            place(jnp.sum(squared_out, 0), D, row_start, 0),
            place(jnp.sum(squared_expand, 1), D, row_start, 0),
            place(jnp.sum(squared_expand, 0), FF, hidden_start, 0),
            place(jnp.sum(squared_contract, 1), FF, hidden_start, 0),
            place(jnp.sum(squared_contract, 0), D, row_start, 0),
            jnp.stack(
                [
                    jnp.sum(attend_in * attend_in),
                    jnp.sum(attend_out * attend_out),
                    jnp.sum(expand * expand),
                    jnp.sum(contract * contract),
                ]
            ),
        ),
        ("dp", "mp"),
    )
    in_rows_new = renewed(attend_in_rows, sums[0], 3 * D)
    in_cols_new = renewed(attend_in_cols, sums[1], D)
    out_rows_new = renewed(attend_out_rows, sums[2], D)
    out_cols_new = renewed(attend_out_cols, sums[3], D)
    expand_rows_new = renewed(expand_rows, sums[4], FF)
    expand_cols_new = renewed(expand_cols, sums[5], D)
    contract_rows_new = renewed(contract_rows, sums[6], D)
    contract_cols_new = renewed(contract_cols, sums[7], FF)
    weight_totals = sums[8]
    update_in = grad_in * lax.rsqrt(
        lax.dynamic_slice_in_dim(in_rows_new, row_start, row_share)[:, None, None]
        * lax.dynamic_slice_in_dim(in_cols_new, head_start, head_share, 1)[None]
        / jnp.mean(in_rows_new)
    )
    update_out = grad_out * lax.rsqrt(
        lax.dynamic_slice_in_dim(out_rows_new, head_start, head_share)[:, None]
        * lax.dynamic_slice_in_dim(out_cols_new, row_start, row_share)[None]
        / jnp.mean(out_rows_new)
    )
    update_expand = grad_expand * lax.rsqrt(
        lax.dynamic_slice_in_dim(expand_rows_new, row_start, row_share)[:, None]
        * lax.dynamic_slice_in_dim(expand_cols_new, hidden_start, hidden_share)[None]
        / jnp.mean(expand_rows_new)
    )
    update_contract = grad_contract * lax.rsqrt(
        lax.dynamic_slice_in_dim(contract_rows_new, hidden_start, hidden_share)[:, None]
        * lax.dynamic_slice_in_dim(contract_cols_new, row_start, row_share)[None]
        / jnp.mean(contract_rows_new)
    )
    update_totals = lax.psum(
        jnp.stack(
            [
                jnp.sum(update_in * update_in),
                jnp.sum(update_out * update_out),
                jnp.sum(update_expand * update_expand),
                jnp.sum(update_contract * update_contract),
            ]
        ),
        ("dp", "mp"),
    )
    in_new = stepped(attend_in, update_in, update_totals[0], weight_totals[0], 3 * D * D)
    out_new = stepped(attend_out, update_out, update_totals[1], weight_totals[1], D * D)
    expand_new = stepped(expand, update_expand, update_totals[2], weight_totals[2], D * FF)
    contract_new = stepped(contract, update_contract, update_totals[3], weight_totals[3], FF * D)
    stem_new, stem_rows_new, stem_cols_new = factored_step(
        stem_weight, grad_stem, stem_rows, stem_cols
    )
    table_new, table_rows_new, table_cols_new = factored_step(
        position_table, grad_table, table_rows, table_cols
    )
    head_new, head_rows_new, head_cols_new = factored_step(
        head_weight, grad_head, head_rows, head_cols
    )
    vectors_new, second_new = vector_step(vectors, grad_vector, vector_second)
    return (
        loss_sum,
        stem_new,
        stem_rows_new,
        stem_cols_new,
        table_new,
        table_rows_new,
        table_cols_new,
        in_new,
        in_new.astype(jnp.bfloat16),
        in_rows_new,
        in_cols_new,
        out_new,
        out_new.astype(jnp.bfloat16),
        out_rows_new,
        out_cols_new,
        expand_new,
        expand_new.astype(jnp.bfloat16),
        expand_rows_new,
        expand_cols_new,
        contract_new,
        contract_new.astype(jnp.bfloat16),
        contract_rows_new,
        contract_cols_new,
        head_new,
        head_rows_new,
        head_cols_new,
        vectors_new,
        grad_vector,
        second_new,
    )


def solution(mesh):
    placed = (
        P(("dp", "mp"), None, None),
        P(("dp", "mp"), None),
        P(("dp", "mp")),
        P(),
        P(),
        P("dp", None, "mp"),
        P("mp", "dp"),
        P("dp", "mp"),
        P("mp", "dp"),
        P(),
        P(),
        P(),
        P(),
        P(),
        P(),
        P(),
        P(),
        P(),
        P(),
        P(),
        P(),
        P(),
        P(),
        P(),
        P(),
        P(),
    )
    return jax.shard_map(
        local,
        mesh=mesh,
        in_specs=placed,
        out_specs=(
            P(),
            P(),
            P(),
            P(),
            P(),
            P(),
            P(),
            P("dp", None, "mp"),
            P("dp", None, "mp"),
            P(),
            P(),
            P("mp", "dp"),
            P("mp", "dp"),
            P(),
            P(),
            P("dp", "mp"),
            P("dp", "mp"),
            P(),
            P(),
            P("mp", "dp"),
            P("mp", "dp"),
            P(),
            P(),
            P(),
            P(),
            P(),
            P(),
            P(),
            P(),
        ),
        check_vma=False,
    )
```

profile of v0, /device:TPU:0, one launch (start us, length us, event | category | flops | bytes accessed | tf_op | source)
XLA Modules:
  0.0 1254.3 jit_solution(16879986944546845351)
XLA Ops:
  25.1 40.5 %all_gather.85 = bf16[768,3,192]{2,1,0:T(4,128)(2,1)} all-gather(bf16[96,3,192]{2,1,0:T(4,128)(2,1)S(1)} %copy.250), channel_id=1, replica_groups=mesh['dp'=8,'mp'=4] {'dp'}, dimensions={0}, use_global_device_ids=true | all-gather | bytes 995328 | tf_op jit(solution)/shard_map/all_gather | solution.py:68
  74.6 31.0 %all_gather.87 = bf16[192,768]{0,1:T(8,128)(2,1)S(1)} all-gather(bf16[192,96]{0,1:T(8,128)(2,1)S(1)} %copy.253), channel_id=1, replica_groups=mesh['dp'=8,'mp'=4] {'dp'}, dimensions={1}, use_global_device_ids=true | all-gather | bytes 331776 | tf_op jit(solution)/shard_map/all_gather | solution.py:69
  190.3 28.7 %reduce-scatter.27.cloned.1.call-done = bf16[1,197,768]{2,1,0:T(8,128)(2,1)} async-done(((bf16[4,197,768]{2,1,0:T(8,128)(2,1)}), bf16[1,197,768]{2,1,0:T(8,128)(2,1)}) %reduce-scatter.27.cloned.1.call-update) | async-done | bytes 302608 | tf_op jit(solution)/shard_map/reduce_scatter | solution.py:51
  219.0 29.4 %reduce-scatter.23.cloned.1.call-done = bf16[1,197,768]{2,1,0:T(8,128)(2,1)} async-done(((bf16[4,197,768]{2,1,0:T(8,128)(2,1)}), bf16[1,197,768]{2,1,0:T(8,128)(2,1)}) %reduce-scatter.23.cloned.1.call-update) | async-done | bytes 302608 | tf_op jit(solution)/shard_map/reduce_scatter | solution.py:51
  257.0 13.9 %all-gather.25.cloned.1.call-done = bf16[4,197,768]{2,1,0:T(8,128)(2,1)} async-done(((bf16[1,197,768]{2,1,0:T(8,128)(2,1)}), bf16[4,197,768]{2,1,0:T(8,128)(2,1)}) %all-gather.25.cloned.1.call-update) | async-done | bytes 1210384 | tf_op jit(solution)/shard_map/all_gather | solution.py:45
  275.2 39.9 %all-gather.29.cloned.1.call-done = bf16[768,768]{0,1:T(8,128)(2,1)} async-done(((bf16[768,96]{0,1:T(8,128)(2,1)}), bf16[768,768]{0,1:T(8,128)(2,1)}) %all-gather.29.cloned.1.call-update) | async-done | bytes 1179664 | tf_op jit(solution)/shard_map/all_gather | solution.py:71
  386.0 13.5 %reduce-scatter.25.cloned.1.call-done = bf16[1,197,768]{2,1,0:T(8,128)(2,1)} async-done(((bf16[4,197,768]{2,1,0:T(8,128)(2,1)}), bf16[1,197,768]{2,1,0:T(8,128)(2,1)}) %reduce-scatter.25.cloned.1.call-update) | async-done | bytes 302608 | tf_op jit(solution)/shard_map/reduce_scatter | solution.py:51
  399.6 28.6 %reduce-scatter.29.cloned.1.call-done = bf16[1,197,768]{2,1,0:T(8,128)(2,1)} async-done(((bf16[4,197,768]{2,1,0:T(8,128)(2,1)}), bf16[1,197,768]{2,1,0:T(8,128)(2,1)}) %reduce-scatter.29.cloned.1.call-update) | async-done | bytes 302608 | tf_op jit(solution)/shard_map/reduce_scatter | solution.py:51
  428.2 28.4 %reduce-scatter.33.cloned.1.call-done = bf16[1,197,768]{2,1,0:T(8,128)(2,1)} async-done(((bf16[4,197,768]{2,1,0:T(8,128)(2,1)}), bf16[1,197,768]{2,1,0:T(8,128)(2,1)}) %reduce-scatter.33.cloned.1.call-update) | async-done | bytes 302608 | tf_op jit(solution)/shard_map/reduce_scatter | solution.py:51
  456.6 29.3 %reduce-scatter.37.cloned.1.call-done = bf16[1,197,768]{2,1,0:T(8,128)(2,1)} async-done(((bf16[4,197,768]{2,1,0:T(8,128)(2,1)}), bf16[1,197,768]{2,1,0:T(8,128)(2,1)}) %reduce-scatter.37.cloned.1.call-update) | async-done | bytes 302608 | tf_op jit(solution)/shard_map/reduce_scatter | solution.py:51
  568.8 13.9 %all-gather.47.cloned.1.call-done = bf16[4,197,768]{2,1,0:T(8,128)(2,1)} async-done(((bf16[1,197,768]{2,1,0:T(8,128)(2,1)}), bf16[4,197,768]{2,1,0:T(8,128)(2,1)}) %all-gather.47.cloned.1.call-update) | async-done | bytes 1210384 | tf_op jit(solution)/shard_map/all_gather | solution.py:57
  614.1 22.9 %reduce-scatter.43.cloned.1.call-done = bf16[1,197,768]{2,1,0:T(8,128)(2,1)} async-done(((bf16[4,197,768]{2,1,0:T(8,128)(2,1)}), bf16[1,197,768]{2,1,0:T(8,128)(2,1)}) %reduce-scatter.43.cloned.1.call-update) | async-done | bytes 302608 | tf_op jit(solution)/shard_map/reduce_scatter | solution.py:61
  637.0 29.3 %reduce-scatter.39.cloned.1.call-done = bf16[1,197,768]{2,1,0:T(8,128)(2,1)} async-done(((bf16[4,197,768]{2,1,0:T(8,128)(2,1)}), bf16[1,197,768]{2,1,0:T(8,128)(2,1)}) %reduce-scatter.39.cloned.1.call-update) | async-done | bytes 302608 | tf_op jit(solution)/shard_map/reduce_scatter | solution.py:61
  715.5 17.4 %all-gather.57.cloned.1.call-done = bf16[4,197,768]{2,1,0:T(8,128)(2,1)} async-done(((bf16[1,197,768]{2,1,0:T(8,128)(2,1)}), bf16[4,197,768]{2,1,0:T(8,128)(2,1)}) %all-gather.57.cloned.1.call-update) | async-done | bytes 1210384 | tf_op jit(solution)/shard_map/all_gather | solution.py:57
  734.8 17.3 %all-gather.45.cloned.1.call-done = bf16[4,197,768]{2,1,0:T(8,128)(2,1)} async-done(((bf16[1,197,768]{2,1,0:T(8,128)(2,1)}), bf16[4,197,768]{2,1,0:T(8,128)(2,1)}) %all-gather.45.cloned.1.call-update) | async-done | bytes 1210384 | tf_op jit(solution)/shard_map/all_gather | solution.py:57
  818.9 15.2 %reduce-scatter.59.cloned.1.call-done = f32[768,96]{0,1:T(8,128)} async-done(((f32[768,768]{0,1:T(8,128)}), f32[768,96]{0,1:T(8,128)}) %reduce-scatter.59.cloned.1.call-update) | async-done | bytes 294928 | tf_op jit(solution)/shard_map/reduce_scatter | solution.py:80
  836.0 63.0 %reduce-scatter.61.cloned.1.call-done = f32[96,192]{1,0:T(8,128)} async-done(((f32[768,192]{1,0:T(8,128)}), f32[96,192]{1,0:T(8,128)}) %reduce-scatter.61.cloned.1.call-update) | async-done | bytes 73744
  900.5 26.2 %reduce-scatter.49.cloned.1.call-done = bf16[1,197,768]{2,1,0:T(8,128)(2,1)} async-done(((bf16[4,197,768]{2,1,0:T(8,128)(2,1)}), bf16[1,197,768]{2,1,0:T(8,128)(2,1)}) %reduce-scatter.49.cloned.1.call-update) | async-done | bytes 302608 | tf_op jit(solution)/shard_map/reduce_scatter | solution.py:61
  929.2 26.0 %reduce-scatter.45.cloned.1.call-done = bf16[1,197,768]{2,1,0:T(8,128)(2,1)} async-done(((bf16[4,197,768]{2,1,0:T(8,128)(2,1)}), bf16[1,197,768]{2,1,0:T(8,128)(2,1)}) %reduce-scatter.45.cloned.1.call-update) | async-done | bytes 302608 | tf_op jit(solution)/shard_map/reduce_scatter | solution.py:61
  955.2 28.8 %reduce-scatter.41.cloned.1.call-done = bf16[1,197,768]{2,1,0:T(8,128)(2,1)} async-done(((bf16[4,197,768]{2,1,0:T(8,128)(2,1)}), bf16[1,197,768]{2,1,0:T(8,128)(2,1)}) %reduce-scatter.41.cloned.1.call-update) | async-done | bytes 302608 | tf_op jit(solution)/shard_map/reduce_scatter | solution.py:61
  984.0 28.4 %reduce-scatter.53.cloned.1.call-done = bf16[1,197,768]{2,1,0:T(8,128)(2,1)} async-done(((bf16[4,197,768]{2,1,0:T(8,128)(2,1)}), bf16[1,197,768]{2,1,0:T(8,128)(2,1)}) %reduce-scatter.53.cloned.1.call-update) | async-done | bytes 302608 | tf_op jit(solution)/shard_map/reduce_scatter | solution.py:61
  1049.6 47.1 %reduce-scatter.55.cloned.1.call-done = f32[96,3,192]{2,0,1:T(8,128)} async-done(((f32[768,3,192]{2,0,1:T(8,128)}), f32[96,3,192]{2,0,1:T(8,128)}) %reduce-scatter.55.cloned.1.call-update) | async-done | bytes 221200 | tf_op jit(solution)/shard_map/reduce_scatter | solution.py:77
  1098.5 41.5 %all-reduce.5 = (f32[3072]{0:T(1024)S(1)}, f32[768]{0:T(1024)S(1)}, f32[768]{0:T(1024)S(1)}, f32[3072]{0:T(1024)S(1)}, f32[768]{0:T(1024)S(1)}, /*index=5*/f32[7...) all-reduce(f32[3072]{0:T(1024)S(1)} %copy-done.155, ...), channel_id=1, replica_groups=mesh['dp'=8,'mp'=4] {'dp','mp'}, use_global_device_ids=true, to_apply=%region_149.150 | all-reduce | flops 12288 | bytes 98304 | tf_op jit(solution)/shard_map/psum | solution.py:360
  1152.4 40.5 %all-reduce.4 = (f32[]{:T(128)}, f32[4]{0:T(128)S(1)}, f32[4]{0:T(128)S(1)}, f32[12520]{0:T(1024)S(1)}) all-reduce(f32[]{:T(128)S(6)} %add.915, f32[4]{0:T(128)S(1)} %pad_maximum_fusion.17, f32[4]{0:T(128)S(1)} %copy-done.289, f32[12520]{0:T(1024)S(1)} %add_add_fusion.16), channel_id=1, replica_groups=mesh['dp'=8,'mp'=4] {'dp','mp'}, use_global_device_ids=true, to_apply=%region_60.61 | all-reduce | flops 12529 | bytes 100232 | tf_op jit(solution)/shard_map/psum | solution.py:85
  (1145 shorter events, 498.5 us)
Async XLA Ops:
  8.0 97.7 %all-gather.39.cloned.1.call-start = ((), (), s32[]{:S(2)}) async-start(), calls=%async_computation.34 | async-start | bytes 1536000 | tf_op jit(solution)/shard_map/all_gather | solution.py:45
  22.1 87.6 %all-gather.23.cloned.1.call-start = ((), (), s32[]{:S(2)}) async-start(), calls=%async_computation.20 | async-start | bytes 1536000 | tf_op jit(solution)/shard_map/all_gather | solution.py:45
  22.9 92.1 %all-gather.31.cloned.1.call-start = ((), (), s32[]{:S(2)}) async-start(), calls=%async_computation.26 | async-start | bytes 1536000 | tf_op jit(solution)/shard_map/all_gather | solution.py:45
  23.6 96.8 %all-gather.35.cloned.1.call-start = ((), (), s32[]{:S(2)}) async-start(), calls=%async_computation.30 | async-start | bytes 1536000 | tf_op jit(solution)/shard_map/all_gather | solution.py:45
  24.2 158.2 %reduce-scatter.35.cloned.1.call-start = ((), (), s32[]{:S(2)}) async-start(), calls=%async_computation.35 | async-start | bytes 1536000 | tf_op jit(solution)/shard_map/reduce_scatter | solution.py:51
  166.1 82.3 %reduce-scatter.23.cloned.1.call-start = ((), (), s32[]{:S(2)}) async-start(), calls=%async_computation.21 | async-start | bytes 1536000 | tf_op jit(solution)/shard_map/reduce_scatter | solution.py:51
  182.4 88.5 %all-gather.25.cloned.1.call-start = ((), (), s32[]{:S(2)}) async-start(), calls=%async_computation.22 | async-start | bytes 1536000 | tf_op jit(solution)/shard_map/all_gather | solution.py:45
  255.4 96.6 %all-gather.37.cloned.1.call-start = ((), (), s32[]{:S(2)}) async-start(), calls=%async_computation.32 | async-start | bytes 1536000 | tf_op jit(solution)/shard_map/all_gather | solution.py:45
  256.1 115.0 %all-gather.41.cloned.1.call-start = ((), (), s32[]{:S(2)}) async-start(), calls=%async_computation.36 | async-start | bytes 1536000 | tf_op jit(solution)/shard_map/all_gather | solution.py:45
  256.9 142.7 %reduce-scatter.25.cloned.1.call-start = ((), (), s32[]{:S(2)}) async-start(), calls=%async_computation.25 | async-start | bytes 1536000 | tf_op jit(solution)/shard_map/reduce_scatter | solution.py:51
  319.9 108.2 %reduce-scatter.29.cloned.1.call-start = ((), (), s32[]{:S(2)}) async-start(), calls=%async_computation.29 | async-start | bytes 1536000 | tf_op jit(solution)/shard_map/reduce_scatter | solution.py:51
  339.4 117.2 %reduce-scatter.33.cloned.1.call-start = ((), (), s32[]{:S(2)}) async-start(), calls=%async_computation.33 | async-start | bytes 1536000 | tf_op jit(solution)/shard_map/reduce_scatter | solution.py:51
  358.6 127.3 %reduce-scatter.37.cloned.1.call-start = ((), (), s32[]{:S(2)}) async-start(), calls=%async_computation.37 | async-start | bytes 1536000 | tf_op jit(solution)/shard_map/reduce_scatter | solution.py:51
  377.8 163.0 %all-gather.55.cloned.1.call-start = ((), (), s32[]{:S(2)}) async-start(), calls=%async_computation.50 | async-start | bytes 1536000 | tf_op jit(solution)/shard_map/all_gather | solution.py:57
  611.5 97.6 %all-gather.49.cloned.1.call-start = ((), (), s32[]{:S(2)}) async-start(), calls=%async_computation.44 | async-start | bytes 1536000 | tf_op jit(solution)/shard_map/all_gather | solution.py:57
  683.3 134.0 %reduce-scatter.57.cloned.1.call-start = ((), (), s32[]{:S(2)}) async-start(), calls=%async_computation.55 | async-start | bytes 2654208 | tf_op jit(solution)/shard_map/reduce_scatter | solution.py:79
  693.0 141.0 %reduce-scatter.59.cloned.1.call-start = ((), (), s32[]{:S(2)}) async-start(), calls=%async_computation.56 | async-start | bytes 2654208 | tf_op jit(solution)/shard_map/reduce_scatter | solution.py:80
  705.4 193.6 %reduce-scatter.61.cloned.1.call-start = ((), (), s32[]{:S(2)}) async-start(), calls=%async_computation.57 | async-start | bytes 884736
  760.8 165.9 %reduce-scatter.49.cloned.1.call-start = ((), (), s32[]{:S(2)}) async-start(), calls=%async_computation.49 | async-start | bytes 1536000 | tf_op jit(solution)/shard_map/reduce_scatter | solution.py:61
  767.2 188.0 %reduce-scatter.45.cloned.1.call-start = ((), (), s32[]{:S(2)}) async-start(), calls=%async_computation.45 | async-start | bytes 1536000 | tf_op jit(solution)/shard_map/reduce_scatter | solution.py:61
  776.3 207.6 %reduce-scatter.41.cloned.1.call-start = ((), (), s32[]{:S(2)}) async-start(), calls=%async_computation.41 | async-start | bytes 1536000 | tf_op jit(solution)/shard_map/reduce_scatter | solution.py:61
  785.6 226.8 %reduce-scatter.53.cloned.1.call-start = ((), (), s32[]{:S(2)}) async-start(), calls=%async_computation.53 | async-start | bytes 1536000 | tf_op jit(solution)/shard_map/reduce_scatter | solution.py:61
  795.1 301.7 %reduce-scatter.55.cloned.1.call-start = ((), (), s32[]{:S(2)}) async-start(), calls=%async_computation.54 | async-start | bytes 2654208 | tf_op jit(solution)/shard_map/reduce_scatter | solution.py:77
  817.0 397.9 %all-reduce.9.cloned.1.call-start = ((), (), s32[]{:S(2)}) async-start(), calls=%async_computation.58 | async-start | bytes 12091392 | tf_op jit(solution)/shard_map/psum | solution.py:85
  (342 other events, 11920.4 us)
Sparse Core Ops, SparseCore 0:
  22.3 20.4 all-gather.38
  44.9 17.7 all-gather.22
  64.8 17.7 all-gather.30
  84.0 17.7 all-gather.34
  136.3 25.4 reduce-scatter.34
  164.3 25.9 reduce-scatter.30
  192.9 26.0 reduce-scatter.26
  222.4 25.9 reduce-scatter.22
  523.0 17.7 all-gather.54
  542.3 17.7 all-gather.50
  561.6 21.0 all-gather.46
  584.8 17.9 all-gather.42
  676.7 17.7 all-gather.48
  695.9 17.7 all-gather.52
  715.1 17.8 all-gather.56
  734.4 17.7 all-gather.44
  1049.7 165.0 all-reduce.8
Sparse Core Ops, SparseCore 1:
  184.2 40.8 all-gather.26
  253.3 17.6 all-gather.24
  273.5 41.5 all-gather.28
  316.7 16.0 all-gather.32
  334.4 17.5 all-gather.36
  353.5 17.5 all-gather.40
  373.6 25.9 reduce-scatter.24
  402.2 25.9 reduce-scatter.28
  430.6 25.9 reduce-scatter.32
  459.9 25.9 reduce-scatter.36
  549.6 26.2 reduce-scatter.50
  578.7 29.9 reduce-scatter.46
  611.0 25.9 reduce-scatter.42
  640.4 25.9 reduce-scatter.38
  693.1 68.7 reduce-scatter.56
  765.9 68.0 reduce-scatter.58
  837.4 61.5 reduce-scatter.60
  901.7 25.0 reduce-scatter.48
  929.2 25.9 reduce-scatter.44
  958.0 25.9 reduce-scatter.40
  986.4 25.9 reduce-scatter.52
  1016.2 80.5 reduce-scatter.54
where the time goes:
time: 1270 us; the launch traced here: 1250 us
  waiting for transfers between devices  642 us (51%)
  blocking collectives  174 us (14%)
  matrix products  170 us (13%)
  other arithmetic  135 us (11%)
  local copies, waits for them, and re-layouts  75.4 us (6%)
  between operations  54.8 us (4%)
    reduce_scatter x8, waiting for transfers between devices, scatter_rows(): lax.psum_scatter(terms.astype(jnp.bfloat16), 'mp', scatter_dimension=0, t...  166 us
    reduce_scatter x8, waiting for transfers between devices, scatter_grads(): lax.psum_scatter(terms.astype(jnp.bfloat16), 'mp', scatter_dimension=0, t...  162 us
    all_gather x8, waiting for transfers between devices, gather_grads(): return lax.all_gather(grads, 'mp', axis=0, tiled=True)  83.5 us
    unnamed x40, waiting for transfers between devices  67.5 us
    all_gather x8, waiting for transfers between devices, gather_rows(): lax.all_gather(rows, 'mp', axis=0, tiled=True)  51.4 us
    unnamed x705, local copies, waits for them, and re-layouts  48.7 us
    reduce_scatter x1, waiting for transfers between devices, reduce_block(): lax.psum_scatter(grads[0], 'dp', scatter_dimension=0, tiled=True)  47.1 us
    psum x1, blocking collectives, local(): lax.psum((place(jnp.sum(squared_in, (1, 2)), D, row_start, 0), place(jnp....  41.5 us
  transfers between devices with their start and end apart: 39, of which 29 were waited for; matrix products, arithmetic and copies ran while one was open for 21% of the time, Pallas kernels for 0%

commit v1 on v0

v1 whole, which is shorter than its diff:
```python
import functools

import jax
import jax.numpy as jnp
from jax import lax
from jax.experimental import pallas as pl
from jax.experimental.pallas import tpu as pltpu
from jax.sharding import PartitionSpec as P

D = 768
HEAD_DIM = 64
FF = 3072
CLASSES = 1000

eps_norm = 1e-06
eps_one = 1e-30
eps_two = 0.001
decay_rate = 0.5
clip_level = 0.3
step_rate = 1.0
smoothing = 0.1

ALL = ("dp", "mp")
f32 = jnp.float32
bf16 = jnp.bfloat16


class Chain:
    def __init__(self, stages):
        self.stages = stages
        self.result = None
        self.flight = next(stages)

    def advance(self, arrived):
        try:
            self.flight = self.stages.send(arrived)
        except StopIteration as end:
            self.flight, self.result = (), end.value


def sync(chains, *values):
    chains = [chain if isinstance(chain, tuple) else (chain,) for chain in chains]
    flights = [(chain[0].flight,) + chain[1:] for chain in chains]
    flights, values = lax.optimization_barrier((flights, values))
    for chain, flight in zip(chains, flights):
        chain[0].advance(flight if len(flight) > 1 else flight[0])
    return values[0] if len(values) == 1 else values


class Plain:
    blocks = None

    def __init__(self, rows, cols):
        self.rows, self.cols = rows, cols
        self.place = jnp.stack(
            [jnp.zeros((), jnp.int32)] * 4 + [lax.axis_index("dp"), lax.axis_index("mp")]
        ).astype(jnp.int32)

    def gather(self, piece):
        full = lax.all_gather(piece, ALL, axis=0)
        full = full.reshape((self.rows, self.cols) + piece.shape).swapaxes(0, 1)
        for _ in range(4):
            yield ()
        return (full.reshape(self.cols, self.rows * piece.shape[0], piece.shape[1]),)

    def whole(self, full):
        return full

    def mixed(self, body, full):
        return body(((full, False),), ())

    def reduce(self, far):
        _, near = yield ()
        grads = jnp.stack([near[1], far[1], near[0], far[0]])
        grads = grads.reshape(self.cols, self.rows, -1, grads.shape[2])
        grads = grads.swapaxes(0, 1).reshape((-1,) + grads.shape[2:])
        total = lax.psum_scatter(grads, ALL, scatter_dimension=0).astype(f32)
        for _ in range(3):
            total = yield total
        return total

    def add(self, values):
        values = lax.psum(values, ALL)
        for _ in range(5):
            values = yield values
        return values

    def add_large(self, values):
        values = lax.psum(values, ALL)
        for _ in range(8):
            values = yield values
        return values


def joined(mine, theirs, index):
    return jnp.where(
        index == 0, jnp.concatenate([mine, theirs]), jnp.concatenate([theirs, mine])
    )


def assemble(place_ref, mine_ref, theirs_ref, full_ref, sems):
    z, x, y, core = (place_ref[i] for i in range(4))
    deep, size = mine_ref.shape[1], mine_ref.shape[2]
    copies = []
    for side, source in enumerate((mine_ref, theirs_ref)):
        owner = core if side == 0 else 1 - core
        for quarter in range(4):
            second, first = quarter % 2, quarter // 2
            its_x = x ^ jnp.where(owner == 1, first, second)
            its_y = y ^ jnp.where(owner == 1, second, first)
            for level in range(deep):
                block = lax.rem(z + level, deep) * 2 + its_x
                copies.append(
                    pltpu.make_async_copy(
                        source.at[quarter, level],
                        full_ref.at[its_y * 2 + owner, block],
                        sems.at[len(copies)],
                    )
                )
    for copy in copies:
        copy.start()
    for copy in copies:
        copy.wait()


class Grid:
    deep, devices, blocks = 4, 32, 8

    def __init__(self):
        dp, mp = lax.axis_index("dp"), lax.axis_index("mp")
        self.z, self.x, self.y, self.core = dp // 2, dp % 2, mp // 2, mp % 2
        self.place = jnp.stack([self.z, self.x, self.y, self.core, dp, mp]).astype(jnp.int32)
        self.at_first = jnp.where(self.core == 0, self.y, self.x)
        self.at_second = jnp.where(self.core == 0, self.x, self.y)
        self.other = self.pairs(lambda z, x, y, c: (z, x, y, 1 - c))
        self.first = self.pairs(lambda z, x, y, c: (z, x ^ c, y ^ (1 - c), c))
        self.second = self.pairs(lambda z, x, y, c: (z, x ^ (1 - c), y ^ c, c))
        self.along_x = self.pairs(lambda z, x, y, c: (z, 1 - x, y, c))
        self.along_y = self.pairs(lambda z, x, y, c: (z, x, 1 - y, c))
        self.up = [self.pairs(lambda z, x, y, c, s=s: ((z + s) % 4, x, y, c)) for s in range(4)]
        self.flip_z = [self.pairs(lambda z, x, y, c, s=s: (z ^ s, x, y, c)) for s in range(4)]

    def pairs(self, move):
        table = []
        for index in range(self.devices):
            z, x, y, c = move(index // 8, index // 4 % 2, index // 2 % 2, index % 2)
            table.append((index, ((z * 2 + x) * 2 + y) * 2 + c))
        return table

    @staticmethod
    def send(values, table):
        return lax.ppermute(values, ALL, table)

    def gather(self, piece):
        got = yield [self.send(piece, self.up[-s]) for s in (1, 2, 3)]
        column = jnp.stack([piece] + got)[None]
        got = yield self.send(column, self.second)
        pair = jnp.concatenate([column, got])
        got = yield self.send(pair, self.first)
        quad = jnp.concatenate([pair, got])
        theirs = yield self.send(quad, self.other)
        return quad, theirs

    def mixed(self, body, quad, theirs):
        full = (4, self.blocks) + quad.shape[2:]
        return body(
            ((quad, "any"), (theirs, "any")), ((full, quad.dtype), ((self.devices,), None))
        )

    def whole(self, quad, theirs):
        r, c = quad.shape[2:]
        full = pl.pallas_call(
            assemble,
            in_specs=[
                pl.BlockSpec(memory_space=pltpu.SMEM),
                pl.BlockSpec(memory_space=pl.ANY),
                pl.BlockSpec(memory_space=pl.ANY),
            ],
            out_specs=pl.BlockSpec(memory_space=pltpu.VMEM),
            out_shape=jax.ShapeDtypeStruct((4, self.blocks, r, c), quad.dtype),
            scratch_shapes=[pltpu.SemaphoreType.DMA((self.devices,))],
            compiler_params=pltpu.CompilerParams(vmem_limit_bytes=16 * 1024 * 1024),
        )(self.place, quad, theirs)
        return full.reshape(4, self.blocks * r, c)

    def reduce(self, far):
        theirs, near = yield self.send(far, self.other)
        shape = (4, self.deep, near.shape[1] // self.blocks, near.shape[2])
        near, theirs = near.reshape(shape), theirs.reshape(shape)

        def chip(index):
            return (
                lax.dynamic_index_in_dim(near, index, 0, keepdims=False).astype(f32)
                + lax.dynamic_index_in_dim(theirs, index, 0, keepdims=False).astype(f32)
            )

        got = yield self.send(jnp.stack([chip(0), chip(1 + self.core)]).astype(bf16), self.first)
        away = (chip(2 - self.core) + got[0].astype(f32)).astype(bf16)
        came = yield self.send(away, self.second)
        column = chip(3) + got[1].astype(f32) + came.astype(f32)
        low = column.astype(bf16)
        total = column[0]
        for part in (yield [self.send(low[s], self.up[s]) for s in (1, 2, 3)]):
            total = total + part.astype(f32)
        return total

    def add(self, values):
        for table in (self.other, self.along_y, self.along_x, self.flip_z[1], self.flip_z[2]):
            values = values + (yield self.send(values, table))
        return values

    def add_large(self, values):
        shape = values.shape
        values = values.reshape((self.devices, -1) + shape[1:])
        steps = (
            (self.core, self.other),
            (self.at_first, self.first),
            (self.at_second, self.second),
        )
        for index, table in steps:
            half = values.shape[0] // 2
            theirs = lax.dynamic_slice_in_dim(values, (1 - index) * half, half, 0)
            got = yield self.send(theirs.astype(bf16), table)
            mine = lax.dynamic_slice_in_dim(values, index * half, half, 0)
            values = mine.astype(f32) + got.astype(f32)
        low = values.astype(bf16)
        parts = [
            lax.dynamic_index_in_dim(low, (self.z + s) % 4, 0, keepdims=False) for s in (1, 2, 3)
        ]
        total = lax.dynamic_index_in_dim(values, self.z, 0, keepdims=False)
        for part in (yield [self.send(part, self.up[s]) for s, part in enumerate(parts, 1)]):
            total = total + part.astype(f32)
        total = total.astype(bf16)
        got = yield [self.send(total, self.up[-s]) for s in (1, 2, 3)]
        pile = jnp.stack([total] + got)
        pile = lax.dynamic_slice_in_dim(jnp.concatenate([pile, pile]), 4 - self.z, 4, 0)
        for index, table in reversed(steps):
            pile = joined(pile, (yield self.send(pile, table)), index)
        return pile.reshape(shape)


def layer_norm(values, gain, shift):
    centred = values - jnp.mean(values, -1, keepdims=True)
    variance = jnp.mean(centred * centred, -1, keepdims=True)
    return centred * lax.rsqrt(variance + eps_norm) * gain + shift


def pieces_of(vectors):
    widths = [D] * 8 + [FF] + [D] * 3 + [CLASSES]
    pieces = []
    offset = 0
    for extent in widths:
        pieces.append(vectors[offset : offset + extent])
        offset = offset + extent
    return pieces


def product(form, left, right):
    return jnp.einsum(form, left, right, preferred_element_type=f32)


def factored_step(weight, square, grad, rows, cols):
    squared = grad * grad + eps_one
    rows_new = decay_rate * rows + (1.0 - decay_rate) * jnp.mean(squared, 1)
    cols_new = decay_rate * cols + (1.0 - decay_rate) * jnp.mean(squared, 0)
    denominator = rows_new[:, None] * cols_new[None, :] / jnp.mean(rows_new)
    update = grad * lax.rsqrt(denominator)
    update = update / jnp.maximum(1.0, jnp.sqrt(jnp.mean(update * update)) / clip_level)
    magnitude = jnp.maximum(eps_two, jnp.sqrt(square / weight.size))
    return (weight - step_rate * magnitude * update, rows_new, cols_new)


def vector_step(vectors, square, grad, second):
    second_new = decay_rate * second + (1.0 - decay_rate) * (grad * grad + eps_one)
    update = grad * lax.rsqrt(second_new)
    update = update / jnp.maximum(1.0, jnp.sqrt(jnp.mean(update * update)) / clip_level)
    magnitude = jnp.maximum(eps_two, jnp.sqrt(square / vectors.size))
    return (vectors - step_rate * magnitude * update, second_new)


def normal_parts(values):
    centred = values - jnp.mean(values, -1, keepdims=True)
    inverse = lax.rsqrt(jnp.mean(centred * centred, -1, keepdims=True) + eps_norm)
    return centred * inverse, inverse


def pull_normal(values, gain, grads):
    hat, inverse = normal_parts(values)
    scaled = grads * gain
    mean_one = jnp.mean(scaled, -1, keepdims=True)
    mean_two = jnp.mean(scaled * hat, -1, keepdims=True)
    below = (scaled - mean_one - hat * mean_two) * inverse
    return below, jnp.sum(grads * hat, 0, keepdims=True), jnp.sum(grads, 0, keepdims=True)


def dot(left, right, left_dim=1, right_dim=0):
    return lax.dot_general(
        left, right, (((left_dim,), (right_dim,)), ((), ())), preferred_element_type=f32
    )


def probabilities(query, key, visible):
    scores = dot(query, key, 1, 1) * HEAD_DIM ** (-0.5)
    scores = jnp.where(visible, scores, -1e30)
    raised = jnp.exp(scores - jnp.max(scores, -1, keepdims=True))
    return raised * (1.0 / jnp.sum(raised, -1, keepdims=True))


def head_masks(share):
    lane = lax.broadcasted_iota(jnp.int32, (1, share), 1) // HEAD_DIM
    return [lane == head for head in range(share // HEAD_DIM)]


def stacked(rows, masks):
    return jnp.concatenate([jnp.where(mask, rows, jnp.zeros((), rows.dtype)) for mask in masks])


def unstacked(every, masks):
    size = every.shape[0] // len(masks)
    result = every[:size]
    for head, mask in enumerate(masks[1:], 1):
        result = jnp.where(mask, every[head * size : (head + 1) * size], result)
    return result


def turn(place_ref, values, result_ref, blocks):
    turned = values.T
    if blocks is None:
        result_ref[...] = turned
        return
    size, deep = turned.shape[0] // blocks, blocks // 2
    for block in range(blocks):
        level = lax.rem(block // 2 - place_ref[0] + deep, deep)
        spot = (1 - (block % 2 ^ place_ref[1])) * deep + level
        rows = pl.ds(pl.multiple_of(spot * size, size), size)
        result_ref[rows, :] = turned[block * size : (block + 1) * size, :]


def attend_kernel(
    place_ref,
    rows_ref,
    weight_ref,
    query_bias_ref,
    value_bias_ref,
    present_ref,
    stream_ref,
    bias_ref,
    gain_ref,
    shift_ref,
    column_ref,
    qkv_ref,
    attended_ref,
    stream_out_ref,
    rows_out_ref,
    turned_one_ref,
    turned_two_ref,
    sum_ref,
    *,
    blocks,
):
    step = pl.program_id(0)
    count, padded = present_ref.shape
    share = attended_ref.shape[2]
    weight = weight_ref[0]

    @pl.when(step == 0)
    def _():
        turn(place_ref, rows_ref[...], turned_one_ref, blocks)

    projected = dot(rows_ref[...], weight[:, : 3 * share])
    query = (projected[:, :share] + query_bias_ref[0]).astype(bf16)
    key = projected[:, share : 2 * share].astype(bf16)
    value = (projected[:, 2 * share :] + value_bias_ref[0]).astype(bf16)
    qkv_ref[0, 0] = query
    qkv_ref[0, 1] = key
    qkv_ref[0, 2] = value
    masks = head_masks(share)
    for image in range(count):
        span = slice(image * padded, (image + 1) * padded)
        visible = present_ref[image : image + 1, :] > 0.5
        low = probabilities(stacked(query[span], masks), key[span], visible).astype(bf16)
        every = dot(low, value[span])
        attended_ref[0, span, :] = unstacked(every, masks).astype(bf16)
    part = dot(attended_ref[0], weight[:, 3 * share :], 1, 1)

    @pl.when(step == 0)
    def _():
        stream_out_ref[...] = stream_ref[...] + bias_ref[...] + part

    @pl.when(step > 0)
    def _():
        stream_out_ref[...] += part

    @pl.when(step == pl.num_programs(0) - 1)
    def _():
        hat, _ = normal_parts(stream_out_ref[...])
        rows_two = (hat * gain_ref[...] + shift_ref[...]).astype(bf16)
        rows_out_ref[...] = rows_two
        turn(place_ref, rows_two, turned_two_ref, blocks)
        for image in range(count):
            span = slice(image * padded, (image + 1) * padded)
            line = jnp.sum(stream_out_ref[span, :] * column_ref[span, :], 0, keepdims=True)
            sum_ref[image : image + 1, :] = line
            sum_ref[image + count : image + count + 1, :] = line


def hidden_kernel(
    place_ref, rows_ref, weight_ref, bias_ref, chooser_ref, column_ref, sum_ref, slope_ref
):
    hidden = dot(rows_ref[...], weight_ref[0]) + bias_ref[0]
    first, second = 0.7978845608028654, 0.044715
    square = hidden * hidden
    bent = jnp.tanh(first * hidden * (1.0 + second * square))
    half = 0.5 * (1.0 + bent)
    active = (hidden * half).astype(bf16)
    sum_ref[0] = dot(chooser_ref[...], active)
    slope = half + 0.5 * hidden * (1.0 - bent * bent) * first * (1.0 + 3.0 * second * square)
    slope_ref[0] = (slope * column_ref[...]).astype(bf16)


def expand_back_kernel(
    place_ref,
    turned_ref,
    weight_ref,
    slope_ref,
    d_active_ref,
    *refs,
):
    grad_ref, bias_ref, d_rows_ref, d_hidden_low = refs[-4:]
    step = pl.program_id(0)
    count = d_active_ref.shape[1] // 2
    padded = slope_ref.shape[1] // count
    bias = jnp.zeros((1, d_hidden_low.shape[1]), f32)
    for image in range(count):
        span = slice(image * padded, (image + 1) * padded)
        d_hidden = slope_ref[0, span, :].astype(f32) * d_active_ref[0, image : image + 1, :]
        bias = bias + jnp.sum(d_hidden, 0, keepdims=True)
        d_hidden_low[span, :] = d_hidden.astype(bf16)
    bias_ref[0] = bias
    grad_ref[0] = dot(turned_ref[...], d_hidden_low[...]).astype(bf16)
    part = dot(d_hidden_low[...], weight_ref[0], 1, 1)

    @pl.when(step == 0)
    def _():
        d_rows_ref[...] = part + refs[0][...] if len(refs) > 4 else part

    @pl.when(step > 0)
    def _():
        d_rows_ref[...] += part


def between_kernel(
    place_ref,
    d_rows_ref,
    d_row_ref,
    column_ref,
    stream_ref,
    gain_ref,
    d_stream_ref,
    d_low_ref,
    turned_ref,
    vector_ref,
    *,
    blocks,
):
    count = d_row_ref.shape[0] // 2
    padded = stream_ref.shape[0] // count
    below, gain, shift = pull_normal(stream_ref[...], gain_ref[...], d_rows_ref[...])
    vector_ref[1:2, :] = gain
    vector_ref[2:3, :] = shift
    bias = jnp.zeros((1, below.shape[1]), f32)
    for image in range(count):
        span = slice(image * padded, (image + 1) * padded)
        d_stream = below[span] + d_row_ref[image : image + 1, :] * column_ref[span, :]
        bias = bias + jnp.sum(d_stream, 0, keepdims=True)
        d_stream_ref[span, :] = d_stream
        d_low_ref[span, :] = d_stream.astype(bf16)
    vector_ref[0:1, :] = bias
    turn(place_ref, d_low_ref[...], turned_ref, blocks)


def attend_back_kernel(
    place_ref,
    turned_ref,
    weight_ref,
    qkv_ref,
    attended_ref,
    column_ref,
    d_low_ref,
    d_turned_ref,
    *refs,
):
    grad_ref, bias_ref, d_rows_ref, d_projected = refs[-4:]
    step = pl.program_id(0)
    share = attended_ref.shape[2]
    count = bias_ref.shape[1] // 2
    padded = attended_ref.shape[1] // count
    scale = HEAD_DIM ** (-0.5)
    weight = weight_ref[0]
    d_attended = dot(d_low_ref[...], weight[:, 3 * share :]).astype(bf16)
    masks = head_masks(share)
    for image in range(count):
        span = slice(image * padded, (image + 1) * padded)
        hidden = column_ref[span, :] < 0.5
        query, key, value = (qkv_ref[0, part, span, :] for part in range(3))
        query = query * jnp.asarray(scale, bf16)
        queries = stacked(query, masks)
        d_images = stacked(d_attended[span], masks)
        scores = jnp.where(hidden, -1e30, dot(key, queries, 1, 1))
        raised = jnp.exp(scores - jnp.max(scores, 0, keepdims=True))
        probs = raised * (1.0 / jnp.sum(raised, 0, keepdims=True))
        d_probs = dot(value, d_images, 1, 1)
        inner = jnp.sum(probs * d_probs, 0, keepdims=True)
        d_scores = (probs * (d_probs - inner)).astype(bf16)
        d_value = dot(probs.astype(bf16), d_images)
        d_key = dot(d_scores, queries)
        d_query = unstacked(dot(d_scores, key, 0, 0), masks) * scale
        bias_ref[0, image : image + 1, :] = jnp.sum(d_query, 0, keepdims=True)
        bias_ref[0, count + image : count + image + 1, :] = jnp.sum(d_value, 0, keepdims=True)
        d_projected[span, :share] = d_query.astype(bf16)
        d_projected[span, share : 2 * share] = d_key.astype(bf16)
        d_projected[span, 2 * share :] = d_value.astype(bf16)
    grad_ref[0, :, : 3 * share] = dot(turned_ref[...], d_projected[...]).astype(bf16)
    grad_ref[0, :, 3 * share :] = dot(d_turned_ref[...], attended_ref[0]).astype(bf16)
    part = dot(d_projected[...], weight[:, : 3 * share], 1, 1)

    @pl.when(step == 0)
    def _():
        d_rows_ref[...] = part + refs[0][...] if len(refs) > 4 else part

    @pl.when(step > 0)
    def _():
        d_rows_ref[...] += part


def stem_back_kernel(
    place_ref, d_rows_ref, d_stream_ref, stream_ref, gain_ref, pixels_ref, both_ref, vector_ref
):
    rows, width = pixels_ref.shape
    padded = both_ref.shape[0] - width
    below, gain, shift = pull_normal(stream_ref[...], gain_ref[...], d_rows_ref[...])
    vector_ref[0:1, :] = gain
    vector_ref[1:2, :] = shift
    below = below + d_stream_ref[...]
    slots = vector_ref.shape[0] - 8
    table = below[:slots]
    for image in range(1, rows // slots):
        table = table + below[image * slots : (image + 1) * slots]
    vector_ref[8:, :] = table
    both_ref[:width, :] = dot(pixels_ref[...].T, below.astype(bf16)).astype(bf16)
    both_ref[width : width + slots, :] = table.astype(bf16)
    both_ref[width + slots :, :] = jnp.zeros((padded - slots, both_ref.shape[1]), bf16)


def classify(pooled, labels, head, gain, shift, bias, inverse_count):
    hat, inverse = normal_parts(pooled)
    low = (hat * gain + shift).astype(bf16)
    logits = dot(low, head) + bias
    logits = logits - jnp.max(logits, -1, keepdims=True)
    raised = jnp.exp(logits)
    total = jnp.sum(raised, -1, keepdims=True)
    lane = lax.broadcasted_iota(jnp.int32, logits.shape, 1)
    target = jnp.where(lane == labels.astype(jnp.int32), 1.0 - smoothing, 0.0) + smoothing / CLASSES
    score = jnp.sum(target * (logits - jnp.log(total)), -1, keepdims=True)
    d_logits = (raised * (1.0 / total) - target) * inverse_count
    d_final = dot(d_logits.astype(bf16), head, 1, 1)
    scaled = d_final * gain
    mean_one = jnp.mean(scaled, -1, keepdims=True)
    mean_two = jnp.mean(scaled * hat, -1, keepdims=True)
    return score, low, d_logits, d_final, hat, (scaled - mean_one - hat * mean_two) * inverse


def split(values):
    high = values.astype(bf16)
    return high, (values - high.astype(f32)).astype(bf16)


def own_head_kernel(
    place_ref,
    active_ref,
    sum_ref,
    facts_ref,
    contract_bias_ref,
    gain_ref,
    shift_ref,
    head_ref,
    head_bias_ref,
    *refs,
    inverse_count,
):
    if len(refs) == 4:
        full_ref, piece_ref, d_row_ref, d_active_ref = refs
    else:
        mine_ref, theirs_ref, piece_ref, d_row_ref, d_active_ref, full_ref, sems = refs
        assemble(place_ref, mine_ref, theirs_ref, full_ref, sems)
    groups, twice, width = active_ref.shape
    rows = sum_ref.shape[1]
    mixed = jnp.zeros((twice, rows), f32)
    for group in range(groups):
        weight = full_ref[group].reshape(rows, width)
        for part in split(active_ref[group]):
            mixed = mixed + dot(part, weight, 1, 1)
    kept, labels = facts_ref[:, 0:1], facts_ref[:, 1:2]
    pooled = (sum_ref[...] + mixed) / kept + contract_bias_ref[...]
    d_pooled = classify(
        pooled,
        labels,
        head_ref[...],
        gain_ref[...],
        shift_ref[...],
        head_bias_ref[...],
        inverse_count,
    )[-1]
    d_row = d_pooled / kept
    d_row_ref[...] = d_row
    d_row_low = d_row.astype(bf16)
    first = lax.broadcasted_iota(jnp.int32, (twice, 1), 0) < twice // 2
    for group in range(groups):
        d_active_ref[group] = dot(d_row_low, full_ref[group].reshape(rows, width))
    for part, (line, fact) in enumerate(zip(split(pooled), split(facts_ref[...]))):
        piece_ref[part * twice : (part + 1) * twice, :rows] = line
        piece_ref[part * twice : (part + 1) * twice, rows:] = fact
    for half in range(groups // 2):
        line = jnp.where(first, active_ref[2 * half], active_ref[2 * half + 1])
        span = slice((2 + half) * twice, (3 + half) * twice)
        piece_ref[span, :rows] = line.astype(bf16)
        piece_ref[span, rows:] = jnp.zeros((twice, piece_ref.shape[1] - rows), bf16)


def all_head_kernel(
    place_ref,
    pieces_ref,
    gain_ref,
    shift_ref,
    head_ref,
    head_bias_ref,
    grad_ref,
    contract_ref,
    vector_ref,
    bias_ref,
    *,
    inverse_count,
):
    pieces = pieces_ref[0].astype(f32)
    count, rows = pieces.shape[0], gain_ref.shape[1]
    twice = pieces.shape[1] // 4

    def part(index):
        return pieces[:, index * twice : (index + 1) * twice].reshape(count * twice, -1)

    lines = part(0) + part(1)
    pooled, kept, labels = lines[:, :rows], lines[:, rows : rows + 1], lines[:, rows + 1 : rows + 2]
    score, low, d_logits, d_final, hat, d_pooled = classify(
        pooled,
        labels,
        head_ref[...],
        gain_ref[...],
        shift_ref[...],
        head_bias_ref[...],
        inverse_count,
    )
    half = lax.broadcasted_iota(jnp.int32, (count * twice, 1), 0) % twice // (twice // 2)
    once = half == 0
    d_logits = jnp.where(once, d_logits, 0.0)
    own = place_ref[5]
    active = jnp.where(own // 2 == 0, part(2)[:, :rows], part(3)[:, :rows]).astype(bf16)
    d_row = jnp.where(half == own % 2, d_pooled / kept, 0.0).astype(bf16)
    share = contract_ref.shape[0]
    line = lax.broadcasted_iota(jnp.int32, (rows, share), 0)
    lane = lax.broadcasted_iota(jnp.int32, (rows, share), 1)
    chooser = (line == lane + place_ref[4] * share).astype(f32).astype(bf16)
    d_row = dot(d_row, chooser).astype(bf16)

    def total(values):
        return jnp.sum(jnp.where(once, values, 0.0), 0, keepdims=True)

    results = (
        (grad_ref, slice(None), dot(low, d_logits.astype(bf16), 0, 0)),
        (contract_ref, slice(None), dot(d_row, active, 0, 0)),
        (vector_ref, slice(0, 1), total(d_pooled)),
        (vector_ref, slice(1, 2), total(d_final * hat)),
        (vector_ref, slice(2, 3), total(d_final)),
        (bias_ref, slice(0, 1), jnp.sum(d_logits, 0, keepdims=True)),
        (bias_ref, slice(1, 2), -total(score) + jnp.zeros((1, bias_ref.shape[1]), f32)),
    )
    for ref, span, value in results:

        @pl.when(pl.program_id(0) == 0)
        def _(ref=ref, span=span, value=value):
            ref[span, :] = value

        @pl.when(pl.program_id(0) > 0)
        def _(ref=ref, span=span, value=value):
            ref[span, :] += value


def layout(data, groups):
    return 0, data, data + 5 * groups, -(-(data + 5 * groups + 6) // 8) * 8


def across(column):
    n = column.shape[0]
    wide = jnp.broadcast_to(column, (n, 128))
    if n < 128:
        wide = jnp.concatenate([wide, jnp.zeros((128 - n, 128), f32)])
    return wide.T[0:1]


def down(row, n):
    return jnp.broadcast_to(row, (128, 128)).T[:n, 0:1]


def put(count, index, line):
    spot = lax.broadcasted_iota(jnp.int32, (count, 1), 0)
    return jnp.where(spot == index, line, 0.0)


def pick(lines, index):
    spot = lax.broadcasted_iota(jnp.int32, (lines.shape[0], 1), 0)
    return jnp.sum(jnp.where(spot == index, lines, 0.0), 0, keepdims=True)


def sums_kernel(
    place_ref,
    attend_ref,
    expand_ref,
    contract_ref,
    squares_ref,
    vector_one_ref,
    vector_two_ref,
    expand_far_ref,
    expand_near_ref,
    heads_far_ref,
    heads_near_ref,
    sums_ref,
    *,
    data,
    groups,
    share,
    patch_count,
):
    block, group = place_ref[4], place_ref[5]
    own = place_ref[2] * 2 + place_ref[3]
    _, at_group, at_single, _ = layout(data, groups)
    sums_ref[...] = jnp.zeros(sums_ref.shape, f32)
    lane = lax.broadcasted_iota(jnp.int32, (1, attend_ref.shape[1]), 1)
    for index, ref in enumerate((attend_ref, expand_ref, contract_ref)):
        grad = ref[...]
        squared = grad * grad + eps_one
        span = slice(at_group + index * groups, at_group + (index + 1) * groups)
        sums_ref[span, :] = put(groups, group, jnp.sum(squared, 0, keepdims=True))
        if index == 0:
            lines = (
                jnp.sum(jnp.where(lane < 3 * share, squared, 0.0), 1, keepdims=True),
                jnp.sum(jnp.where(lane < 3 * share, 0.0, squared), 1, keepdims=True),
            )
        else:
            lines = (jnp.sum(squared, 1, keepdims=True),)
        for part, line in enumerate(lines):
            spot = (index + (index > 0) + part) * 128
            sums_ref[:data, spot : spot + 128] = put(data, block, across(line))
    sums_ref[:data, 512:640] = put(data, block, squares_ref[...])
    at_group += 3 * groups
    lines = jnp.zeros((groups, expand_far_ref.shape[2]), f32)
    for ref, order in ((expand_far_ref, (3, 1)), (expand_near_ref, (2, 0))):
        for step, distance in enumerate(order):
            lines = lines + put(groups, own ^ distance, ref[step])
    sums_ref[at_group : at_group + groups, :] = lines
    at_group += groups
    count = heads_far_ref.shape[1] // 2
    for at, span in ((0, slice(count)), (256, slice(count, 2 * count))):
        lines = jnp.zeros((groups, share), f32)
        for ref, order in ((heads_far_ref, (3, 1)), (heads_near_ref, (2, 0))):
            for step, distance in enumerate(order):
                line = jnp.sum(ref[step][span], 0, keepdims=True)
                lines = lines + put(groups, own ^ distance, line)
        sums_ref[at_group : at_group + groups, at : at + share] = lines
    stem_bias = jnp.sum(vector_one_ref[8 : 8 + patch_count, :], 0, keepdims=True)
    singles = (stem_bias, vector_one_ref[0:2, :], vector_two_ref[0:3, :])
    for line in singles:
        sums_ref[at_single : at_single + line.shape[0], :] = line
        at_single += line.shape[0]


def renew_kernel(
    place_ref,
    sums_ref,
    rows_ref,
    cols_ref,
    attend_ref,
    expand_ref,
    contract_ref,
    rows_new_ref,
    cols_new_ref,
    update_ref,
    scalar_ref,
    square_ref,
    *,
    data,
    groups,
    share,
):
    block, group = place_ref[4], place_ref[5]
    size = attend_ref.shape[0]
    width = attend_ref.shape[1]
    _, at_group, _, _ = layout(data, groups)
    length, hidden = data * size, groups * width
    lane = lax.broadcasted_iota(jnp.int32, (1, width), 1)
    first = lane < 3 * share
    spare = lax.broadcasted_iota(jnp.int32, (1, 128), 1) < size
    counts = (3 * length, length, hidden, hidden)
    means = []
    for index, count in enumerate(counts):
        span = slice(index * 128, (index + 1) * 128)
        new = decay_rate * rows_ref[:, span] + (1.0 - decay_rate) * (sums_ref[:data, span] / count)
        rows_new_ref[:, span] = new
        means.append(jnp.sum(jnp.where(spare, new, 0.0), keepdims=True) / length)
    for index, count in enumerate((length, length, length)):
        span = slice(index * groups, (index + 1) * groups)
        lines = sums_ref[at_group + index * groups : at_group + (index + 1) * groups, :]
        new = decay_rate * cols_ref[span, :] + (1.0 - decay_rate) * (lines / count)
        cols_new_ref[span, :] = new
        if index == 0:
            means[1] = jnp.sum(jnp.where(first, 0.0, new), keepdims=True) / length
        if index == 2:
            means[3] = jnp.sum(new, keepdims=True) / hidden
    scalars = jnp.zeros((1, 128), f32)
    place_lane = lax.broadcasted_iota(jnp.int32, (1, 128), 1)
    for index, ref in enumerate((attend_ref, expand_ref, contract_ref)):
        across_row = pick(cols_new_ref[index * groups : (index + 1) * groups, :], group)

        def row(which):
            span = slice(which * 128, (which + 1) * 128)
            return down(pick(rows_new_ref[:, span], block), size)

        if index == 0:
            denominator = jnp.where(
                first, row(0) * across_row / means[0], row(1) * across_row / means[1]
            )
        else:
            denominator = row(index + 1) * across_row / means[index + 1]
        update = ref[...] * lax.rsqrt(denominator)
        update_ref[index] = update
        squared = update * update
        if index == 0:
            totals = (jnp.where(first, squared, 0.0), jnp.where(first, 0.0, squared))
        else:
            totals = (squared,)
        for part, total in enumerate(totals):
            spot = index + (index > 0) + part
            scalars = jnp.where(place_lane == spot, jnp.sum(total, keepdims=True), scalars)
    scalar_ref[...] = jnp.broadcast_to(scalars, scalar_ref.shape)
    squares = jnp.sum(sums_ref[:data, 512:640], 0, keepdims=True)
    square_ref[...] = jnp.broadcast_to(squares, square_ref.shape)


def step_kernel(
    place_ref,
    update_ref,
    scalar_ref,
    square_ref,
    attend_ref,
    expand_ref,
    contract_ref,
    in_ref,
    in_low_ref,
    out_ref,
    out_low_ref,
    expand_new_ref,
    expand_low_ref,
    contract_new_ref,
    contract_low_ref,
    *,
    sizes,
):
    share = in_ref.shape[2]
    scales = []
    for index, size in enumerate(sizes):
        total = scalar_ref[0:1, index : index + 1]
        square = square_ref[0:1, index : index + 1]
        clip = jnp.maximum(1.0, jnp.sqrt(total / size) / clip_level)
        scales.append(step_rate * jnp.maximum(eps_two, jnp.sqrt(square / size)) / clip)
    lane = lax.broadcasted_iota(jnp.int32, (1, attend_ref.shape[1]), 1)
    scale = jnp.where(lane < 3 * share, scales[0], scales[1])
    attend = attend_ref[...] - scale * update_ref[0]
    for part in range(3):
        lines = attend[:, part * share : (part + 1) * share]
        in_ref[part] = lines
        in_low_ref[part] = lines.astype(bf16)
    out = attend[:, 3 * share :].T
    out_ref[...] = out
    out_low_ref[...] = out.astype(bf16)
    expand = expand_ref[...] - scales[2] * update_ref[1]
    expand_new_ref[...] = expand
    expand_low_ref[...] = expand.astype(bf16)
    contract = (contract_ref[...] - scales[3] * update_ref[2]).T
    contract_new_ref[...] = contract
    contract_low_ref[...] = contract.astype(bf16)


def call(body, groups, place, operands, results, scratch=(), flops=0, turns=None):
    def group(step, place_ref):
        if turns is None:
            return step
        return (place_ref[2] * 2 + place_ref[3]) ^ (turns[0] + turns[1] * step)

    def spec(shape, by_group, index):
        if by_group == "any":
            return pl.BlockSpec(memory_space=pl.ANY)
        if by_group:
            return pl.BlockSpec((1,) + shape[1:], lambda g, p: (index(g, p),) + (0,) * (len(shape) - 1))
        return pl.BlockSpec(shape, lambda g, p: (0,) * len(shape))

    return pl.pallas_call(
        body,
        grid_spec=pltpu.PrefetchScalarGridSpec(
            num_scalar_prefetch=1,
            grid=(groups,),
            in_specs=[spec(value.shape, by_group, group) for value, by_group in operands],
            out_specs=[spec(shape, by_group, lambda g, p: g) for shape, _, by_group in results],
            scratch_shapes=[
                pltpu.SemaphoreType.DMA(shape) if kind is None else pltpu.VMEM(shape, kind)
                for shape, kind in scratch
            ],
        ),
        out_shape=[jax.ShapeDtypeStruct(shape, kind) for shape, kind, _ in results],
        compiler_params=pltpu.CompilerParams(vmem_limit_bytes=48 * 1024 * 1024),
        cost_estimate=pl.CostEstimate(flops=flops, bytes_accessed=16_000_000, transcendentals=0),
    )(place, *[value for value, _ in operands])


def local(
    patches,
    keep_mask,
    labels,
    stem_weight,
    position_table,
    attend_in,
    attend_out,
    expand,
    contract,
    head_weight,
    vectors,
    stem_rows,
    stem_cols,
    table_rows,
    table_cols,
    attend_in_rows,
    attend_in_cols,
    attend_out_rows,
    attend_out_cols,
    expand_rows,
    expand_cols,
    contract_rows,
    contract_cols,
    head_rows,
    head_cols,
    vector_second,
):
    data_size, model_size = lax.axis_size("dp"), lax.axis_size("mp")
    links = Grid() if (data_size, model_size) == (8, 4) else Plain(data_size, model_size)
    here = links.place
    count, patch_count, _ = patches.shape
    groups = model_size
    pair = groups // 2
    image_count = count * data_size * model_size
    inverse_count = 1.0 / image_count
    row_share, _, head_share = attend_in.shape
    hidden_share = expand.shape[1]
    in_share = 3 * head_share
    slots = patch_count + 1
    padded = -(-slots // 16) * 16
    rows = count * padded
    (
        stem_bias,
        gain_one,
        shift_one,
        query_bias,
        value_bias,
        attend_bias,
        gain_two,
        shift_two,
        expand_bias,
        contract_bias,
        gain_last,
        shift_last,
        head_bias,
    ) = pieces_of(vectors)

    attend_own = jnp.concatenate([attend_in.reshape(row_share, in_share), attend_out.T], 1)
    attend_chain = Chain(links.gather(attend_own.astype(bf16)))
    contract_own = contract.T
    squares = jnp.stack([jnp.sum(w * w) for w in (attend_in, attend_out, expand, contract)])
    squares = jnp.pad(squares[None], ((0, 0), (0, 124)))
    stem_low = stem_weight.astype(bf16)
    pixels = jnp.pad(patches, ((0, 0), (0, padded - patch_count), (0, 0))).reshape(rows, -1)
    table = jnp.concatenate(
        [position_table[1:] + stem_bias, position_table[:1], jnp.zeros((padded - slots, D), f32)]
    )
    present = jnp.concatenate(
        [
            keep_mask.astype(f32),
            jnp.ones((count, 1), f32),
            jnp.zeros((count, padded - slots), f32),
        ],
        1,
    )
    expand_piece, contract_piece = expand.astype(bf16), contract_own.astype(bf16)
    (
        attend_own,
        contract_own,
        squares,
        stem_low,
        pixels,
        table,
        present,
        expand_piece,
        contract_piece,
    ) = sync(
        [attend_chain],
        attend_own,
        contract_own,
        squares,
        stem_low,
        pixels,
        table,
        present,
        expand_piece,
        contract_piece,
    )
    expand_chain = Chain(links.gather(expand_piece))
    stream_zero = dot(pixels, stem_low).reshape(count, padded, D) + table
    stream_zero = stream_zero.reshape(rows, D)
    rows_one = layer_norm(stream_zero, gain_one, shift_one).astype(bf16)
    stream_zero, rows_one, contract_piece, head_weight, position_table, stem_weight = sync(
        [attend_chain, expand_chain],
        stream_zero,
        rows_one,
        contract_piece,
        head_weight,
        position_table,
        stem_weight,
    )
    contract_chain = Chain(links.gather(contract_piece))
    head_low = head_weight.astype(bf16)
    whole_squares = [jnp.sum(w * w) for w in (stem_weight, position_table, head_weight, vectors)]
    kept = jnp.sum(present, 1)[:, None]
    facts = jnp.concatenate([kept, labels[:, None].astype(f32), jnp.zeros((count, 126), f32)], 1)
    facts = jnp.concatenate([facts, facts])
    chooser = (jnp.eye(count)[:, :, None] * present[None]).reshape(count, rows).astype(bf16)
    chooser = jnp.concatenate([chooser, chooser])
    column = present.reshape(rows, 1)

    def by_block(values):
        return jnp.pad(values.reshape(data_size, row_share), ((0, 0), (0, 128 - row_share)))

    old_rows = jnp.concatenate(
        [by_block(v) for v in (attend_in_rows, attend_out_cols, expand_rows, contract_cols)], 1
    )
    in_cols = attend_in_cols.reshape(3, groups, head_share).swapaxes(0, 1)
    old_cols = jnp.concatenate(
        [
            jnp.concatenate(
                [in_cols.reshape(groups, -1), attend_out_rows.reshape(groups, -1)], 1
            ),
            expand_cols.reshape(groups, -1),
            contract_rows.reshape(groups, -1),
        ]
    )
    head_low, whole_squares, facts, chooser, column, old_rows, old_cols = sync(
        [attend_chain, contract_chain],
        head_low,
        whole_squares,
        facts,
        chooser,
        column,
        old_rows,
        old_cols,
    )
    sync([attend_chain, expand_chain])
    attend_all = links.whole(*attend_chain.result)

    qkv, attended, stream_one, rows_two, turned_one, turned_two, stream_sum = call(
        functools.partial(attend_kernel, blocks=links.blocks),
        groups,
        here,
        (
            (rows_one, False),
            (attend_all, True),
            (query_bias.reshape(groups, 1, head_share), True),
            (value_bias.reshape(groups, 1, head_share), True),
            (present, False),
            (stream_zero, False),
            (attend_bias[None], False),
            (gain_two[None], False),
            (shift_two[None], False),
            (column, False),
        ),
        (
            ((groups, 3, rows, head_share), bf16, True),
            ((groups, rows, head_share), bf16, True),
            ((rows, D), f32, False),
            ((rows, D), bf16, False),
            ((D, rows), bf16, False),
            ((D, rows), bf16, False),
            ((2 * count, D), f32, False),
        ),
        flops=2 * rows * D * 4 * D,
    )
    rows_two, stream_sum = sync([expand_chain, contract_chain], rows_two, stream_sum)
    rows_two = sync([expand_chain], rows_two)
    expand_all = links.whole(*expand_chain.result)
    active_sum, slope = call(
        hidden_kernel,
        groups,
        here,
        (
            (rows_two, False),
            (expand_all, True),
            (expand_bias.reshape(groups, 1, hidden_share), True),
            (chooser, False),
            (column, False),
        ),
        (
            ((groups, 2 * count, hidden_share), f32, True),
            ((groups, rows, hidden_share), bf16, True),
        ),
        flops=2 * rows * D * FF,
    )
    active_sum, slope = sync([contract_chain], active_sum, slope)
    active_sum, slope = sync([contract_chain], active_sum, slope)
    vectors_last = (contract_bias[None], gain_last[None], shift_last[None])

    def own_head(operands, scratch):
        return call(
            functools.partial(own_head_kernel, inverse_count=inverse_count),
            1,
            here,
            ((active_sum, False), (stream_sum, False), (facts, False))
            + tuple((value, False) for value in vectors_last + (head_low, head_bias[None]))
            + operands,
            (
                ((8 * count, D + 128), bf16, False),
                ((2 * count, D), f32, False),
                ((groups, 2 * count, hidden_share), f32, False),
            ),
            scratch,
        )

    piece, d_row, d_active_row = links.mixed(own_head, *contract_chain.result)

    pieces_chain = Chain(links.gather(piece))
    turns = ((3, -2), (2, -2))

    def expand_back(turn_order, d_active, *before):
        return call(
            expand_back_kernel,
            pair,
            here,
            (
                (turned_two, False),
                (expand_all, True),
                (slope, True),
                (d_active, True),
            )
            + tuple((value, False) for value in before),
            (
                ((pair, D, hidden_share), bf16, True),
                ((pair, 1, hidden_share), f32, True),
                ((rows, D), f32, False),
            ),
            (((rows, hidden_share), bf16),),
            flops=2 * rows * D * FF,
            turns=turn_order,
        )

    far_grad, expand_far, d_rows_two = expand_back(turns[0], d_active_row)
    far_grad, d_rows_two = sync([pieces_chain], far_grad, d_rows_two)
    expand_sum = Chain(links.reduce(far_grad))
    near_grad, expand_near, d_rows_two = expand_back(turns[1], d_active_row, d_rows_two)
    d_rows_two = sync([pieces_chain, (expand_sum, near_grad)], d_rows_two)
    d_stream, d_attend_low, d_turned, vector_two = call(
        functools.partial(between_kernel, blocks=links.blocks),
        1,
        here,
        (
            (d_rows_two, False),
            (d_row, False),
            (column, False),
            (stream_one, False),
            (gain_two[None], False),
        ),
        (
            ((rows, D), f32, False),
            ((rows, D), bf16, False),
            ((D, rows), bf16, False),
            ((8, D), f32, False),
        ),
    )

    def attend_back(turn_order, *before):
        return call(
            attend_back_kernel,
            pair,
            here,
            (
                (turned_one, False),
                (attend_all, True),
                (qkv, True),
                (attended, True),
                (column, False),
                (d_attend_low, False),
                (d_turned, False),
            )
            + tuple((value, False) for value in before),
            (
                ((pair, D, D), bf16, True),
                ((pair, 2 * count, head_share), f32, True),
                ((rows, D), f32, False),
            ),
            (((rows, 3 * head_share), bf16),),
            flops=2 * rows * D * 4 * D,
            turns=turn_order,
        )

    far_grad, heads_far, d_rows_one = attend_back(turns[0])
    far_grad, d_rows_one = sync([pieces_chain, expand_sum], far_grad, d_rows_one)
    attend_sum = Chain(links.reduce(far_grad))
    near_grad, heads_near, d_rows_one = attend_back(turns[1], d_rows_one)
    d_rows_one = sync([pieces_chain, expand_sum, (attend_sum, near_grad)], d_rows_one)
    spread = data_size * model_size
    unit = 16 * spread if spread <= 32 else spread
    both_rows = -(-(D + padded) // unit) * unit
    both, vector_one = call(
        stem_back_kernel,
        1,
        here,
        (
            (d_rows_one, False),
            (d_stream, False),
            (stream_zero, False),
            (gain_one[None], False),
            (pixels, False),
        ),
        (((both_rows, D), bf16, False), ((8 + padded, D), f32, False)),
        flops=2 * rows * D * D,
    )
    pieces = links.whole(*pieces_chain.result).reshape((-1,) + piece.shape)
    steps = max(1, pieces.shape[0] // 32)
    grad_head, grad_contract, vector_last, vector_head = call(
        functools.partial(all_head_kernel, inverse_count=inverse_count),
        steps,
        here,
        (
            (pieces.reshape((steps, -1) + piece.shape), True),
            (gain_last[None], False),
            (shift_last[None], False),
            (head_low, False),
            (head_bias[None], False),
        ),
        (
            ((D, CLASSES), f32, False),
            ((row_share, hidden_share), f32, False),
            ((8, D), f32, False),
            ((8, CLASSES), f32, False),
        ),
    )
    loss_sum = vector_head[1, 0]
    both, grad_contract, grad_head = sync(
        [attend_sum, expand_sum], both, grad_contract, grad_head
    )
    grad_expand = expand_sum.result
    both_sum = Chain(links.add_large(both))
    grad_expand = sync([attend_sum, both_sum], grad_expand)
    head_new, head_rows_new, head_cols_new = factored_step(
        head_weight, whole_squares[2], grad_head, head_rows, head_cols
    )
    head_new, grad_expand = sync([attend_sum, both_sum], head_new, grad_expand)
    grad_attend = attend_sum.result

    names = dict(data=data_size, groups=groups, share=head_share)
    _, at_group, at_single, lines = layout(data_size, groups)
    (sums,) = call(
        functools.partial(sums_kernel, patch_count=patch_count, **names),
        1,
        here,
        tuple(
            (value, False)
            for value in (
                grad_attend,
                grad_expand,
                grad_contract,
                squares,
                vector_one,
                vector_two,
                expand_far,
                expand_near,
                heads_far,
                heads_near,
            )
        ),
        (((lines, D), f32, False),),
    )
    sums_chain = Chain(links.add(sums))
    for _ in range(5):
        sync([sums_chain, both_sum])
    sums = sums_chain.result
    rows_new, cols_new, update, scalars, square_totals = call(
        functools.partial(renew_kernel, **names),
        1,
        here,
        tuple(
            (value, False)
            for value in (sums, old_rows, old_cols, grad_attend, grad_expand, grad_contract)
        ),
        (
            (old_rows.shape, f32, False),
            (old_cols.shape, f32, False),
            ((3, row_share, D), f32, False),
            ((8, 128), f32, False),
            ((8, 128), f32, False),
        ),
    )
    scalars_chain = Chain(links.add(scalars))
    sync([scalars_chain, both_sum])
    both = both_sum.result.astype(f32)
    grad_table = jnp.concatenate([both[D + patch_count : D + slots], both[D : D + patch_count]])
    stem_new, stem_rows_new, stem_cols_new = factored_step(
        stem_weight, whole_squares[0], both[:D], stem_rows, stem_cols
    )
    sync([scalars_chain])
    stem_new = sync([scalars_chain], stem_new)
    table_new, table_rows_new, table_cols_new = factored_step(
        position_table, whole_squares[1], grad_table, table_rows, table_cols
    )
    table_new = sync([scalars_chain], table_new)

    def of_groups(index, start=0, stop=D):
        spot = at_group + index * groups
        return sums[spot : spot + groups, start:stop].reshape(-1)

    single = sums[at_single : at_single + 6]
    grad_vector = jnp.concatenate(
        [
            single[0],
            single[1],
            single[2],
            of_groups(4, 0, head_share),
            of_groups(4, 256, 256 + head_share),
            single[3],
            single[4],
            single[5],
            of_groups(3),
            vector_last[0],
            vector_last[1],
            vector_last[2],
            vector_head[0],
        ]
    )
    vectors_new, second_new = vector_step(vectors, whole_squares[3], grad_vector, vector_second)
    vectors_new = sync([scalars_chain], vectors_new)
    block = call(
        functools.partial(step_kernel, sizes=(3 * D * D, D * D, D * FF, FF * D)),
        1,
        here,
        tuple(
            (value, False)
            for value in (
                update,
                scalars_chain.result,
                square_totals,
                attend_own,
                expand,
                contract_own,
            )
        ),
        tuple(
            (shape, kind, False)
            for shape in (
                (3, row_share, head_share),
                (head_share, row_share),
                (row_share, hidden_share),
                (hidden_share, row_share),
            )
            for kind in (f32, bf16)
        ),
    )
    in_new, in_copy, out_new, out_copy, expand_new, expand_copy, contract_new, contract_copy = block

    def of_blocks(index):
        return rows_new[:, index * 128 : index * 128 + row_share].reshape(-1)

    in_cols_new = cols_new[:groups, :in_share].reshape(groups, 3, head_share).swapaxes(0, 1)
    return (
        loss_sum,
        stem_new,
        stem_rows_new,
        stem_cols_new,
        table_new,
        table_rows_new,
        table_cols_new,
        in_new.swapaxes(0, 1),
        in_copy.swapaxes(0, 1),
        of_blocks(0),
        in_cols_new.reshape(3, D),
        out_new,
        out_copy,
        cols_new[:groups, in_share:].reshape(-1),
        of_blocks(1),
        expand_new,
        expand_copy,
        of_blocks(2),
        cols_new[groups : 2 * groups].reshape(-1),
        contract_new,
        contract_copy,
        cols_new[2 * groups :].reshape(-1),
        of_blocks(3),
        head_new,
        head_rows_new,
        head_cols_new,
        vectors_new,
        grad_vector,
        second_new,
    )


def solution(mesh):
    placed = (
        P(ALL, None, None),
        P(ALL, None),
        P(ALL),
        P(),
        P(),
        P("dp", None, "mp"),
        P("mp", "dp"),
        P("dp", "mp"),
        P("mp", "dp"),
    ) + (P(),) * 17
    block = (P("dp", None, "mp"), P("mp", "dp"), P("dp", "mp"), P("mp", "dp"))
    given = [P()] * 7
    for spec in block:
        given += [spec, spec, P(), P()]
    given += [P()] * 6
    return jax.shard_map(
        local, mesh=mesh, in_specs=placed, out_specs=tuple(given), check_vma=False
    )
```

time: 1270 us -> 390 us (0.31)
  waiting for transfers between devices: 642 us -> 50.7 us
  blocking collectives: 174 us -> 0 us
  matrix products: 170 us -> 1.29 us
  Pallas kernels: 0 us -> 134 us
  starting transfers between devices: 3.62 us -> 65.7 us
  other arithmetic: 135 us -> 79 us
  between operations: 54.8 us -> 10 us
  local copies, waits for them, and re-layouts: 75.4 us -> 44.3 us
    reduce_scatter x19 -> x0, waiting for transfers between devices: 390 us -> none  [the longest x8 166 us: scatter_rows(): lax.psum_scatter(terms.astype(jnp.bfloat16), 'mp', scatter_dimension=0, t...]
    all_gather x18 -> x0, waiting for transfers between devices: 175 us -> none  [the longest x8 83.5 us: gather_grads(): return lax.all_gather(grads, 'mp', axis=0, tiled=True)]
    dot_general x84 -> x1, matrix products: 155 us -> 1.29 us  [dot(): lax.dot_general(left, right, (((left_dim,), (right_dim,)), ((), ())), pre...]
    pallas_call x0 -> x16, Pallas kernels: none -> 134 us  [the longest x13 116 us: call(): pl.pallas_call(body, grid_spec=pltpu.PrefetchScalarGridSpec(num_scalar_pr...]
    all_gather x6 -> x0, blocking collectives: 91.8 us -> none  [the longest x1 40.5 us: fetch_block(): lax.all_gather(attend_in.astype(jnp.bfloat16), 'dp', axis=0, tiled=True)]
    psum x2 -> x0, blocking collectives: 82 us -> none  [the longest x1 41.5 us: local(): lax.psum((place(jnp.sum(squared_in, (1, 2)), D, row_start, 0), place(jnp....]
    unnamed x40 -> x0, waiting for transfers between devices: 67.5 us -> none
    ppermute x0 -> x58, starting transfers between devices: none -> 65.7 us  [send(): return lax.ppermute(values, ALL, table)]
  transfers between devices with their start and end apart: 39 -> 58, of which waited for: 29 -> 21; matrix products, arithmetic and copies ran while one was open for 21% -> 20% of each run, Pallas kernels for 0% -> 32%
where the time goes in v1:
time: 390 us; the launch traced here: 385 us
  Pallas kernels  134 us (34%)
  other arithmetic  79 us (20%)
  starting transfers between devices  65.7 us (17%)
  waiting for transfers between devices  50.7 us (13%)
  local copies, waits for them, and re-layouts  44.3 us (11%)
  between operations  10 us (3%)
    pallas_call x13, Pallas kernels, call(): pl.pallas_call(body, grid_spec=pltpu.PrefetchScalarGridSpec(num_scalar_pr...  116 us
    ppermute x58, starting transfers between devices, send(): return lax.ppermute(values, ALL, table)  65.7 us
    ppermute x58, waiting for transfers between devices, send(): return lax.ppermute(values, ALL, table)  50.7 us
    unnamed x196, local copies, waits for them, and re-layouts  26.7 us
    pallas_call x3, Pallas kernels, whole(): pl.pallas_call(assemble, in_specs=[pl.BlockSpec(memory_space=pltpu.SMEM),...  17.9 us
    sub x3, other arithmetic, factored_step(): return (weight - step_rate * magnitude * update, rows_new, cols_new)  8.96 us
  transfers between devices with their start and end apart: 58, of which 21 were waited for; matrix products, arithmetic and copies ran while one was open for 20% of the time, Pallas kernels for 32%

profile of v1, /device:TPU:0, one launch (start us, length us, event | category | flops | bytes accessed | tf_op | source)
XLA Modules:
  0.0 384.6 jit_solution(14624644699771823222)
XLA Ops:
  4.1 5.0 %collective-permute-start = (bf16[96,768]{1,0:T(8,128)(2,1)}, bf16[96,768]{1,0:T(8,128)(2,1)}, u32[]{:S(2)}, u32[]{:S(2)}) collective-permute-start(bf16[96,768]{1,0:T(8,128)(2,1)} %get-tuple-element.453), channel_id=1, source_target_pairs={{0,24},{1,25},{2,26},{3,27},{4,28},{5,29},{6,30},{7,31},{8,0},{9,1... | collective-permute-start | bytes 442376 | tf_op jit(solution)/shard_map/ppermute | solution.py:152
  37.4 6.6 %collective-permute-done.5 = bf16[96,768]{1,0:T(8,128)(2,1)S(1)} collective-permute-done((bf16[96,768]{1,0:T(8,128)(2,1)}, bf16[96,768]{1,0:T(8,128)(2,1)S(1)}, u32[]{:S(2)}, u32[]{:S(2)}) %collective-permute-start.5) | collective-permute-done | bytes 147488 | tf_op jit(solution)/shard_map/ppermute | solution.py:152
  53.6 3.3 multiply_reduce_fusion.1
  58.1 3.5 copy.93
  69.2 8.4 %collective-permute-done.12 = bf16[1,4,96,768]{3,2,1,0:T(8,128)(2,1)S(1)} collective-permute-done((bf16[1,4,96,768]{3,2,1,0:T(8,128)(2,1)S(1)}, bf16[1,4,96,768]{3,2,1,0:T(8,128)(2,1)S(1)}, u32[]{:S(2)}, u32[]{:S(2)}) %collective-permute-start.12) | collective-permute-done | bytes 589856 | tf_op jit(solution)/shard_map/ppermute | solution.py:152
  87.9 7.7 %shard_map.473 = bf16[4,8,96,768]{3,2,1,0:T(8,128)(2,1)S(1)} custom-call(s32[6]{0:T(128)S(1)} %stack.125.place_ref, bf16[4,4,96,768]{3,2,1,0:T(8,128)(2,1)S(1)} %copy-done.2, bf16[4,4,96,768]{3,2,1,0:T(8,128)(2,1)S(1)} %copy-done.21), custom_call_target="tpu_custom_call" | custom-call | tf_op jit(solution)/shard_map/pallas_call | solution.py:172
  97.7 18.9 %shard_map.474 = (bf16[4,3,832,192]{3,2,1,0:T(8,128)(2,1)}, bf16[4,832,192]{2,1,0:T(8,128)(2,1)}, f32[832,768]{1,0:T(8,128)}, bf16[832,768]{1,0:T(8,128)(2,1)S(1...) custom-call(s32[6]{0:T(128)S(1)} %stack.125.place_ref, ...), custom_call_target="tpu_custom_call" | custom-call | flops 3925868544 | bytes 16000000 | tf_op jit(solution)/shard_map/pallas_call | solution.py:914
  123.7 7.7 %shard_map.475 = bf16[4,8,96,768]{3,2,1,0:T(8,128)(2,1)S(1)} custom-call(s32[6]{0:T(128)S(1)} %stack.125.place_ref, bf16[4,4,96,768]{3,2,1,0:T(8,128)(2,1)S(1)} %pad_maximum_fusion.1.mine_ref, bf16[4,4,96,768]{3,2,1,0:T(8,128)(2,1)S(1)} %collective-permute-done.16.theirs_ref), custom_call_target="tpu_custom_call" | custom-call | tf_op jit(solution)/shard_map/pallas_call | solution.py:172
  133.5 12.3 %shard_map.476 = (f32[4,8,768]{2,1,0:T(8,128)S(1)}, bf16[4,832,768]{2,1,0:T(8,128)(2,1)}) custom-call(s32[6]{0:T(128)S(1)} %stack.125.place_ref, bf16[832,768]{1,0:T(8,128)(2,1)S(1)} %get-tuple-element.213.rows_ref, bf16[4,768,768]{2,1,0:T(8,128)(2,1)} %bitcast.154, f32[4,1,768]{2,1,0:T(1,128)S(1)} %bitcast.166, ...), custom_call_target="tpu_custom_call" | custom-call | flops 3925868544 | bytes 16000000 | tf_op jit(solution)/shard_map/pallas_call | solution.py:914
  147.5 4.4 %collective-permute-done.17.refs_1_ = bf16[4,4,96,768]{3,2,1,0:T(8,128)(2,1)S(1)} collective-permute-done((bf16[4,4,96,768]{3,2,1,0:T(8,128)(2,1)S(1)}, bf16[4,4,96,768]{3,2,1,0:T(8,128)(2,1)S(1)}, u32[]{:S(2)}, u32[]{:S(2)}) %collective-permute-start.17) | collective-permute-done | bytes 2359328 | tf_op jit(solution)/shard_map/ppermute | solution.py:152
  153.3 10.6 %shard_map.477 = (bf16[32,896]{1,0:T(8,128)(2,1)S(1)}, f32[8,768]{1,0:T(8,128)S(1)}, f32[4,8,768]{2,1,0:T(8,128)S(1)}) custom-call(s32[6]{0:T(128)S(1)} %stack.125.place_ref, f32[4,8,768]{2,1,0:T(8,128)S(1)} %get-tuple-element.221.active_ref, f32[8,768]{1,0:T(8,128)S(1)} %get-tuple-element.222.sum_ref, f32[8,128]{1,0:T(8,128)S(1)} %maximum_maximum_fusion.2.facts_ref, ...), custom_call_target="tpu_custom_call" | custom-call | bytes 16000000 | tf_op jit(solution)/shard_map/pallas_call | solution.py:914
  168.3 9.2 %shard_map.478 = (bf16[2,768,768]{2,1,0:T(8,128)(2,1)}, f32[2,1,768]{2,1,0:T(1,128)S(1)}, f32[832,768]{1,0:T(8,128)}) custom-call(s32[6]{0:T(128)S(1)} %stack.125.place_ref, bf16[768,832]{1,0:T(8,128)(2,1)S(1)} %get-tuple-element.227.turned_ref, bf16[4,768,768]{2,1,0:T(8,128)(2,1)} %bitcast.155, bf16[4,832,768]{2,1,0:T(8,128)(2,1)} %get-tuple-element.228.slope_ref, ...), custom_call_target="tpu_custom_call" | custom-call | flops 3925868544 | bytes 16000000 | tf_op jit(solution)/shard_map/pallas_call | solution.py:914
  179.7 9.8 %shard_map.479 = (bf16[2,768,768]{2,1,0:T(8,128)(2,1)S(1)}, f32[2,1,768]{2,1,0:T(1,128)S(1)}, f32[832,768]{1,0:T(8,128)}) custom-call(s32[6]{0:T(128)S(1)} %stack.125.place_ref, bf16[768,832]{1,0:T(8,128)(2,1)S(1)} %copy-done.28, bf16[4,768,768]{2,1,0:T(8,128)(2,1)} %bitcast.156, bf16[4,832,768]{2,1,0:T(8,128)(2,1)} %get-tuple-element.228.slope_ref, ...), custom_call_target="tpu_custom_call" | custom-call | flops 3925868544 | bytes 16000000 | tf_op jit(solution)/shard_map/pallas_call | solution.py:914
  194.8 5.7 %shard_map.480 = (f32[832,768]{1,0:T(8,128)S(1)}, bf16[832,768]{1,0:T(8,128)(2,1)S(1)}, bf16[768,832]{1,0:T(8,128)(2,1)S(1)}, f32[8,768]{1,0:T(8,128)S(1)}) custom-call(s32[6]{0:T(128)S(1)} %stack.125.place_ref, f32[832,768]{1,0:T(8,128)} %get-tuple-element.245.d_rows_ref, f32[8,768]{1,0:T(8,128)S(1)} %get-tuple-element.246.d_row_ref, ...), custom_call_target="tpu_custom_call" | custom-call | bytes 16000000 | tf_op jit(solution)/shard_map/pallas_call | solution.py:914
  200.5 17.1 %shard_map.481 = (bf16[2,768,768]{2,1,0:T(8,128)(2,1)}, f32[2,8,192]{2,1,0:T(8,128)S(1)}, f32[832,768]{1,0:T(8,128)}) custom-call(s32[6]{0:T(128)S(1)} %stack.125.place_ref, bf16[768,832]{1,0:T(8,128)(2,1)S(1)} %copy-done.8, bf16[4,768,768]{2,1,0:T(8,128)(2,1)} %bitcast.149, bf16[4,3,832,192]{3,2,1,0:T(8,128)(2,1)} %get-tuple-element.243.qkv_ref, ...), custom_call_target="tpu_custom_call" | custom-call | flops 3925868544 | bytes 16000000 | tf_op jit(solution)/shard_map/pallas_call | solution.py:914
  225.3 17.0 %shard_map.482 = (bf16[2,768,768]{2,1,0:T(8,128)(2,1)}, f32[2,8,192]{2,1,0:T(8,128)S(1)}, f32[832,768]{1,0:T(8,128)}) custom-call(s32[6]{0:T(128)S(1)} %stack.125.place_ref, bf16[768,832]{1,0:T(8,128)(2,1)S(1)} %copy-done.9, bf16[4,768,768]{2,1,0:T(8,128)(2,1)} %bitcast.150, bf16[4,3,832,192]{3,2,1,0:T(8,128)(2,1)} %get-tuple-element.243.qkv_ref, ...), custom_call_target="tpu_custom_call" | custom-call | flops 3925868544 | bytes 16000000 | tf_op jit(solution)/shard_map/pallas_call | solution.py:914
  257.4 5.0 %shard_map.484 = (f32[768,1000]{1,0:T(8,128)}, f32[96,768]{1,0:T(8,128)S(1)}, f32[8,768]{1,0:T(8,128)S(1)}, f32[8,1000]{1,0:T(8,128)S(1)}) custom-call(s32[6]{0:T(128)S(1)} %stack.125.place_ref, bf16[1,32,32,896]{3,2,1,0:T(8,128)(2,1)S(1)} %bitcast.151, f32[1,768]{1,0:T(1,128)S(1)} %broadcast_in_dim.82.gain_ref, f32[1,768]{1,0:T(1,128)S(1)} %broadcast_in_dim.83.shift_ref, ...), custom_call_target="tpu_custom_call" | custom-call | bytes 16000000 | tf_op jit(solution)/shard_map/pallas_call | solution.py:914
  262.3 6.4 %shard_map.485 = (bf16[1024,768]{1,0:T(8,128)(2,1)S(1)}, f32[216,768]{1,0:T(8,128)S(1)}) custom-call(s32[6]{0:T(128)S(1)} %stack.125.place_ref, f32[832,768]{1,0:T(8,128)S(1)} %copy-done.18, f32[832,768]{1,0:T(8,128)} %copy-done.17, f32[832,768]{1,0:T(8,128)} %copy-done.32, f32[1,768]{1,0:T(1,128)S(1)} %broadcast_in_dim.86.gain_ref, ...), custom_call_target="tpu_custom_call" | custom-call | flops 981467136 | bytes 16000000 | tf_op jit(solution)/shard_map/pallas_call | solution.py:914
  274.6 3.6 multiply_reduce_fusion
  296.1 4.5 %collective-permute-done.35 = bf16[96,768]{1,0:T(8,128)(2,1)S(1)} collective-permute-done((bf16[96,768]{1,0:T(8,128)(2,1)S(1)}, bf16[96,768]{1,0:T(8,128)(2,1)S(1)}, u32[]{:S(2)}, u32[]{:S(2)}) %collective-permute-start.35) | collective-permute-done | bytes 147488 | tf_op jit(solution)/shard_map/ppermute | solution.py:152
  309.0 3.9 %collective-permute-start.41 = (bf16[32,768]{1,0:T(8,128)(2,1)S(1)}, bf16[32,768]{1,0:T(8,128)(2,1)S(1)}, u32[]{:S(2)}, u32[]{:S(2)}) collective-permute-start(bf16[32,768]{1,0:T(8,128)(2,1)S(1)} %get-tuple-element.473), channel_id=1, source_target_pairs={{0,8},{1,9},{2,10},{3,11},{4,12},{5,13},{6,14},{7,15},{8,16},{9,17... | collective-permute-start | bytes 147464 | tf_op jit(solution)/shard_map/ppermute | solution.py:152
  329.6 5.1 %collective-permute-done.48 = f32[40,768]{1,0:T(8,128)S(1)} collective-permute-done((f32[40,768]{1,0:T(8,128)S(1)}, f32[40,768]{1,0:T(8,128)S(1)}, u32[]{:S(2)}, u32[]{:S(2)}) %collective-permute-start.48) | collective-permute-done | bytes 122912 | tf_op jit(solution)/shard_map/ppermute | solution.py:152
  341.8 3.5 copy.106
  361.1 4.4 %multiply_subtract_fusion.1 = f32[768,768]{1,0:T(8,128)} fusion(f32[768,768]{1,0:T(8,128)} %param.29, f32[]{:T(128)S(6)} %max.27, f32[]{:T(128)S(6)} %max.26, f32[]{:T(128)S(6)} %div.135, f32[768]{0:T(1024)S(1)} %get-tuple-element.495, f32[768]{0:T(1024)S(1)} %get-tuple-element.442, f32[24,32,768]{2,1,0:T(8,128)} %slice.235), kind=kLoop, calls=%fused_computation.15 | loop fusion | flops 3538944 | bytes 7084044 | tf_op jit(solution)/shard_map/sub | solution.py:270
  (468 shorter events, 190.8 us)
Async XLA Ops:
  4.1 23.5 %collective-permute-start = (bf16[96,768]{1,0:T(8,128)(2,1)}, bf16[96,768]{1,0:T(8,128)(2,1)}, u32[]{:S(2)}, u32[]{:S(2)}) collective-permute-start(bf16[96,768]{1,0:T(8,128)(2,1)} %get-tuple-element.453), channel_id=1, source_target_pairs={{0,24},{1,25},{2,26},{3,27},{4,28},{5,29},{6,30},{7,31},{8,0},{9,1... | collective-permute-start | bytes 442376 | tf_op jit(solution)/shard_map/ppermute | solution.py:152
  9.1 18.5 %collective-permute-start.1 = (bf16[96,768]{1,0:T(8,128)(2,1)}, bf16[96,768]{1,0:T(8,128)(2,1)}, u32[]{:S(2)}, u32[]{:S(2)}) collective-permute-start(bf16[96,768]{1,0:T(8,128)(2,1)} %get-tuple-element.453), channel_id=1, source_target_pairs={{0,16},{1,17},{2,18},{3,19},{4,20},{5,21},{6,22},{7,23},{8,24},{9,... | collective-permute-start | bytes 442376 | tf_op jit(solution)/shard_map/ppermute | solution.py:152
  9.1 18.5 %collective-permute-start.2 = (bf16[96,768]{1,0:T(8,128)(2,1)}, bf16[96,768]{1,0:T(8,128)(2,1)}, u32[]{:S(2)}, u32[]{:S(2)}) collective-permute-start(bf16[96,768]{1,0:T(8,128)(2,1)} %get-tuple-element.453), channel_id=1, source_target_pairs={{0,8},{1,9},{2,10},{3,11},{4,12},{5,13},{6,14},{7,15},{8,16},{9,17... | collective-permute-start | bytes 442376 | tf_op jit(solution)/shard_map/ppermute | solution.py:152
  30.5 13.5 %collective-permute-start.5 = (bf16[96,768]{1,0:T(8,128)(2,1)}, bf16[96,768]{1,0:T(8,128)(2,1)S(1)}, u32[]{:S(2)}, u32[]{:S(2)}) collective-permute-start(bf16[96,768]{1,0:T(8,128)(2,1)} %get-tuple-element.185), channel_id=1, source_target_pairs={{0,16},{1,17},{2,18},{3,19},{4,20},{5,21},{6,22},{7,23},{8,24},{9,... | collective-permute-start | bytes 442376 | tf_op jit(solution)/shard_map/ppermute | solution.py:152
  31.6 12.4 %collective-permute-start.6 = (bf16[96,768]{1,0:T(8,128)(2,1)}, bf16[96,768]{1,0:T(8,128)(2,1)S(1)}, u32[]{:S(2)}, u32[]{:S(2)}) collective-permute-start(bf16[96,768]{1,0:T(8,128)(2,1)} %get-tuple-element.185), channel_id=1, source_target_pairs={{0,8},{1,9},{2,10},{3,11},{4,12},{5,13},{6,14},{7,15},{8,16},{9,17... | collective-permute-start | bytes 442376 | tf_op jit(solution)/shard_map/ppermute | solution.py:152
  46.0 18.7 %collective-permute-start.7 = (bf16[2,4,96,768]{3,2,1,0:T(8,128)(2,1)}, bf16[2,4,96,768]{3,2,1,0:T(8,128)(2,1)}, u32[]{:S(2)}, u32[]{:S(2)}) collective-permute-start(bf16[2,4,96,768]{3,2,1,0:T(8,128)(2,1)} %pad_maximum_fusion.3), channel_id=1, source_target_pairs={{0,2},{1,5},{2,0},{3,7},{4,6},{5,1},{6,4},{7,3},{8,10},{9,13},{10,... | collective-permute-start | bytes 3538952 | tf_op jit(solution)/shard_map/ppermute | solution.py:152
  48.9 15.7 %collective-permute-start.10 = (bf16[96,768]{1,0:T(8,128)(2,1)S(1)}, bf16[96,768]{1,0:T(8,128)(2,1)}, u32[]{:S(2)}, u32[]{:S(2)}) collective-permute-start(bf16[96,768]{1,0:T(8,128)(2,1)S(1)} %copy-done.50), channel_id=1, source_target_pairs={{0,8},{1,9},{2,10},{3,11},{4,12},{5,13},{6,14},{7,15},{8,16},{9,17... | collective-permute-start | bytes 442376 | tf_op jit(solution)/shard_map/ppermute | solution.py:152
  51.3 13.3 %collective-permute-start.8 = (bf16[96,768]{1,0:T(8,128)(2,1)S(1)}, bf16[96,768]{1,0:T(8,128)(2,1)}, u32[]{:S(2)}, u32[]{:S(2)}) collective-permute-start(bf16[96,768]{1,0:T(8,128)(2,1)S(1)} %copy-done.50), channel_id=1, source_target_pairs={{0,24},{1,25},{2,26},{3,27},{4,28},{5,29},{6,30},{7,31},{8,0},{9,1... | collective-permute-start | bytes 442376 | tf_op jit(solution)/shard_map/ppermute | solution.py:152
  80.1 36.6 %collective-permute-start.13 = (bf16[2,4,96,768]{3,2,1,0:T(8,128)(2,1)}, bf16[2,4,96,768]{3,2,1,0:T(8,128)(2,1)}, u32[]{:S(2)}, u32[]{:S(2)}) collective-permute-start(bf16[2,4,96,768]{3,2,1,0:T(8,128)(2,1)} %pad_maximum_fusion.4), channel_id=1, source_target_pairs={{0,2},{1,5},{2,0},{3,7},{4,6},{5,1},{6,4},{7,3},{8,10},{9,13},{10,... | collective-permute-start | bytes 3538952 | tf_op jit(solution)/shard_map/ppermute | solution.py:152
  82.5 34.1 %collective-permute-start.14 = (bf16[1,4,96,768]{3,2,1,0:T(8,128)(2,1)}, bf16[1,4,96,768]{3,2,1,0:T(8,128)(2,1)}, u32[]{:S(2)}, u32[]{:S(2)}) collective-permute-start(bf16[1,4,96,768]{3,2,1,0:T(8,128)(2,1)} %maximum_bitcast_fusion.1), channel_id=1, source_target_pairs={{0,4},{1,3},{2,6},{3,1},{4,0},{5,7},{6,2},{7,5},{8,12},{9,11},{10,... | collective-permute-start | bytes 1769480 | tf_op jit(solution)/shard_map/ppermute | solution.py:152
  120.5 25.3 %collective-permute-start.15 = (bf16[2,4,96,768]{3,2,1,0:T(8,128)(2,1)S(1)}, bf16[2,4,96,768]{3,2,1,0:T(8,128)(2,1)S(1)}, u32[]{:S(2)}, u32[]{:S(2)}) collective-permute-start(bf16[2,4,96,768]{3,2,1,0:T(8,128)(2,1)S(1)} %pad_maximum_fusion.5), channel_id=1, source_target_pairs={{0,2},{1,5},{2,0},{3,7},{4,6},{5,1},{6,4},{7,3},{8,10},{9,13},{10,... | collective-permute-start | bytes 3538952 | tf_op jit(solution)/shard_map/ppermute | solution.py:152
  163.9 13.7 %collective-permute-start.18 = (bf16[32,896]{1,0:T(8,128)(2,1)S(1)}, bf16[32,896]{1,0:T(8,128)(2,1)S(1)}, u32[]{:S(2)}, u32[]{:S(2)}) collective-permute-start(bf16[32,896]{1,0:T(8,128)(2,1)S(1)} %get-tuple-element.226), channel_id=1, source_target_pairs={{0,24},{1,25},{2,26},{3,27},{4,28},{5,29},{6,30},{7,31},{8,0},{9,1... | collective-permute-start | bytes 172040 | tf_op jit(solution)/shard_map/ppermute | solution.py:152
  177.6 11.9 %collective-permute-start.22 = (bf16[2,768,768]{2,1,0:T(8,128)(2,1)}, bf16[2,768,768]{2,1,0:T(8,128)(2,1)}, u32[]{:S(2)}, u32[]{:S(2)}) collective-permute-start(bf16[2,768,768]{2,1,0:T(8,128)(2,1)} %get-tuple-element.235), channel_id=1, source_target_pairs={{0,1},{1,0},{2,3},{3,2},{4,5},{5,4},{6,7},{7,6},{8,9},{9,8},{10,11... | collective-permute-start | bytes 7077896 | tf_op jit(solution)/shard_map/ppermute | solution.py:152
  192.6 25.1 %collective-permute-start.24 = (bf16[2,4,96,768]{3,2,1,0:T(8,128)(2,1)S(1)}, bf16[2,4,96,768]{3,2,1,0:T(8,128)(2,1)S(1)}, u32[]{:S(2)}, u32[]{:S(2)}) collective-permute-start(bf16[2,4,96,768]{3,2,1,0:T(8,128)(2,1)S(1)} %pad_maximum_fusion.6), channel_id=1, source_target_pairs={{0,2},{1,5},{2,0},{3,7},{4,6},{5,1},{6,4},{7,3},{8,10},{9,13},{10,... | collective-permute-start | bytes 3538952 | tf_op jit(solution)/shard_map/ppermute | solution.py:152
  194.2 23.5 %collective-permute-start.23 = (bf16[2,4,32,896]{3,2,1,0:T(8,128)(2,1)S(1)}, bf16[2,4,32,896]{3,2,1,0:T(8,128)(2,1)S(1)}, u32[]{:S(2)}, u32[]{:S(2)}) collective-permute-start(bf16[2,4,32,896]{3,2,1,0:T(8,128)(2,1)S(1)} %pad_maximum_fusion.10), channel_id=1, source_target_pairs={{0,2},{1,5},{2,0},{3,7},{4,6},{5,1},{6,4},{7,3},{8,10},{9,13},{10,... | collective-permute-start | bytes 1376264 | tf_op jit(solution)/shard_map/ppermute | solution.py:152
  217.7 24.7 %collective-permute-start.27 = (bf16[2,768,768]{2,1,0:T(8,128)(2,1)}, bf16[2,768,768]{2,1,0:T(8,128)(2,1)}, u32[]{:S(2)}, u32[]{:S(2)}) collective-permute-start(bf16[2,768,768]{2,1,0:T(8,128)(2,1)} %get-tuple-element.254), channel_id=1, source_target_pairs={{0,1},{1,0},{2,3},{3,2},{4,5},{5,4},{6,7},{7,6},{8,9},{9,8},{10,11... | collective-permute-start | bytes 7077896 | tf_op jit(solution)/shard_map/ppermute | solution.py:152
  219.5 22.9 %collective-permute-start.25 = (bf16[4,4,32,896]{3,2,1,0:T(8,128)(2,1)}, bf16[4,4,32,896]{3,2,1,0:T(8,128)(2,1)}, u32[]{:S(2)}, u32[]{:S(2)}) collective-permute-start(bf16[4,4,32,896]{3,2,1,0:T(8,128)(2,1)} %pad_maximum_fusion.8.mine_ref), channel_id=1, source_target_pairs={{0,1},{1,0},{2,3},{3,2},{4,5},{5,4},{6,7},{7,6},{8,9},{9,8},{10,11... | collective-permute-start | bytes 2752520 | tf_op jit(solution)/shard_map/ppermute | solution.py:152
  221.4 21.0 %collective-permute-start.26 = (bf16[4,96,768]{2,1,0:T(8,128)(2,1)S(1)}, bf16[4,96,768]{2,1,0:T(8,128)(2,1)S(1)}, u32[]{:S(2)}, u32[]{:S(2)}) collective-permute-start(bf16[4,96,768]{2,1,0:T(8,128)(2,1)S(1)} %fusion.6), channel_id=1, source_target_pairs={{0,4},{1,3},{2,6},{3,1},{4,0},{5,7},{6,2},{7,5},{8,12},{9,11},{10,... | collective-permute-start | bytes 1769480 | tf_op jit(solution)/shard_map/ppermute | solution.py:152
  245.5 23.2 %collective-permute-start.28 = (bf16[2,4,96,768]{3,2,1,0:T(8,128)(2,1)}, bf16[2,4,96,768]{3,2,1,0:T(8,128)(2,1)}, u32[]{:S(2)}, u32[]{:S(2)}) collective-permute-start(bf16[2,4,96,768]{3,2,1,0:T(8,128)(2,1)} %pad_maximum_fusion.7), channel_id=1, source_target_pairs={{0,2},{1,5},{2,0},{3,7},{4,6},{5,1},{6,4},{7,3},{8,10},{9,13},{10,... | collective-permute-start | bytes 3538952 | tf_op jit(solution)/shard_map/ppermute | solution.py:152
  250.3 18.4 %collective-permute-start.29 = (bf16[96,768]{1,0:T(8,128)(2,1)}, bf16[96,768]{1,0:T(8,128)(2,1)}, u32[]{:S(2)}, u32[]{:S(2)}) collective-permute-start(bf16[96,768]{1,0:T(8,128)(2,1)} %get-tuple-element.464), channel_id=1, source_target_pairs={{0,8},{1,9},{2,10},{3,11},{4,12},{5,13},{6,14},{7,15},{8,16},{9,17... | collective-permute-start | bytes 442376 | tf_op jit(solution)/shard_map/ppermute | solution.py:152
  251.7 17.0 %collective-permute-start.30 = (bf16[96,768]{1,0:T(8,128)(2,1)S(1)}, bf16[96,768]{1,0:T(8,128)(2,1)}, u32[]{:S(2)}, u32[]{:S(2)}) collective-permute-start(bf16[96,768]{1,0:T(8,128)(2,1)S(1)} %get-tuple-element.463), channel_id=1, source_target_pairs={{0,16},{1,17},{2,18},{3,19},{4,20},{5,21},{6,22},{7,23},{8,24},{9,... | collective-permute-start | bytes 442376 | tf_op jit(solution)/shard_map/ppermute | solution.py:152
  253.7 15.0 %collective-permute-start.31 = (bf16[96,768]{1,0:T(8,128)(2,1)S(1)}, bf16[96,768]{1,0:T(8,128)(2,1)}, u32[]{:S(2)}, u32[]{:S(2)}) collective-permute-start(bf16[96,768]{1,0:T(8,128)(2,1)S(1)} %get-tuple-element.462), channel_id=1, source_target_pairs={{0,24},{1,25},{2,26},{3,27},{4,28},{5,29},{6,30},{7,31},{8,0},{9,1... | collective-permute-start | bytes 442376 | tf_op jit(solution)/shard_map/ppermute | solution.py:152
  270.3 12.7 %collective-permute-start.33 = (bf16[16,32,768]{2,1,0:T(8,128)(2,1)}, bf16[16,32,768]{2,1,0:T(8,128)(2,1)}, u32[]{:S(2)}, u32[]{:S(2)}) collective-permute-start(bf16[16,32,768]{2,1,0:T(8,128)(2,1)} %constant_dynamic-slice_fusion), channel_id=1, source_target_pairs={{0,1},{1,0},{2,3},{3,2},{4,5},{5,4},{6,7},{7,6},{8,9},{9,8},{10,11... | collective-permute-start | bytes 2359304 | tf_op jit(solution)/shard_map/ppermute | solution.py:152
  284.5 16.1 %collective-permute-start.37 = (bf16[8,32,768]{2,1,0:T(8,128)(2,1)S(1)}, bf16[8,32,768]{2,1,0:T(8,128)(2,1)S(1)}, u32[]{:S(2)}, u32[]{:S(2)}) collective-permute-start(bf16[8,32,768]{2,1,0:T(8,128)(2,1)S(1)} %dynamic-slice_convert_fusion), channel_id=1, source_target_pairs={{0,2},{1,5},{2,0},{3,7},{4,6},{5,1},{6,4},{7,3},{8,10},{9,13},{10,... | collective-permute-start | bytes 1179656 | tf_op jit(solution)/shard_map/ppermute | solution.py:152
  (121 other events, 995.1 us)

commit v2 on v1

v2 whole, which is shorter than its diff:
```python
import functools

import jax
import jax.numpy as jnp
from jax import lax
from jax.experimental import pallas as pl
from jax.experimental.pallas import tpu as pltpu
from jax.sharding import PartitionSpec as P

D = 768
HEAD_DIM = 64
FF = 3072
CLASSES = 1000

eps_norm = 1e-06
eps_one = 1e-30
eps_two = 0.001
decay_rate = 0.5
clip_level = 0.3
step_rate = 1.0
smoothing = 0.1

ALL = ("dp", "mp")
f32 = jnp.float32
bf16 = jnp.bfloat16


def after(value, *others):
    return lax.optimization_barrier((value,) + others)[0]


class Chain:
    def __init__(self, stages):
        self.stages = stages
        self.result = None
        self.sent, self.flight = next(stages)

    def advance(self, arrived):
        try:
            self.sent, self.flight = self.stages.send(arrived)
        except StopIteration as end:
            self.sent, self.flight, self.result = (), (), end.value


def sync(chains, *values):
    chains = [chain if isinstance(chain, tuple) else (chain,) for chain in chains]
    flights = [(chain[0].flight,) + chain[1:] for chain in chains]
    flights, values = lax.optimization_barrier((flights, values))
    for chain, flight in zip(chains, flights):
        chain[0].advance(flight if len(flight) > 1 else flight[0])
    return values[0] if len(values) == 1 else values


class Plain:
    blocks = None

    def __init__(self, rows, cols):
        self.rows, self.cols = rows, cols
        self.place = jnp.stack(
            [jnp.zeros((), jnp.int32)] * 4
            + [lax.axis_index("dp"), lax.axis_index("mp"), jnp.zeros((), jnp.int32)]
            + [jnp.full((), 4, jnp.int32)]
        ).astype(jnp.int32)

    def gather(self, piece):
        full = lax.all_gather(piece, ALL, axis=0)
        full = full.reshape((self.rows, self.cols) + piece.shape).swapaxes(0, 1)
        for _ in range(4):
            yield (), ()
        return (full.reshape(self.cols, self.rows * piece.shape[0], piece.shape[1]),)

    def whole(self, full):
        return full

    def reduce(self, far):
        _, near = yield (), ()
        grads = jnp.stack([near[1], far[1], near[0], far[0]])
        grads = grads.reshape(self.cols, self.rows, -1, grads.shape[2])
        grads = grads.swapaxes(0, 1).reshape((-1,) + grads.shape[2:])
        total = lax.psum_scatter(grads, ALL, scatter_dimension=0).astype(f32)
        for _ in range(3):
            total = yield (), total
        return total

    def add(self, values):
        values = lax.psum(values, ALL)
        for _ in range(5):
            values = yield (), values
        return values

    def add_large(self, far, near):
        values = lax.psum((near, far), ALL)
        for _ in range(8):
            values = yield (), values
        return values


def group_copies(place_ref, piece_refs, full_ref, sems, distance):
    near_ref, far_ref = piece_refs[2:] if distance % 2 else piece_refs[:2]
    flip = distance // 2
    x = place_ref[1]
    source = far_ref if flip else near_ref
    along_y = [
        pltpu.make_async_copy(source.at[0], full_ref.at[:, x], sems.at[0]),
        pltpu.make_async_copy(source.at[1], full_ref.at[:, 1 - x], sems.at[1]),
    ]
    along_x = [
        pltpu.make_async_copy(near_ref.at[flip], full_ref.at[:, x], sems.at[0]),
        pltpu.make_async_copy(far_ref.at[flip], full_ref.at[:, 1 - x], sems.at[1]),
    ]
    return along_y, along_x


def each_copy(place_ref, distance, choices, act):
    owner = place_ref[3] ^ (distance % 2)
    for core in range(2):

        @pl.when(owner == core)
        def _(copies=choices[core]):
            for copy in copies:
                act(copy)


def start_copy(copy):
    copy.start()


def wait_copy(copy):
    copy.wait()


def column_kernel(place_ref, *refs):
    *piece_refs, column_ref = refs
    for step, ref in enumerate(piece_refs):
        column_ref[0, lax.rem(place_ref[0] + step, len(piece_refs))] = ref[...]


class Grid:
    deep, devices, blocks = 4, 32, 8

    def __init__(self):
        dp, mp = lax.axis_index("dp"), lax.axis_index("mp")
        self.z, self.x, self.y, self.core = dp // 2, dp % 2, mp // 2, mp % 2
        self.at_first = jnp.where(self.core == 0, self.y, self.x)
        self.at_second = jnp.where(self.core == 0, self.x, self.y)
        chunk = self.core * 4 + self.at_first * 2 + self.at_second
        other_chunk = (1 - self.core) * 4 + self.at_second * 2 + self.at_first
        self.place = jnp.stack([self.z, self.x, self.y, self.core, dp, mp, chunk, other_chunk])
        self.place = self.place.astype(jnp.int32)
        self.other = self.pairs(lambda z, x, y, c: (z, x, y, 1 - c))
        self.first = self.pairs(lambda z, x, y, c: (z, x ^ c, y ^ (1 - c), c))
        self.second = self.pairs(lambda z, x, y, c: (z, x ^ (1 - c), y ^ c, c))
        self.along_x = self.pairs(lambda z, x, y, c: (z, 1 - x, y, c))
        self.along_y = self.pairs(lambda z, x, y, c: (z, x, 1 - y, c))
        self.up = [self.pairs(lambda z, x, y, c, s=s: ((z + s) % 4, x, y, c)) for s in range(4)]
        self.flip_z = [self.pairs(lambda z, x, y, c, s=s: (z ^ s, x, y, c)) for s in range(4)]

    def pairs(self, move):
        table = []
        for index in range(self.devices):
            z, x, y, c = move(index // 8, index // 4 % 2, index // 2 % 2, index % 2)
            table.append((index, ((z * 2 + x) * 2 + y) * 2 + c))
        return table

    @staticmethod
    def send(values, table):
        return lax.ppermute(values, ALL, table)

    def gather(self, piece):
        got = yield piece, [self.send(piece, self.up[-s]) for s in (1, 2, 3)]
        column = pl.pallas_call(
            column_kernel,
            in_specs=[pl.BlockSpec(memory_space=pltpu.SMEM)]
            + [pl.BlockSpec(memory_space=pltpu.VMEM)] * self.deep,
            out_specs=pl.BlockSpec(memory_space=pltpu.VMEM),
            out_shape=jax.ShapeDtypeStruct((1, self.deep) + piece.shape, piece.dtype),
        )(self.place, piece, *got)
        got = yield column, self.send(column, self.second)
        pair = jnp.concatenate([column, got])
        rest, theirs = yield pair, (self.send(pair, self.first), self.send(pair, self.other))
        rest_theirs = yield rest, self.send(rest, self.other)
        return pair, rest, theirs, rest_theirs

    def whole(self, *pieces):
        blocks, (r, c) = self.blocks, pieces[0].shape[2:]

        def body(place_ref, *refs):
            full_ref, sems = refs[-2:]
            own = place_ref[2] * 2 + place_ref[3]
            groups = [
                (i, group_copies(place_ref, refs[:4], full_ref.at[own ^ i], sems.at[i], i))
                for i in range(4)
            ]
            for act in (start_copy, wait_copy):
                for distance, choices in groups:
                    each_copy(place_ref, distance, choices, act)

        full = pl.pallas_call(
            body,
            in_specs=[pl.BlockSpec(memory_space=pltpu.SMEM)]
            + [pl.BlockSpec(memory_space=pl.ANY)] * 4,
            out_specs=pl.BlockSpec(memory_space=pltpu.VMEM),
            out_shape=jax.ShapeDtypeStruct((4, self.deep, 2, r, c), pieces[0].dtype),
            scratch_shapes=[pltpu.SemaphoreType.DMA((4, 2))],
            compiler_params=pltpu.CompilerParams(vmem_limit_bytes=16 * 1024 * 1024),
        )(self.place, *pieces)
        return full.reshape(4, blocks * r, c)

    def reduce(self, far):
        theirs, near = yield far, self.send(far, self.other)
        shape = (4, self.deep, near.shape[1] // self.blocks, near.shape[2])
        near, theirs = near.reshape(shape), theirs.reshape(shape)

        def chip(index):
            return (
                lax.dynamic_index_in_dim(near, index, 0, keepdims=False).astype(f32)
                + lax.dynamic_index_in_dim(theirs, index, 0, keepdims=False).astype(f32)
            )

        sent = jnp.stack([chip(0), chip(1 + self.core)]).astype(bf16)
        got = yield sent, self.send(sent, self.first)
        away = (chip(2 - self.core) + got[0].astype(f32)).astype(bf16)
        came = yield away, self.send(away, self.second)
        column = chip(3) + got[1].astype(f32) + came.astype(f32)
        low = column.astype(bf16)
        total = column[0]
        for part in (yield low, [self.send(low[s], self.up[s]) for s in (1, 2, 3)]):
            total = total + part.astype(f32)
        return total

    def add(self, values):
        for table in (self.other, self.along_y, self.along_x, self.flip_z[1], self.flip_z[2]):
            values = values + (yield values, self.send(values, table))
        return values

    def add_large(self, far, near):
        values = near.astype(f32) + (yield far, self.send(far, self.other)).astype(f32)
        for table in (self.first, self.second):
            half = values.shape[0] // 2
            sent = values[half:].astype(bf16)
            got = yield sent, self.send(sent, table)
            values = values[:half] + got.astype(f32)
        pile = values.astype(bf16)
        for table in (self.flip_z[1], self.flip_z[2]):
            got = yield pile, self.send(pile, table)
            pile = (pile.astype(f32) + got.astype(f32)).astype(bf16)
        for table in (self.second, self.first):
            pile = jnp.concatenate([pile, (yield pile, self.send(pile, table))])
        return pile, (yield pile, self.send(pile, self.other))


def normal_parts(values):
    centred = values - jnp.mean(values, -1, keepdims=True)
    inverse = lax.rsqrt(jnp.mean(centred * centred, -1, keepdims=True) + eps_norm)
    return centred * inverse, inverse


def pull_normal(values, gain, grads):
    hat, inverse = normal_parts(values)
    scaled = grads * gain
    mean_one = jnp.mean(scaled, -1, keepdims=True)
    mean_two = jnp.mean(scaled * hat, -1, keepdims=True)
    below = (scaled - mean_one - hat * mean_two) * inverse
    return below, jnp.sum(grads * hat, 0, keepdims=True), jnp.sum(grads, 0, keepdims=True)


STEM_BIAS, GAIN_ONE, SHIFT_ONE, QUERY_BIAS, VALUE_BIAS, ATTEND_BIAS, GAIN_TWO, SHIFT_TWO = range(8)
EXPAND_BIAS, CONTRACT_BIAS, GAIN_LAST, SHIFT_LAST, HEAD_BIAS = 8, 12, 13, 14, 15


def line(vectors_ref, index):
    return vectors_ref[index : index + 1, :]


def share_of(vectors_ref, index, group, share):
    result = vectors_ref[index : index + 1, :share]
    for other in range(1, vectors_ref.shape[1] // share):
        part = vectors_ref[index : index + 1, other * share : (other + 1) * share]
        result = jnp.where(group == other, part, result)
    return result


def own_group(place_ref, order):
    step = pl.program_id(0)
    distance = order[0]
    for index, value in enumerate(order[1:], 1):
        distance = jnp.where(step == index, value, distance)
    return (place_ref[2] * 2 + place_ref[3]) ^ distance


def dot(left, right, left_dim=1, right_dim=0):
    return lax.dot_general(
        left, right, (((left_dim,), (right_dim,)), ((), ())), preferred_element_type=f32
    )


def put(count, index, line):
    spot = lax.broadcasted_iota(jnp.int32, (count, 1), 0)
    return jnp.where(spot == index, line, 0.0)


def pick(lines, index):
    spot = lax.broadcasted_iota(jnp.int32, (lines.shape[0], 1), 0)
    return jnp.sum(jnp.where(spot == index, lines, 0.0), 0, keepdims=True)


def upright(row):
    n = row.shape[1]
    more = -n % 128
    if more:
        row = jnp.concatenate([row, jnp.zeros((1, more), f32)], 1)
    return jnp.broadcast_to(row, (128, n + more)).T[:n, 0:1]


def lying(column):
    n = column.shape[0]
    wide = jnp.broadcast_to(column, (n, 128))
    more = -n % 128
    if more:
        wide = jnp.concatenate([wide, jnp.zeros((more, 128), f32)])
    return wide.T[0:1, :n]


def probabilities(query, key, visible):
    scores = dot(query, key, 1, 1) * HEAD_DIM ** (-0.5)
    scores = jnp.where(visible, scores, -1e30)
    raised = jnp.exp(scores - jnp.max(scores, -1, keepdims=True))
    return raised * (1.0 / jnp.sum(raised, -1, keepdims=True))


def head_masks(share):
    lane = lax.broadcasted_iota(jnp.int32, (1, share), 1) // HEAD_DIM
    return [lane == head for head in range(share // HEAD_DIM)]


def stacked(rows, masks):
    return jnp.concatenate([jnp.where(mask, rows, jnp.zeros((), rows.dtype)) for mask in masks])


def unstacked(every, masks):
    size = every.shape[0] // len(masks)
    result = every[:size]
    for head, mask in enumerate(masks[1:], 1):
        result = jnp.where(mask, every[head * size : (head + 1) * size], result)
    return result


def turn(place_ref, values, result_ref, blocks):
    turned = values.T
    if blocks is None:
        result_ref[...] = turned
        return
    size, deep = turned.shape[0] // blocks, blocks // 2
    for block in range(blocks):
        level = lax.rem(block // 2 - place_ref[0] + deep, deep)
        spot = (1 - (block % 2 ^ place_ref[1])) * deep + level
        rows = pl.ds(pl.multiple_of(spot * size, size), size)
        result_ref[rows, :] = turned[block * size : (block + 1) * size, :]


def pieces_kernel(
    place_ref,
    in_ref,
    out_ref,
    expand_ref,
    contract_ref,
    own_ref,
    attend_low_ref,
    expand_low_ref,
    contract_low_ref,
    square_ref,
):
    share = out_ref.shape[0]
    lane = lax.broadcasted_iota(jnp.int32, (1, 128), 1)
    for part in range(3):
        own_ref[:, part * share : (part + 1) * share] = in_ref[part]
    own_ref[:, 3 * share :] = out_ref[...].T
    attend_low_ref[...] = own_ref[...].astype(bf16)
    expand_low_ref[...] = expand_ref[...].astype(bf16)
    contract_low_ref[...] = contract_ref[...].astype(bf16)
    totals = jnp.zeros((1, 128), f32)
    for index, ref in enumerate((in_ref, out_ref, expand_ref, contract_ref)):
        values = ref[...]
        total = jnp.sum(values * values, keepdims=True).reshape(1, 1)
        totals = jnp.where(lane == index, total, totals)
    square_ref[...] = totals


def stem_kernel(
    place_ref,
    labels_ref,
    pixels_ref,
    stem_ref,
    table_ref,
    vectors_ref,
    mask_ref,
    stream_ref,
    rows_ref,
    present_ref,
    column_ref,
    facts_ref,
):
    count, patch_count = mask_ref.shape
    padded = present_ref.shape[1]
    low = stem_ref[...].astype(bf16)
    slot = lax.broadcasted_iota(jnp.int32, (padded, 1), 0)
    table = table_ref[...] + jnp.where(slot < patch_count, line(vectors_ref, STEM_BIAS), 0.0)
    for image in range(count):
        span = slice(image * padded, (image + 1) * padded)
        stream = dot(pixels_ref[span, :], low) + table
        stream_ref[span, :] = stream
        hat, _ = normal_parts(stream)
        normed = hat * line(vectors_ref, GAIN_ONE) + line(vectors_ref, SHIFT_ONE)
        rows_ref[span, :] = normed.astype(bf16)
    lane = lax.broadcasted_iota(jnp.int32, (count, padded), 1)
    present_ref[...] = jnp.where(lane == patch_count, 1.0, 0.0)
    present_ref[:, :patch_count] = mask_ref[...].astype(f32)
    lane = lax.broadcasted_iota(jnp.int32, (1, 128), 1)
    for image in range(count):
        present = present_ref[image : image + 1, :]
        column_ref[image * padded : (image + 1) * padded, :] = upright(present)
        kept = jnp.sum(present, 1, keepdims=True)
        label = labels_ref[image].astype(f32)
        fact = jnp.where(lane == 0, kept, jnp.where(lane == 1, label, 0.0))
        facts_ref[image : image + 1, :] = fact
        facts_ref[count + image : count + image + 1, :] = fact


def attend_kernel(
    place_ref,
    weight,
    rows_ref,
    vectors_ref,
    present_ref,
    stream_ref,
    column_ref,
    qkv_ref,
    attended_ref,
    stream_out_ref,
    rows_out_ref,
    turned_one_ref,
    turned_two_ref,
    sum_ref,
    *,
    blocks,
    order,
):
    step = pl.program_id(0)
    count, padded = present_ref.shape
    share = attended_ref.shape[2]

    @pl.when(step == 0)
    def _():
        turn(place_ref, rows_ref[...], turned_one_ref, blocks)

    group = own_group(place_ref, order)
    projected = dot(rows_ref[...], weight(0, 3 * share))
    query = projected[:, :share] + share_of(vectors_ref, QUERY_BIAS, group, share)
    query = query.astype(bf16)
    key = projected[:, share : 2 * share].astype(bf16)
    value = projected[:, 2 * share :] + share_of(vectors_ref, VALUE_BIAS, group, share)
    value = value.astype(bf16)
    qkv_ref[0, 0] = query
    qkv_ref[0, 1] = key
    qkv_ref[0, 2] = value
    masks = head_masks(share)
    for image in range(count):
        span = slice(image * padded, (image + 1) * padded)
        visible = present_ref[image : image + 1, :] > 0.5
        low = probabilities(stacked(query[span], masks), key[span], visible).astype(bf16)
        every = dot(low, value[span])
        attended_ref[0, span, :] = unstacked(every, masks).astype(bf16)
    part = dot(attended_ref[0], weight(3 * share, 4 * share), 1, 1)

    @pl.when(step == 0)
    def _():
        stream_out_ref[...] = stream_ref[...] + line(vectors_ref, ATTEND_BIAS) + part

    @pl.when(step > 0)
    def _():
        stream_out_ref[...] += part

    @pl.when(step == pl.num_programs(0) - 1)
    def _():
        hat, _ = normal_parts(stream_out_ref[...])
        rows_two = hat * line(vectors_ref, GAIN_TWO) + line(vectors_ref, SHIFT_TWO)
        rows_two = rows_two.astype(bf16)
        rows_out_ref[...] = rows_two
        turn(place_ref, rows_two, turned_two_ref, blocks)
        for image in range(count):
            span = slice(image * padded, (image + 1) * padded)
            total = jnp.sum(stream_out_ref[span, :] * column_ref[span, :], 0, keepdims=True)
            sum_ref[image : image + 1, :] = total
            sum_ref[image + count : image + count + 1, :] = total


def hidden_kernel(
    place_ref,
    weight,
    rows_ref,
    vectors_ref,
    present_ref,
    column_ref,
    sum_ref,
    slope_ref,
    *,
    order,
):
    bias = pick(vectors_ref[EXPAND_BIAS : EXPAND_BIAS + len(order), :], own_group(place_ref, order))
    hidden = dot(rows_ref[...], weight()) + bias
    first, second = 0.7978845608028654, 0.044715
    square = hidden * hidden
    half = 0.5 + 0.5 * jnp.tanh(hidden * (first + first * second * square))
    active = (hidden * half).astype(bf16)
    count, padded = present_ref.shape
    row = lax.broadcasted_iota(jnp.int32, (2 * count, 1), 0)
    sums = jnp.zeros(sum_ref.shape[1:], f32)
    for image in range(count):
        chooser = jnp.broadcast_to(present_ref[image : image + 1, :], (2 * count, padded))
        total = dot(chooser.astype(bf16), active[image * padded : (image + 1) * padded])
        sums = jnp.where(row % count == image, total, sums)
    sum_ref[0] = sums
    steep = hidden * (2.0 * first + 6.0 * first * second * square)
    slope = half * (1.0 + steep * (1.0 - half))
    slope_ref[0] = (slope * column_ref[...]).astype(bf16)


def expand_back_kernel(
    place_ref,
    weight,
    turned_ref,
    slope_ref,
    d_active_ref,
    far_ref,
    near_ref,
    bias_ref,
    d_rows_ref,
    d_hidden_low,
):
    step = pl.program_id(0)
    count = d_active_ref.shape[1] // 2
    padded = slope_ref.shape[1] // count
    bias = jnp.zeros((1, d_hidden_low.shape[1]), f32)
    for image in range(count):
        span = slice(image * padded, (image + 1) * padded)
        d_hidden = slope_ref[0, span, :].astype(f32) * d_active_ref[0, image : image + 1, :]
        bias = bias + jnp.sum(d_hidden, 0, keepdims=True)
        d_hidden_low[span, :] = d_hidden.astype(bf16)
    bias_ref[0] = bias
    grad = dot(turned_ref[...], d_hidden_low[...]).astype(bf16)
    half = pl.num_programs(0) // 2

    @pl.when(step < half)
    def _():
        far_ref[0] = grad

    @pl.when(step >= half)
    def _():
        near_ref[0] = grad

    part = dot(d_hidden_low[...], weight(), 1, 1)

    @pl.when(step == 0)
    def _():
        d_rows_ref[...] = part

    @pl.when(step > 0)
    def _():
        d_rows_ref[...] += part


def between_kernel(
    place_ref,
    d_rows_ref,
    d_row_ref,
    column_ref,
    stream_ref,
    vectors_ref,
    d_stream_ref,
    d_low_ref,
    turned_ref,
    vector_ref,
    *,
    blocks,
):
    count = d_row_ref.shape[0] // 2
    padded = stream_ref.shape[0] // count
    gain = line(vectors_ref, GAIN_TWO)
    below, gain, shift = pull_normal(stream_ref[...], gain, d_rows_ref[...])
    vector_ref[1:2, :] = gain
    vector_ref[2:3, :] = shift
    bias = jnp.zeros((1, below.shape[1]), f32)
    for image in range(count):
        span = slice(image * padded, (image + 1) * padded)
        d_stream = below[span] + d_row_ref[image : image + 1, :] * column_ref[span, :]
        bias = bias + jnp.sum(d_stream, 0, keepdims=True)
        d_stream_ref[span, :] = d_stream
        d_low_ref[span, :] = d_stream.astype(bf16)
    vector_ref[0:1, :] = bias
    turn(place_ref, d_low_ref[...], turned_ref, blocks)


def attend_back_kernel(
    place_ref,
    weight,
    turned_ref,
    qkv_ref,
    attended_ref,
    column_ref,
    d_low_ref,
    d_turned_ref,
    *refs,
):
    grad_ref, bias_ref, d_rows_ref, d_projected = refs[-4:]
    step = pl.program_id(0)
    share = attended_ref.shape[2]
    count = bias_ref.shape[1] // 2
    padded = attended_ref.shape[1] // count
    scale = HEAD_DIM ** (-0.5)
    d_attended = dot(d_low_ref[...], weight(3 * share, 4 * share)).astype(bf16)
    masks = head_masks(share)
    for image in range(count):
        span = slice(image * padded, (image + 1) * padded)
        hidden = column_ref[span, :] < 0.5
        query, key, value = (qkv_ref[0, part, span, :] for part in range(3))
        query = query * jnp.asarray(scale, bf16)
        queries = stacked(query, masks)
        d_images = stacked(d_attended[span], masks)
        scores = jnp.where(hidden, -1e30, dot(key, queries, 1, 1))
        raised = jnp.exp(scores - jnp.max(scores, 0, keepdims=True))
        probs = raised * (1.0 / jnp.sum(raised, 0, keepdims=True))
        d_probs = dot(value, d_images, 1, 1)
        inner = jnp.sum(probs * d_probs, 0, keepdims=True)
        d_scores = (probs * (d_probs - inner)).astype(bf16)
        d_value = dot(probs.astype(bf16), d_images)
        d_key = dot(d_scores, queries)
        d_query = unstacked(dot(d_scores, key, 0, 0), masks) * scale
        bias_ref[0, image : image + 1, :] = jnp.sum(d_query, 0, keepdims=True)
        bias_ref[0, count + image : count + image + 1, :] = jnp.sum(d_value, 0, keepdims=True)
        d_projected[span, :share] = d_query.astype(bf16)
        d_projected[span, share : 2 * share] = d_key.astype(bf16)
        d_projected[span, 2 * share :] = d_value.astype(bf16)
    grad_ref[0, :, : 3 * share] = dot(turned_ref[...], d_projected[...]).astype(bf16)
    grad_ref[0, :, 3 * share :] = dot(d_turned_ref[...], attended_ref[0]).astype(bf16)
    part = dot(d_projected[...], weight(0, 3 * share), 1, 1)

    @pl.when(step == 0)
    def _():
        d_rows_ref[...] = part + refs[0][...] if len(refs) > 4 else part

    @pl.when(step > 0)
    def _():
        d_rows_ref[...] += part


def stem_back_kernel(
    place_ref,
    d_rows_ref,
    d_stream_ref,
    stream_ref,
    vectors_ref,
    pixels_ref,
    far_ref,
    near_ref,
    vector_ref,
):
    rows, width = pixels_ref.shape
    gain = line(vectors_ref, GAIN_ONE)
    below, gain, shift = pull_normal(stream_ref[...], gain, d_rows_ref[...])
    vector_ref[0:1, :] = gain
    vector_ref[1:2, :] = shift
    below = below + d_stream_ref[...]
    slots = vector_ref.shape[0] - 8
    table = below[:slots]
    for image in range(1, rows // slots):
        table = table + below[image * slots : (image + 1) * slots]
    vector_ref[8:, :] = table
    stem = dot(pixels_ref[...].T, below.astype(bf16)).astype(bf16)
    half, size, columns = near_ref.shape
    empty = jnp.zeros((2 * half * size - width - slots, columns), bf16)
    whole = jnp.concatenate([stem, table.astype(bf16), empty])
    for chunk in range(2 * half):
        near, far = place_ref[6] ^ chunk, place_ref[7] ^ chunk

        @pl.when(near < half)
        def _(chunk=chunk, near=near):
            near_ref[near] = whole[chunk * size : (chunk + 1) * size]

        @pl.when(far < half)
        def _(chunk=chunk, far=far):
            far_ref[far] = whole[chunk * size : (chunk + 1) * size]


def head_vectors(vectors_ref):
    rest = CLASSES - vectors_ref.shape[1]
    bias = jnp.concatenate(
        [line(vectors_ref, HEAD_BIAS), vectors_ref[HEAD_BIAS + 1 : HEAD_BIAS + 2, :rest]], 1
    )
    return line(vectors_ref, GAIN_LAST), line(vectors_ref, SHIFT_LAST), bias


def classify(pooled, labels, head, gain, shift, bias, inverse_count):
    hat, inverse = normal_parts(pooled)
    low = (hat * gain + shift).astype(bf16)
    logits = dot(low, head, 1, 1) + bias
    logits = logits - jnp.max(logits, -1, keepdims=True)
    raised = jnp.exp(logits)
    total = jnp.sum(raised, -1, keepdims=True)
    lane = lax.broadcasted_iota(jnp.int32, logits.shape, 1)
    target = jnp.where(lane == labels.astype(jnp.int32), 1.0 - smoothing, 0.0) + smoothing / CLASSES
    score = jnp.sum(target * (logits - jnp.log(total)), -1, keepdims=True)
    d_logits = (raised * (1.0 / total) - target) * inverse_count
    d_final = dot(d_logits.astype(bf16), head)
    scaled = d_final * gain
    mean_one = jnp.mean(scaled, -1, keepdims=True)
    mean_two = jnp.mean(scaled * hat, -1, keepdims=True)
    return score, low, d_logits, d_final, hat, (scaled - mean_one - hat * mean_two) * inverse


def split(values):
    high = values.astype(bf16)
    return high, (values - high.astype(f32)).astype(bf16)


def own_head_kernel(
    place_ref,
    active_ref,
    sum_ref,
    facts_ref,
    vectors_ref,
    head_ref,
    *refs,
    inverse_count,
):
    groups, twice, width = active_ref.shape
    rows = sum_ref.shape[1]
    if len(refs) == 4:
        full_ref, piece_ref, d_row_ref, d_active_ref = refs
        chosen = []
    else:
        piece_ref, d_row_ref, d_active_ref, full_ref, sems = refs[4:]
        chosen = [
            (r, group_copies(place_ref, refs[:4], full_ref.at[r], sems.at[r], r))
            for r in range(groups)
        ]
    for distance, choices in chosen:
        each_copy(place_ref, distance, choices, start_copy)
    mixed = jnp.zeros((2 * twice, rows), f32)
    for group in range(groups):
        for distance, choices in chosen[group : group + 1]:
            each_copy(place_ref, distance, choices, wait_copy)
        weight = full_ref[group].reshape(rows, width)
        mixed = mixed + dot(jnp.concatenate(split(active_ref[group])), weight, 1, 1)
    mixed = mixed[:twice] + mixed[twice:]
    kept, labels = facts_ref[:, 0:1], facts_ref[:, 1:2]
    pooled = (sum_ref[...] + mixed) / kept + line(vectors_ref, CONTRACT_BIAS)
    d_pooled = classify(
        pooled, labels, head_ref[...], *head_vectors(vectors_ref), inverse_count
    )[-1]
    d_row = d_pooled / kept
    d_row_ref[...] = d_row
    d_row_low = d_row.astype(bf16)
    first = lax.broadcasted_iota(jnp.int32, (twice, 1), 0) < twice // 2
    for group in range(groups):
        d_active_ref[group] = dot(d_row_low, full_ref[group].reshape(rows, width))
    for part, (pool, fact) in enumerate(zip(split(pooled), split(facts_ref[...]))):
        piece_ref[part * twice : (part + 1) * twice, :rows] = pool
        piece_ref[part * twice : (part + 1) * twice, rows:] = fact
    own = place_ref[2] * 2 + place_ref[3]
    for half in range(groups // 2):
        sums = jnp.where(first, active_ref[own ^ (2 * half)], active_ref[own ^ (2 * half + 1)])
        span = slice((2 + half) * twice, (3 + half) * twice)
        piece_ref[span, :rows] = sums.astype(bf16)
        piece_ref[span, rows:] = jnp.zeros((twice, piece_ref.shape[1] - rows), bf16)


def all_head_kernel(
    place_ref,
    pieces_ref,
    vectors_ref,
    head_ref,
    weight_ref,
    old_rows_ref,
    old_cols_ref,
    new_ref,
    new_rows_ref,
    new_cols_ref,
    contract_ref,
    vector_ref,
    bias_ref,
    grad_ref,
    *,
    inverse_count,
):
    pieces = pieces_ref[0].astype(f32)
    count, rows = pieces.shape[0], vectors_ref.shape[1]
    twice = pieces.shape[1] // 4

    def part(index):
        return pieces[:, index * twice : (index + 1) * twice].reshape(count * twice, -1)

    lines = part(0) + part(1)
    pooled, kept, labels = lines[:, :rows], lines[:, rows : rows + 1], lines[:, rows + 1 : rows + 2]
    score, low, d_logits, d_final, hat, d_pooled = classify(
        pooled, labels, head_ref[...], *head_vectors(vectors_ref), inverse_count
    )
    half = lax.broadcasted_iota(jnp.int32, (count * twice, 1), 0) % twice // (twice // 2)
    once = half == 0
    d_logits = jnp.where(once, d_logits, 0.0)
    own = place_ref[5]
    active = jnp.where(own // 2 == 0, part(2)[:, :rows], part(3)[:, :rows]).astype(bf16)
    d_row = jnp.where(half == own % 2, d_pooled / kept, 0.0).astype(bf16)
    share = contract_ref.shape[0]
    place = lax.broadcasted_iota(jnp.int32, (rows, share), 0)
    lane = lax.broadcasted_iota(jnp.int32, (rows, share), 1)
    chooser = (place == lane + place_ref[4] * share).astype(f32).astype(bf16)
    d_row = dot(d_row, chooser).astype(bf16)

    def total(values):
        return jnp.sum(jnp.where(once, values, 0.0), 0, keepdims=True)

    results = (
        (grad_ref, slice(None), dot(d_logits.astype(bf16), low, 0, 0)),
        (contract_ref, slice(None), dot(d_row, active, 0, 0)),
        (vector_ref, slice(0, 1), total(d_pooled)),
        (vector_ref, slice(1, 2), total(d_final * hat)),
        (vector_ref, slice(2, 3), total(d_final)),
        (bias_ref, slice(0, 1), jnp.sum(d_logits, 0, keepdims=True)),
        (bias_ref, slice(1, 2), -total(score) + jnp.zeros((1, bias_ref.shape[1]), f32)),
    )
    for ref, span, value in results:

        @pl.when(pl.program_id(0) == 0)
        def _(ref=ref, span=span, value=value):
            ref[span, :] = value

        @pl.when(pl.program_id(0) > 0)
        def _(ref=ref, span=span, value=value):
            ref[span, :] += value

    @pl.when(pl.program_id(0) == pl.num_programs(0) - 1)
    def _():
        new_ref[...], new_cols_ref[...], new_rows_ref[...] = factored(
            weight_ref[...], grad_ref[...], old_cols_ref[...], old_rows_ref[...], True
        )


def factored(weight, grad, down_old, across_old, turned, valid=None, count=None):
    down_old = upright(down_old)
    squared = grad * grad + eps_one
    n, m = grad.shape
    if valid is not None:
        squared = jnp.where(valid, squared, 0.0)
        n = count
    down_new = decay_rate * down_old + (1.0 - decay_rate) * (
        jnp.sum(squared, 1, keepdims=True) / m
    )
    across_new = decay_rate * across_old + (1.0 - decay_rate) * (
        jnp.sum(squared, 0, keepdims=True) / n
    )
    if turned:
        mean = jnp.sum(across_new, keepdims=True) / m
    else:
        mean = jnp.sum(down_new, keepdims=True) / n
    divisor = down_new if valid is None else jnp.where(valid, down_new, 1.0)
    update = grad * lax.rsqrt(divisor * across_new / mean)
    size = n * m
    clip = jnp.sqrt(jnp.sum(update * update, keepdims=True) / size) / clip_level
    magnitude = jnp.sqrt(jnp.sum(weight * weight, keepdims=True) / size)
    scale = step_rate * jnp.maximum(eps_two, magnitude) / jnp.maximum(1.0, clip)
    return weight - scale * update, lying(down_new), across_new


def stem_step_kernel(
    place_ref,
    near_ref,
    far_ref,
    stem_ref,
    stem_rows_ref,
    stem_cols_ref,
    table_ref,
    table_rows_ref,
    table_cols_ref,
    stem_new_ref,
    stem_rows_new_ref,
    stem_cols_new_ref,
    table_new_ref,
    table_rows_new_ref,
    table_cols_new_ref,
    both_ref,
    *,
    slots,
):
    n, padded = stem_ref.shape[0], table_ref.shape[0]
    half, size = near_ref.shape[:2]
    for chunk in range(2 * half):
        near, far = place_ref[6] ^ chunk, place_ref[7] ^ chunk
        span = slice(chunk * size, (chunk + 1) * size)

        @pl.when(near < half)
        def _(span=span, near=near):
            both_ref[span, :] = near_ref[near]

        @pl.when(far < half)
        def _(span=span, far=far):
            both_ref[span, :] = far_ref[far]

    stem_new_ref[...], stem_rows_new_ref[...], stem_cols_new_ref[...] = factored(
        stem_ref[...], both_ref[:n, :].astype(f32), stem_rows_ref[...], stem_cols_ref[...], False
    )
    valid = lax.broadcasted_iota(jnp.int32, (padded, 1), 0) < slots
    table_new_ref[...], table_rows_new_ref[...], table_cols_new_ref[...] = factored(
        table_ref[...],
        both_ref[n : n + padded, :].astype(f32),
        table_rows_ref[...],
        table_cols_ref[...],
        False,
        valid,
        slots,
    )


def layout(data, groups):
    return 0, data, data + 4 * groups, -(-(data + 4 * groups + 6) // 8) * 8


def across(column):
    n = column.shape[0]
    wide = jnp.broadcast_to(column, (n, 128))
    if n < 128:
        wide = jnp.concatenate([wide, jnp.zeros((128 - n, 128), f32)])
    return wide.T[0:1]


def down(row, n):
    return jnp.broadcast_to(row, (128, 128)).T[:n, 0:1]


def sums_kernel(
    place_ref,
    attend_ref,
    expand_ref,
    contract_ref,
    squares_ref,
    vector_one_ref,
    vector_two_ref,
    expand_bias_ref,
    heads_far_ref,
    heads_near_ref,
    sums_ref,
    *,
    data,
    groups,
    share,
    patch_count,
):
    block, group = place_ref[4], place_ref[5]
    own = place_ref[2] * 2 + place_ref[3]
    _, at_group, at_single, _ = layout(data, groups)
    sums_ref[...] = jnp.zeros(sums_ref.shape, f32)
    lane = lax.broadcasted_iota(jnp.int32, (1, attend_ref.shape[1]), 1)
    for index, ref in enumerate((attend_ref, expand_ref, contract_ref)):
        grad = ref[...]
        squared = grad * grad + eps_one
        span = slice(at_group + index * groups, at_group + (index + 1) * groups)
        sums_ref[span, :] = put(groups, group, jnp.sum(squared, 0, keepdims=True))
        if index == 0:
            lines = (
                jnp.sum(jnp.where(lane < 3 * share, squared, 0.0), 1, keepdims=True),
                jnp.sum(jnp.where(lane < 3 * share, 0.0, squared), 1, keepdims=True),
            )
        else:
            lines = (jnp.sum(squared, 1, keepdims=True),)
        for part, line in enumerate(lines):
            spot = (index + (index > 0) + part) * 128
            sums_ref[:data, spot : spot + 128] = put(data, block, across(line))
    sums_ref[:data, 512:640] = put(data, block, squares_ref[...])
    at_group += 3 * groups
    lines = jnp.zeros((groups, expand_bias_ref.shape[2]), f32)
    for distance in range(groups):
        lines = lines + put(groups, own ^ distance, expand_bias_ref[distance])
    sums_ref[at_group : at_group + groups, :] = lines
    count = heads_far_ref.shape[1] // 2
    for part in range(2):
        lines = jnp.zeros((groups, share), f32)
        for ref, order in ((heads_far_ref, (3, 1)), (heads_near_ref, (2, 0))):
            for step, distance in enumerate(order):
                lines = lines + put(
                    groups,
                    own ^ distance,
                    jnp.sum(ref[step][part * count : (part + 1) * count], 0, keepdims=True),
                )
        sums_ref[part * groups : (part + 1) * groups, 3 * share :] = lines
    stem_bias = jnp.sum(vector_one_ref[8 : 8 + patch_count, :], 0, keepdims=True)
    singles = (stem_bias, vector_one_ref[0:2, :], vector_two_ref[0:3, :])
    for line in singles:
        sums_ref[at_single : at_single + line.shape[0], :] = line
        at_single += line.shape[0]


def vector_kernel(
    place_ref,
    sums_ref,
    last_ref,
    head_ref,
    vectors_ref,
    second_ref,
    grad_ref,
    new_ref,
    second_new_ref,
    *,
    data,
    groups,
    share,
    length,
):
    _, at_group, at_single, _ = layout(data, groups)
    width = vectors_ref.shape[1]

    def single(index):
        return sums_ref[at_single + index : at_single + index + 1, :]

    def joined(part):
        lines = sums_ref[part * groups : (part + 1) * groups, 3 * share :]
        return jnp.concatenate([lines[g : g + 1] for g in range(groups)], 1)

    grad_ref[...] = jnp.zeros(grad_ref.shape, f32)
    spot = at_group + 3 * groups
    rest = CLASSES - width
    for index, value in (
        (STEM_BIAS, single(0)),
        (GAIN_ONE, single(1)),
        (SHIFT_ONE, single(2)),
        (QUERY_BIAS, joined(0)),
        (VALUE_BIAS, joined(1)),
        (ATTEND_BIAS, single(3)),
        (GAIN_TWO, single(4)),
        (SHIFT_TWO, single(5)),
        (EXPAND_BIAS, sums_ref[spot : spot + groups, :]),
        (CONTRACT_BIAS, last_ref[0:3, :]),
        (HEAD_BIAS, head_ref[0:1, :width]),
    ):
        grad_ref[index : index + value.shape[0], :] = value
    grad_ref[HEAD_BIAS + 1 : HEAD_BIAS + 2, :rest] = head_ref[0:1, width:]
    grad = grad_ref[...]
    row = lax.broadcasted_iota(jnp.int32, grad.shape, 0)
    lane = lax.broadcasted_iota(jnp.int32, grad.shape, 1)
    valid = row * width + lane < length
    second = decay_rate * second_ref[...] + (1.0 - decay_rate) * (grad * grad + eps_one)
    update = grad * lax.rsqrt(jnp.where(valid, second, 1.0))
    total = jnp.sum(update * update, keepdims=True) / length
    square = jnp.sum(vectors_ref[...] * vectors_ref[...], keepdims=True) / length
    scale = step_rate * jnp.maximum(eps_two, jnp.sqrt(square))
    scale = scale / jnp.maximum(1.0, jnp.sqrt(total) / clip_level)
    new_ref[...] = vectors_ref[...] - scale * update
    second_new_ref[...] = second


def renew_kernel(
    place_ref,
    sums_ref,
    rows_ref,
    cols_ref,
    attend_ref,
    expand_ref,
    contract_ref,
    rows_new_ref,
    cols_new_ref,
    update_ref,
    scalar_ref,
    square_ref,
    *,
    data,
    groups,
    share,
):
    block, group = place_ref[4], place_ref[5]
    size = attend_ref.shape[0]
    width = attend_ref.shape[1]
    _, at_group, _, _ = layout(data, groups)
    length, hidden = data * size, groups * width
    lane = lax.broadcasted_iota(jnp.int32, (1, width), 1)
    first = lane < 3 * share
    spare = lax.broadcasted_iota(jnp.int32, (1, 128), 1) < size
    counts = (3 * length, length, hidden, hidden)
    means = []
    for index, count in enumerate(counts):
        span = slice(index * 128, (index + 1) * 128)
        new = decay_rate * rows_ref[:, span] + (1.0 - decay_rate) * (sums_ref[:data, span] / count)
        rows_new_ref[:, span] = new
        means.append(jnp.sum(jnp.where(spare, new, 0.0), keepdims=True) / length)
    for index, count in enumerate((length, length, length)):
        span = slice(index * groups, (index + 1) * groups)
        lines = sums_ref[at_group + index * groups : at_group + (index + 1) * groups, :]
        new = decay_rate * cols_ref[span, :] + (1.0 - decay_rate) * (lines / count)
        cols_new_ref[span, :] = new
        if index == 0:
            means[1] = jnp.sum(jnp.where(first, 0.0, new), keepdims=True) / length
        if index == 2:
            means[3] = jnp.sum(new, keepdims=True) / hidden
    scalars = jnp.zeros((1, 128), f32)
    place_lane = lax.broadcasted_iota(jnp.int32, (1, 128), 1)
    for index, ref in enumerate((attend_ref, expand_ref, contract_ref)):
        across_row = pick(cols_new_ref[index * groups : (index + 1) * groups, :], group)

        def row(which):
            span = slice(which * 128, (which + 1) * 128)
            return down(pick(rows_new_ref[:, span], block), size)

        if index == 0:
            denominator = jnp.where(
                first, row(0) * across_row / means[0], row(1) * across_row / means[1]
            )
        else:
            denominator = row(index + 1) * across_row / means[index + 1]
        update = ref[...] * lax.rsqrt(denominator)
        update_ref[index] = update
        squared = update * update
        if index == 0:
            totals = (jnp.where(first, squared, 0.0), jnp.where(first, 0.0, squared))
        else:
            totals = (squared,)
        for part, total in enumerate(totals):
            spot = index + (index > 0) + part
            scalars = jnp.where(place_lane == spot, jnp.sum(total, keepdims=True), scalars)
    scalar_ref[...] = jnp.broadcast_to(scalars, scalar_ref.shape)
    squares = jnp.sum(sums_ref[:data, 512:640], 0, keepdims=True)
    square_ref[...] = jnp.broadcast_to(squares, square_ref.shape)


def step_kernel(
    place_ref,
    update_ref,
    scalar_ref,
    square_ref,
    attend_ref,
    expand_ref,
    contract_ref,
    in_ref,
    in_low_ref,
    out_ref,
    out_low_ref,
    expand_new_ref,
    expand_low_ref,
    contract_new_ref,
    contract_low_ref,
    *,
    sizes,
):
    share = in_ref.shape[2]
    scales = []
    for index, size in enumerate(sizes):
        total = scalar_ref[0:1, index : index + 1]
        square = square_ref[0:1, index : index + 1]
        clip = jnp.maximum(1.0, jnp.sqrt(total / size) / clip_level)
        scales.append(step_rate * jnp.maximum(eps_two, jnp.sqrt(square / size)) / clip)
    lane = lax.broadcasted_iota(jnp.int32, (1, attend_ref.shape[1]), 1)
    scale = jnp.where(lane < 3 * share, scales[0], scales[1])
    attend = attend_ref[...] - scale * update_ref[0]
    for part in range(3):
        lines = attend[:, part * share : (part + 1) * share]
        in_ref[part] = lines
        in_low_ref[part] = lines.astype(bf16)
    out = attend[:, 3 * share :].T
    out_ref[...] = out
    out_low_ref[...] = out.astype(bf16)
    expand = expand_ref[...] - scales[2] * update_ref[1]
    expand_new_ref[...] = expand
    expand_low_ref[...] = expand.astype(bf16)
    contract = contract_ref[...] - scales[3] * update_ref[2]
    contract_new_ref[...] = contract
    contract_low_ref[...] = contract.astype(bf16)


def call(
    body, order, place, operands, results, scratch=(), flops=0, weights=None
):
    steps = len(order)
    pieces = weights is not None and len(weights) == 4

    def distance(step):
        at = order[0]
        for index, value in enumerate(order[1:], 1):
            at = jnp.where(step == index, value, at)
        return at

    def spec(shape, mark):
        zeros = (0,) * (len(shape) - 1)
        if mark == "any":
            return pl.BlockSpec(memory_space=pl.ANY)
        if mark == "smem":
            return pl.BlockSpec(memory_space=pltpu.SMEM)
        if mark is False:
            return pl.BlockSpec(shape, lambda g, p: (0,) + zeros)
        if mark is True:
            return pl.BlockSpec(
                (1,) + shape[1:], lambda g, p: ((p[2] * 2 + p[3]) ^ distance(g),) + zeros
            )
        if mark == "far":
            return pl.BlockSpec((1,) + shape[1:], lambda g, p: (distance(g),) + zeros)
        return pl.BlockSpec((1,) + shape[1:], lambda g, p: (mark(g),) + zeros)

    operands, scratch = tuple(operands), tuple(scratch)
    kernel = body
    if weights is not None:
        operands = tuple((weight, "any" if pieces else True) for weight in weights) + operands
    if pieces:
        some = weights[0]
        height, width = some.shape[0] * some.shape[1] * some.shape[2], some.shape[3]
        full = (steps, some.shape[1], some.shape[0]) + some.shape[2:]
        scratch += ((full, some.dtype), ((steps, 2), None))

        def kernel(place_ref, *refs):
            full_ref, sems = refs[-2:]
            step = pl.program_id(0)
            copies = [
                (r, group_copies(place_ref, refs[:4], full_ref.at[i], sems.at[i], r))
                for i, r in enumerate(order)
            ]

            @pl.when(step == 0)
            def _():
                for distance, choices in copies:
                    each_copy(place_ref, distance, choices, start_copy)

            for index in range(steps):

                @pl.when(step == index)
                def _(index=index):
                    each_copy(place_ref, *copies[index], wait_copy)

            def weight(start=0, stop=width):
                return full_ref[step, :, :, :, start:stop].reshape(height, stop - start)

            body(place_ref, weight, *refs[4:-2])

    elif weights is not None:

        def kernel(place_ref, weight_ref, *refs):
            def weight(start=0, stop=weight_ref.shape[2]):
                return weight_ref[0, :, start:stop]

            body(place_ref, weight, *refs)

    return pl.pallas_call(
        kernel,
        grid_spec=pltpu.PrefetchScalarGridSpec(
            num_scalar_prefetch=1,
            grid=(steps,),
            in_specs=[spec(value.shape, mark) for value, mark in operands],
            out_specs=[spec(shape, mark) for shape, _, mark in results],
            scratch_shapes=[
                pltpu.SemaphoreType.DMA(shape) if kind is None else pltpu.VMEM(shape, kind)
                for shape, kind in scratch
            ],
        ),
        out_shape=[jax.ShapeDtypeStruct(shape, kind) for shape, kind, _ in results],
        compiler_params=pltpu.CompilerParams(vmem_limit_bytes=48 * 1024 * 1024),
        cost_estimate=pl.CostEstimate(flops=flops, bytes_accessed=16_000_000, transcendentals=0),
    )(place, *[value for value, _ in operands])


def local(
    patches,
    keep_mask,
    labels,
    stem_weight,
    position_table,
    attend_in,
    attend_out,
    expand,
    contract,
    head_weight,
    vectors,
    stem_rows,
    stem_cols,
    table_rows,
    table_cols,
    attend_in_rows,
    attend_in_cols,
    attend_out_rows,
    attend_out_cols,
    expand_rows,
    expand_cols,
    contract_rows,
    contract_cols,
    head_rows,
    head_cols,
    vector_second,
):
    data_size, model_size = lax.axis_size("dp"), lax.axis_size("mp")
    links = Grid() if (data_size, model_size) == (8, 4) else Plain(data_size, model_size)
    here = links.place
    count, patch_count, _ = patches.shape
    groups = model_size
    pair = groups // 2
    image_count = count * data_size * model_size
    inverse_count = 1.0 / image_count
    row_share, _, head_share = attend_in.shape
    hidden_share = expand.shape[1]
    in_share = 3 * head_share
    slots = patch_count + 1
    padded = -(-slots // 16) * 16
    rows = count * padded
    contract_own = contract.T
    attend_own, attend_piece, expand_piece, contract_piece, squares = call(
        pieces_kernel,
        (0,),
        here,
        (
            (attend_in.swapaxes(0, 1), False),
            (attend_out, False),
            (expand, False),
            (contract_own, False),
        ),
        (((row_share, D), f32, False),)
        + (((row_share, D), bf16, False),) * 3
        + (((1, 128), f32, False),),
    )
    attend_chain = Chain(links.gather(attend_piece))
    pixels = jnp.pad(patches, ((0, 0), (0, padded - patch_count), (0, 0))).reshape(rows, -1)
    empty = jnp.zeros((padded - slots, D), f32)
    table = jnp.concatenate([position_table[1:], position_table[:1], empty])
    vector_lines = jnp.pad(vectors, (0, 24 * D - vectors.shape[0])).reshape(24, D)
    (
        pixels,
        table,
        vector_lines,
        expand_piece,
        contract_piece,
        head_weight,
    ) = sync(
        [attend_chain],
        pixels,
        table,
        vector_lines,
        expand_piece,
        contract_piece,
        head_weight,
    )
    expand_chain = Chain(links.gather(expand_piece))
    stream_zero, rows_one, present, column, facts = call(
        stem_kernel,
        (0,),
        here,
        (
            (labels, "smem"),
            (after(pixels, attend_chain.sent), False),
            (stem_weight, False),
            (table, False),
            (vector_lines, False),
            (keep_mask, False),
        ),
        (
            ((rows, D), f32, False),
            ((rows, D), bf16, False),
            ((count, padded), f32, False),
            ((rows, 1), f32, False),
            ((2 * count, 128), f32, False),
        ),
        flops=2 * rows * D * D,
    )
    stream_zero, rows_one, contract_piece, head_weight = sync(
        [attend_chain, expand_chain],
        stream_zero,
        rows_one,
        contract_piece,
        head_weight,
    )
    contract_chain = Chain(links.gather(contract_piece))
    head_turned = head_weight.T
    head_low = head_turned.astype(bf16)

    head_low, _ = sync([attend_chain, contract_chain], head_low, expand_chain.sent)
    sync([attend_chain, expand_chain], contract_chain.sent)
    attend_all = attend_chain.result
    every = tuple(range(groups))

    qkv, attended, stream_one, rows_two, turned_one, turned_two, stream_sum = call(
        functools.partial(attend_kernel, blocks=links.blocks, order=every),
        every,
        here,
        (
            (rows_one, False),
            (vector_lines, False),
            (present, False),
            (stream_zero, False),
            (column, False),
        ),
        (
            ((groups, 3, rows, head_share), bf16, "far"),
            ((groups, rows, head_share), bf16, "far"),
            ((rows, D), f32, False),
            ((rows, D), bf16, False),
            ((D, rows), bf16, False),
            ((D, rows), bf16, False),
            ((2 * count, D), f32, False),
        ),
        flops=2 * rows * D * 4 * D,
        weights=attend_all,
    )
    rows_two, stream_sum = sync([expand_chain, contract_chain], rows_two, stream_sum)
    rows_two = sync([expand_chain], rows_two)
    expand_all = expand_chain.result
    active_sum, slope = call(
        functools.partial(hidden_kernel, order=every),
        every,
        here,
        (
            (rows_two, False),
            (vector_lines, False),
            (present, False),
            (column, False),
        ),
        (
            ((groups, 2 * count, hidden_share), f32, "far"),
            ((groups, rows, hidden_share), bf16, "far"),
        ),
        flops=2 * rows * D * FF,
        weights=expand_all,
    )
    active_sum, slope = sync([contract_chain], active_sum, slope)
    active_sum, slope = sync([contract_chain], active_sum, slope)

    contract_all = contract_chain.result
    scratch = ()
    if len(contract_all) == 4:
        scratch = (
            ((groups, data_size // 2, 2, row_share, hidden_share), bf16),
            ((groups, 2), None),
        )
    piece, d_row, d_active_row = call(
        functools.partial(own_head_kernel, inverse_count=inverse_count),
        (0,),
        here,
        tuple((value, False) for value in (active_sum, stream_sum, facts, vector_lines, head_low))
        + tuple((value, "any" if scratch else False) for value in contract_all),
        (
            ((8 * count, D + 128), bf16, False),
            ((2 * count, D), f32, False),
            ((groups, 2 * count, hidden_share), f32, False),
        ),
        scratch,
    )

    pieces_chain = Chain(links.gather(piece))
    far_grad, near_grad, expand_bias_grad, d_rows_two = call(
        expand_back_kernel,
        (3, 1, 2, 0),
        here,
        (
            (turned_two, False),
            (slope, "far"),
            (d_active_row, "far"),
        ),
        (
            ((pair, D, hidden_share), bf16, lambda g: jnp.minimum(g, pair - 1)),
            ((pair, D, hidden_share), bf16, lambda g: jnp.maximum(g - pair, 0)),
            ((groups, 1, hidden_share), f32, "far"),
            ((rows, D), f32, False),
        ),
        (((rows, hidden_share), bf16),),
        flops=4 * rows * D * FF,
        weights=expand_all,
    )
    far_grad, near_grad, d_rows_two = sync([pieces_chain], far_grad, near_grad, d_rows_two)
    expand_sum = Chain(links.reduce(far_grad))
    d_stream, d_attend_low, d_turned, vector_two = call(
        functools.partial(between_kernel, blocks=links.blocks),
        (0,),
        here,
        (
            (d_rows_two, False),
            (d_row, False),
            (column, False),
            (stream_one, False),
            (vector_lines, False),
        ),
        (
            ((rows, D), f32, False),
            ((rows, D), bf16, False),
            ((D, rows), bf16, False),
            ((8, D), f32, False),
        ),
    )

    d_stream, d_attend_low, d_turned = sync(
        [pieces_chain, (expand_sum, near_grad)], d_stream, d_attend_low, d_turned
    )

    def attend_back(order, *before):
        return call(
            attend_back_kernel,
            order,
            here,
            (
                (turned_one, False),
                (qkv, "far"),
                (attended, "far"),
                (column, False),
                (d_attend_low, False),
                (d_turned, False),
            )
            + tuple((value, False) for value in before),
            (
                ((pair, D, D), bf16, lambda g: g),
                ((pair, 2 * count, head_share), f32, lambda g: g),
                ((rows, D), f32, False),
            ),
            (((rows, 3 * head_share), bf16),),
            flops=2 * rows * D * 4 * D,
            weights=attend_all,
        )

    far_grad, heads_far, d_rows_one = attend_back((3, 1))
    far_grad, d_rows_one = sync([pieces_chain, expand_sum], far_grad, d_rows_one)
    attend_sum = Chain(links.reduce(far_grad))
    near_grad, heads_near, d_rows_one = attend_back((2, 0), d_rows_one)
    d_rows_one = sync([pieces_chain, expand_sum, (attend_sum, near_grad)], d_rows_one)
    both_far, both_near, vector_one = call(
        stem_back_kernel,
        (0,),
        here,
        (
            (after(d_rows_one, attend_sum.sent, expand_sum.sent), False),
            (d_stream, False),
            (stream_zero, False),
            (vector_lines, False),
            (pixels, False),
        ),
        (
            ((4, 128, D), bf16, False),
            ((4, 128, D), bf16, False),
            ((8 + padded, D), f32, False),
        ),
        flops=2 * rows * D * D,
    )
    pieces, both_far, both_near = sync(
        [attend_sum, expand_sum], pieces_chain.result, both_far, both_near
    )
    grad_expand = expand_sum.result
    both_sum = Chain(links.add_large(both_far, both_near))
    pieces = links.whole(*pieces).reshape((-1,) + piece.shape)
    pieces, grad_expand = sync([attend_sum, both_sum], pieces, grad_expand)
    steps = max(1, pieces.shape[0] // 32)
    head_new, head_rows_new, head_cols_new, grad_contract, vector_last, vector_head = call(
        functools.partial(all_head_kernel, inverse_count=inverse_count),
        (0,) * steps,
        here,
        (
            (pieces.reshape((steps, -1) + piece.shape), lambda g: g),
            (vector_lines, False),
            (head_low, False),
            (head_turned, False),
            (head_rows[None], False),
            (head_cols[None], False),
        ),
        (
            ((CLASSES, D), f32, False),
            ((1, D), f32, False),
            ((1, CLASSES), f32, False),
            ((row_share, hidden_share), f32, False),
            ((8, D), f32, False),
            ((8, CLASSES), f32, False),
        ),
        (((CLASSES, D), f32),),
    )
    loss_sum = vector_head[1, 0]
    grad_expand, grad_contract = sync([attend_sum, both_sum], grad_expand, grad_contract)
    grad_attend = attend_sum.result

    names = dict(data=data_size, groups=groups, share=head_share)
    lines = layout(data_size, groups)[3]
    (sums,) = call(
        functools.partial(sums_kernel, patch_count=patch_count, **names),
        (0,),
        here,
        tuple(
            (value, False)
            for value in (
                grad_attend,
                grad_expand,
                grad_contract,
                squares,
                vector_one,
                vector_two,
                expand_bias_grad,
                heads_far,
                heads_near,
            )
        ),
        (((lines, D), f32, False),),
    )
    sums_chain = Chain(links.add(sums))
    sync([sums_chain, both_sum])
    (
        attend_in_rows,
        attend_out_cols,
        expand_rows,
        contract_cols,
        attend_in_cols,
        attend_out_rows,
        expand_cols,
        contract_rows,
    ) = sync(
        [sums_chain, both_sum],
        attend_in_rows,
        attend_out_cols,
        expand_rows,
        contract_cols,
        attend_in_cols,
        attend_out_rows,
        expand_cols,
        contract_rows,
    )
    def by_block(values):
        return jnp.pad(values.reshape(data_size, row_share), ((0, 0), (0, 128 - row_share)))

    old_rows = jnp.concatenate(
        [by_block(v) for v in (attend_in_rows, attend_out_cols, expand_rows, contract_cols)], 1
    )
    in_cols = attend_in_cols.reshape(3, groups, head_share).swapaxes(0, 1)
    old_cols = jnp.concatenate(
        [
            jnp.concatenate(
                [in_cols.reshape(groups, -1), attend_out_rows.reshape(groups, -1)], 1
            ),
            expand_cols.reshape(groups, -1),
            contract_rows.reshape(groups, -1),
        ]
    )
    old_rows, old_cols, table_rows, vector_second = sync(
        [sums_chain, both_sum], old_rows, old_cols, table_rows, vector_second
    )
    table_down = jnp.concatenate(
        [table_rows[1:], table_rows[:1], jnp.zeros((padded - slots,), f32)]
    )
    downs = (stem_rows[None], table_down[None])
    second_lines = jnp.pad(vector_second, (0, 24 * D - vectors.shape[0])).reshape(24, D)
    second_lines, downs = sync([sums_chain, both_sum], second_lines, downs)
    sync([sums_chain, both_sum])
    sums = sums_chain.result
    rows_new, cols_new, update, scalars, square_totals = call(
        functools.partial(renew_kernel, **names),
        (0,),
        here,
        tuple(
            (value, False)
            for value in (sums, old_rows, old_cols, grad_attend, grad_expand, grad_contract)
        ),
        (
            (old_rows.shape, f32, False),
            (old_cols.shape, f32, False),
            ((3, row_share, D), f32, False),
            ((8, 128), f32, False),
            ((8, 128), f32, False),
        ),
    )
    scalars_chain = Chain(links.add(scalars))
    rows_new, cols_new, sums = sync([scalars_chain, both_sum], rows_new, cols_new, sums)
    stem_new, stem_rows_new, stem_cols_new, table_new, table_rows_new, table_cols_new = call(
        functools.partial(stem_step_kernel, slots=slots),
        (0,),
        here,
        tuple(
            (value, False)
            for value in both_sum.result
            + (stem_weight, downs[0], stem_cols[None], table, downs[1], table_cols[None])
        ),
        tuple(
            (shape, f32, False)
            for shape in ((D, D), (1, D), (1, D), (padded, D), (1, padded), (1, D))
        ),
        (((1024, D), bf16),),
    )
    stem_new, table_new, table_rows_new, rows_new, cols_new, sums = sync(
        [scalars_chain], stem_new, table_new, table_rows_new, rows_new, cols_new, sums
    )

    vector_lines_new = call(
        functools.partial(vector_kernel, length=vectors.shape[0], **names),
        (0,),
        here,
        tuple(
            (value, False) for value in (sums, vector_last, vector_head, vector_lines, second_lines)
        ),
        (((24, D), f32, False),) * 3,
    )
    vector_lines_new, table_new, table_rows_new, rows_new, cols_new = sync(
        [scalars_chain], vector_lines_new, table_new, table_rows_new, rows_new, cols_new
    )
    grad_vector, vectors_new, second_new = (
        lines.reshape(-1)[: vectors.shape[0]] for lines in vector_lines_new
    )
    table_rows_new = table_rows_new.reshape(-1)
    table_new = jnp.concatenate([table_new[patch_count:slots], table_new[:patch_count]])
    table_rows_new = jnp.concatenate(
        [table_rows_new[patch_count:slots], table_rows_new[:patch_count]]
    )
    table_new, rows_new, cols_new = sync([scalars_chain], table_new, rows_new, cols_new)

    def of_blocks(index):
        return rows_new[:, index * 128 : index * 128 + row_share].reshape(-1)

    in_cols_new = cols_new[:groups, :in_share].reshape(groups, 3, head_share).swapaxes(0, 1)
    statistics = (
        of_blocks(0),
        in_cols_new.reshape(3, D),
        cols_new[:groups, in_share:].reshape(-1),
        of_blocks(1),
        of_blocks(2),
        cols_new[groups : 2 * groups].reshape(-1),
        cols_new[2 * groups :].reshape(-1),
        of_blocks(3),
    )
    statistics = sync([scalars_chain], statistics)
    block = call(
        functools.partial(step_kernel, sizes=(3 * D * D, D * D, D * FF, FF * D)),
        (0,),
        here,
        tuple(
            (value, False)
            for value in (
                update,
                scalars_chain.result,
                square_totals,
                attend_own,
                expand,
                contract_own,
            )
        ),
        tuple(
            (shape, kind, False)
            for shape in (
                (3, row_share, head_share),
                (head_share, row_share),
                (row_share, hidden_share),
                (row_share, hidden_share),
            )
            for kind in (f32, bf16)
        ),
    )
    in_new, in_copy, out_new, out_copy, expand_new, expand_copy, contract_new, contract_copy = block

    return (
        loss_sum,
        stem_new,
        stem_rows_new.reshape(-1),
        stem_cols_new.reshape(-1),
        table_new,
        table_rows_new,
        table_cols_new.reshape(-1),
        in_new.swapaxes(0, 1),
        in_copy.swapaxes(0, 1),
        statistics[0],
        statistics[1],
        out_new,
        out_copy,
        statistics[2],
        statistics[3],
        expand_new,
        expand_copy,
        statistics[4],
        statistics[5],
        contract_new.T,
        contract_copy.T,
        statistics[6],
        statistics[7],
        head_new.T,
        head_rows_new.reshape(-1),
        head_cols_new.reshape(-1),
        vectors_new,
        grad_vector,
        second_new,
    )


def solution(mesh):
    placed = (
        P(ALL, None, None),
        P(ALL, None),
        P(ALL),
        P(),
        P(),
        P("dp", None, "mp"),
        P("mp", "dp"),
        P("dp", "mp"),
        P("mp", "dp"),
    ) + (P(),) * 17
    block = (P("dp", None, "mp"), P("mp", "dp"), P("dp", "mp"), P("mp", "dp"))
    given = [P()] * 7
    for spec in block:
        given += [spec, spec, P(), P()]
    given += [P()] * 6
    return jax.shard_map(
        local, mesh=mesh, in_specs=placed, out_specs=tuple(given), check_vma=False
    )
```

time: 390 us -> 323 us (0.83)
  other arithmetic: 79 us -> 21.1 us
  local copies, waits for them, and re-layouts: 44.3 us -> 26.3 us
  waiting for transfers between devices: 50.7 us -> 67.8 us
  between operations: 10 us -> 2.02 us
  Pallas kernels: 134 us -> 141 us
  starting transfers between devices: 65.7 us -> 60 us
    reduce_sum x17 -> x0, other arithmetic: 20.1 us -> none  [the longest x3 7.7 us: factored_step(): jnp.mean(update * update)]
    ppermute x58, waiting for transfers between devices: 50.7 us -> 67.8 us  [send(): return lax.ppermute(values, ALL, table)]
    unnamed x196 -> x155, local copies, waits for them, and re-layouts: 26.7 us -> 14.4 us
    sub x4 -> x0, other arithmetic: 9.59 us -> none  [the longest x3 8.96 us: factored_step(): return (weight - step_rate * magnitude * update, rows_new, cols_new)]
    convert_element_type x12 -> x4, other arithmetic: 10 us -> 1.44 us  [the longest x1 1.29 us: local(): head_low = head_turned.astype(bf16)]
    pallas_call x16 -> x21, Pallas kernels: 134 us -> 141 us  [the longest x16 132 us: call(): pl.pallas_call(kernel, grid_spec=pltpu.PrefetchScalarGridSpec(num_scalar_...]
    broadcast_in_dim x5 -> x0, other arithmetic: 7.47 us -> none  [the longest x4 4.81 us: gather(): column = jnp.stack([piece] + got)[None]]
    ppermute x58, starting transfers between devices: 65.7 us -> 60 us  [send(): return lax.ppermute(values, ALL, table)]
  transfers between devices with their start and end apart: 58 -> 58, of which waited for: 21 -> 21; matrix products, arithmetic and copies ran while one was open for 20% -> 8% of each run, Pallas kernels for 32% -> 41%
where the time goes in v2:
time: 323 us; the launch traced here: 319 us
  Pallas kernels  141 us (44%)
  waiting for transfers between devices  67.8 us (21%)
  starting transfers between devices  60 us (19%)
  local copies, waits for them, and re-layouts  26.3 us (8%)
  other arithmetic  21.1 us (7%)
    pallas_call x16, Pallas kernels, call(): pl.pallas_call(kernel, grid_spec=pltpu.PrefetchScalarGridSpec(num_scalar_...  132 us
    ppermute x58, waiting for transfers between devices, send(): return lax.ppermute(values, ALL, table)  67.8 us
    ppermute x58, starting transfers between devices, send(): return lax.ppermute(values, ALL, table)  60 us
    unnamed x155, local copies, waits for them, and re-layouts  14.4 us
    pallas_call x4, Pallas kernels, gather(): pl.pallas_call(column_kernel, in_specs=[pl.BlockSpec(memory_space=pltpu.S...  7.6 us
  transfers between devices with their start and end apart: 58, of which 21 were waited for; matrix products, arithmetic and copies ran while one was open for 8% of the time, Pallas kernels for 41%

profile of v2, /device:TPU:0, one launch (start us, length us, event | category | flops | bytes accessed | tf_op | source)
XLA Modules:
  0.0 318.5 jit_solution(2766131730067034493)
XLA Ops:
  6.0 5.1 %collective-permute-start = (bf16[96,768]{1,0:T(8,128)(2,1)S(1)}, bf16[96,768]{1,0:T(8,128)(2,1)S(1)}, u32[]{:S(2)}, u32[]{:S(2)}) collective-permute-start(bf16[96,768]{1,0:T(8,128)(2,1)S(1)} %get-tuple-element.237.refs_0_), channel_id=1, source_target_pairs={{0,24},{1,25},{2,26},{3,27},{4,28},{5,29},{6,30},{7,31},{8,0},{9,1... | collective-permute-start | bytes 442376 | tf_op jit(solution)/shard_map/ppermute | solution.py:167
  16.7 7.0 %collective-permute-done.1.refs_2_ = bf16[96,768]{1,0:T(8,128)(2,1)} collective-permute-done((bf16[96,768]{1,0:T(8,128)(2,1)S(1)}, bf16[96,768]{1,0:T(8,128)(2,1)}, u32[]{:S(2)}, u32[]{:S(2)}) %collective-permute-start.1) | collective-permute-done | bytes 147488 | tf_op jit(solution)/shard_map/ppermute | solution.py:167
  33.7 4.1 %shard_map.475 = (f32[832,768]{1,0:T(8,128)}, bf16[832,768]{1,0:T(8,128)(2,1)S(1)}, f32[4,208]{1,0:T(4,128)S(1)}, f32[832,1]{1,0:T(8,128)S(1)}, f32[8,128]{1,0:T(8,128)S(1)}) custom-call(s32[8]{0:T(128)S(1)} %copy-done.27, s32[4]{0:T(128)S(1)} %copy-done.40, bf16[832,768]{1,0:T(8,128)(2,1)S(1)} %bitcast.73, f32[768,768]{1,0:T(8,128)S(1)} %copy-done.1, ...), custom_call_target="tpu_custom_call" | custom-call | flops 981467136 | bytes 16000000 | tf_op jit(solution)/shard_map/pallas_call | solution.py:1245
  37.8 4.7 %collective-permute-done.5.refs_2_ = bf16[96,768]{1,0:T(8,128)(2,1)S(1)} collective-permute-done((bf16[96,768]{1,0:T(8,128)(2,1)S(1)}, bf16[96,768]{1,0:T(8,128)(2,1)S(1)}, u32[]{:S(2)}, u32[]{:S(2)}) %collective-permute-start.5) | collective-permute-done | bytes 147488 | tf_op jit(solution)/shard_map/ppermute | solution.py:167
  45.2 4.0 %collective-permute-start.9 = (bf16[96,768]{1,0:T(8,128)(2,1)}, bf16[96,768]{1,0:T(8,128)(2,1)}, u32[]{:S(2)}, u32[]{:S(2)}) collective-permute-start(bf16[96,768]{1,0:T(8,128)(2,1)} %get-tuple-element.252.refs_0_), channel_id=1, source_target_pairs={{0,24},{1,25},{2,26},{3,27},{4,28},{5,29},{6,30},{7,31},{8,0},{9,1... | collective-permute-start | bytes 442376 | tf_op jit(solution)/shard_map/ppermute | solution.py:167
  52.5 3.8 %collective-permute-done.10.refs_2_ = bf16[96,768]{1,0:T(8,128)(2,1)} collective-permute-done((bf16[96,768]{1,0:T(8,128)(2,1)}, bf16[96,768]{1,0:T(8,128)(2,1)}, u32[]{:S(2)}, u32[]{:S(2)}) %collective-permute-start.10) | collective-permute-done | bytes 147488 | tf_op jit(solution)/shard_map/ppermute | solution.py:167
  63.1 6.7 %collective-permute-done.13 = bf16[1,4,96,768]{3,2,1,0:T(8,128)(2,1)} collective-permute-done((bf16[1,4,96,768]{3,2,1,0:T(8,128)(2,1)}, bf16[1,4,96,768]{3,2,1,0:T(8,128)(2,1)}, u32[]{:S(2)}, u32[]{:S(2)}) %collective-permute-start.13) | collective-permute-done | bytes 589856 | tf_op jit(solution)/shard_map/ppermute | solution.py:167
  73.3 20.4 %shard_map.478 = (bf16[4,3,832,192]{3,2,1,0:T(8,128)(2,1)}, bf16[4,832,192]{2,1,0:T(8,128)(2,1)}, f32[832,768]{1,0:T(8,128)}, bf16[832,768]{1,0:T(8,128)(2,1)}, ...) custom-call(s32[8]{0:T(128)S(1)} %copy-done.28, ...), custom_call_target="tpu_custom_call" | custom-call | flops 3925868544 | bytes 16000000 | tf_op jit(solution)/shard_map/pallas_call | solution.py:1245
  97.5 12.1 %shard_map.479 = (f32[4,8,768]{2,1,0:T(8,128)S(1)}, bf16[4,832,768]{2,1,0:T(8,128)(2,1)}) custom-call(s32[8]{0:T(128)S(1)} %copy-done.28, bf16[2,4,96,768]{3,2,1,0:T(8,128)(2,1)S(1)} %pad_maximum_fusion.1.refs_0_, bf16[2,4,96,768]{3,2,1,0:T(8,128)(2,1)S(1)} %collective-permute-done.14.refs_1_, bf16[2,4,96,768]{3,2,1,0:T(8,128)(2,1)S(1)} %collective-permute-done.15.refs_2_, ...), custom_call_target="tpu_custom_call" | custom-call | flops 3925868544 | bytes 16000000 | tf_op jit(solution)/shard_map/pallas_call | solution.py:1245
  114.2 6.8 %shard_map.480 = (bf16[32,896]{1,0:T(8,128)(2,1)S(1)}, f32[8,768]{1,0:T(8,128)S(1)}, f32[4,8,768]{2,1,0:T(8,128)S(1)}) custom-call(s32[8]{0:T(128)S(1)} %copy-done.28, f32[4,8,768]{2,1,0:T(8,128)S(1)} %get-tuple-element.282.active_ref, f32[8,768]{1,0:T(8,128)S(1)} %get-tuple-element.283.sum_ref, f32[8,128]{1,0:T(8,128)S(1)} %get-tuple-element.284.facts_ref, ...), custom_call_target="tpu_custom_call" | custom-call | bytes 16000000 | tf_op jit(solution)/shard_map/pallas_call | solution.py:1245
  124.4 19.2 %shard_map.481 = (bf16[2,768,768]{2,1,0:T(8,128)(2,1)}, bf16[2,768,768]{2,1,0:T(8,128)(2,1)}, f32[4,1,768]{2,1,0:T(1,128)S(1)}, f32[832,768]{1,0:T(8,128)}) custom-call(s32[8]{0:T(128)S(1)} %copy-done.28, bf16[2,4,96,768]{3,2,1,0:T(8,128)(2,1)S(1)} %pad_maximum_fusion.1.refs_0_, bf16[2,4,96,768]{3,2,1,0:T(8,128)(2,1)S(1)} %collective-permute-done.14.refs_1_, ...), custom_call_target="tpu_custom_call" | custom-call | flops 7851737088 | bytes 16000000 | tf_op jit(solution)/shard_map/pallas_call | solution.py:1245
  149.1 5.7 %shard_map.483 = (f32[832,768]{1,0:T(8,128)S(1)}, bf16[832,768]{1,0:T(8,128)(2,1)S(1)}, bf16[768,832]{1,0:T(8,128)(2,1)S(1)}, f32[8,768]{1,0:T(8,128)S(1)}) custom-call(s32[8]{0:T(128)S(1)} %copy-done.29, f32[832,768]{1,0:T(8,128)} %get-tuple-element.300.d_rows_ref, f32[8,768]{1,0:T(8,128)S(1)} %get-tuple-element.301.d_row_ref, ...), custom_call_target="tpu_custom_call" | custom-call | bytes 16000000 | tf_op jit(solution)/shard_map/pallas_call | solution.py:1245
  162.1 18.8 %shard_map.484 = (bf16[2,768,768]{2,1,0:T(8,128)(2,1)}, f32[2,8,192]{2,1,0:T(8,128)S(1)}, f32[832,768]{1,0:T(8,128)}) custom-call(s32[8]{0:T(128)S(1)} %copy-done.29, bf16[2,4,96,768]{3,2,1,0:T(8,128)(2,1)S(1)} %pad_maximum_fusion.refs_0_, bf16[2,4,96,768]{3,2,1,0:T(8,128)(2,1)} %collective-permute-done.7.refs_1_, ...), custom_call_target="tpu_custom_call" | custom-call | flops 3925868544 | bytes 16000000 | tf_op jit(solution)/shard_map/pallas_call | solution.py:1245
  185.6 19.4 %shard_map.485 = (bf16[2,768,768]{2,1,0:T(8,128)(2,1)}, f32[2,8,192]{2,1,0:T(8,128)S(1)}, f32[832,768]{1,0:T(8,128)}) custom-call(s32[8]{0:T(128)S(1)} %copy-done.29, bf16[2,4,96,768]{3,2,1,0:T(8,128)(2,1)S(1)} %pad_maximum_fusion.refs_0_, bf16[2,4,96,768]{3,2,1,0:T(8,128)(2,1)} %collective-permute-done.7.refs_1_, ...), custom_call_target="tpu_custom_call" | custom-call | flops 3925868544 | bytes 16000000 | tf_op jit(solution)/shard_map/pallas_call | solution.py:1245
  215.1 6.4 %shard_map.486 = (bf16[4,128,768]{2,1,0:T(8,128)(2,1)S(1)}, bf16[4,128,768]{2,1,0:T(8,128)(2,1)S(1)}, f32[216,768]{1,0:T(8,128)S(1)}) custom-call(s32[8]{0:T(128)S(1)} %copy-done.29, f32[832,768]{1,0:T(8,128)S(1)} %copy-done.10, f32[832,768]{1,0:T(8,128)} %copy-done.9, f32[832,768]{1,0:T(8,128)} %get-tuple-element.267.refs_7_.stream_ref, ...), custom_call_target="tpu_custom_call" | custom-call | flops 981467136 | bytes 16000000 | tf_op jit(solution)/shard_map/pallas_call | solution.py:1245
  228.1 7.6 %collective-permute-done.36 = bf16[4,96,768]{2,1,0:T(8,128)(2,1)S(1)} collective-permute-done((bf16[4,96,768]{2,1,0:T(8,128)(2,1)S(1)}, bf16[4,96,768]{2,1,0:T(8,128)(2,1)S(1)}, u32[]{:S(2)}, u32[]{:S(2)}) %collective-permute-start.36) | collective-permute-done | bytes 589856 | tf_op jit(solution)/shard_map/ppermute | solution.py:167
  238.4 3.7 %collective-permute-start.38 = (bf16[96,768]{1,0:T(8,128)(2,1)S(1)}, bf16[96,768]{1,0:T(8,128)(2,1)S(1)}, u32[]{:S(2)}, u32[]{:S(2)}) collective-permute-start(bf16[96,768]{1,0:T(8,128)(2,1)S(1)} %get-tuple-element.455), channel_id=1, source_target_pairs={{0,8},{1,9},{2,10},{3,11},{4,12},{5,13},{6,14},{7,15},{8,16},{9,17... | collective-permute-start | bytes 442376 | tf_op jit(solution)/shard_map/ppermute | solution.py:167
  244.5 9.3 %shard_map.488 = (f32[1000,768]{1,0:T(8,128)}, f32[1,768]{1,0:T(1,128)S(1)}, f32[1,1000]{1,0:T(1,128)}, f32[96,768]{1,0:T(8,128)S(1)}, f32[8,768]{1,0:T(8,128)S(1)}, /*index=5*/f32[8,1000]{1,0:T(8,128)S(1)}) custom-call(s32[8]{0:T(128)S(1)} %copy-done.29, bf16[1,32,32,896]{3,2,1,0:T(8,128)(2,1)S(1)} %bitcast.75, f32[24,768]{1,0:T(8,128)S(1)} %copy-done.8, ...), custom_call_target="tpu_custom_call" | custom-call | bytes 16000000 | tf_op jit(solution)/shard_map/pallas_call | solution.py:1245
  262.9 3.8 %collective-permute-done.44 = f32[32,768]{1,0:T(8,128)S(1)} collective-permute-done((f32[32,768]{1,0:T(8,128)S(1)}, f32[32,768]{1,0:T(8,128)S(1)}, u32[]{:S(2)}, u32[]{:S(2)}) %collective-permute-start.44) | collective-permute-done | bytes 98336 | tf_op jit(solution)/shard_map/ppermute | solution.py:167
  270.3 3.3 %collective-permute-done.46 = f32[32,768]{1,0:T(8,128)S(1)} collective-permute-done((f32[32,768]{1,0:T(8,128)S(1)}, f32[32,768]{1,0:T(8,128)S(1)}, u32[]{:S(2)}, u32[]{:S(2)}) %collective-permute-start.46) | collective-permute-done | bytes 98336 | tf_op jit(solution)/shard_map/ppermute | solution.py:167
  273.6 3.7 %collective-permute-done.47 = bf16[1,128,768]{2,1,0:T(8,128)(2,1)S(1)} collective-permute-done((bf16[1,128,768]{2,1,0:T(8,128)(2,1)S(1)}, bf16[1,128,768]{2,1,0:T(8,128)(2,1)S(1)}, u32[]{:S(2)}, u32[]{:S(2)}) %collective-permute-start.47) | collective-permute-done | bytes 196640 | tf_op jit(solution)/shard_map/ppermute | solution.py:167
  280.4 3.8 %collective-permute-done.48 = f32[32,768]{1,0:T(8,128)S(1)} collective-permute-done((f32[32,768]{1,0:T(8,128)S(1)}, f32[32,768]{1,0:T(8,128)S(1)}, u32[]{:S(2)}, u32[]{:S(2)}) %collective-permute-start.48) | collective-permute-done | bytes 98336 | tf_op jit(solution)/shard_map/ppermute | solution.py:167
  285.2 6.0 %collective-permute-done.50 = f32[32,768]{1,0:T(8,128)S(1)} collective-permute-done((f32[32,768]{1,0:T(8,128)S(1)}, f32[32,768]{1,0:T(8,128)S(1)}, u32[]{:S(2)}, u32[]{:S(2)}) %collective-permute-start.50) | collective-permute-done | bytes 98336 | tf_op jit(solution)/shard_map/ppermute | solution.py:167
  295.6 4.3 %shard_map.491 = (f32[768,768]{1,0:T(8,128)}, f32[1,768]{1,0:T(1,128)S(1)}, f32[1,768]{1,0:T(1,128)S(1)}, f32[208,768]{1,0:T(8,128)S(1)}, f32[1,208]{1,0:T(1,128)S(1)}, /*index=5*/f32[1,768]{1,0:T(1,128)S(1)}) custom-call(s32[8]{0:T(128)S(1)} %copy-done.29, bf16[4,128,768]{2,1,0:T(8,128)(2,1)S(1)} %pad_maximum_fusion.5.near_ref, ...), custom_call_target="tpu_custom_call" | custom-call | bytes 16000000 | tf_op jit(solution)/shard_map/pallas_call | solution.py:1245
  (365 shorter events, 126.9 us)
Async XLA Ops:
  11.1 12.6 %collective-permute-start.1 = (bf16[96,768]{1,0:T(8,128)(2,1)S(1)}, bf16[96,768]{1,0:T(8,128)(2,1)}, u32[]{:S(2)}, u32[]{:S(2)}) collective-permute-start(bf16[96,768]{1,0:T(8,128)(2,1)S(1)} %get-tuple-element.237.refs_0_), channel_id=1, source_target_pairs={{0,16},{1,17},{2,18},{3,19},{4,20},{5,21},{6,22},{7,23},{8,24},{9,... | collective-permute-start | bytes 442376 | tf_op jit(solution)/shard_map/ppermute | solution.py:167
  25.7 16.8 %collective-permute-start.3 = (bf16[1,4,96,768]{3,2,1,0:T(8,128)(2,1)}, bf16[1,4,96,768]{3,2,1,0:T(8,128)(2,1)S(1)}, u32[]{:S(2)}, u32[]{:S(2)}) collective-permute-start(bf16[1,4,96,768]{3,2,1,0:T(8,128)(2,1)} %shard_map.474), channel_id=1, source_target_pairs={{0,4},{1,3},{2,6},{3,1},{4,0},{5,7},{6,2},{7,5},{8,12},{9,11},{10,... | collective-permute-start | bytes 1769480 | tf_op jit(solution)/shard_map/ppermute | solution.py:167
  28.6 13.8 %collective-permute-start.5 = (bf16[96,768]{1,0:T(8,128)(2,1)S(1)}, bf16[96,768]{1,0:T(8,128)(2,1)S(1)}, u32[]{:S(2)}, u32[]{:S(2)}) collective-permute-start(bf16[96,768]{1,0:T(8,128)(2,1)S(1)} %get-tuple-element.243.refs_0_), channel_id=1, source_target_pairs={{0,16},{1,17},{2,18},{3,19},{4,20},{5,21},{6,22},{7,23},{8,24},{9,... | collective-permute-start | bytes 442376 | tf_op jit(solution)/shard_map/ppermute | solution.py:167
  43.3 16.4 %collective-permute-start.7 = (bf16[2,4,96,768]{3,2,1,0:T(8,128)(2,1)S(1)}, bf16[2,4,96,768]{3,2,1,0:T(8,128)(2,1)}, u32[]{:S(2)}, u32[]{:S(2)}) collective-permute-start(bf16[2,4,96,768]{3,2,1,0:T(8,128)(2,1)S(1)} %pad_maximum_fusion.refs_0_), channel_id=1, source_target_pairs={{0,2},{1,5},{2,0},{3,7},{4,6},{5,1},{6,4},{7,3},{8,10},{9,13},{10,... | collective-permute-start | bytes 3538952 | tf_op jit(solution)/shard_map/ppermute | solution.py:167
  43.8 15.8 %collective-permute-start.8 = (bf16[2,4,96,768]{3,2,1,0:T(8,128)(2,1)S(1)}, bf16[2,4,96,768]{3,2,1,0:T(8,128)(2,1)}, u32[]{:S(2)}, u32[]{:S(2)}) collective-permute-start(bf16[2,4,96,768]{3,2,1,0:T(8,128)(2,1)S(1)} %pad_maximum_fusion.refs_0_), channel_id=1, source_target_pairs={{0,1},{1,0},{2,3},{3,2},{4,5},{5,4},{6,7},{7,6},{8,9},{9,8},{10,11... | collective-permute-start | bytes 3538952 | tf_op jit(solution)/shard_map/ppermute | solution.py:167
  45.2 12.9 %collective-permute-start.9 = (bf16[96,768]{1,0:T(8,128)(2,1)}, bf16[96,768]{1,0:T(8,128)(2,1)}, u32[]{:S(2)}, u32[]{:S(2)}) collective-permute-start(bf16[96,768]{1,0:T(8,128)(2,1)} %get-tuple-element.252.refs_0_), channel_id=1, source_target_pairs={{0,24},{1,25},{2,26},{3,27},{4,28},{5,29},{6,30},{7,31},{8,0},{9,1... | collective-permute-start | bytes 442376 | tf_op jit(solution)/shard_map/ppermute | solution.py:167
  71.2 22.6 %collective-permute-start.14 = (bf16[2,4,96,768]{3,2,1,0:T(8,128)(2,1)S(1)}, bf16[2,4,96,768]{3,2,1,0:T(8,128)(2,1)S(1)}, u32[]{:S(2)}, u32[]{:S(2)}) collective-permute-start(bf16[2,4,96,768]{3,2,1,0:T(8,128)(2,1)S(1)} %pad_maximum_fusion.1.refs_0_), channel_id=1, source_target_pairs={{0,2},{1,5},{2,0},{3,7},{4,6},{5,1},{6,4},{7,3},{8,10},{9,13},{10,... | collective-permute-start | bytes 3538952 | tf_op jit(solution)/shard_map/ppermute | solution.py:167
  71.8 22.0 %collective-permute-start.15 = (bf16[2,4,96,768]{3,2,1,0:T(8,128)(2,1)S(1)}, bf16[2,4,96,768]{3,2,1,0:T(8,128)(2,1)S(1)}, u32[]{:S(2)}, u32[]{:S(2)}) collective-permute-start(bf16[2,4,96,768]{3,2,1,0:T(8,128)(2,1)S(1)} %pad_maximum_fusion.1.refs_0_), channel_id=1, source_target_pairs={{0,1},{1,0},{2,3},{3,2},{4,5},{5,4},{6,7},{7,6},{8,9},{9,8},{10,11... | collective-permute-start | bytes 3538952 | tf_op jit(solution)/shard_map/ppermute | solution.py:167
  72.1 21.5 %collective-permute-start.16 = (bf16[1,4,96,768]{3,2,1,0:T(8,128)(2,1)S(1)}, bf16[1,4,96,768]{3,2,1,0:T(8,128)(2,1)S(1)}, u32[]{:S(2)}, u32[]{:S(2)}) collective-permute-start(bf16[1,4,96,768]{3,2,1,0:T(8,128)(2,1)S(1)} %copy-done.49), channel_id=1, source_target_pairs={{0,4},{1,3},{2,6},{3,1},{4,0},{5,7},{6,2},{7,5},{8,12},{9,11},{10,... | collective-permute-start | bytes 1769480 | tf_op jit(solution)/shard_map/ppermute | solution.py:167
  95.1 16.3 %collective-permute-start.17 = (bf16[2,4,96,768]{3,2,1,0:T(8,128)(2,1)S(1)}, bf16[2,4,96,768]{3,2,1,0:T(8,128)(2,1)S(1)}, u32[]{:S(2)}, u32[]{:S(2)}) collective-permute-start(bf16[2,4,96,768]{3,2,1,0:T(8,128)(2,1)S(1)} %pad_maximum_fusion.2.refs_0_), channel_id=1, source_target_pairs={{0,2},{1,5},{2,0},{3,7},{4,6},{5,1},{6,4},{7,3},{8,10},{9,13},{10,... | collective-permute-start | bytes 3538952 | tf_op jit(solution)/shard_map/ppermute | solution.py:167
  95.7 15.7 %collective-permute-start.18 = (bf16[2,4,96,768]{3,2,1,0:T(8,128)(2,1)S(1)}, bf16[2,4,96,768]{3,2,1,0:T(8,128)(2,1)S(1)}, u32[]{:S(2)}, u32[]{:S(2)}) collective-permute-start(bf16[2,4,96,768]{3,2,1,0:T(8,128)(2,1)S(1)} %pad_maximum_fusion.2.refs_0_), channel_id=1, source_target_pairs={{0,1},{1,0},{2,3},{3,2},{4,5},{5,4},{6,7},{7,6},{8,9},{9,8},{10,11... | collective-permute-start | bytes 3538952 | tf_op jit(solution)/shard_map/ppermute | solution.py:167
  121.0 23.1 %collective-permute-start.21 = (bf16[32,896]{1,0:T(8,128)(2,1)S(1)}, bf16[32,896]{1,0:T(8,128)(2,1)S(1)}, u32[]{:S(2)}, u32[]{:S(2)}) collective-permute-start(bf16[32,896]{1,0:T(8,128)(2,1)S(1)} %get-tuple-element.288.refs_0_), channel_id=1, source_target_pairs={{0,24},{1,25},{2,26},{3,27},{4,28},{5,29},{6,30},{7,31},{8,0},{9,1... | collective-permute-start | bytes 172040 | tf_op jit(solution)/shard_map/ppermute | solution.py:167
  121.3 22.9 %collective-permute-start.22 = (bf16[32,896]{1,0:T(8,128)(2,1)S(1)}, bf16[32,896]{1,0:T(8,128)(2,1)S(1)}, u32[]{:S(2)}, u32[]{:S(2)}) collective-permute-start(bf16[32,896]{1,0:T(8,128)(2,1)S(1)} %get-tuple-element.288.refs_0_), channel_id=1, source_target_pairs={{0,16},{1,17},{2,18},{3,19},{4,20},{5,21},{6,22},{7,23},{8,24},{9,... | collective-permute-start | bytes 172040 | tf_op jit(solution)/shard_map/ppermute | solution.py:167
  123.0 21.2 %collective-permute-start.23 = (bf16[32,896]{1,0:T(8,128)(2,1)S(1)}, bf16[32,896]{1,0:T(8,128)(2,1)S(1)}, u32[]{:S(2)}, u32[]{:S(2)}) collective-permute-start(bf16[32,896]{1,0:T(8,128)(2,1)S(1)} %get-tuple-element.288.refs_0_), channel_id=1, source_target_pairs={{0,8},{1,9},{2,10},{3,11},{4,12},{5,13},{6,14},{7,15},{8,16},{9,17... | collective-permute-start | bytes 172040 | tf_op jit(solution)/shard_map/ppermute | solution.py:167
  158.9 23.5 %collective-permute-start.28 = (bf16[2,4,96,768]{3,2,1,0:T(8,128)(2,1)S(1)}, bf16[2,4,96,768]{3,2,1,0:T(8,128)(2,1)}, u32[]{:S(2)}, u32[]{:S(2)}) collective-permute-start(bf16[2,4,96,768]{3,2,1,0:T(8,128)(2,1)S(1)} %pad_maximum_fusion.3), channel_id=1, source_target_pairs={{0,2},{1,5},{2,0},{3,7},{4,6},{5,1},{6,4},{7,3},{8,10},{9,13},{10,... | collective-permute-start | bytes 3538952 | tf_op jit(solution)/shard_map/ppermute | solution.py:167
  160.8 20.0 %collective-permute-start.26 = (bf16[2,4,32,896]{3,2,1,0:T(8,128)(2,1)S(1)}, bf16[2,4,32,896]{3,2,1,0:T(8,128)(2,1)S(1)}, u32[]{:S(2)}, u32[]{:S(2)}) collective-permute-start(bf16[2,4,32,896]{3,2,1,0:T(8,128)(2,1)S(1)} %pad_maximum_fusion.7.refs_0_), channel_id=1, source_target_pairs={{0,2},{1,5},{2,0},{3,7},{4,6},{5,1},{6,4},{7,3},{8,10},{9,13},{10,... | collective-permute-start | bytes 1376264 | tf_op jit(solution)/shard_map/ppermute | solution.py:167
  162.1 18.8 %collective-permute-start.27 = (bf16[2,4,32,896]{3,2,1,0:T(8,128)(2,1)S(1)}, bf16[2,4,32,896]{3,2,1,0:T(8,128)(2,1)S(1)}, u32[]{:S(2)}, u32[]{:S(2)}) collective-permute-start(bf16[2,4,32,896]{3,2,1,0:T(8,128)(2,1)S(1)} %pad_maximum_fusion.7.refs_0_), channel_id=1, source_target_pairs={{0,1},{1,0},{2,3},{3,2},{4,5},{5,4},{6,7},{7,6},{8,9},{9,8},{10,11... | collective-permute-start | bytes 1376264 | tf_op jit(solution)/shard_map/ppermute | solution.py:167
  182.4 22.5 %collective-permute-start.31 = (bf16[2,768,768]{2,1,0:T(8,128)(2,1)}, bf16[2,768,768]{2,1,0:T(8,128)(2,1)}, u32[]{:S(2)}, u32[]{:S(2)}) collective-permute-start(bf16[2,768,768]{2,1,0:T(8,128)(2,1)} %get-tuple-element.318), channel_id=1, source_target_pairs={{0,1},{1,0},{2,3},{3,2},{4,5},{5,4},{6,7},{7,6},{8,9},{9,8},{10,11... | collective-permute-start | bytes 7077896 | tf_op jit(solution)/shard_map/ppermute | solution.py:167
  184.6 20.3 %collective-permute-start.30 = (bf16[4,96,768]{2,1,0:T(8,128)(2,1)S(1)}, bf16[4,96,768]{2,1,0:T(8,128)(2,1)S(1)}, u32[]{:S(2)}, u32[]{:S(2)}) collective-permute-start(bf16[4,96,768]{2,1,0:T(8,128)(2,1)S(1)} %fusion), channel_id=1, source_target_pairs={{0,4},{1,3},{2,6},{3,1},{4,0},{5,7},{6,2},{7,5},{8,12},{9,11},{10,... | collective-permute-start | bytes 1769480 | tf_op jit(solution)/shard_map/ppermute | solution.py:167
  185.6 19.4 %collective-permute-start.29 = (bf16[2,4,32,896]{3,2,1,0:T(8,128)(2,1)S(1)}, bf16[2,4,32,896]{3,2,1,0:T(8,128)(2,1)S(1)}, u32[]{:S(2)}, u32[]{:S(2)}) collective-permute-start(bf16[2,4,32,896]{3,2,1,0:T(8,128)(2,1)S(1)} %copy-done.20), channel_id=1, source_target_pairs={{0,1},{1,0},{2,3},{3,2},{4,5},{5,4},{6,7},{7,6},{8,9},{9,8},{10,11... | collective-permute-start | bytes 1376264 | tf_op jit(solution)/shard_map/ppermute | solution.py:167
  207.0 17.3 %collective-permute-start.32 = (bf16[2,4,96,768]{3,2,1,0:T(8,128)(2,1)S(1)}, bf16[2,4,96,768]{3,2,1,0:T(8,128)(2,1)S(1)}, u32[]{:S(2)}, u32[]{:S(2)}) collective-permute-start(bf16[2,4,96,768]{3,2,1,0:T(8,128)(2,1)S(1)} %pad_maximum_fusion.4), channel_id=1, source_target_pairs={{0,2},{1,5},{2,0},{3,7},{4,6},{5,1},{6,4},{7,3},{8,10},{9,13},{10,... | collective-permute-start | bytes 3538952 | tf_op jit(solution)/shard_map/ppermute | solution.py:167
  211.2 13.1 %collective-permute-start.34 = (bf16[96,768]{1,0:T(8,128)(2,1)S(1)}, bf16[96,768]{1,0:T(8,128)(2,1)S(1)}, u32[]{:S(2)}, u32[]{:S(2)}) collective-permute-start(bf16[96,768]{1,0:T(8,128)(2,1)S(1)} %get-tuple-element.457), channel_id=1, source_target_pairs={{0,16},{1,17},{2,18},{3,19},{4,20},{5,21},{6,22},{7,23},{8,24},{9,... | collective-permute-start | bytes 442376 | tf_op jit(solution)/shard_map/ppermute | solution.py:167
  236.0 17.9 %collective-permute-start.41 = (bf16[2,128,768]{2,1,0:T(8,128)(2,1)S(1)}, bf16[2,128,768]{2,1,0:T(8,128)(2,1)S(1)}, u32[]{:S(2)}, u32[]{:S(2)}) collective-permute-start(bf16[2,128,768]{2,1,0:T(8,128)(2,1)S(1)} %slice.207), channel_id=1, source_target_pairs={{0,2},{1,5},{2,0},{3,7},{4,6},{5,1},{6,4},{7,3},{8,10},{9,13},{10,... | collective-permute-start | bytes 1179656 | tf_op jit(solution)/shard_map/ppermute | solution.py:167
  238.4 15.5 %collective-permute-start.38 = (bf16[96,768]{1,0:T(8,128)(2,1)S(1)}, bf16[96,768]{1,0:T(8,128)(2,1)S(1)}, u32[]{:S(2)}, u32[]{:S(2)}) collective-permute-start(bf16[96,768]{1,0:T(8,128)(2,1)S(1)} %get-tuple-element.455), channel_id=1, source_target_pairs={{0,8},{1,9},{2,10},{3,11},{4,12},{5,13},{6,14},{7,15},{8,16},{9,17... | collective-permute-start | bytes 442376 | tf_op jit(solution)/shard_map/ppermute | solution.py:167
  (112 other events, 900.4 us)

commit v3 on v2

--- a/solution.py
+++ b/solution.py
@@ -208,23 +208,31 @@
 
     def reduce(self, far):
         theirs, near = yield far, self.send(far, self.other)
-        shape = (4, self.deep, near.shape[1] // self.blocks, near.shape[2])
-        near, theirs = near.reshape(shape), theirs.reshape(shape)
-
-        def chip(index):
-            return (
-                lax.dynamic_index_in_dim(near, index, 0, keepdims=False).astype(f32)
-                + lax.dynamic_index_in_dim(theirs, index, 0, keepdims=False).astype(f32)
-            )
-
-        sent = jnp.stack([chip(0), chip(1 + self.core)]).astype(bf16)
+        size, width = near.shape[1] // self.blocks, near.shape[2]
+        near = near.reshape(2, self.deep, 2, size, width)
+        theirs = theirs.reshape(near.shape)
+
+        def chip(y, x):
+            spot, part = (y, 0, x, 0, 0), (1, self.deep, 1, size, width)
+            total = lax.dynamic_slice(near, spot, part).astype(f32)
+            total = total + lax.dynamic_slice(theirs, spot, part).astype(f32)
+            return total.reshape(self.deep, size, width)
+
+        sent = jnp.stack(
+            [chip(0, 1 - self.x), chip(self.core, jnp.where(self.core == 0, self.x, 1 - self.x))]
+        ).astype(bf16)
         got = yield sent, self.send(sent, self.first)
-        away = (chip(2 - self.core) + got[0].astype(f32)).astype(bf16)
+        kept = chip(1 - self.core, jnp.where(self.core == 0, 1 - self.x, self.x))
+        away = (kept + got[0].astype(f32)).astype(bf16)
         came = yield away, self.send(away, self.second)
-        column = chip(3) + got[1].astype(f32) + came.astype(f32)
+        column = chip(1, self.x) + got[1].astype(f32) + came.astype(f32)
         low = column.astype(bf16)
-        total = column[0]
-        for part in (yield low, [self.send(low[s], self.up[s]) for s in (1, 2, 3)]):
+
+        def level(values, step):
+            return lax.dynamic_index_in_dim(values, (self.z + step) % 4, 0, keepdims=False)
+
+        total = level(column, 0)
+        for part in (yield low, [self.send(level(low, s), self.up[s]) for s in (1, 2, 3)]):
             total = total + part.astype(f32)
         return total
 
@@ -272,6 +280,29 @@
     return vectors_ref[index : index + 1, :]
 
 
+def to_column(present_ref, column_ref):
+    padded = present_ref.shape[1]
+    for image in range(present_ref.shape[0]):
+        span = slice(image * padded, (image + 1) * padded)
+        column_ref[span, :] = upright(present_ref[image : image + 1, :])
+
+
+def to_lines(flat_ref, lines_ref):
+    width = lines_ref.shape[1]
+    lines_ref[...] = jnp.zeros(lines_ref.shape, f32)
+    for row, start in enumerate(range(0, flat_ref.shape[0], width)):
+        extent = min(width, flat_ref.shape[0] - start)
+        values = flat_ref[pl.ds(start, extent)]
+        lines_ref[row : row + 1, :extent] = values.reshape(1, extent)
+
+
+def from_lines(lines, flat_ref):
+    width = lines.shape[1]
+    for row, start in enumerate(range(0, flat_ref.shape[0], width)):
+        extent = min(width, flat_ref.shape[0] - start)
+        flat_ref[pl.ds(start, extent)] = lines[row, :extent]
+
+
 def share_of(vectors_ref, index, group, share):
     result = vectors_ref[index : index + 1, :share]
     for other in range(1, vectors_ref.shape[1] // share):
@@ -345,31 +376,21 @@
     return result
 
 
-def turn(place_ref, values, result_ref, blocks):
-    turned = values.T
-    if blocks is None:
-        result_ref[...] = turned
-        return
-    size, deep = turned.shape[0] // blocks, blocks // 2
-    for block in range(blocks):
-        level = lax.rem(block // 2 - place_ref[0] + deep, deep)
-        spot = (1 - (block % 2 ^ place_ref[1])) * deep + level
-        rows = pl.ds(pl.multiple_of(spot * size, size), size)
-        result_ref[rows, :] = turned[block * size : (block + 1) * size, :]
-
-
 def pieces_kernel(
     place_ref,
     in_ref,
     out_ref,
     expand_ref,
     contract_ref,
+    vectors_ref,
     own_ref,
     attend_low_ref,
     expand_low_ref,
     contract_low_ref,
     square_ref,
+    lines_ref,
 ):
+    to_lines(vectors_ref, lines_ref)
     share = out_ref.shape[0]
     lane = lax.broadcasted_iota(jnp.int32, (1, 128), 1)
     for part in range(3):
@@ -386,6 +407,11 @@
     square_ref[...] = totals
 
 
+def in_slots(table_ref, padded):
+    empty = jnp.zeros((padded - table_ref.shape[0], table_ref.shape[1]), f32)
+    return jnp.concatenate([table_ref[1:], table_ref[0:1], empty])
+
+
 def stem_kernel(
     place_ref,
     labels_ref,
@@ -397,14 +423,14 @@
     stream_ref,
     rows_ref,
     present_ref,
-    column_ref,
     facts_ref,
 ):
     count, patch_count = mask_ref.shape
     padded = present_ref.shape[1]
     low = stem_ref[...].astype(bf16)
     slot = lax.broadcasted_iota(jnp.int32, (padded, 1), 0)
-    table = table_ref[...] + jnp.where(slot < patch_count, line(vectors_ref, STEM_BIAS), 0.0)
+    table = in_slots(table_ref, padded)
+    table = table + jnp.where(slot < patch_count, line(vectors_ref, STEM_BIAS), 0.0)
     for image in range(count):
         span = slice(image * padded, (image + 1) * padded)
         stream = dot(pixels_ref[span, :], low) + table
@@ -418,7 +444,6 @@
     lane = lax.broadcasted_iota(jnp.int32, (1, 128), 1)
     for image in range(count):
         present = present_ref[image : image + 1, :]
-        column_ref[image * padded : (image + 1) * padded, :] = upright(present)
         kept = jnp.sum(present, 1, keepdims=True)
         label = labels_ref[image].astype(f32)
         fact = jnp.where(lane == 0, kept, jnp.where(lane == 1, label, 0.0))
@@ -433,25 +458,17 @@
     vectors_ref,
     present_ref,
     stream_ref,
-    column_ref,
     qkv_ref,
     attended_ref,
     stream_out_ref,
     rows_out_ref,
-    turned_one_ref,
-    turned_two_ref,
     sum_ref,
     *,
-    blocks,
     order,
 ):
     step = pl.program_id(0)
     count, padded = present_ref.shape
     share = attended_ref.shape[2]
-
-    @pl.when(step == 0)
-    def _():
-        turn(place_ref, rows_ref[...], turned_one_ref, blocks)
 
     group = own_group(place_ref, order)
     projected = dot(rows_ref[...], weight(0, 3 * share))
@@ -484,12 +501,11 @@
     def _():
         hat, _ = normal_parts(stream_out_ref[...])
         rows_two = hat * line(vectors_ref, GAIN_TWO) + line(vectors_ref, SHIFT_TWO)
-        rows_two = rows_two.astype(bf16)
-        rows_out_ref[...] = rows_two
-        turn(place_ref, rows_two, turned_two_ref, blocks)
+        rows_out_ref[...] = rows_two.astype(bf16)
         for image in range(count):
             span = slice(image * padded, (image + 1) * padded)
-            total = jnp.sum(stream_out_ref[span, :] * column_ref[span, :], 0, keepdims=True)
+            here = upright(present_ref[image : image + 1, :])
+            total = jnp.sum(stream_out_ref[span, :] * here, 0, keepdims=True)
             sum_ref[image : image + 1, :] = total
             sum_ref[image + count : image + count + 1, :] = total
 
@@ -500,9 +516,9 @@
     rows_ref,
     vectors_ref,
     present_ref,
-    column_ref,
     sum_ref,
     slope_ref,
+    column_ref,
     *,
     order,
 ):
@@ -513,6 +529,11 @@
     half = 0.5 + 0.5 * jnp.tanh(hidden * (first + first * second * square))
     active = (hidden * half).astype(bf16)
     count, padded = present_ref.shape
+
+    @pl.when(pl.program_id(0) == 0)
+    def _():
+        to_column(present_ref, column_ref)
+
     row = lax.broadcasted_iota(jnp.int32, (2 * count, 1), 0)
     sums = jnp.zeros(sum_ref.shape[1:], f32)
     for image in range(count):
@@ -528,7 +549,7 @@
 def expand_back_kernel(
     place_ref,
     weight,
-    turned_ref,
+    rows_ref,
     slope_ref,
     d_active_ref,
     far_ref,
@@ -547,16 +568,15 @@
         bias = bias + jnp.sum(d_hidden, 0, keepdims=True)
         d_hidden_low[span, :] = d_hidden.astype(bf16)
     bias_ref[0] = bias
-    grad = dot(turned_ref[...], d_hidden_low[...]).astype(bf16)
     half = pl.num_programs(0) // 2
 
     @pl.when(step < half)
     def _():
-        far_ref[0] = grad
+        far_ref[0] = dot(rows_ref[...], d_hidden_low[...], 0, 0).astype(bf16)
 
     @pl.when(step >= half)
     def _():
-        near_ref[0] = grad
+        near_ref[0] = dot(rows_ref[...], d_hidden_low[...], 0, 0).astype(bf16)
 
     part = dot(d_hidden_low[...], weight(), 1, 1)
 
@@ -573,15 +593,12 @@
     place_ref,
     d_rows_ref,
     d_row_ref,
-    column_ref,
+    present_ref,
     stream_ref,
     vectors_ref,
     d_stream_ref,
     d_low_ref,
-    turned_ref,
     vector_ref,
-    *,
-    blocks,
 ):
     count = d_row_ref.shape[0] // 2
     padded = stream_ref.shape[0] // count
@@ -592,32 +609,36 @@
     bias = jnp.zeros((1, below.shape[1]), f32)
     for image in range(count):
         span = slice(image * padded, (image + 1) * padded)
-        d_stream = below[span] + d_row_ref[image : image + 1, :] * column_ref[span, :]
+        here = upright(present_ref[image : image + 1, :])
+        d_stream = below[span] + d_row_ref[image : image + 1, :] * here
         bias = bias + jnp.sum(d_stream, 0, keepdims=True)
         d_stream_ref[span, :] = d_stream
         d_low_ref[span, :] = d_stream.astype(bf16)
     vector_ref[0:1, :] = bias
-    turn(place_ref, d_low_ref[...], turned_ref, blocks)
 
 
 def attend_back_kernel(
     place_ref,
     weight,
-    turned_ref,
+    rows_ref,
     qkv_ref,
     attended_ref,
-    column_ref,
+    present_ref,
     d_low_ref,
-    d_turned_ref,
     *refs,
 ):
-    grad_ref, bias_ref, d_rows_ref, d_projected = refs[-4:]
+    grad_ref, bias_ref, d_rows_ref, d_projected, column_ref = refs[-5:]
     step = pl.program_id(0)
     share = attended_ref.shape[2]
     count = bias_ref.shape[1] // 2
     padded = attended_ref.shape[1] // count
     scale = HEAD_DIM ** (-0.5)
     d_attended = dot(d_low_ref[...], weight(3 * share, 4 * share)).astype(bf16)
+
+    @pl.when(step == 0)
+    def _():
+        to_column(present_ref, column_ref)
+
     masks = head_masks(share)
     for image in range(count):
         span = slice(image * padded, (image + 1) * padded)
@@ -640,13 +661,13 @@
         d_projected[span, :share] = d_query.astype(bf16)
         d_projected[span, share : 2 * share] = d_key.astype(bf16)
         d_projected[span, 2 * share :] = d_value.astype(bf16)
-    grad_ref[0, :, : 3 * share] = dot(turned_ref[...], d_projected[...]).astype(bf16)
-    grad_ref[0, :, 3 * share :] = dot(d_turned_ref[...], attended_ref[0]).astype(bf16)
+    grad_ref[0, :, : 3 * share] = dot(rows_ref[...], d_projected[...], 0, 0).astype(bf16)
+    grad_ref[0, :, 3 * share :] = dot(d_low_ref[...], attended_ref[0], 0, 0).astype(bf16)
     part = dot(d_projected[...], weight(0, 3 * share), 1, 1)
 
     @pl.when(step == 0)
     def _():
-        d_rows_ref[...] = part + refs[0][...] if len(refs) > 4 else part
+        d_rows_ref[...] = part + refs[0][...] if len(refs) > 5 else part
 
     @pl.when(step > 0)
     def _():
@@ -675,7 +696,7 @@
     for image in range(1, rows // slots):
         table = table + below[image * slots : (image + 1) * slots]
     vector_ref[8:, :] = table
-    stem = dot(pixels_ref[...].T, below.astype(bf16)).astype(bf16)
+    stem = dot(pixels_ref[...], below.astype(bf16), 0, 0).astype(bf16)
     half, size, columns = near_ref.shape
     empty = jnp.zeros((2 * half * size - width - slots, columns), bf16)
     whole = jnp.concatenate([stem, table.astype(bf16), empty])
@@ -840,9 +861,15 @@
 
     @pl.when(pl.program_id(0) == pl.num_programs(0) - 1)
     def _():
-        new_ref[...], new_cols_ref[...], new_rows_ref[...] = factored(
-            weight_ref[...], grad_ref[...], old_cols_ref[...], old_rows_ref[...], True
+        new_ref[...], cols, rows_ = factored(
+            weight_ref[...],
+            grad_ref[...],
+            old_cols_ref[...].reshape(1, -1),
+            old_rows_ref[...].reshape(1, -1),
+            True,
         )
+        new_cols_ref[...] = cols[0]
+        new_rows_ref[...] = rows_[0]
 
 
 def factored(weight, grad, down_old, across_old, turned, valid=None, count=None):
@@ -889,9 +916,9 @@
     table_cols_new_ref,
     both_ref,
     *,
-    slots,
+    padded,
 ):
-    n, padded = stem_ref.shape[0], table_ref.shape[0]
+    n, slots = stem_ref.shape[0], table_ref.shape[0]
     half, size = near_ref.shape[:2]
     for chunk in range(2 * half):
         near, far = place_ref[6] ^ chunk, place_ref[7] ^ chunk
@@ -905,19 +932,32 @@
         def _(span=span, far=far):
             both_ref[span, :] = far_ref[far]
 
-    stem_new_ref[...], stem_rows_new_ref[...], stem_cols_new_ref[...] = factored(
-        stem_ref[...], both_ref[:n, :].astype(f32), stem_rows_ref[...], stem_cols_ref[...], False
-    )
-    valid = lax.broadcasted_iota(jnp.int32, (padded, 1), 0) < slots
-    table_new_ref[...], table_rows_new_ref[...], table_cols_new_ref[...] = factored(
-        table_ref[...],
+    stem_new_ref[...], rows, cols = factored(
+        stem_ref[...],
+        both_ref[:n, :].astype(f32),
+        stem_rows_ref[...].reshape(1, -1),
+        stem_cols_ref[...].reshape(1, -1),
+        False,
+    )
+    stem_rows_new_ref[...] = rows[0]
+    stem_cols_new_ref[...] = cols[0]
+    old = table_rows_ref[...].reshape(1, slots)
+    empty = jnp.zeros((1, padded - slots), f32)
+    table, rows, cols = factored(
+        in_slots(table_ref, padded),
         both_ref[n : n + padded, :].astype(f32),
-        table_rows_ref[...],
-        table_cols_ref[...],
+        jnp.concatenate([old[:, 1:], old[:, 0:1], empty], 1),
+        table_cols_ref[...].reshape(1, -1),
         False,
-        valid,
+        lax.broadcasted_iota(jnp.int32, (padded, 1), 0) < slots,
         slots,
     )
+    table_new_ref[1:] = table[: slots - 1]
+    table_new_ref[0:1] = table[slots - 1 : slots]
+    table_rows_new_ref[...] = jnp.concatenate(
+        [rows[:, slots - 1 : slots], rows[:, : slots - 1]], 1
+    )[0]
+    table_cols_new_ref[...] = cols[0]
 
 
 def layout(data, groups):
@@ -982,14 +1022,12 @@
     sums_ref[at_group : at_group + groups, :] = lines
     count = heads_far_ref.shape[1] // 2
     for part in range(2):
+        span = slice(part * count, (part + 1) * count)
         lines = jnp.zeros((groups, share), f32)
         for ref, order in ((heads_far_ref, (3, 1)), (heads_near_ref, (2, 0))):
             for step, distance in enumerate(order):
-                lines = lines + put(
-                    groups,
-                    own ^ distance,
-                    jnp.sum(ref[step][part * count : (part + 1) * count], 0, keepdims=True),
-                )
+                total = jnp.sum(ref[step][span], 0, keepdims=True)
+                lines = lines + put(groups, own ^ distance, total)
         sums_ref[part * groups : (part + 1) * groups, 3 * share :] = lines
     stem_bias = jnp.sum(vector_one_ref[8 : 8 + patch_count, :], 0, keepdims=True)
     singles = (stem_bias, vector_one_ref[0:2, :], vector_two_ref[0:3, :])
@@ -1005,15 +1043,18 @@
     head_ref,
     vectors_ref,
     second_ref,
+    grad_out,
+    new_out,
+    second_out,
     grad_ref,
-    new_ref,
-    second_new_ref,
+    lines_ref,
     *,
     data,
     groups,
     share,
-    length,
 ):
+    to_lines(second_ref, lines_ref)
+    length = second_ref.shape[0]
     _, at_group, at_single, _ = layout(data, groups)
     width = vectors_ref.shape[1]
 
@@ -1046,29 +1087,44 @@
     row = lax.broadcasted_iota(jnp.int32, grad.shape, 0)
     lane = lax.broadcasted_iota(jnp.int32, grad.shape, 1)
     valid = row * width + lane < length
-    second = decay_rate * second_ref[...] + (1.0 - decay_rate) * (grad * grad + eps_one)
+    second = decay_rate * lines_ref[...] + (1.0 - decay_rate) * (grad * grad + eps_one)
     update = grad * lax.rsqrt(jnp.where(valid, second, 1.0))
     total = jnp.sum(update * update, keepdims=True) / length
     square = jnp.sum(vectors_ref[...] * vectors_ref[...], keepdims=True) / length
     scale = step_rate * jnp.maximum(eps_two, jnp.sqrt(square))
     scale = scale / jnp.maximum(1.0, jnp.sqrt(total) / clip_level)
-    new_ref[...] = vectors_ref[...] - scale * update
-    second_new_ref[...] = second
+    from_lines(grad, grad_out)
+    from_lines(vectors_ref[...] - scale * update, new_out)
+    from_lines(second, second_out)
 
 
 def renew_kernel(
     place_ref,
     sums_ref,
-    rows_ref,
-    cols_ref,
+    in_rows_ref,
+    out_cols_ref,
+    expand_rows_ref,
+    contract_cols_ref,
+    in_cols_ref,
+    out_rows_ref,
+    expand_cols_ref,
+    contract_rows_ref,
     attend_ref,
     expand_ref,
     contract_ref,
-    rows_new_ref,
-    cols_new_ref,
+    in_rows_out,
+    out_cols_out,
+    expand_rows_out,
+    contract_cols_out,
+    in_cols_out,
+    out_rows_out,
+    expand_cols_out,
+    contract_rows_out,
     update_ref,
     scalar_ref,
     square_ref,
+    rows_new_ref,
+    cols_new_ref,
     *,
     data,
     groups,
@@ -1082,18 +1138,47 @@
     lane = lax.broadcasted_iota(jnp.int32, (1, width), 1)
     first = lane < 3 * share
     spare = lax.broadcasted_iota(jnp.int32, (1, 128), 1) < size
+    for index, ref in enumerate((in_rows_ref, out_cols_ref, expand_rows_ref, contract_cols_ref)):
+        for part in range(data):
+            values = ref[pl.ds(part * size, size)].reshape(1, size)
+            rows_new_ref[part : part + 1, index * 128 : index * 128 + size] = values
+    for part in range(groups):
+        span = slice(part * share, (part + 1) * share)
+        for which in range(3):
+            cols_new_ref[part : part + 1, which * share : (which + 1) * share] = in_cols_ref[
+                which : which + 1, span
+            ]
+        values = out_rows_ref[pl.ds(part * share, share)].reshape(1, share)
+        cols_new_ref[part : part + 1, 3 * share :] = values
+        for index, ref in enumerate((expand_cols_ref, contract_rows_ref), 1):
+            values = ref[pl.ds(part * width, width)].reshape(1, width)
+            cols_new_ref[index * groups + part : index * groups + part + 1, :] = values
     counts = (3 * length, length, hidden, hidden)
     means = []
     for index, count in enumerate(counts):
         span = slice(index * 128, (index + 1) * 128)
-        new = decay_rate * rows_ref[:, span] + (1.0 - decay_rate) * (sums_ref[:data, span] / count)
+        new = decay_rate * rows_new_ref[:, span]
+        new = new + (1.0 - decay_rate) * (sums_ref[:data, span] / count)
         rows_new_ref[:, span] = new
         means.append(jnp.sum(jnp.where(spare, new, 0.0), keepdims=True) / length)
+        out = (in_rows_out, out_cols_out, expand_rows_out, contract_cols_out)[index]
+        for part in range(data):
+            out[pl.ds(part * size, size)] = new[part, :size]
     for index, count in enumerate((length, length, length)):
         span = slice(index * groups, (index + 1) * groups)
         lines = sums_ref[at_group + index * groups : at_group + (index + 1) * groups, :]
-        new = decay_rate * cols_ref[span, :] + (1.0 - decay_rate) * (lines / count)
+        new = decay_rate * cols_new_ref[span, :] + (1.0 - decay_rate) * (lines / count)
         cols_new_ref[span, :] = new
+        for part in range(groups):
+            if index == 0:
+                for which in range(3):
+                    in_cols_out[which : which + 1, part * share : (part + 1) * share] = new[
+                        part : part + 1, which * share : (which + 1) * share
+                    ]
+                out_rows_out[pl.ds(part * share, share)] = new[part, 3 * share :]
+            else:
+                out = (expand_cols_out, contract_rows_out)[index - 1]
+                out[pl.ds(part * width, width)] = new[part]
         if index == 0:
             means[1] = jnp.sum(jnp.where(first, 0.0, new), keepdims=True) / length
         if index == 2:
@@ -1173,7 +1258,7 @@
 
 
 def call(
-    body, order, place, operands, results, scratch=(), flops=0, weights=None
+    body, order, place, operands, results, scratch=(), flops=0, weights=None, limit=48
 ):
     steps = len(order)
     pieces = weights is not None and len(weights) == 4
@@ -1255,7 +1340,7 @@
             ],
         ),
         out_shape=[jax.ShapeDtypeStruct(shape, kind) for shape, kind, _ in results],
-        compiler_params=pltpu.CompilerParams(vmem_limit_bytes=48 * 1024 * 1024),
+        compiler_params=pltpu.CompilerParams(vmem_limit_bytes=limit * 1024 * 1024),
         cost_estimate=pl.CostEstimate(flops=flops, bytes_accessed=16_000_000, transcendentals=0),
     )(place, *[value for value, _ in operands])
 
@@ -1303,7 +1388,7 @@
     padded = -(-slots // 16) * 16
     rows = count * padded
     contract_own = contract.T
-    attend_own, attend_piece, expand_piece, contract_piece, squares = call(
+    attend_own, attend_piece, expand_piece, contract_piece, squares, vector_lines = call(
         pieces_kernel,
         (0,),
         here,
@@ -1312,34 +1397,20 @@
             (attend_out, False),
             (expand, False),
             (contract_own, False),
+            (vectors, False),
         ),
         (((row_share, D), f32, False),)
         + (((row_share, D), bf16, False),) * 3
-        + (((1, 128), f32, False),),
+        + (((1, 128), f32, False), ((24, D), f32, False)),
+        limit=60,
     )
     attend_chain = Chain(links.gather(attend_piece))
     pixels = jnp.pad(patches, ((0, 0), (0, padded - patch_count), (0, 0))).reshape(rows, -1)
-    empty = jnp.zeros((padded - slots, D), f32)
-    table = jnp.concatenate([position_table[1:], position_table[:1], empty])
-    vector_lines = jnp.pad(vectors, (0, 24 * D - vectors.shape[0])).reshape(24, D)
-    (
-        pixels,
-        table,
-        vector_lines,
-        expand_piece,
-        contract_piece,
-        head_weight,
-    ) = sync(
-        [attend_chain],
-        pixels,
-        table,
-        vector_lines,
-        expand_piece,
-        contract_piece,
-        head_weight,
+    pixels, vector_lines, expand_piece, contract_piece, head_weight = sync(
+        [attend_chain], pixels, vector_lines, expand_piece, contract_piece, head_weight
     )
     expand_chain = Chain(links.gather(expand_piece))
-    stream_zero, rows_one, present, column, facts = call(
+    stream_zero, rows_one, present, facts = call(
         stem_kernel,
         (0,),
         here,
@@ -1347,7 +1418,7 @@
             (labels, "smem"),
             (after(pixels, attend_chain.sent), False),
             (stem_weight, False),
-            (table, False),
+            (position_table, False),
             (vector_lines, False),
             (keep_mask, False),
         ),
@@ -1355,7 +1426,6 @@
             ((rows, D), f32, False),
             ((rows, D), bf16, False),
             ((count, padded), f32, False),
-            ((rows, 1), f32, False),
             ((2 * count, 128), f32, False),
         ),
         flops=2 * rows * D * D,
@@ -1371,13 +1441,13 @@
     head_turned = head_weight.T
     head_low = head_turned.astype(bf16)
 
-    head_low, _ = sync([attend_chain, contract_chain], head_low, expand_chain.sent)
-    sync([attend_chain, expand_chain], contract_chain.sent)
+    head_low = sync([attend_chain, expand_chain, contract_chain], head_low)
+    sync([attend_chain], contract_chain.sent, expand_chain.sent)
     attend_all = attend_chain.result
     every = tuple(range(groups))
 
-    qkv, attended, stream_one, rows_two, turned_one, turned_two, stream_sum = call(
-        functools.partial(attend_kernel, blocks=links.blocks, order=every),
+    qkv, attended, stream_one, rows_two, stream_sum = call(
+        functools.partial(attend_kernel, order=every),
         every,
         here,
         (
@@ -1385,15 +1455,12 @@
             (vector_lines, False),
             (present, False),
             (stream_zero, False),
-            (column, False),
         ),
         (
             ((groups, 3, rows, head_share), bf16, "far"),
             ((groups, rows, head_share), bf16, "far"),
             ((rows, D), f32, False),
             ((rows, D), bf16, False),
-            ((D, rows), bf16, False),
-            ((D, rows), bf16, False),
             ((2 * count, D), f32, False),
         ),
         flops=2 * rows * D * 4 * D,
@@ -1410,12 +1477,12 @@
             (rows_two, False),
             (vector_lines, False),
             (present, False),
-            (column, False),
         ),
         (
             ((groups, 2 * count, hidden_share), f32, "far"),
             ((groups, rows, hidden_share), bf16, "far"),
         ),
+        (((rows, 1), f32),),
         flops=2 * rows * D * FF,
         weights=expand_all,
     )
@@ -1449,7 +1516,7 @@
         (3, 1, 2, 0),
         here,
         (
-            (turned_two, False),
+            (rows_two, False),
             (slope, "far"),
             (d_active_row, "far"),
         ),
@@ -1465,27 +1532,26 @@
     )
     far_grad, near_grad, d_rows_two = sync([pieces_chain], far_grad, near_grad, d_rows_two)
     expand_sum = Chain(links.reduce(far_grad))
-    d_stream, d_attend_low, d_turned, vector_two = call(
-        functools.partial(between_kernel, blocks=links.blocks),
+    d_stream, d_attend_low, vector_two = call(
+        between_kernel,
         (0,),
         here,
         (
             (d_rows_two, False),
             (d_row, False),
-            (column, False),
+            (present, False),
             (stream_one, False),
             (vector_lines, False),
         ),
         (
             ((rows, D), f32, False),
             ((rows, D), bf16, False),
-            ((D, rows), bf16, False),
             ((8, D), f32, False),
         ),
     )
 
-    d_stream, d_attend_low, d_turned = sync(
-        [pieces_chain, (expand_sum, near_grad)], d_stream, d_attend_low, d_turned
+    d_stream, d_attend_low = sync(
+        [pieces_chain, (expand_sum, near_grad)], d_stream, d_attend_low
     )
 
     def attend_back(order, *before):
@@ -1494,12 +1560,11 @@
             order,
             here,
             (
-                (turned_one, False),
+                (rows_one, False),
                 (qkv, "far"),
                 (attended, "far"),
-                (column, False),
+                (present, False),
                 (d_attend_low, False),
-                (d_turned, False),
             )
             + tuple((value, False) for value in before),
             (
@@ -1507,7 +1572,7 @@
                 ((pair, 2 * count, head_share), f32, lambda g: g),
                 ((rows, D), f32, False),
             ),
-            (((rows, 3 * head_share), bf16),),
+            (((rows, 3 * head_share), bf16), ((rows, 1), f32)),
             flops=2 * rows * D * 4 * D,
             weights=attend_all,
         )
@@ -1552,13 +1617,13 @@
             (vector_lines, False),
             (head_low, False),
             (head_turned, False),
-            (head_rows[None], False),
-            (head_cols[None], False),
+            (head_rows, False),
+            (head_cols, False),
         ),
         (
             ((CLASSES, D), f32, False),
-            ((1, D), f32, False),
-            ((1, CLASSES), f32, False),
+            ((D,), f32, False),
+            ((CLASSES,), f32, False),
             ((row_share, hidden_share), f32, False),
             ((8, D), f32, False),
             ((8, CLASSES), f32, False),
@@ -1592,8 +1657,10 @@
         (((lines, D), f32, False),),
     )
     sums_chain = Chain(links.add(sums))
-    sync([sums_chain, both_sum])
-    (
+    for _ in range(5):
+        sync([sums_chain, both_sum])
+    sums = sums_chain.result
+    statistics = (
         attend_in_rows,
         attend_out_cols,
         expand_rows,
@@ -1602,118 +1669,64 @@
         attend_out_rows,
         expand_cols,
         contract_rows,
-    ) = sync(
-        [sums_chain, both_sum],
-        attend_in_rows,
-        attend_out_cols,
-        expand_rows,
-        contract_cols,
-        attend_in_cols,
-        attend_out_rows,
-        expand_cols,
-        contract_rows,
-    )
-    def by_block(values):
-        return jnp.pad(values.reshape(data_size, row_share), ((0, 0), (0, 128 - row_share)))
-
-    old_rows = jnp.concatenate(
-        [by_block(v) for v in (attend_in_rows, attend_out_cols, expand_rows, contract_cols)], 1
-    )
-    in_cols = attend_in_cols.reshape(3, groups, head_share).swapaxes(0, 1)
-    old_cols = jnp.concatenate(
-        [
-            jnp.concatenate(
-                [in_cols.reshape(groups, -1), attend_out_rows.reshape(groups, -1)], 1
-            ),
-            expand_cols.reshape(groups, -1),
-            contract_rows.reshape(groups, -1),
-        ]
-    )
-    old_rows, old_cols, table_rows, vector_second = sync(
-        [sums_chain, both_sum], old_rows, old_cols, table_rows, vector_second
-    )
-    table_down = jnp.concatenate(
-        [table_rows[1:], table_rows[:1], jnp.zeros((padded - slots,), f32)]
-    )
-    downs = (stem_rows[None], table_down[None])
-    second_lines = jnp.pad(vector_second, (0, 24 * D - vectors.shape[0])).reshape(24, D)
-    second_lines, downs = sync([sums_chain, both_sum], second_lines, downs)
-    sync([sums_chain, both_sum])
-    sums = sums_chain.result
-    rows_new, cols_new, update, scalars, square_totals = call(
+    )
+    *statistics, update, scalars, square_totals = call(
         functools.partial(renew_kernel, **names),
         (0,),
         here,
         tuple(
             (value, False)
-            for value in (sums, old_rows, old_cols, grad_attend, grad_expand, grad_contract)
-        ),
-        (
-            (old_rows.shape, f32, False),
-            (old_cols.shape, f32, False),
+            for value in (sums,) + statistics + (grad_attend, grad_expand, grad_contract)
+        ),
+        tuple((value.shape, f32, False) for value in statistics)
+        + (
             ((3, row_share, D), f32, False),
             ((8, 128), f32, False),
             ((8, 128), f32, False),
         ),
-    )
+        (((data_size, 512), f32), ((3 * groups, D), f32)),
+    )
+    (
+        in_rows_new,
+        out_cols_new,
+        expand_rows_new,
+        contract_cols_new,
+        in_cols_new,
+        out_rows_new,
+        expand_cols_new,
+        contract_rows_new,
+    ) = statistics
     scalars_chain = Chain(links.add(scalars))
-    rows_new, cols_new, sums = sync([scalars_chain, both_sum], rows_new, cols_new, sums)
+    sums = sync([scalars_chain, both_sum], sums)
     stem_new, stem_rows_new, stem_cols_new, table_new, table_rows_new, table_cols_new = call(
-        functools.partial(stem_step_kernel, slots=slots),
+        functools.partial(stem_step_kernel, padded=padded),
         (0,),
         here,
         tuple(
             (value, False)
             for value in both_sum.result
-            + (stem_weight, downs[0], stem_cols[None], table, downs[1], table_cols[None])
+            + (stem_weight, stem_rows, stem_cols, position_table, table_rows, table_cols)
         ),
         tuple(
-            (shape, f32, False)
-            for shape in ((D, D), (1, D), (1, D), (padded, D), (1, padded), (1, D))
+            (value.shape, f32, False)
+            for value in (stem_weight, stem_rows, stem_cols, position_table, table_rows, table_cols)
         ),
         (((1024, D), bf16),),
     )
-    stem_new, table_new, table_rows_new, rows_new, cols_new, sums = sync(
-        [scalars_chain], stem_new, table_new, table_rows_new, rows_new, cols_new, sums
-    )
-
-    vector_lines_new = call(
-        functools.partial(vector_kernel, length=vectors.shape[0], **names),
+    stem_new, sums = sync([scalars_chain], stem_new, sums)
+    grad_vector, vectors_new, second_new = call(
+        functools.partial(vector_kernel, **names),
         (0,),
         here,
         tuple(
-            (value, False) for value in (sums, vector_last, vector_head, vector_lines, second_lines)
-        ),
-        (((24, D), f32, False),) * 3,
-    )
-    vector_lines_new, table_new, table_rows_new, rows_new, cols_new = sync(
-        [scalars_chain], vector_lines_new, table_new, table_rows_new, rows_new, cols_new
-    )
-    grad_vector, vectors_new, second_new = (
-        lines.reshape(-1)[: vectors.shape[0]] for lines in vector_lines_new
-    )
-    table_rows_new = table_rows_new.reshape(-1)
-    table_new = jnp.concatenate([table_new[patch_count:slots], table_new[:patch_count]])
-    table_rows_new = jnp.concatenate(
-        [table_rows_new[patch_count:slots], table_rows_new[:patch_count]]
-    )
-    table_new, rows_new, cols_new = sync([scalars_chain], table_new, rows_new, cols_new)
-
-    def of_blocks(index):
-        return rows_new[:, index * 128 : index * 128 + row_share].reshape(-1)
-
-    in_cols_new = cols_new[:groups, :in_share].reshape(groups, 3, head_share).swapaxes(0, 1)
-    statistics = (
-        of_blocks(0),
-        in_cols_new.reshape(3, D),
-        cols_new[:groups, in_share:].reshape(-1),
-        of_blocks(1),
-        of_blocks(2),
-        cols_new[groups : 2 * groups].reshape(-1),
-        cols_new[2 * groups :].reshape(-1),
-        of_blocks(3),
-    )
-    statistics = sync([scalars_chain], statistics)
+            (value, False) for value in (sums, vector_last, vector_head, vector_lines, vector_second)
+        ),
+        ((vectors.shape, f32, False),) * 3,
+        (((24, D), f32), ((24, D), f32)),
+    )
+    vectors_new = sync([scalars_chain], vectors_new)
+    sync([scalars_chain])
+    sync([scalars_chain])
     block = call(
         functools.partial(step_kernel, sizes=(3 * D * D, D * D, D * FF, FF * D)),
         (0,),
@@ -1745,30 +1758,30 @@
     return (
         loss_sum,
         stem_new,
-        stem_rows_new.reshape(-1),
-        stem_cols_new.reshape(-1),
+        stem_rows_new,
+        stem_cols_new,
         table_new,
         table_rows_new,
-        table_cols_new.reshape(-1),
+        table_cols_new,
         in_new.swapaxes(0, 1),
         in_copy.swapaxes(0, 1),
-        statistics[0],
-        statistics[1],
+        in_rows_new,
+        in_cols_new,
         out_new,
         out_copy,
-        statistics[2],
-        statistics[3],
+        out_rows_new,
+        out_cols_new,
         expand_new,
         expand_copy,
-        statistics[4],
-        statistics[5],
+        expand_rows_new,
+        expand_cols_new,
         contract_new.T,
         contract_copy.T,
-        statistics[6],
-        statistics[7],
+        contract_rows_new,
+        contract_cols_new,
         head_new.T,
-        head_rows_new.reshape(-1),
-        head_cols_new.reshape(-1),
+        head_rows_new,
+        head_cols_new,
         vectors_new,
         grad_vector,
         second_new,

time: 323 us -> 327 us (1.012)
  Pallas kernels: 141 us -> 154 us
  local copies, waits for them, and re-layouts: 26.3 us -> 14.9 us
  waiting for transfers between devices: 67.8 us -> 75 us
  starting transfers between devices: 60 us -> 54.6 us
    pallas_call x16, Pallas kernels: 132 us -> 145 us  [call(): pl.pallas_call(kernel, grid_spec=pltpu.PrefetchScalarGridSpec(num_scalar_...]
    ppermute x58, waiting for transfers between devices: 67.8 us -> 75 us  [send(): return lax.ppermute(values, ALL, table)]
    reshape x24 -> x0, local copies, waits for them, and re-layouts: 5.93 us -> none  [the longest x4 2.66 us: of_blocks(): return rows_new[:, index * 128:index * 128 + row_share].reshape(-1)]
    ppermute x58, starting transfers between devices: 60 us -> 54.6 us  [send(): return lax.ppermute(values, ALL, table)]
    slice x15 -> x0, local copies, waits for them, and re-layouts: 5.11 us -> none  [the longest x3 1.94 us: local(): table = jnp.concatenate([position_table[1:], position_table[:1], empty])]
    unnamed x155 -> x157, local copies, waits for them, and re-layouts: 14.4 us -> 13.6 us
  transfers between devices with their start and end apart: 58 -> 58, of which waited for: 21 -> 24; matrix products, arithmetic and copies ran while one was open for 8% -> 5% of each run, Pallas kernels for 41% -> 40%
where the time goes in v3:
time: 327 us; the launch traced here: 323 us
  Pallas kernels  154 us (47%)
  waiting for transfers between devices  75 us (23%)
  starting transfers between devices  54.6 us (17%)
  other arithmetic  22.4 us (7%)
  local copies, waits for them, and re-layouts  14.9 us (5%)
    pallas_call x16, Pallas kernels, call(): pl.pallas_call(kernel, grid_spec=pltpu.PrefetchScalarGridSpec(num_scalar_...  145 us
    ppermute x58, waiting for transfers between devices, send(): return lax.ppermute(values, ALL, table)  75 us
    ppermute x58, starting transfers between devices, send(): return lax.ppermute(values, ALL, table)  54.6 us
    unnamed x157, local copies, waits for them, and re-layouts  13.6 us
    pallas_call x4, Pallas kernels, gather(): pl.pallas_call(column_kernel, in_specs=[pl.BlockSpec(memory_space=pltpu.S...  7.6 us
  transfers between devices with their start and end apart: 58, of which 24 were waited for; matrix products, arithmetic and copies ran while one was open for 5% of the time, Pallas kernels for 40%

profile of v3, /device:TPU:0, one launch (start us, length us, event | category | flops | bytes accessed | tf_op | source)
XLA Modules:
  0.0 323.1 jit_solution(593715637471653348)
XLA Ops:
  4.2 5.0 %collective-permute-start = (bf16[96,768]{1,0:T(8,128)(2,1)}, bf16[96,768]{1,0:T(8,128)(2,1)S(1)}, u32[]{:S(2)}, u32[]{:S(2)}) collective-permute-start(bf16[96,768]{1,0:T(8,128)(2,1)} %get-tuple-element.198.refs_0_), channel_id=1, source_target_pairs={{0,24},{1,25},{2,26},{3,27},{4,28},{5,29},{6,30},{7,31},{8,0},{9,1... | collective-permute-start | bytes 442376 | tf_op jit(solution)/shard_map/ppermute | solution.py:167
  13.9 8.1 %collective-permute-done.1.refs_2_ = bf16[96,768]{1,0:T(8,128)(2,1)S(1)} collective-permute-done((bf16[96,768]{1,0:T(8,128)(2,1)}, bf16[96,768]{1,0:T(8,128)(2,1)S(1)}, u32[]{:S(2)}, u32[]{:S(2)}) %collective-permute-start.1) | collective-permute-done | bytes 147488 | tf_op jit(solution)/shard_map/ppermute | solution.py:167
  32.6 3.9 %shard_map.475 = (f32[832,768]{1,0:T(8,128)}, bf16[832,768]{1,0:T(8,128)(2,1)S(1)}, f32[4,208]{1,0:T(4,128)S(1)}, f32[8,128]{1,0:T(8,128)S(1)}) custom-call(s32[8]{0:T(128)S(1)} %copy-done.25, s32[4]{0:T(128)S(1)} %copy-done.45, bf16[832,768]{1,0:T(8,128)(2,1)S(1)} %bitcast.117, f32[768,768]{1,0:T(8,128)S(1)} %copy-done.1, f32[197,768]{1,0:T(8,128)S(1)} %copy-done.6, ...), custom_call_target="tpu_custom_call" | custom-call | flops 981467136 | bytes 16000000 | tf_op jit(solution)/shard_map/pallas_call | solution.py:1330
  36.6 4.8 %collective-permute-done.5.refs_2_ = bf16[96,768]{1,0:T(8,128)(2,1)S(1)} collective-permute-done((bf16[96,768]{1,0:T(8,128)(2,1)S(1)}, bf16[96,768]{1,0:T(8,128)(2,1)S(1)}, u32[]{:S(2)}, u32[]{:S(2)}) %collective-permute-start.5) | collective-permute-done | bytes 147488 | tf_op jit(solution)/shard_map/ppermute | solution.py:167
  47.3 6.3 %collective-permute-done.10.refs_1_ = bf16[96,768]{1,0:T(8,128)(2,1)S(1)} collective-permute-done((bf16[96,768]{1,0:T(8,128)(2,1)S(1)}, bf16[96,768]{1,0:T(8,128)(2,1)S(1)}, u32[]{:S(2)}, u32[]{:S(2)}) %collective-permute-start.10) | collective-permute-done | bytes 147488 | tf_op jit(solution)/shard_map/ppermute | solution.py:167
  56.8 4.3 %collective-permute-done.11.refs_2_ = bf16[96,768]{1,0:T(8,128)(2,1)S(1)} collective-permute-done((bf16[96,768]{1,0:T(8,128)(2,1)S(1)}, bf16[96,768]{1,0:T(8,128)(2,1)S(1)}, u32[]{:S(2)}, u32[]{:S(2)}) %collective-permute-start.11) | collective-permute-done | bytes 147488 | tf_op jit(solution)/shard_map/ppermute | solution.py:167
  61.4 3.5 %collective-permute-done.7.refs_1_ = bf16[2,4,96,768]{3,2,1,0:T(8,128)(2,1)} collective-permute-done((bf16[2,4,96,768]{3,2,1,0:T(8,128)(2,1)S(1)}, bf16[2,4,96,768]{3,2,1,0:T(8,128)(2,1)}, u32[]{:S(2)}, u32[]{:S(2)}) %collective-permute-start.7) | collective-permute-done | bytes 1179680 | tf_op jit(solution)/shard_map/ppermute | solution.py:167
  70.3 18.7 %shard_map.478 = (bf16[4,3,832,192]{3,2,1,0:T(8,128)(2,1)}, bf16[4,832,192]{2,1,0:T(8,128)(2,1)}, f32[832,768]{1,0:T(8,128)}, bf16[832,768]{1,0:T(8,128)(2,1)S(1)}, f32[8,768]{1,0:T(8,128)S(1)}) custom-call(s32[8]{0:T(128)S(1)} %copy-done.26, bf16[2,4,96,768]{3,2,1,0:T(8,128)(2,1)S(1)} %pad_maximum_fusion.refs_0_, ...), custom_call_target="tpu_custom_call" | custom-call | flops 3925868544 | bytes 16000000 | tf_op jit(solution)/shard_map/pallas_call | solution.py:1330
  94.1 12.6 %shard_map.479 = (f32[4,8,768]{2,1,0:T(8,128)S(1)}, bf16[4,832,768]{2,1,0:T(8,128)(2,1)}) custom-call(s32[8]{0:T(128)S(1)} %copy-done.26, bf16[2,4,96,768]{3,2,1,0:T(8,128)(2,1)} %pad_maximum_fusion.1.refs_0_, bf16[2,4,96,768]{3,2,1,0:T(8,128)(2,1)} %collective-permute-done.13.refs_1_, bf16[2,4,96,768]{3,2,1,0:T(8,128)(2,1)} %collective-permute-done.14.refs_2_, ...), custom_call_target="tpu_custom_call" | custom-call | flops 3925868544 | bytes 16000000 | tf_op jit(solution)/shard_map/pallas_call | solution.py:1330
  109.6 18.0 %shard_map.480 = (bf16[32,896]{1,0:T(8,128)(2,1)S(1)}, f32[8,768]{1,0:T(8,128)S(1)}, f32[4,8,768]{2,1,0:T(8,128)S(1)}) custom-call(s32[8]{0:T(128)S(1)} %copy-done.26, f32[4,8,768]{2,1,0:T(8,128)S(1)} %get-tuple-element.242.active_ref, f32[8,768]{1,0:T(8,128)S(1)} %get-tuple-element.243.sum_ref, f32[8,128]{1,0:T(8,128)S(1)} %get-tuple-element.244.facts_ref, ...), custom_call_target="tpu_custom_call" | custom-call | bytes 16000000 | tf_op jit(solution)/shard_map/pallas_call | solution.py:1330
  132.0 18.2 %shard_map.481 = (bf16[2,768,768]{2,1,0:T(8,128)(2,1)}, bf16[2,768,768]{2,1,0:T(8,128)(2,1)}, f32[4,1,768]{2,1,0:T(1,128)S(1)}, f32[832,768]{1,0:T(8,128)}) custom-call(s32[8]{0:T(128)S(1)} %copy-done.26, bf16[2,4,96,768]{3,2,1,0:T(8,128)(2,1)} %pad_maximum_fusion.1.refs_0_, bf16[2,4,96,768]{3,2,1,0:T(8,128)(2,1)} %collective-permute-done.13.refs_1_, ...), custom_call_target="tpu_custom_call" | custom-call | flops 7851737088 | bytes 16000000 | tf_op jit(solution)/shard_map/pallas_call | solution.py:1330
  153.8 5.4 %shard_map.483 = (f32[832,768]{1,0:T(8,128)S(1)}, bf16[832,768]{1,0:T(8,128)(2,1)S(1)}, f32[8,768]{1,0:T(8,128)S(1)}) custom-call(s32[8]{0:T(128)S(1)} %copy-done.27, f32[832,768]{1,0:T(8,128)} %get-tuple-element.259.d_rows_ref, f32[8,768]{1,0:T(8,128)S(1)} %get-tuple-element.260.d_row_ref, f32[4,208]{1,0:T(4,128)S(1)} %get-tuple-element.227.refs_6_.present_ref.refs_7_, ...), custom_call_target="tpu_custom_call" | custom-call | bytes 16000000 | tf_op jit(solution)/shard_map/pallas_call | solution.py:1330
  165.1 18.6 %shard_map.484 = (bf16[2,768,768]{2,1,0:T(8,128)(2,1)}, f32[2,8,192]{2,1,0:T(8,128)S(1)}, f32[832,768]{1,0:T(8,128)}) custom-call(s32[8]{0:T(128)S(1)} %copy-done.27, bf16[2,4,96,768]{3,2,1,0:T(8,128)(2,1)S(1)} %pad_maximum_fusion.refs_0_, bf16[2,4,96,768]{3,2,1,0:T(8,128)(2,1)} %collective-permute-done.7.refs_1_, ...), custom_call_target="tpu_custom_call" | custom-call | flops 3925868544 | bytes 16000000 | tf_op jit(solution)/shard_map/pallas_call | solution.py:1330
  189.6 20.0 %shard_map.485 = (bf16[2,768,768]{2,1,0:T(8,128)(2,1)}, f32[2,8,192]{2,1,0:T(8,128)S(1)}, f32[832,768]{1,0:T(8,128)}) custom-call(s32[8]{0:T(128)S(1)} %copy-done.27, bf16[2,4,96,768]{3,2,1,0:T(8,128)(2,1)S(1)} %pad_maximum_fusion.refs_0_, bf16[2,4,96,768]{3,2,1,0:T(8,128)(2,1)} %collective-permute-done.7.refs_1_, ...), custom_call_target="tpu_custom_call" | custom-call | flops 3925868544 | bytes 16000000 | tf_op jit(solution)/shard_map/pallas_call | solution.py:1330
  222.3 7.3 %shard_map.486 = (bf16[4,128,768]{2,1,0:T(8,128)(2,1)}, bf16[4,128,768]{2,1,0:T(8,128)(2,1)S(1)}, f32[216,768]{1,0:T(8,128)S(1)}) custom-call(s32[8]{0:T(128)S(1)} %copy-done.27, f32[832,768]{1,0:T(8,128)S(1)} %copy-done.5, f32[832,768]{1,0:T(8,128)} %copy-done.4, f32[832,768]{1,0:T(8,128)} %get-tuple-element.228.refs_7_.stream_ref, ...), custom_call_target="tpu_custom_call" | custom-call | flops 981467136 | bytes 16000000 | tf_op jit(solution)/shard_map/pallas_call | solution.py:1330
  239.5 4.7 %collective-permute-done.36 = bf16[4,96,768]{2,1,0:T(8,128)(2,1)S(1)} collective-permute-done((bf16[4,96,768]{2,1,0:T(8,128)(2,1)}, bf16[4,96,768]{2,1,0:T(8,128)(2,1)S(1)}, u32[]{:S(2)}, u32[]{:S(2)}) %collective-permute-start.36) | collective-permute-done | bytes 589856 | tf_op jit(solution)/shard_map/ppermute | solution.py:167
  253.9 9.3 %shard_map.488 = (f32[1000,768]{1,0:T(8,128)}, f32[768]{0:T(1024)}, f32[1000]{0:T(1024)}, f32[96,768]{1,0:T(8,128)S(1)}, f32[8,768]{1,0:T(8,128)S(1)}, /*index=5*/f32[8,1000]{1,0:T(8,128)S(1)}) custom-call(s32[8]{0:T(128)S(1)} %copy-done.27, bf16[1,32,32,896]{3,2,1,0:T(8,128)(2,1)S(1)} %bitcast.119, f32[24,768]{1,0:T(8,128)S(1)} %copy-done.3, ...), custom_call_target="tpu_custom_call" | custom-call | bytes 16000000 | tf_op jit(solution)/shard_map/pallas_call | solution.py:1330
  272.9 3.7 %collective-permute-done.44 = f32[32,768]{1,0:T(8,128)S(1)} collective-permute-done((f32[32,768]{1,0:T(8,128)S(1)}, f32[32,768]{1,0:T(8,128)S(1)}, u32[]{:S(2)}, u32[]{:S(2)}) %collective-permute-start.44) | collective-permute-done | bytes 98336 | tf_op jit(solution)/shard_map/ppermute | solution.py:167
  282.7 4.0 %collective-permute-done.47 = bf16[1,128,768]{2,1,0:T(8,128)(2,1)S(1)} collective-permute-done((bf16[1,128,768]{2,1,0:T(8,128)(2,1)S(1)}, bf16[1,128,768]{2,1,0:T(8,128)(2,1)S(1)}, u32[]{:S(2)}, u32[]{:S(2)}) %collective-permute-start.47) | collective-permute-done | bytes 196640 | tf_op jit(solution)/shard_map/ppermute | solution.py:167
  288.1 4.6 %collective-permute-done.48 = f32[32,768]{1,0:T(8,128)S(1)} collective-permute-done((f32[32,768]{1,0:T(8,128)S(1)}, f32[32,768]{1,0:T(8,128)S(1)}, u32[]{:S(2)}, u32[]{:S(2)}) %collective-permute-start.48) | collective-permute-done | bytes 98336 | tf_op jit(solution)/shard_map/ppermute | solution.py:167
  293.8 6.0 %collective-permute-done.50 = f32[32,768]{1,0:T(8,128)S(1)} collective-permute-done((f32[32,768]{1,0:T(8,128)S(1)}, f32[32,768]{1,0:T(8,128)S(1)}, u32[]{:S(2)}, u32[]{:S(2)}) %collective-permute-start.50) | collective-permute-done | bytes 98336 | tf_op jit(solution)/shard_map/ppermute | solution.py:167
  304.9 4.3 %shard_map.491 = (f32[768,768]{1,0:T(8,128)}, f32[768]{0:T(1024)}, f32[768]{0:T(1024)}, f32[197,768]{1,0:T(8,128)}, f32[197]{0:T(256)}, /*index=5*/f32[768]{0:T(1024)}) custom-call(s32[8]{0:T(128)S(1)} %copy-done.27, bf16[4,128,768]{2,1,0:T(8,128)(2,1)S(1)} %pad_maximum_fusion.5.near_ref, bf16[4,128,768]{2,1,0:T(8,128)(2,1)S(1)} %collective-permute-done.53.far_ref, ...), custom_call_target="tpu_custom_call" | custom-call | bytes 16000000 | tf_op jit(solution)/shard_map/pallas_call | solution.py:1330
  312.9 3.6 %collective-permute-done.56 = f32[8,128]{1,0:T(8,128)S(1)} collective-permute-done((f32[8,128]{1,0:T(8,128)S(1)}, f32[8,128]{1,0:T(8,128)S(1)}, u32[]{:S(2)}, u32[]{:S(2)}) %collective-permute-start.56) | collective-permute-done | bytes 4128 | tf_op jit(solution)/shard_map/ppermute | solution.py:167
  317.0 4.0 %collective-permute-done.57 = f32[8,128]{1,0:T(8,128)S(1)} collective-permute-done((f32[8,128]{1,0:T(8,128)S(1)}, f32[8,128]{1,0:T(8,128)S(1)}, u32[]{:S(2)}, u32[]{:S(2)}) %collective-permute-start.57) | collective-permute-done | bytes 4128 | tf_op jit(solution)/shard_map/ppermute | solution.py:167
  (309 shorter events, 122.1 us)
Async XLA Ops:
  24.7 16.7 %collective-permute-start.3 = (bf16[1,4,96,768]{3,2,1,0:T(8,128)(2,1)}, bf16[1,4,96,768]{3,2,1,0:T(8,128)(2,1)S(1)}, u32[]{:S(2)}, u32[]{:S(2)}) collective-permute-start(bf16[1,4,96,768]{3,2,1,0:T(8,128)(2,1)} %shard_map.474), channel_id=1, source_target_pairs={{0,4},{1,3},{2,6},{3,1},{4,0},{5,7},{6,2},{7,5},{8,12},{9,11},{10,... | collective-permute-start | bytes 1769480 | tf_op jit(solution)/shard_map/ppermute | solution.py:167
  27.6 13.8 %collective-permute-start.5 = (bf16[96,768]{1,0:T(8,128)(2,1)S(1)}, bf16[96,768]{1,0:T(8,128)(2,1)S(1)}, u32[]{:S(2)}, u32[]{:S(2)}) collective-permute-start(bf16[96,768]{1,0:T(8,128)(2,1)S(1)} %copy-done.65), channel_id=1, source_target_pairs={{0,16},{1,17},{2,18},{3,19},{4,20},{5,21},{6,22},{7,23},{8,24},{9,... | collective-permute-start | bytes 442376 | tf_op jit(solution)/shard_map/ppermute | solution.py:167
  42.2 22.7 %collective-permute-start.7 = (bf16[2,4,96,768]{3,2,1,0:T(8,128)(2,1)S(1)}, bf16[2,4,96,768]{3,2,1,0:T(8,128)(2,1)}, u32[]{:S(2)}, u32[]{:S(2)}) collective-permute-start(bf16[2,4,96,768]{3,2,1,0:T(8,128)(2,1)S(1)} %pad_maximum_fusion.refs_0_), channel_id=1, source_target_pairs={{0,2},{1,5},{2,0},{3,7},{4,6},{5,1},{6,4},{7,3},{8,10},{9,13},{10,... | collective-permute-start | bytes 3538952 | tf_op jit(solution)/shard_map/ppermute | solution.py:167
  42.8 22.1 %collective-permute-start.8 = (bf16[2,4,96,768]{3,2,1,0:T(8,128)(2,1)S(1)}, bf16[2,4,96,768]{3,2,1,0:T(8,128)(2,1)}, u32[]{:S(2)}, u32[]{:S(2)}) collective-permute-start(bf16[2,4,96,768]{3,2,1,0:T(8,128)(2,1)S(1)} %pad_maximum_fusion.refs_0_), channel_id=1, source_target_pairs={{0,1},{1,0},{2,3},{3,2},{4,5},{5,4},{6,7},{7,6},{8,9},{9,8},{10,11... | collective-permute-start | bytes 3538952 | tf_op jit(solution)/shard_map/ppermute | solution.py:167
  44.9 16.5 %collective-permute-start.9 = (bf16[1,4,96,768]{3,2,1,0:T(8,128)(2,1)}, bf16[1,4,96,768]{3,2,1,0:T(8,128)(2,1)S(1)}, u32[]{:S(2)}, u32[]{:S(2)}) collective-permute-start(bf16[1,4,96,768]{3,2,1,0:T(8,128)(2,1)} %shard_map.476), channel_id=1, source_target_pairs={{0,4},{1,3},{2,6},{3,1},{4,0},{5,7},{6,2},{7,5},{8,12},{9,11},{10,... | collective-permute-start | bytes 1769480 | tf_op jit(solution)/shard_map/ppermute | solution.py:167
  46.3 14.8 %collective-permute-start.11 = (bf16[96,768]{1,0:T(8,128)(2,1)S(1)}, bf16[96,768]{1,0:T(8,128)(2,1)S(1)}, u32[]{:S(2)}, u32[]{:S(2)}) collective-permute-start(bf16[96,768]{1,0:T(8,128)(2,1)S(1)} %copy-done.64), channel_id=1, source_target_pairs={{0,16},{1,17},{2,18},{3,19},{4,20},{5,21},{6,22},{7,23},{8,24},{9,... | collective-permute-start | bytes 442376 | tf_op jit(solution)/shard_map/ppermute | solution.py:167
  66.1 23.0 %collective-permute-start.13 = (bf16[2,4,96,768]{3,2,1,0:T(8,128)(2,1)}, bf16[2,4,96,768]{3,2,1,0:T(8,128)(2,1)}, u32[]{:S(2)}, u32[]{:S(2)}) collective-permute-start(bf16[2,4,96,768]{3,2,1,0:T(8,128)(2,1)} %pad_maximum_fusion.1.refs_0_), channel_id=1, source_target_pairs={{0,2},{1,5},{2,0},{3,7},{4,6},{5,1},{6,4},{7,3},{8,10},{9,13},{10,... | collective-permute-start | bytes 3538952 | tf_op jit(solution)/shard_map/ppermute | solution.py:167
  66.6 22.5 %collective-permute-start.14 = (bf16[2,4,96,768]{3,2,1,0:T(8,128)(2,1)}, bf16[2,4,96,768]{3,2,1,0:T(8,128)(2,1)}, u32[]{:S(2)}, u32[]{:S(2)}) collective-permute-start(bf16[2,4,96,768]{3,2,1,0:T(8,128)(2,1)} %pad_maximum_fusion.1.refs_0_), channel_id=1, source_target_pairs={{0,1},{1,0},{2,3},{3,2},{4,5},{5,4},{6,7},{7,6},{8,9},{9,8},{10,11... | collective-permute-start | bytes 3538952 | tf_op jit(solution)/shard_map/ppermute | solution.py:167
  69.8 19.2 %collective-permute-start.15 = (bf16[1,4,96,768]{3,2,1,0:T(8,128)(2,1)}, bf16[1,4,96,768]{3,2,1,0:T(8,128)(2,1)S(1)}, u32[]{:S(2)}, u32[]{:S(2)}) collective-permute-start(bf16[1,4,96,768]{3,2,1,0:T(8,128)(2,1)} %shard_map.477), channel_id=1, source_target_pairs={{0,4},{1,3},{2,6},{3,1},{4,0},{5,7},{6,2},{7,5},{8,12},{9,11},{10,... | collective-permute-start | bytes 1769480 | tf_op jit(solution)/shard_map/ppermute | solution.py:167
  90.2 16.5 %collective-permute-start.17 = (bf16[2,4,96,768]{3,2,1,0:T(8,128)(2,1)S(1)}, bf16[2,4,96,768]{3,2,1,0:T(8,128)(2,1)S(1)}, u32[]{:S(2)}, u32[]{:S(2)}) collective-permute-start(bf16[2,4,96,768]{3,2,1,0:T(8,128)(2,1)S(1)} %pad_maximum_fusion.2.refs_0_), channel_id=1, source_target_pairs={{0,2},{1,5},{2,0},{3,7},{4,6},{5,1},{6,4},{7,3},{8,10},{9,13},{10,... | collective-permute-start | bytes 3538952 | tf_op jit(solution)/shard_map/ppermute | solution.py:167
  91.5 15.2 %collective-permute-start.18 = (bf16[2,4,96,768]{3,2,1,0:T(8,128)(2,1)S(1)}, bf16[2,4,96,768]{3,2,1,0:T(8,128)(2,1)S(1)}, u32[]{:S(2)}, u32[]{:S(2)}) collective-permute-start(bf16[2,4,96,768]{3,2,1,0:T(8,128)(2,1)S(1)} %pad_maximum_fusion.2.refs_0_), channel_id=1, source_target_pairs={{0,1},{1,0},{2,3},{3,2},{4,5},{5,4},{6,7},{7,6},{8,9},{9,8},{10,11... | collective-permute-start | bytes 3538952 | tf_op jit(solution)/shard_map/ppermute | solution.py:167
  127.6 22.6 %collective-permute-start.21 = (bf16[32,896]{1,0:T(8,128)(2,1)S(1)}, bf16[32,896]{1,0:T(8,128)(2,1)S(1)}, u32[]{:S(2)}, u32[]{:S(2)}) collective-permute-start(bf16[32,896]{1,0:T(8,128)(2,1)S(1)} %get-tuple-element.248.refs_0_), channel_id=1, source_target_pairs={{0,24},{1,25},{2,26},{3,27},{4,28},{5,29},{6,30},{7,31},{8,0},{9,1... | collective-permute-start | bytes 172040 | tf_op jit(solution)/shard_map/ppermute | solution.py:167
  127.7 22.6 %collective-permute-start.22 = (bf16[32,896]{1,0:T(8,128)(2,1)S(1)}, bf16[32,896]{1,0:T(8,128)(2,1)S(1)}, u32[]{:S(2)}, u32[]{:S(2)}) collective-permute-start(bf16[32,896]{1,0:T(8,128)(2,1)S(1)} %get-tuple-element.248.refs_0_), channel_id=1, source_target_pairs={{0,16},{1,17},{2,18},{3,19},{4,20},{5,21},{6,22},{7,23},{8,24},{9,... | collective-permute-start | bytes 172040 | tf_op jit(solution)/shard_map/ppermute | solution.py:167
  128.8 21.5 %collective-permute-start.23 = (bf16[32,896]{1,0:T(8,128)(2,1)S(1)}, bf16[32,896]{1,0:T(8,128)(2,1)S(1)}, u32[]{:S(2)}, u32[]{:S(2)}) collective-permute-start(bf16[32,896]{1,0:T(8,128)(2,1)S(1)} %get-tuple-element.248.refs_0_), channel_id=1, source_target_pairs={{0,8},{1,9},{2,10},{3,11},{4,12},{5,13},{6,14},{7,15},{8,16},{9,17... | collective-permute-start | bytes 172040 | tf_op jit(solution)/shard_map/ppermute | solution.py:167
  162.9 22.8 %collective-permute-start.28 = (bf16[2,4,96,768]{3,2,1,0:T(8,128)(2,1)S(1)}, bf16[2,4,96,768]{3,2,1,0:T(8,128)(2,1)S(1)}, u32[]{:S(2)}, u32[]{:S(2)}) collective-permute-start(bf16[2,4,96,768]{3,2,1,0:T(8,128)(2,1)S(1)} %pad_maximum_fusion.3), channel_id=1, source_target_pairs={{0,2},{1,5},{2,0},{3,7},{4,6},{5,1},{6,4},{7,3},{8,10},{9,13},{10,... | collective-permute-start | bytes 3538952 | tf_op jit(solution)/shard_map/ppermute | solution.py:167
  163.8 20.2 %collective-permute-start.26 = (bf16[2,4,32,896]{3,2,1,0:T(8,128)(2,1)S(1)}, bf16[2,4,32,896]{3,2,1,0:T(8,128)(2,1)S(1)}, u32[]{:S(2)}, u32[]{:S(2)}) collective-permute-start(bf16[2,4,32,896]{3,2,1,0:T(8,128)(2,1)S(1)} %pad_maximum_fusion.6.refs_0_), channel_id=1, source_target_pairs={{0,2},{1,5},{2,0},{3,7},{4,6},{5,1},{6,4},{7,3},{8,10},{9,13},{10,... | collective-permute-start | bytes 1376264 | tf_op jit(solution)/shard_map/ppermute | solution.py:167
  165.1 19.0 %collective-permute-start.27 = (bf16[2,4,32,896]{3,2,1,0:T(8,128)(2,1)S(1)}, bf16[2,4,32,896]{3,2,1,0:T(8,128)(2,1)S(1)}, u32[]{:S(2)}, u32[]{:S(2)}) collective-permute-start(bf16[2,4,32,896]{3,2,1,0:T(8,128)(2,1)S(1)} %pad_maximum_fusion.6.refs_0_), channel_id=1, source_target_pairs={{0,1},{1,0},{2,3},{3,2},{4,5},{5,4},{6,7},{7,6},{8,9},{9,8},{10,11... | collective-permute-start | bytes 1376264 | tf_op jit(solution)/shard_map/ppermute | solution.py:167
  186.7 22.9 %collective-permute-start.31 = (bf16[2,768,768]{2,1,0:T(8,128)(2,1)}, bf16[2,768,768]{2,1,0:T(8,128)(2,1)}, u32[]{:S(2)}, u32[]{:S(2)}) collective-permute-start(bf16[2,768,768]{2,1,0:T(8,128)(2,1)} %get-tuple-element.274), channel_id=1, source_target_pairs={{0,1},{1,0},{2,3},{3,2},{4,5},{5,4},{6,7},{7,6},{8,9},{9,8},{10,11... | collective-permute-start | bytes 7077896 | tf_op jit(solution)/shard_map/ppermute | solution.py:167
  188.6 20.9 %collective-permute-start.30 = (bf16[4,96,768]{2,1,0:T(8,128)(2,1)S(1)}, bf16[4,96,768]{2,1,0:T(8,128)(2,1)S(1)}, u32[]{:S(2)}, u32[]{:S(2)}) collective-permute-start(bf16[4,96,768]{2,1,0:T(8,128)(2,1)S(1)} %fusion.3), channel_id=1, source_target_pairs={{0,4},{1,3},{2,6},{3,1},{4,0},{5,7},{6,2},{7,5},{8,12},{9,11},{10,... | collective-permute-start | bytes 1769480 | tf_op jit(solution)/shard_map/ppermute | solution.py:167
  189.5 20.0 %collective-permute-start.29 = (bf16[2,4,32,896]{3,2,1,0:T(8,128)(2,1)S(1)}, bf16[2,4,32,896]{3,2,1,0:T(8,128)(2,1)S(1)}, u32[]{:S(2)}, u32[]{:S(2)}) collective-permute-start(bf16[2,4,32,896]{3,2,1,0:T(8,128)(2,1)S(1)} %copy-done.18), channel_id=1, source_target_pairs={{0,1},{1,0},{2,3},{3,2},{4,5},{5,4},{6,7},{7,6},{8,9},{9,8},{10,11... | collective-permute-start | bytes 1376264 | tf_op jit(solution)/shard_map/ppermute | solution.py:167
  213.0 18.3 %collective-permute-start.32 = (bf16[2,4,96,768]{3,2,1,0:T(8,128)(2,1)}, bf16[2,4,96,768]{3,2,1,0:T(8,128)(2,1)}, u32[]{:S(2)}, u32[]{:S(2)}) collective-permute-start(bf16[2,4,96,768]{3,2,1,0:T(8,128)(2,1)} %pad_maximum_fusion.4), channel_id=1, source_target_pairs={{0,2},{1,5},{2,0},{3,7},{4,6},{5,1},{6,4},{7,3},{8,10},{9,13},{10,... | collective-permute-start | bytes 3538952 | tf_op jit(solution)/shard_map/ppermute | solution.py:167
  218.0 13.2 %collective-permute-start.34 = (bf16[96,768]{1,0:T(8,128)(2,1)S(1)}, bf16[96,768]{1,0:T(8,128)(2,1)S(1)}, u32[]{:S(2)}, u32[]{:S(2)}) collective-permute-start(bf16[96,768]{1,0:T(8,128)(2,1)S(1)} %get-tuple-element.379), channel_id=1, source_target_pairs={{0,16},{1,17},{2,18},{3,19},{4,20},{5,21},{6,22},{7,23},{8,24},{9,... | collective-permute-start | bytes 442376 | tf_op jit(solution)/shard_map/ppermute | solution.py:167
  245.5 17.7 %collective-permute-start.41 = (bf16[2,128,768]{2,1,0:T(8,128)(2,1)S(1)}, bf16[2,128,768]{2,1,0:T(8,128)(2,1)S(1)}, u32[]{:S(2)}, u32[]{:S(2)}) collective-permute-start(bf16[2,128,768]{2,1,0:T(8,128)(2,1)S(1)} %slice.52), channel_id=1, source_target_pairs={{0,2},{1,5},{2,0},{3,7},{4,6},{5,1},{6,4},{7,3},{8,10},{9,13},{10,... | collective-permute-start | bytes 1179656 | tf_op jit(solution)/shard_map/ppermute | solution.py:167
  248.3 15.0 %collective-permute-start.38 = (bf16[96,768]{1,0:T(8,128)(2,1)S(1)}, bf16[96,768]{1,0:T(8,128)(2,1)S(1)}, u32[]{:S(2)}, u32[]{:S(2)}) collective-permute-start(bf16[96,768]{1,0:T(8,128)(2,1)S(1)} %get-tuple-element.377), channel_id=1, source_target_pairs={{0,8},{1,9},{2,10},{3,11},{4,12},{5,13},{6,14},{7,15},{8,16},{9,17... | collective-permute-start | bytes 442376 | tf_op jit(solution)/shard_map/ppermute | solution.py:167
  (112 other events, 793.7 us)

commit v4 on v3

--- a/solution.py
+++ b/solution.py
@@ -202,7 +202,7 @@
             out_specs=pl.BlockSpec(memory_space=pltpu.VMEM),
             out_shape=jax.ShapeDtypeStruct((4, self.deep, 2, r, c), pieces[0].dtype),
             scratch_shapes=[pltpu.SemaphoreType.DMA((4, 2))],
-            compiler_params=pltpu.CompilerParams(vmem_limit_bytes=16 * 1024 * 1024),
+            compiler_params=pltpu.CompilerParams(vmem_limit_bytes=60 * 1024 * 1024),
         )(self.place, *pieces)
         return full.reshape(4, blocks * r, c)
 
@@ -242,13 +242,15 @@
         return values
 
     def add_large(self, far, near):
-        values = near.astype(f32) + (yield far, self.send(far, self.other)).astype(f32)
-        for table in (self.first, self.second):
-            half = values.shape[0] // 2
-            sent = values[half:].astype(bf16)
-            got = yield sent, self.send(sent, table)
-            values = values[:half] + got.astype(f32)
-        pile = values.astype(bf16)
+        parts = [near, (yield far, self.send(far, self.other))]
+
+        def total(start, stop):
+            return sum(part[start:stop].astype(f32) for part in parts)
+
+        for table, half in ((self.first, 2), (self.second, 1)):
+            sent = total(half, 2 * half).astype(bf16)
+            parts = [part[:half] for part in parts] + [(yield sent, self.send(sent, table))]
+        pile = total(0, 1).astype(bf16)
         for table in (self.flip_z[1], self.flip_z[2]):
             got = yield pile, self.send(pile, table)
             pile = (pile.astype(f32) + got.astype(f32)).astype(bf16)
@@ -800,16 +802,10 @@
     pieces_ref,
     vectors_ref,
     head_ref,
-    weight_ref,
-    old_rows_ref,
-    old_cols_ref,
-    new_ref,
-    new_rows_ref,
-    new_cols_ref,
+    grad_ref,
     contract_ref,
     vector_ref,
     bias_ref,
-    grad_ref,
     *,
     inverse_count,
 ):
@@ -859,17 +855,26 @@
         def _(ref=ref, span=span, value=value):
             ref[span, :] += value
 
-    @pl.when(pl.program_id(0) == pl.num_programs(0) - 1)
-    def _():
-        new_ref[...], cols, rows_ = factored(
-            weight_ref[...],
-            grad_ref[...],
-            old_cols_ref[...].reshape(1, -1),
-            old_rows_ref[...].reshape(1, -1),
-            True,
-        )
-        new_cols_ref[...] = cols[0]
-        new_rows_ref[...] = rows_[0]
+
+def head_step_kernel(
+    place_ref,
+    weight_ref,
+    grad_ref,
+    old_rows_ref,
+    old_cols_ref,
+    new_ref,
+    new_rows_ref,
+    new_cols_ref,
+):
+    new_ref[...], cols, rows = factored(
+        weight_ref[...],
+        grad_ref[...],
+        old_cols_ref[...].reshape(1, -1),
+        old_rows_ref[...].reshape(1, -1),
+        True,
+    )
+    new_cols_ref[...] = cols[0]
+    new_rows_ref[...] = rows[0]
 
 
 def factored(weight, grad, down_old, across_old, turned, valid=None, count=None):
@@ -1605,10 +1610,11 @@
     )
     grad_expand = expand_sum.result
     both_sum = Chain(links.add_large(both_far, both_near))
+    pieces, grad_expand, _ = sync([both_sum], pieces, grad_expand, attend_sum.sent)
     pieces = links.whole(*pieces).reshape((-1,) + piece.shape)
     pieces, grad_expand = sync([attend_sum, both_sum], pieces, grad_expand)
     steps = max(1, pieces.shape[0] // 32)
-    head_new, head_rows_new, head_cols_new, grad_contract, vector_last, vector_head = call(
+    grad_head, grad_contract, vector_last, vector_head = call(
         functools.partial(all_head_kernel, inverse_count=inverse_count),
         (0,) * steps,
         here,
@@ -1616,19 +1622,13 @@
             (pieces.reshape((steps, -1) + piece.shape), lambda g: g),
             (vector_lines, False),
             (head_low, False),
-            (head_turned, False),
-            (head_rows, False),
-            (head_cols, False),
         ),
         (
             ((CLASSES, D), f32, False),
-            ((D,), f32, False),
-            ((CLASSES,), f32, False),
             ((row_share, hidden_share), f32, False),
             ((8, D), f32, False),
             ((8, CLASSES), f32, False),
         ),
-        (((CLASSES, D), f32),),
     )
     loss_sum = vector_head[1, 0]
     grad_expand, grad_contract = sync([attend_sum, both_sum], grad_expand, grad_contract)
@@ -1657,8 +1657,18 @@
         (((lines, D), f32, False),),
     )
     sums_chain = Chain(links.add(sums))
-    for _ in range(5):
-        sync([sums_chain, both_sum])
+    sync([sums_chain])
+    sync([sums_chain, both_sum])
+    head_new, head_rows_new, head_cols_new = call(
+        head_step_kernel,
+        (0,),
+        here,
+        tuple((value, False) for value in (head_turned, grad_head, head_rows, head_cols)),
+        (((CLASSES, D), f32, False), ((D,), f32, False), ((CLASSES,), f32, False)),
+    )
+    sync([sums_chain])
+    head_new = sync([sums_chain, both_sum], head_new)
+    sync([sums_chain, both_sum])
     sums = sums_chain.result
     statistics = (
         attend_in_rows,
@@ -1697,6 +1707,8 @@
         contract_rows_new,
     ) = statistics
     scalars_chain = Chain(links.add(scalars))
+    sums = sync([scalars_chain], sums)
+    sums = sync([scalars_chain, both_sum], sums)
     sums = sync([scalars_chain, both_sum], sums)
     stem_new, stem_rows_new, stem_cols_new, table_new, table_rows_new, table_cols_new = call(
         functools.partial(stem_step_kernel, padded=padded),
@@ -1725,8 +1737,6 @@
         (((24, D), f32), ((24, D), f32)),
     )
     vectors_new = sync([scalars_chain], vectors_new)
-    sync([scalars_chain])
-    sync([scalars_chain])
     block = call(
         functools.partial(step_kernel, sizes=(3 * D * D, D * D, D * FF, FF * D)),
         (0,),

time: 327 us -> 324 us (level)
  waiting for transfers between devices: 75 us -> 65.3 us
  starting transfers between devices: 54.6 us -> 59.8 us
  local copies, waits for them, and re-layouts: 14.9 us -> 10.4 us
  Pallas kernels: 154 us -> 158 us
    ppermute x58, waiting for transfers between devices: 75 us -> 65.3 us  [send(): return lax.ppermute(values, ALL, table)]
    ppermute x58, starting transfers between devices: 54.6 us -> 59.8 us  [send(): return lax.ppermute(values, ALL, table)]
    unnamed x157 -> x145, local copies, waits for them, and re-layouts: 13.6 us -> 9.08 us
    convert_element_type x1 -> x3, other arithmetic: 0.04 us -> 4.3 us  [the longest x2 3.02 us: add_large(): sent = total(half, 2 * half).astype(bf16)]
    pallas_call x16 -> x17, Pallas kernels: 145 us -> 147 us  [call(): pl.pallas_call(kernel, grid_spec=pltpu.PrefetchScalarGridSpec(num_scalar_...]
  transfers between devices with their start and end apart: 58 -> 58, of which waited for: 24 -> 21; matrix products, arithmetic and copies ran while one was open for 5% -> 6% of each run, Pallas kernels for 40% -> 41%
where the time goes in v4:
time: 324 us; the launch traced here: 320 us
  Pallas kernels  158 us (49%)
  waiting for transfers between devices  65.3 us (20%)
  starting transfers between devices  59.8 us (18%)
  other arithmetic  24.9 us (8%)
  local copies, waits for them, and re-layouts  10.4 us (3%)
    pallas_call x17, Pallas kernels, call(): pl.pallas_call(kernel, grid_spec=pltpu.PrefetchScalarGridSpec(num_scalar_...  147 us
    ppermute x58, waiting for transfers between devices, send(): return lax.ppermute(values, ALL, table)  65.3 us
    ppermute x58, starting transfers between devices, send(): return lax.ppermute(values, ALL, table)  59.8 us
    unnamed x145, local copies, waits for them, and re-layouts  9.08 us
    pallas_call x4, Pallas kernels, gather(): pl.pallas_call(column_kernel, in_specs=[pl.BlockSpec(memory_space=pltpu.S...  7.6 us
  transfers between devices with their start and end apart: 58, of which 21 were waited for; matrix products, arithmetic and copies ran while one was open for 6% of the time, Pallas kernels for 41%

profile of v4, /device:TPU:0, one launch (start us, length us, event | category | flops | bytes accessed | tf_op | source)
XLA Modules:
  0.0 320.0 jit_solution(12243407050634768350)
XLA Ops:
  4.2 5.0 %collective-permute-start = (bf16[96,768]{1,0:T(8,128)(2,1)}, bf16[96,768]{1,0:T(8,128)(2,1)S(1)}, u32[]{:S(2)}, u32[]{:S(2)}) collective-permute-start(bf16[96,768]{1,0:T(8,128)(2,1)} %get-tuple-element.207.refs_0_), channel_id=1, source_target_pairs={{0,24},{1,25},{2,26},{3,27},{4,28},{5,29},{6,30},{7,31},{8,0},{9,1... | collective-permute-start | bytes 442376 | tf_op jit(solution)/shard_map/ppermute | solution.py:167
  13.9 8.1 %collective-permute-done.1.refs_2_ = bf16[96,768]{1,0:T(8,128)(2,1)S(1)} collective-permute-done((bf16[96,768]{1,0:T(8,128)(2,1)}, bf16[96,768]{1,0:T(8,128)(2,1)S(1)}, u32[]{:S(2)}, u32[]{:S(2)}) %collective-permute-start.1) | collective-permute-done | bytes 147488 | tf_op jit(solution)/shard_map/ppermute | solution.py:167
  32.6 4.0 %shard_map.475 = (f32[832,768]{1,0:T(8,128)}, bf16[832,768]{1,0:T(8,128)(2,1)S(1)}, f32[4,208]{1,0:T(4,128)S(1)}, f32[8,128]{1,0:T(8,128)S(1)}) custom-call(s32[8]{0:T(128)S(1)} %copy-done.24, s32[4]{0:T(128)S(1)} %copy-done.45, bf16[832,768]{1,0:T(8,128)(2,1)S(1)} %bitcast.118, f32[768,768]{1,0:T(8,128)S(1)} %copy-done.4, f32[197,768]{1,0:T(8,128)S(1)} %copy-done.11, ...), custom_call_target="tpu_custom_call" | custom-call | flops 981467136 | bytes 16000000 | tf_op jit(solution)/shard_map/pallas_call | solution.py:1335
  36.6 4.7 %collective-permute-done.5.refs_2_ = bf16[96,768]{1,0:T(8,128)(2,1)S(1)} collective-permute-done((bf16[96,768]{1,0:T(8,128)(2,1)S(1)}, bf16[96,768]{1,0:T(8,128)(2,1)S(1)}, u32[]{:S(2)}, u32[]{:S(2)}) %collective-permute-start.5) | collective-permute-done | bytes 147488 | tf_op jit(solution)/shard_map/ppermute | solution.py:167
  48.3 6.3 %collective-permute-done.10.refs_1_ = bf16[96,768]{1,0:T(8,128)(2,1)S(1)} collective-permute-done((bf16[96,768]{1,0:T(8,128)(2,1)S(1)}, bf16[96,768]{1,0:T(8,128)(2,1)S(1)}, u32[]{:S(2)}, u32[]{:S(2)}) %collective-permute-start.10) | collective-permute-done | bytes 147488 | tf_op jit(solution)/shard_map/ppermute | solution.py:167
  55.8 6.2 %collective-permute-done.11.refs_2_ = bf16[96,768]{1,0:T(8,128)(2,1)S(1)} collective-permute-done((bf16[96,768]{1,0:T(8,128)(2,1)S(1)}, bf16[96,768]{1,0:T(8,128)(2,1)S(1)}, u32[]{:S(2)}, u32[]{:S(2)}) %collective-permute-start.11) | collective-permute-done | bytes 147488 | tf_op jit(solution)/shard_map/ppermute | solution.py:167
  62.3 3.8 %collective-permute-done.7.refs_1_ = bf16[2,4,96,768]{3,2,1,0:T(8,128)(2,1)} collective-permute-done((bf16[2,4,96,768]{3,2,1,0:T(8,128)(2,1)}, bf16[2,4,96,768]{3,2,1,0:T(8,128)(2,1)}, u32[]{:S(2)}, u32[]{:S(2)}) %collective-permute-start.7) | collective-permute-done | bytes 1179680 | tf_op jit(solution)/shard_map/ppermute | solution.py:167
  71.5 19.7 %shard_map.478 = (bf16[4,3,832,192]{3,2,1,0:T(8,128)(2,1)}, bf16[4,832,192]{2,1,0:T(8,128)(2,1)}, f32[832,768]{1,0:T(8,128)}, bf16[832,768]{1,0:T(8,128)(2,1)S(1)}, f32[8,768]{1,0:T(8,128)S(1)}) custom-call(s32[8]{0:T(128)S(1)} %copy-done.25, bf16[2,4,96,768]{3,2,1,0:T(8,128)(2,1)} %pad_maximum_fusion.refs_0_, ...), custom_call_target="tpu_custom_call" | custom-call | flops 3925868544 | bytes 16000000 | tf_op jit(solution)/shard_map/pallas_call | solution.py:1335
  94.5 12.6 %shard_map.479 = (f32[4,8,768]{2,1,0:T(8,128)S(1)}, bf16[4,832,768]{2,1,0:T(8,128)(2,1)}) custom-call(s32[8]{0:T(128)S(1)} %copy-done.25, bf16[2,4,96,768]{3,2,1,0:T(8,128)(2,1)} %pad_maximum_fusion.1.refs_0_, bf16[2,4,96,768]{3,2,1,0:T(8,128)(2,1)} %collective-permute-done.13.refs_1_, bf16[2,4,96,768]{3,2,1,0:T(8,128)(2,1)} %collective-permute-done.14.refs_2_, ...), custom_call_target="tpu_custom_call" | custom-call | flops 3925868544 | bytes 16000000 | tf_op jit(solution)/shard_map/pallas_call | solution.py:1335
  110.7 17.9 %shard_map.480 = (bf16[32,896]{1,0:T(8,128)(2,1)S(1)}, f32[8,768]{1,0:T(8,128)S(1)}, f32[4,8,768]{2,1,0:T(8,128)S(1)}) custom-call(s32[8]{0:T(128)S(1)} %copy-done.25, f32[4,8,768]{2,1,0:T(8,128)S(1)} %get-tuple-element.251.active_ref, f32[8,768]{1,0:T(8,128)S(1)} %get-tuple-element.252.sum_ref, f32[8,128]{1,0:T(8,128)S(1)} %get-tuple-element.253.facts_ref, ...), custom_call_target="tpu_custom_call" | custom-call | bytes 16000000 | tf_op jit(solution)/shard_map/pallas_call | solution.py:1335
  131.7 18.2 %shard_map.481 = (bf16[2,768,768]{2,1,0:T(8,128)(2,1)}, bf16[2,768,768]{2,1,0:T(8,128)(2,1)}, f32[4,1,768]{2,1,0:T(1,128)S(1)}, f32[832,768]{1,0:T(8,128)}) custom-call(s32[8]{0:T(128)S(1)} %copy-done.25, bf16[2,4,96,768]{3,2,1,0:T(8,128)(2,1)} %pad_maximum_fusion.1.refs_0_, bf16[2,4,96,768]{3,2,1,0:T(8,128)(2,1)} %collective-permute-done.13.refs_1_, ...), custom_call_target="tpu_custom_call" | custom-call | flops 7851737088 | bytes 16000000 | tf_op jit(solution)/shard_map/pallas_call | solution.py:1335
  153.4 5.4 %shard_map.483 = (f32[832,768]{1,0:T(8,128)S(1)}, bf16[832,768]{1,0:T(8,128)(2,1)S(1)}, f32[8,768]{1,0:T(8,128)S(1)}) custom-call(s32[8]{0:T(128)S(1)} %copy-done.26, f32[832,768]{1,0:T(8,128)} %get-tuple-element.268.d_rows_ref, f32[8,768]{1,0:T(8,128)S(1)} %get-tuple-element.269.d_row_ref, f32[4,208]{1,0:T(4,128)S(1)} %get-tuple-element.236.refs_6_.present_ref.refs_7_, ...), custom_call_target="tpu_custom_call" | custom-call | bytes 16000000 | tf_op jit(solution)/shard_map/pallas_call | solution.py:1335
  164.7 18.5 %shard_map.484 = (bf16[2,768,768]{2,1,0:T(8,128)(2,1)}, f32[2,8,192]{2,1,0:T(8,128)S(1)}, f32[832,768]{1,0:T(8,128)}) custom-call(s32[8]{0:T(128)S(1)} %copy-done.26, bf16[2,4,96,768]{3,2,1,0:T(8,128)(2,1)} %pad_maximum_fusion.refs_0_, bf16[2,4,96,768]{3,2,1,0:T(8,128)(2,1)} %collective-permute-done.7.refs_1_, ...), custom_call_target="tpu_custom_call" | custom-call | flops 3925868544 | bytes 16000000 | tf_op jit(solution)/shard_map/pallas_call | solution.py:1335
  187.5 19.8 %shard_map.485 = (bf16[2,768,768]{2,1,0:T(8,128)(2,1)}, f32[2,8,192]{2,1,0:T(8,128)S(1)}, f32[832,768]{1,0:T(8,128)}) custom-call(s32[8]{0:T(128)S(1)} %copy-done.26, bf16[2,4,96,768]{3,2,1,0:T(8,128)(2,1)} %pad_maximum_fusion.refs_0_, bf16[2,4,96,768]{3,2,1,0:T(8,128)(2,1)} %collective-permute-done.7.refs_1_, ...), custom_call_target="tpu_custom_call" | custom-call | flops 3925868544 | bytes 16000000 | tf_op jit(solution)/shard_map/pallas_call | solution.py:1335
  220.4 7.2 %shard_map.486 = (bf16[4,128,768]{2,1,0:T(8,128)(2,1)}, bf16[4,128,768]{2,1,0:T(8,128)(2,1)S(1)}, f32[216,768]{1,0:T(8,128)S(1)}) custom-call(s32[8]{0:T(128)S(1)} %copy-done.26, f32[832,768]{1,0:T(8,128)S(1)} %copy-done.10, f32[832,768]{1,0:T(8,128)} %copy-done.9, f32[832,768]{1,0:T(8,128)} %get-tuple-element.237.refs_7_.stream_ref, ...), custom_call_target="tpu_custom_call" | custom-call | flops 981467136 | bytes 16000000 | tf_op jit(solution)/shard_map/pallas_call | solution.py:1335
  236.9 3.5 %shard_map.487 = bf16[4,4,2,32,896]{4,3,2,1,0:T(8,128)(2,1)} custom-call(s32[8]{0:T(128)} %stack.43.place_ref, bf16[2,4,32,896]{3,2,1,0:T(8,128)(2,1)} %copy-done.51, bf16[2,4,32,896]{3,2,1,0:T(8,128)(2,1)} %copy-done.54, bf16[2,4,32,896]{3,2,1,0:T(8,128)(2,1)} %copy-done.56, bf16[2,4,32,896]{3,2,1,0:T(8,128)(2,1)} %copy-done.57), custom_call_target="tpu_custom_call" | custom-call | tf_op jit(solution)/shard_map/pallas_call | solution.py:198
  240.4 5.2 %collective-permute-done.36 = bf16[4,96,768]{2,1,0:T(8,128)(2,1)} collective-permute-done((bf16[4,96,768]{2,1,0:T(8,128)(2,1)}, bf16[4,96,768]{2,1,0:T(8,128)(2,1)}, u32[]{:S(2)}, u32[]{:S(2)}) %collective-permute-start.36) | collective-permute-done | bytes 589856 | tf_op jit(solution)/shard_map/ppermute | solution.py:167
  255.8 5.3 %shard_map.488 = (f32[1000,768]{1,0:T(8,128)}, f32[96,768]{1,0:T(8,128)S(1)}, f32[8,768]{1,0:T(8,128)S(1)}, f32[8,1000]{1,0:T(8,128)S(1)}) custom-call(s32[8]{0:T(128)S(1)} %copy-done.27, bf16[1,32,32,896]{3,2,1,0:T(8,128)(2,1)S(1)} %bitcast.120, f32[24,768]{1,0:T(8,128)S(1)} %copy-done.8, bf16[1000,768]{1,0:T(8,128)(2,1)S(1)} %copy-done), custom_call_target="tpu_custom_call" | custom-call | bytes 16000000 | tf_op jit(solution)/shard_map/pallas_call | solution.py:1335
  261.0 3.9 %collective-permute-done.40 = bf16[96,768]{1,0:T(8,128)(2,1)S(1)} collective-permute-done((bf16[96,768]{1,0:T(8,128)(2,1)S(1)}, bf16[96,768]{1,0:T(8,128)(2,1)S(1)}, u32[]{:S(2)}, u32[]{:S(2)}) %collective-permute-start.40) | collective-permute-done | bytes 147488 | tf_op jit(solution)/shard_map/ppermute | solution.py:167
  267.2 3.7 %collective-permute-start.45 = (bf16[1,128,768]{2,1,0:T(8,128)(2,1)S(1)}, bf16[1,128,768]{2,1,0:T(8,128)(2,1)S(1)}, u32[]{:S(2)}, u32[]{:S(2)}) collective-permute-start(bf16[1,128,768]{2,1,0:T(8,128)(2,1)S(1)} %add_convert_fusion.7), channel_id=1, source_target_pairs={{0,8},{1,9},{2,10},{3,11},{4,12},{5,13},{6,14},{7,15},{8,0},{9,1},... | collective-permute-start | bytes 589832 | tf_op jit(solution)/shard_map/ppermute | solution.py:167
  272.3 4.1 %collective-permute-done.45 = bf16[1,128,768]{2,1,0:T(8,128)(2,1)S(1)} collective-permute-done((bf16[1,128,768]{2,1,0:T(8,128)(2,1)S(1)}, bf16[1,128,768]{2,1,0:T(8,128)(2,1)S(1)}, u32[]{:S(2)}, u32[]{:S(2)}) %collective-permute-start.45) | collective-permute-done | bytes 196640 | tf_op jit(solution)/shard_map/ppermute | solution.py:167
  283.0 5.0 %shard_map.490 = (f32[1000,768]{1,0:T(8,128)}, f32[768]{0:T(1024)}, f32[1000]{0:T(1024)}) custom-call(s32[8]{0:T(128)S(1)} %copy-done.27, f32[1000,768]{1,0:T(8,128)S(1)} %bitcast.117, f32[1000,768]{1,0:T(8,128)S(1)} %copy-done.7, f32[768]{0:T(1024)S(1)} %copy-done.33, f32[1000]{0:T(1024)S(1)} %copy-done.34), custom_call_target="tpu_custom_call" | custom-call | bytes 16000000 | tf_op jit(solution)/shard_map/pallas_call | solution.py:1335
  291.2 5.5 %collective-permute-done.49 = f32[32,768]{1,0:T(8,128)S(1)} collective-permute-done((f32[32,768]{1,0:T(8,128)S(1)}, f32[32,768]{1,0:T(8,128)S(1)}, u32[]{:S(2)}, u32[]{:S(2)}) %collective-permute-start.49) | collective-permute-done | bytes 98336 | tf_op jit(solution)/shard_map/ppermute | solution.py:167
  308.8 4.4 %shard_map.492 = (f32[768,768]{1,0:T(8,128)}, f32[768]{0:T(1024)}, f32[768]{0:T(1024)}, f32[197,768]{1,0:T(8,128)}, f32[197]{0:T(256)}, /*index=5*/f32[768]{0:T(1024)}) custom-call(s32[8]{0:T(128)S(1)} %copy-done.27, bf16[4,128,768]{2,1,0:T(8,128)(2,1)S(1)} %pad_maximum_fusion.5.near_ref, bf16[4,128,768]{2,1,0:T(8,128)(2,1)S(1)} %collective-permute-done.55.far_ref, ...), custom_call_target="tpu_custom_call" | custom-call | bytes 16000000 | tf_op jit(solution)/shard_map/pallas_call | solution.py:1335
  (296 shorter events, 120.2 us)
Async XLA Ops:
  24.7 16.7 %collective-permute-start.3 = (bf16[1,4,96,768]{3,2,1,0:T(8,128)(2,1)}, bf16[1,4,96,768]{3,2,1,0:T(8,128)(2,1)S(1)}, u32[]{:S(2)}, u32[]{:S(2)}) collective-permute-start(bf16[1,4,96,768]{3,2,1,0:T(8,128)(2,1)} %shard_map.474), channel_id=1, source_target_pairs={{0,4},{1,3},{2,6},{3,1},{4,0},{5,7},{6,2},{7,5},{8,12},{9,11},{10,... | collective-permute-start | bytes 1769480 | tf_op jit(solution)/shard_map/ppermute | solution.py:167
  27.6 13.8 %collective-permute-start.5 = (bf16[96,768]{1,0:T(8,128)(2,1)S(1)}, bf16[96,768]{1,0:T(8,128)(2,1)S(1)}, u32[]{:S(2)}, u32[]{:S(2)}) collective-permute-start(bf16[96,768]{1,0:T(8,128)(2,1)S(1)} %copy-done.59), channel_id=1, source_target_pairs={{0,16},{1,17},{2,18},{3,19},{4,20},{5,21},{6,22},{7,23},{8,24},{9,... | collective-permute-start | bytes 442376 | tf_op jit(solution)/shard_map/ppermute | solution.py:167
  43.2 22.8 %collective-permute-start.7 = (bf16[2,4,96,768]{3,2,1,0:T(8,128)(2,1)}, bf16[2,4,96,768]{3,2,1,0:T(8,128)(2,1)}, u32[]{:S(2)}, u32[]{:S(2)}) collective-permute-start(bf16[2,4,96,768]{3,2,1,0:T(8,128)(2,1)} %pad_maximum_fusion.refs_0_), channel_id=1, source_target_pairs={{0,2},{1,5},{2,0},{3,7},{4,6},{5,1},{6,4},{7,3},{8,10},{9,13},{10,... | collective-permute-start | bytes 3538952 | tf_op jit(solution)/shard_map/ppermute | solution.py:167
  43.7 22.3 %collective-permute-start.8 = (bf16[2,4,96,768]{3,2,1,0:T(8,128)(2,1)}, bf16[2,4,96,768]{3,2,1,0:T(8,128)(2,1)}, u32[]{:S(2)}, u32[]{:S(2)}) collective-permute-start(bf16[2,4,96,768]{3,2,1,0:T(8,128)(2,1)} %pad_maximum_fusion.refs_0_), channel_id=1, source_target_pairs={{0,1},{1,0},{2,3},{3,2},{4,5},{5,4},{6,7},{7,6},{8,9},{9,8},{10,11... | collective-permute-start | bytes 3538952 | tf_op jit(solution)/shard_map/ppermute | solution.py:167
  45.8 16.5 %collective-permute-start.9 = (bf16[1,4,96,768]{3,2,1,0:T(8,128)(2,1)}, bf16[1,4,96,768]{3,2,1,0:T(8,128)(2,1)S(1)}, u32[]{:S(2)}, u32[]{:S(2)}) collective-permute-start(bf16[1,4,96,768]{3,2,1,0:T(8,128)(2,1)} %shard_map.476), channel_id=1, source_target_pairs={{0,4},{1,3},{2,6},{3,1},{4,0},{5,7},{6,2},{7,5},{8,12},{9,11},{10,... | collective-permute-start | bytes 1769480 | tf_op jit(solution)/shard_map/ppermute | solution.py:167
  47.2 14.8 %collective-permute-start.11 = (bf16[96,768]{1,0:T(8,128)(2,1)S(1)}, bf16[96,768]{1,0:T(8,128)(2,1)S(1)}, u32[]{:S(2)}, u32[]{:S(2)}) collective-permute-start(bf16[96,768]{1,0:T(8,128)(2,1)S(1)} %copy-done.58), channel_id=1, source_target_pairs={{0,16},{1,17},{2,18},{3,19},{4,20},{5,21},{6,22},{7,23},{8,24},{9,... | collective-permute-start | bytes 442376 | tf_op jit(solution)/shard_map/ppermute | solution.py:167
  67.3 24.0 %collective-permute-start.13 = (bf16[2,4,96,768]{3,2,1,0:T(8,128)(2,1)}, bf16[2,4,96,768]{3,2,1,0:T(8,128)(2,1)}, u32[]{:S(2)}, u32[]{:S(2)}) collective-permute-start(bf16[2,4,96,768]{3,2,1,0:T(8,128)(2,1)} %pad_maximum_fusion.1.refs_0_), channel_id=1, source_target_pairs={{0,2},{1,5},{2,0},{3,7},{4,6},{5,1},{6,4},{7,3},{8,10},{9,13},{10,... | collective-permute-start | bytes 3538952 | tf_op jit(solution)/shard_map/ppermute | solution.py:167
  67.8 23.5 %collective-permute-start.14 = (bf16[2,4,96,768]{3,2,1,0:T(8,128)(2,1)}, bf16[2,4,96,768]{3,2,1,0:T(8,128)(2,1)}, u32[]{:S(2)}, u32[]{:S(2)}) collective-permute-start(bf16[2,4,96,768]{3,2,1,0:T(8,128)(2,1)} %pad_maximum_fusion.1.refs_0_), channel_id=1, source_target_pairs={{0,1},{1,0},{2,3},{3,2},{4,5},{5,4},{6,7},{7,6},{8,9},{9,8},{10,11... | collective-permute-start | bytes 3538952 | tf_op jit(solution)/shard_map/ppermute | solution.py:167
  71.0 20.3 %collective-permute-start.15 = (bf16[1,4,96,768]{3,2,1,0:T(8,128)(2,1)}, bf16[1,4,96,768]{3,2,1,0:T(8,128)(2,1)S(1)}, u32[]{:S(2)}, u32[]{:S(2)}) collective-permute-start(bf16[1,4,96,768]{3,2,1,0:T(8,128)(2,1)} %shard_map.477), channel_id=1, source_target_pairs={{0,4},{1,3},{2,6},{3,1},{4,0},{5,7},{6,2},{7,5},{8,12},{9,11},{10,... | collective-permute-start | bytes 1769480 | tf_op jit(solution)/shard_map/ppermute | solution.py:167
  91.5 16.3 %collective-permute-start.17 = (bf16[2,4,96,768]{3,2,1,0:T(8,128)(2,1)S(1)}, bf16[2,4,96,768]{3,2,1,0:T(8,128)(2,1)S(1)}, u32[]{:S(2)}, u32[]{:S(2)}) collective-permute-start(bf16[2,4,96,768]{3,2,1,0:T(8,128)(2,1)S(1)} %pad_maximum_fusion.2.refs_0_), channel_id=1, source_target_pairs={{0,2},{1,5},{2,0},{3,7},{4,6},{5,1},{6,4},{7,3},{8,10},{9,13},{10,... | collective-permute-start | bytes 3538952 | tf_op jit(solution)/shard_map/ppermute | solution.py:167
  92.9 14.9 %collective-permute-start.18 = (bf16[2,4,96,768]{3,2,1,0:T(8,128)(2,1)S(1)}, bf16[2,4,96,768]{3,2,1,0:T(8,128)(2,1)S(1)}, u32[]{:S(2)}, u32[]{:S(2)}) collective-permute-start(bf16[2,4,96,768]{3,2,1,0:T(8,128)(2,1)S(1)} %pad_maximum_fusion.2.refs_0_), channel_id=1, source_target_pairs={{0,1},{1,0},{2,3},{3,2},{4,5},{5,4},{6,7},{7,6},{8,9},{9,8},{10,11... | collective-permute-start | bytes 3538952 | tf_op jit(solution)/shard_map/ppermute | solution.py:167
  128.6 21.3 %collective-permute-start.21 = (bf16[32,896]{1,0:T(8,128)(2,1)S(1)}, bf16[32,896]{1,0:T(8,128)(2,1)S(1)}, u32[]{:S(2)}, u32[]{:S(2)}) collective-permute-start(bf16[32,896]{1,0:T(8,128)(2,1)S(1)} %get-tuple-element.257.refs_0_), channel_id=1, source_target_pairs={{0,24},{1,25},{2,26},{3,27},{4,28},{5,29},{6,30},{7,31},{8,0},{9,1... | collective-permute-start | bytes 172040 | tf_op jit(solution)/shard_map/ppermute | solution.py:167
  128.6 21.3 %collective-permute-start.22 = (bf16[32,896]{1,0:T(8,128)(2,1)S(1)}, bf16[32,896]{1,0:T(8,128)(2,1)S(1)}, u32[]{:S(2)}, u32[]{:S(2)}) collective-permute-start(bf16[32,896]{1,0:T(8,128)(2,1)S(1)} %get-tuple-element.257.refs_0_), channel_id=1, source_target_pairs={{0,16},{1,17},{2,18},{3,19},{4,20},{5,21},{6,22},{7,23},{8,24},{9,... | collective-permute-start | bytes 172040 | tf_op jit(solution)/shard_map/ppermute | solution.py:167
  129.7 20.2 %collective-permute-start.23 = (bf16[32,896]{1,0:T(8,128)(2,1)S(1)}, bf16[32,896]{1,0:T(8,128)(2,1)S(1)}, u32[]{:S(2)}, u32[]{:S(2)}) collective-permute-start(bf16[32,896]{1,0:T(8,128)(2,1)S(1)} %get-tuple-element.257.refs_0_), channel_id=1, source_target_pairs={{0,8},{1,9},{2,10},{3,11},{4,12},{5,13},{6,14},{7,15},{8,16},{9,17... | collective-permute-start | bytes 172040 | tf_op jit(solution)/shard_map/ppermute | solution.py:167
  162.5 21.2 %collective-permute-start.28 = (bf16[2,4,96,768]{3,2,1,0:T(8,128)(2,1)S(1)}, bf16[2,4,96,768]{3,2,1,0:T(8,128)(2,1)}, u32[]{:S(2)}, u32[]{:S(2)}) collective-permute-start(bf16[2,4,96,768]{3,2,1,0:T(8,128)(2,1)S(1)} %pad_maximum_fusion.3), channel_id=1, source_target_pairs={{0,2},{1,5},{2,0},{3,7},{4,6},{5,1},{6,4},{7,3},{8,10},{9,13},{10,... | collective-permute-start | bytes 3538952 | tf_op jit(solution)/shard_map/ppermute | solution.py:167
  163.4 20.2 %collective-permute-start.26 = (bf16[2,4,32,896]{3,2,1,0:T(8,128)(2,1)S(1)}, bf16[2,4,32,896]{3,2,1,0:T(8,128)(2,1)S(1)}, u32[]{:S(2)}, u32[]{:S(2)}) collective-permute-start(bf16[2,4,32,896]{3,2,1,0:T(8,128)(2,1)S(1)} %pad_maximum_fusion.6.refs_0_), channel_id=1, source_target_pairs={{0,2},{1,5},{2,0},{3,7},{4,6},{5,1},{6,4},{7,3},{8,10},{9,13},{10,... | collective-permute-start | bytes 1376264 | tf_op jit(solution)/shard_map/ppermute | solution.py:167
  164.7 19.0 %collective-permute-start.27 = (bf16[2,4,32,896]{3,2,1,0:T(8,128)(2,1)S(1)}, bf16[2,4,32,896]{3,2,1,0:T(8,128)(2,1)S(1)}, u32[]{:S(2)}, u32[]{:S(2)}) collective-permute-start(bf16[2,4,32,896]{3,2,1,0:T(8,128)(2,1)S(1)} %pad_maximum_fusion.6.refs_0_), channel_id=1, source_target_pairs={{0,1},{1,0},{2,3},{3,2},{4,5},{5,4},{6,7},{7,6},{8,9},{9,8},{10,11... | collective-permute-start | bytes 1376264 | tf_op jit(solution)/shard_map/ppermute | solution.py:167
  184.6 22.8 %collective-permute-start.31 = (bf16[2,768,768]{2,1,0:T(8,128)(2,1)}, bf16[2,768,768]{2,1,0:T(8,128)(2,1)}, u32[]{:S(2)}, u32[]{:S(2)}) collective-permute-start(bf16[2,768,768]{2,1,0:T(8,128)(2,1)} %get-tuple-element.283), channel_id=1, source_target_pairs={{0,1},{1,0},{2,3},{3,2},{4,5},{5,4},{6,7},{7,6},{8,9},{9,8},{10,11... | collective-permute-start | bytes 7077896 | tf_op jit(solution)/shard_map/ppermute | solution.py:167
  186.5 20.9 %collective-permute-start.30 = (bf16[4,96,768]{2,1,0:T(8,128)(2,1)S(1)}, bf16[4,96,768]{2,1,0:T(8,128)(2,1)S(1)}, u32[]{:S(2)}, u32[]{:S(2)}) collective-permute-start(bf16[4,96,768]{2,1,0:T(8,128)(2,1)S(1)} %fusion.3), channel_id=1, source_target_pairs={{0,4},{1,3},{2,6},{3,1},{4,0},{5,7},{6,2},{7,5},{8,12},{9,11},{10,... | collective-permute-start | bytes 1769480 | tf_op jit(solution)/shard_map/ppermute | solution.py:167
  187.4 20.0 %collective-permute-start.29 = (bf16[2,4,32,896]{3,2,1,0:T(8,128)(2,1)S(1)}, bf16[2,4,32,896]{3,2,1,0:T(8,128)(2,1)S(1)}, u32[]{:S(2)}, u32[]{:S(2)}) collective-permute-start(bf16[2,4,32,896]{3,2,1,0:T(8,128)(2,1)S(1)} %copy-done.55), channel_id=1, source_target_pairs={{0,1},{1,0},{2,3},{3,2},{4,5},{5,4},{6,7},{7,6},{8,9},{9,8},{10,11... | collective-permute-start | bytes 1376264 | tf_op jit(solution)/shard_map/ppermute | solution.py:167
  210.8 18.6 %collective-permute-start.32 = (bf16[2,4,96,768]{3,2,1,0:T(8,128)(2,1)}, bf16[2,4,96,768]{3,2,1,0:T(8,128)(2,1)}, u32[]{:S(2)}, u32[]{:S(2)}) collective-permute-start(bf16[2,4,96,768]{3,2,1,0:T(8,128)(2,1)} %pad_maximum_fusion.4), channel_id=1, source_target_pairs={{0,2},{1,5},{2,0},{3,7},{4,6},{5,1},{6,4},{7,3},{8,10},{9,13},{10,... | collective-permute-start | bytes 3538952 | tf_op jit(solution)/shard_map/ppermute | solution.py:167
  215.2 14.2 %collective-permute-start.33 = (bf16[96,768]{1,0:T(8,128)(2,1)S(1)}, bf16[96,768]{1,0:T(8,128)(2,1)S(1)}, u32[]{:S(2)}, u32[]{:S(2)}) collective-permute-start(bf16[96,768]{1,0:T(8,128)(2,1)S(1)} %get-tuple-element.398), channel_id=1, source_target_pairs={{0,8},{1,9},{2,10},{3,11},{4,12},{5,13},{6,14},{7,15},{8,16},{9,17... | collective-permute-start | bytes 442376 | tf_op jit(solution)/shard_map/ppermute | solution.py:167
  232.0 13.6 %collective-permute-start.36 = (bf16[4,96,768]{2,1,0:T(8,128)(2,1)}, bf16[4,96,768]{2,1,0:T(8,128)(2,1)}, u32[]{:S(2)}, u32[]{:S(2)}) collective-permute-start(bf16[4,96,768]{2,1,0:T(8,128)(2,1)} %fusion.1), channel_id=1, source_target_pairs={{0,4},{1,3},{2,6},{3,1},{4,0},{5,7},{6,2},{7,5},{8,12},{9,11},{10,... | collective-permute-start | bytes 1769480 | tf_op jit(solution)/shard_map/ppermute | solution.py:167
  247.1 17.9 %collective-permute-start.42 = (bf16[1,128,768]{2,1,0:T(8,128)(2,1)S(1)}, bf16[1,128,768]{2,1,0:T(8,128)(2,1)S(1)}, u32[]{:S(2)}, u32[]{:S(2)}) collective-permute-start(bf16[1,128,768]{2,1,0:T(8,128)(2,1)S(1)} %add_convert_fusion.8), channel_id=1, source_target_pairs={{0,4},{1,3},{2,6},{3,1},{4,0},{5,7},{6,2},{7,5},{8,12},{9,11},{10,... | collective-permute-start | bytes 589832 | tf_op jit(solution)/shard_map/ppermute | solution.py:167
  (106 other events, 887.7 us)

commit v5 on v4

--- a/solution.py
+++ b/solution.py
@@ -1612,7 +1612,8 @@
     both_sum = Chain(links.add_large(both_far, both_near))
     pieces, grad_expand, _ = sync([both_sum], pieces, grad_expand, attend_sum.sent)
     pieces = links.whole(*pieces).reshape((-1,) + piece.shape)
-    pieces, grad_expand = sync([attend_sum, both_sum], pieces, grad_expand)
+    pieces, grad_expand = sync([attend_sum], pieces, grad_expand)
+    pieces, grad_expand, _ = sync([both_sum], pieces, grad_expand, attend_sum.sent)
     steps = max(1, pieces.shape[0] // 32)
     grad_head, grad_contract, vector_last, vector_head = call(
         functools.partial(all_head_kernel, inverse_count=inverse_count),
@@ -1631,7 +1632,7 @@
         ),
     )
     loss_sum = vector_head[1, 0]
-    grad_expand, grad_contract = sync([attend_sum, both_sum], grad_expand, grad_contract)
+    grad_expand, grad_contract = sync([attend_sum], grad_expand, grad_contract)
     grad_attend = attend_sum.result
 
     names = dict(data=data_size, groups=groups, share=head_share)
@@ -1657,7 +1658,7 @@
         (((lines, D), f32, False),),
     )
     sums_chain = Chain(links.add(sums))
-    sync([sums_chain])
+    sync([sums_chain, both_sum])
     sync([sums_chain, both_sum])
     head_new, head_rows_new, head_cols_new = call(
         head_step_kernel,

time: 324 us -> 320 us (0.988)
    unnamed x145 -> x147, local copies, waits for them, and re-layouts: 9.08 us -> 7.33 us
  transfers between devices with their start and end apart: 58 -> 58, of which waited for: 21 -> 25; matrix products, arithmetic and copies ran while one was open for 6% -> 5% of each run, Pallas kernels for 41% -> 42%
where the time goes in v5:
time: 320 us; the launch traced here: 316 us
  Pallas kernels  158 us (49%)
  waiting for transfers between devices  66.5 us (21%)
  starting transfers between devices  57.4 us (18%)
  other arithmetic  23.9 us (7%)
  local copies, waits for them, and re-layouts  8.6 us (3%)
    pallas_call x17, Pallas kernels, call(): pl.pallas_call(kernel, grid_spec=pltpu.PrefetchScalarGridSpec(num_scalar_...  147 us
    ppermute x58, waiting for transfers between devices, send(): return lax.ppermute(values, ALL, table)  66.5 us
    ppermute x58, starting transfers between devices, send(): return lax.ppermute(values, ALL, table)  57.4 us
    pallas_call x4, Pallas kernels, gather(): pl.pallas_call(column_kernel, in_specs=[pl.BlockSpec(memory_space=pltpu.S...  7.6 us
    unnamed x147, local copies, waits for them, and re-layouts  7.33 us
  transfers between devices with their start and end apart: 58, of which 25 were waited for; matrix products, arithmetic and copies ran while one was open for 5% of the time, Pallas kernels for 42%

profile of v5, /device:TPU:0, one launch (start us, length us, event | category | flops | bytes accessed | tf_op | source)
XLA Modules:
  0.0 316.1 jit_solution(5510790544540568337)
XLA Ops:
  4.2 5.0 %collective-permute-start = (bf16[96,768]{1,0:T(8,128)(2,1)}, bf16[96,768]{1,0:T(8,128)(2,1)S(1)}, u32[]{:S(2)}, u32[]{:S(2)}) collective-permute-start(bf16[96,768]{1,0:T(8,128)(2,1)} %get-tuple-element.210.refs_0_), channel_id=1, source_target_pairs={{0,24},{1,25},{2,26},{3,27},{4,28},{5,29},{6,30},{7,31},{8,0},{9,1... | collective-permute-start | bytes 442376 | tf_op jit(solution)/shard_map/ppermute | solution.py:167
  13.9 8.1 %collective-permute-done.1.refs_2_ = bf16[96,768]{1,0:T(8,128)(2,1)S(1)} collective-permute-done((bf16[96,768]{1,0:T(8,128)(2,1)}, bf16[96,768]{1,0:T(8,128)(2,1)S(1)}, u32[]{:S(2)}, u32[]{:S(2)}) %collective-permute-start.1) | collective-permute-done | bytes 147488 | tf_op jit(solution)/shard_map/ppermute | solution.py:167
  32.6 4.0 %shard_map.475 = (f32[832,768]{1,0:T(8,128)}, bf16[832,768]{1,0:T(8,128)(2,1)S(1)}, f32[4,208]{1,0:T(4,128)S(1)}, f32[8,128]{1,0:T(8,128)S(1)}) custom-call(s32[8]{0:T(128)S(1)} %copy-done.24, s32[4]{0:T(128)S(1)} %copy-done.45, bf16[832,768]{1,0:T(8,128)(2,1)S(1)} %bitcast.118, f32[768,768]{1,0:T(8,128)S(1)} %copy-done.4, f32[197,768]{1,0:T(8,128)S(1)} %copy-done.11, ...), custom_call_target="tpu_custom_call" | custom-call | flops 981467136 | bytes 16000000 | tf_op jit(solution)/shard_map/pallas_call | solution.py:1335
  36.6 4.7 %collective-permute-done.5.refs_2_ = bf16[96,768]{1,0:T(8,128)(2,1)S(1)} collective-permute-done((bf16[96,768]{1,0:T(8,128)(2,1)S(1)}, bf16[96,768]{1,0:T(8,128)(2,1)S(1)}, u32[]{:S(2)}, u32[]{:S(2)}) %collective-permute-start.5) | collective-permute-done | bytes 147488 | tf_op jit(solution)/shard_map/ppermute | solution.py:167
  48.4 6.3 %collective-permute-done.10.refs_1_ = bf16[96,768]{1,0:T(8,128)(2,1)S(1)} collective-permute-done((bf16[96,768]{1,0:T(8,128)(2,1)S(1)}, bf16[96,768]{1,0:T(8,128)(2,1)S(1)}, u32[]{:S(2)}, u32[]{:S(2)}) %collective-permute-start.10) | collective-permute-done | bytes 147488 | tf_op jit(solution)/shard_map/ppermute | solution.py:167
  55.9 6.2 %collective-permute-done.11.refs_2_ = bf16[96,768]{1,0:T(8,128)(2,1)S(1)} collective-permute-done((bf16[96,768]{1,0:T(8,128)(2,1)S(1)}, bf16[96,768]{1,0:T(8,128)(2,1)S(1)}, u32[]{:S(2)}, u32[]{:S(2)}) %collective-permute-start.11) | collective-permute-done | bytes 147488 | tf_op jit(solution)/shard_map/ppermute | solution.py:167
  62.4 3.8 %collective-permute-done.7.refs_1_ = bf16[2,4,96,768]{3,2,1,0:T(8,128)(2,1)} collective-permute-done((bf16[2,4,96,768]{3,2,1,0:T(8,128)(2,1)}, bf16[2,4,96,768]{3,2,1,0:T(8,128)(2,1)}, u32[]{:S(2)}, u32[]{:S(2)}) %collective-permute-start.7) | collective-permute-done | bytes 1179680 | tf_op jit(solution)/shard_map/ppermute | solution.py:167
  71.6 19.7 %shard_map.478 = (bf16[4,3,832,192]{3,2,1,0:T(8,128)(2,1)}, bf16[4,832,192]{2,1,0:T(8,128)(2,1)}, f32[832,768]{1,0:T(8,128)}, bf16[832,768]{1,0:T(8,128)(2,1)S(1)}, f32[8,768]{1,0:T(8,128)S(1)}) custom-call(s32[8]{0:T(128)S(1)} %copy-done.25, bf16[2,4,96,768]{3,2,1,0:T(8,128)(2,1)} %pad_maximum_fusion.refs_0_, ...), custom_call_target="tpu_custom_call" | custom-call | flops 3925868544 | bytes 16000000 | tf_op jit(solution)/shard_map/pallas_call | solution.py:1335
  94.5 12.6 %shard_map.479 = (f32[4,8,768]{2,1,0:T(8,128)S(1)}, bf16[4,832,768]{2,1,0:T(8,128)(2,1)}) custom-call(s32[8]{0:T(128)S(1)} %copy-done.25, bf16[2,4,96,768]{3,2,1,0:T(8,128)(2,1)} %pad_maximum_fusion.1.refs_0_, bf16[2,4,96,768]{3,2,1,0:T(8,128)(2,1)} %collective-permute-done.13.refs_1_, bf16[2,4,96,768]{3,2,1,0:T(8,128)(2,1)} %collective-permute-done.14.refs_2_, ...), custom_call_target="tpu_custom_call" | custom-call | flops 3925868544 | bytes 16000000 | tf_op jit(solution)/shard_map/pallas_call | solution.py:1335
  110.7 17.9 %shard_map.480 = (bf16[32,896]{1,0:T(8,128)(2,1)S(1)}, f32[8,768]{1,0:T(8,128)S(1)}, f32[4,8,768]{2,1,0:T(8,128)S(1)}) custom-call(s32[8]{0:T(128)S(1)} %copy-done.25, f32[4,8,768]{2,1,0:T(8,128)S(1)} %get-tuple-element.254.active_ref, f32[8,768]{1,0:T(8,128)S(1)} %get-tuple-element.255.sum_ref, f32[8,128]{1,0:T(8,128)S(1)} %get-tuple-element.256.facts_ref, ...), custom_call_target="tpu_custom_call" | custom-call | bytes 16000000 | tf_op jit(solution)/shard_map/pallas_call | solution.py:1335
  131.7 18.2 %shard_map.481 = (bf16[2,768,768]{2,1,0:T(8,128)(2,1)}, bf16[2,768,768]{2,1,0:T(8,128)(2,1)}, f32[4,1,768]{2,1,0:T(1,128)S(1)}, f32[832,768]{1,0:T(8,128)}) custom-call(s32[8]{0:T(128)S(1)} %copy-done.25, bf16[2,4,96,768]{3,2,1,0:T(8,128)(2,1)} %pad_maximum_fusion.1.refs_0_, bf16[2,4,96,768]{3,2,1,0:T(8,128)(2,1)} %collective-permute-done.13.refs_1_, ...), custom_call_target="tpu_custom_call" | custom-call | flops 7851737088 | bytes 16000000 | tf_op jit(solution)/shard_map/pallas_call | solution.py:1335
  153.4 5.4 %shard_map.483 = (f32[832,768]{1,0:T(8,128)S(1)}, bf16[832,768]{1,0:T(8,128)(2,1)S(1)}, f32[8,768]{1,0:T(8,128)S(1)}) custom-call(s32[8]{0:T(128)S(1)} %copy-done.26, f32[832,768]{1,0:T(8,128)} %get-tuple-element.271.d_rows_ref, f32[8,768]{1,0:T(8,128)S(1)} %get-tuple-element.272.d_row_ref, f32[4,208]{1,0:T(4,128)S(1)} %get-tuple-element.239.refs_6_.present_ref.refs_7_, ...), custom_call_target="tpu_custom_call" | custom-call | bytes 16000000 | tf_op jit(solution)/shard_map/pallas_call | solution.py:1335
  164.7 18.6 %shard_map.484 = (bf16[2,768,768]{2,1,0:T(8,128)(2,1)}, f32[2,8,192]{2,1,0:T(8,128)S(1)}, f32[832,768]{1,0:T(8,128)}) custom-call(s32[8]{0:T(128)S(1)} %copy-done.26, bf16[2,4,96,768]{3,2,1,0:T(8,128)(2,1)} %pad_maximum_fusion.refs_0_, bf16[2,4,96,768]{3,2,1,0:T(8,128)(2,1)} %collective-permute-done.7.refs_1_, ...), custom_call_target="tpu_custom_call" | custom-call | flops 3925868544 | bytes 16000000 | tf_op jit(solution)/shard_map/pallas_call | solution.py:1335
  187.5 19.8 %shard_map.485 = (bf16[2,768,768]{2,1,0:T(8,128)(2,1)}, f32[2,8,192]{2,1,0:T(8,128)S(1)}, f32[832,768]{1,0:T(8,128)}) custom-call(s32[8]{0:T(128)S(1)} %copy-done.26, bf16[2,4,96,768]{3,2,1,0:T(8,128)(2,1)} %pad_maximum_fusion.refs_0_, bf16[2,4,96,768]{3,2,1,0:T(8,128)(2,1)} %collective-permute-done.7.refs_1_, ...), custom_call_target="tpu_custom_call" | custom-call | flops 3925868544 | bytes 16000000 | tf_op jit(solution)/shard_map/pallas_call | solution.py:1335
  212.0 3.1 fusion.14
  220.3 7.2 %shard_map.486 = (bf16[4,128,768]{2,1,0:T(8,128)(2,1)}, bf16[4,128,768]{2,1,0:T(8,128)(2,1)S(1)}, f32[216,768]{1,0:T(8,128)S(1)}) custom-call(s32[8]{0:T(128)S(1)} %copy-done.26, f32[832,768]{1,0:T(8,128)S(1)} %copy-done.10, f32[832,768]{1,0:T(8,128)} %copy-done.9, f32[832,768]{1,0:T(8,128)} %get-tuple-element.240.refs_7_.stream_ref, ...), custom_call_target="tpu_custom_call" | custom-call | flops 981467136 | bytes 16000000 | tf_op jit(solution)/shard_map/pallas_call | solution.py:1335
  233.9 3.5 %shard_map.487 = bf16[4,4,2,32,896]{4,3,2,1,0:T(8,128)(2,1)} custom-call(s32[8]{0:T(128)} %stack.43.place_ref, bf16[2,4,32,896]{3,2,1,0:T(8,128)(2,1)} %copy-done.51, bf16[2,4,32,896]{3,2,1,0:T(8,128)(2,1)} %copy-done.54, bf16[2,4,32,896]{3,2,1,0:T(8,128)(2,1)} %copy-done.56, bf16[2,4,32,896]{3,2,1,0:T(8,128)(2,1)} %copy-done.57), custom_call_target="tpu_custom_call" | custom-call | tf_op jit(solution)/shard_map/pallas_call | solution.py:198
  237.5 4.7 %collective-permute-done.38 = bf16[4,96,768]{2,1,0:T(8,128)(2,1)} collective-permute-done((bf16[4,96,768]{2,1,0:T(8,128)(2,1)}, bf16[4,96,768]{2,1,0:T(8,128)(2,1)}, u32[]{:S(2)}, u32[]{:S(2)}) %collective-permute-start.38) | collective-permute-done | bytes 589856 | tf_op jit(solution)/shard_map/ppermute | solution.py:167
  246.3 3.2 %collective-permute-start.39 = (bf16[96,768]{1,0:T(8,128)(2,1)S(1)}, bf16[96,768]{1,0:T(8,128)(2,1)S(1)}, u32[]{:S(2)}, u32[]{:S(2)}) collective-permute-start(bf16[96,768]{1,0:T(8,128)(2,1)S(1)} %get-tuple-element.401), channel_id=1, source_target_pairs={{0,8},{1,9},{2,10},{3,11},{4,12},{5,13},{6,14},{7,15},{8,16},{9,17... | collective-permute-start | bytes 442376 | tf_op jit(solution)/shard_map/ppermute | solution.py:167
  252.2 5.3 %shard_map.488 = (f32[1000,768]{1,0:T(8,128)}, f32[96,768]{1,0:T(8,128)S(1)}, f32[8,768]{1,0:T(8,128)S(1)}, f32[8,1000]{1,0:T(8,128)S(1)}) custom-call(s32[8]{0:T(128)S(1)} %copy-done.27, bf16[1,32,32,896]{3,2,1,0:T(8,128)(2,1)S(1)} %bitcast.120, f32[24,768]{1,0:T(8,128)S(1)} %copy-done.8, bf16[1000,768]{1,0:T(8,128)(2,1)S(1)} %copy-done), custom_call_target="tpu_custom_call" | custom-call | bytes 16000000 | tf_op jit(solution)/shard_map/pallas_call | solution.py:1335
  268.6 3.8 %collective-permute-done.44 = f32[32,768]{1,0:T(8,128)S(1)} collective-permute-done((f32[32,768]{1,0:T(8,128)S(1)}, f32[32,768]{1,0:T(8,128)S(1)}, u32[]{:S(2)}, u32[]{:S(2)}) %collective-permute-start.44) | collective-permute-done | bytes 98336 | tf_op jit(solution)/shard_map/ppermute | solution.py:167
  279.0 5.0 %shard_map.490 = (f32[1000,768]{1,0:T(8,128)}, f32[768]{0:T(1024)}, f32[1000]{0:T(1024)}) custom-call(s32[8]{0:T(128)S(1)} %copy-done.27, f32[1000,768]{1,0:T(8,128)S(1)} %bitcast.117, f32[1000,768]{1,0:T(8,128)S(1)} %copy-done.7, f32[768]{0:T(1024)S(1)} %copy-done.33, f32[1000]{0:T(1024)S(1)} %copy-done.34), custom_call_target="tpu_custom_call" | custom-call | bytes 16000000 | tf_op jit(solution)/shard_map/pallas_call | solution.py:1335
  287.2 5.7 %collective-permute-done.49 = f32[32,768]{1,0:T(8,128)S(1)} collective-permute-done((f32[32,768]{1,0:T(8,128)S(1)}, f32[32,768]{1,0:T(8,128)S(1)}, u32[]{:S(2)}, u32[]{:S(2)}) %collective-permute-start.49) | collective-permute-done | bytes 98336 | tf_op jit(solution)/shard_map/ppermute | solution.py:167
  305.0 4.4 %shard_map.492 = (f32[768,768]{1,0:T(8,128)}, f32[768]{0:T(1024)}, f32[768]{0:T(1024)}, f32[197,768]{1,0:T(8,128)}, f32[197]{0:T(256)}, /*index=5*/f32[768]{0:T(1024)}) custom-call(s32[8]{0:T(128)S(1)} %copy-done.27, bf16[4,128,768]{2,1,0:T(8,128)(2,1)S(1)} %pad_maximum_fusion.5.near_ref, bf16[4,128,768]{2,1,0:T(8,128)(2,1)S(1)} %collective-permute-done.55.far_ref, ...), custom_call_target="tpu_custom_call" | custom-call | bytes 16000000 | tf_op jit(solution)/shard_map/pallas_call | solution.py:1335
  (298 shorter events, 118.2 us)
Async XLA Ops:
  9.3 12.7 %collective-permute-start.2 = (bf16[96,768]{1,0:T(8,128)(2,1)}, bf16[96,768]{1,0:T(8,128)(2,1)S(1)}, u32[]{:S(2)}, u32[]{:S(2)}) collective-permute-start(bf16[96,768]{1,0:T(8,128)(2,1)} %get-tuple-element.210.refs_0_), channel_id=1, source_target_pairs={{0,8},{1,9},{2,10},{3,11},{4,12},{5,13},{6,14},{7,15},{8,16},{9,17... | collective-permute-start | bytes 442376 | tf_op jit(solution)/shard_map/ppermute | solution.py:167
  24.7 16.7 %collective-permute-start.3 = (bf16[1,4,96,768]{3,2,1,0:T(8,128)(2,1)}, bf16[1,4,96,768]{3,2,1,0:T(8,128)(2,1)S(1)}, u32[]{:S(2)}, u32[]{:S(2)}) collective-permute-start(bf16[1,4,96,768]{3,2,1,0:T(8,128)(2,1)} %shard_map.474), channel_id=1, source_target_pairs={{0,4},{1,3},{2,6},{3,1},{4,0},{5,7},{6,2},{7,5},{8,12},{9,11},{10,... | collective-permute-start | bytes 1769480 | tf_op jit(solution)/shard_map/ppermute | solution.py:167
  27.6 13.8 %collective-permute-start.5 = (bf16[96,768]{1,0:T(8,128)(2,1)S(1)}, bf16[96,768]{1,0:T(8,128)(2,1)S(1)}, u32[]{:S(2)}, u32[]{:S(2)}) collective-permute-start(bf16[96,768]{1,0:T(8,128)(2,1)S(1)} %copy-done.60), channel_id=1, source_target_pairs={{0,16},{1,17},{2,18},{3,19},{4,20},{5,21},{6,22},{7,23},{8,24},{9,... | collective-permute-start | bytes 442376 | tf_op jit(solution)/shard_map/ppermute | solution.py:167
  43.3 22.8 %collective-permute-start.7 = (bf16[2,4,96,768]{3,2,1,0:T(8,128)(2,1)}, bf16[2,4,96,768]{3,2,1,0:T(8,128)(2,1)}, u32[]{:S(2)}, u32[]{:S(2)}) collective-permute-start(bf16[2,4,96,768]{3,2,1,0:T(8,128)(2,1)} %pad_maximum_fusion.refs_0_), channel_id=1, source_target_pairs={{0,2},{1,5},{2,0},{3,7},{4,6},{5,1},{6,4},{7,3},{8,10},{9,13},{10,... | collective-permute-start | bytes 3538952 | tf_op jit(solution)/shard_map/ppermute | solution.py:167
  43.9 22.3 %collective-permute-start.8 = (bf16[2,4,96,768]{3,2,1,0:T(8,128)(2,1)}, bf16[2,4,96,768]{3,2,1,0:T(8,128)(2,1)}, u32[]{:S(2)}, u32[]{:S(2)}) collective-permute-start(bf16[2,4,96,768]{3,2,1,0:T(8,128)(2,1)} %pad_maximum_fusion.refs_0_), channel_id=1, source_target_pairs={{0,1},{1,0},{2,3},{3,2},{4,5},{5,4},{6,7},{7,6},{8,9},{9,8},{10,11... | collective-permute-start | bytes 3538952 | tf_op jit(solution)/shard_map/ppermute | solution.py:167
  46.0 16.5 %collective-permute-start.9 = (bf16[1,4,96,768]{3,2,1,0:T(8,128)(2,1)}, bf16[1,4,96,768]{3,2,1,0:T(8,128)(2,1)S(1)}, u32[]{:S(2)}, u32[]{:S(2)}) collective-permute-start(bf16[1,4,96,768]{3,2,1,0:T(8,128)(2,1)} %shard_map.476), channel_id=1, source_target_pairs={{0,4},{1,3},{2,6},{3,1},{4,0},{5,7},{6,2},{7,5},{8,12},{9,11},{10,... | collective-permute-start | bytes 1769480 | tf_op jit(solution)/shard_map/ppermute | solution.py:167
  47.4 14.8 %collective-permute-start.11 = (bf16[96,768]{1,0:T(8,128)(2,1)S(1)}, bf16[96,768]{1,0:T(8,128)(2,1)S(1)}, u32[]{:S(2)}, u32[]{:S(2)}) collective-permute-start(bf16[96,768]{1,0:T(8,128)(2,1)S(1)} %copy-done.59), channel_id=1, source_target_pairs={{0,16},{1,17},{2,18},{3,19},{4,20},{5,21},{6,22},{7,23},{8,24},{9,... | collective-permute-start | bytes 442376 | tf_op jit(solution)/shard_map/ppermute | solution.py:167
  67.3 24.0 %collective-permute-start.13 = (bf16[2,4,96,768]{3,2,1,0:T(8,128)(2,1)}, bf16[2,4,96,768]{3,2,1,0:T(8,128)(2,1)}, u32[]{:S(2)}, u32[]{:S(2)}) collective-permute-start(bf16[2,4,96,768]{3,2,1,0:T(8,128)(2,1)} %pad_maximum_fusion.1.refs_0_), channel_id=1, source_target_pairs={{0,2},{1,5},{2,0},{3,7},{4,6},{5,1},{6,4},{7,3},{8,10},{9,13},{10,... | collective-permute-start | bytes 3538952 | tf_op jit(solution)/shard_map/ppermute | solution.py:167
  67.9 23.5 %collective-permute-start.14 = (bf16[2,4,96,768]{3,2,1,0:T(8,128)(2,1)}, bf16[2,4,96,768]{3,2,1,0:T(8,128)(2,1)}, u32[]{:S(2)}, u32[]{:S(2)}) collective-permute-start(bf16[2,4,96,768]{3,2,1,0:T(8,128)(2,1)} %pad_maximum_fusion.1.refs_0_), channel_id=1, source_target_pairs={{0,1},{1,0},{2,3},{3,2},{4,5},{5,4},{6,7},{7,6},{8,9},{9,8},{10,11... | collective-permute-start | bytes 3538952 | tf_op jit(solution)/shard_map/ppermute | solution.py:167
  71.1 20.3 %collective-permute-start.15 = (bf16[1,4,96,768]{3,2,1,0:T(8,128)(2,1)}, bf16[1,4,96,768]{3,2,1,0:T(8,128)(2,1)S(1)}, u32[]{:S(2)}, u32[]{:S(2)}) collective-permute-start(bf16[1,4,96,768]{3,2,1,0:T(8,128)(2,1)} %shard_map.477), channel_id=1, source_target_pairs={{0,4},{1,3},{2,6},{3,1},{4,0},{5,7},{6,2},{7,5},{8,12},{9,11},{10,... | collective-permute-start | bytes 1769480 | tf_op jit(solution)/shard_map/ppermute | solution.py:167
  91.6 16.3 %collective-permute-start.17 = (bf16[2,4,96,768]{3,2,1,0:T(8,128)(2,1)S(1)}, bf16[2,4,96,768]{3,2,1,0:T(8,128)(2,1)S(1)}, u32[]{:S(2)}, u32[]{:S(2)}) collective-permute-start(bf16[2,4,96,768]{3,2,1,0:T(8,128)(2,1)S(1)} %pad_maximum_fusion.2.refs_0_), channel_id=1, source_target_pairs={{0,2},{1,5},{2,0},{3,7},{4,6},{5,1},{6,4},{7,3},{8,10},{9,13},{10,... | collective-permute-start | bytes 3538952 | tf_op jit(solution)/shard_map/ppermute | solution.py:167
  92.9 14.9 %collective-permute-start.18 = (bf16[2,4,96,768]{3,2,1,0:T(8,128)(2,1)S(1)}, bf16[2,4,96,768]{3,2,1,0:T(8,128)(2,1)S(1)}, u32[]{:S(2)}, u32[]{:S(2)}) collective-permute-start(bf16[2,4,96,768]{3,2,1,0:T(8,128)(2,1)S(1)} %pad_maximum_fusion.2.refs_0_), channel_id=1, source_target_pairs={{0,1},{1,0},{2,3},{3,2},{4,5},{5,4},{6,7},{7,6},{8,9},{9,8},{10,11... | collective-permute-start | bytes 3538952 | tf_op jit(solution)/shard_map/ppermute | solution.py:167
  128.6 21.3 %collective-permute-start.21 = (bf16[32,896]{1,0:T(8,128)(2,1)S(1)}, bf16[32,896]{1,0:T(8,128)(2,1)S(1)}, u32[]{:S(2)}, u32[]{:S(2)}) collective-permute-start(bf16[32,896]{1,0:T(8,128)(2,1)S(1)} %get-tuple-element.260.refs_0_), channel_id=1, source_target_pairs={{0,24},{1,25},{2,26},{3,27},{4,28},{5,29},{6,30},{7,31},{8,0},{9,1... | collective-permute-start | bytes 172040 | tf_op jit(solution)/shard_map/ppermute | solution.py:167
  128.6 21.3 %collective-permute-start.22 = (bf16[32,896]{1,0:T(8,128)(2,1)S(1)}, bf16[32,896]{1,0:T(8,128)(2,1)S(1)}, u32[]{:S(2)}, u32[]{:S(2)}) collective-permute-start(bf16[32,896]{1,0:T(8,128)(2,1)S(1)} %get-tuple-element.260.refs_0_), channel_id=1, source_target_pairs={{0,16},{1,17},{2,18},{3,19},{4,20},{5,21},{6,22},{7,23},{8,24},{9,... | collective-permute-start | bytes 172040 | tf_op jit(solution)/shard_map/ppermute | solution.py:167
  129.7 20.2 %collective-permute-start.23 = (bf16[32,896]{1,0:T(8,128)(2,1)S(1)}, bf16[32,896]{1,0:T(8,128)(2,1)S(1)}, u32[]{:S(2)}, u32[]{:S(2)}) collective-permute-start(bf16[32,896]{1,0:T(8,128)(2,1)S(1)} %get-tuple-element.260.refs_0_), channel_id=1, source_target_pairs={{0,8},{1,9},{2,10},{3,11},{4,12},{5,13},{6,14},{7,15},{8,16},{9,17... | collective-permute-start | bytes 172040 | tf_op jit(solution)/shard_map/ppermute | solution.py:167
  162.4 21.2 %collective-permute-start.28 = (bf16[2,4,96,768]{3,2,1,0:T(8,128)(2,1)S(1)}, bf16[2,4,96,768]{3,2,1,0:T(8,128)(2,1)}, u32[]{:S(2)}, u32[]{:S(2)}) collective-permute-start(bf16[2,4,96,768]{3,2,1,0:T(8,128)(2,1)S(1)} %pad_maximum_fusion.3), channel_id=1, source_target_pairs={{0,2},{1,5},{2,0},{3,7},{4,6},{5,1},{6,4},{7,3},{8,10},{9,13},{10,... | collective-permute-start | bytes 3538952 | tf_op jit(solution)/shard_map/ppermute | solution.py:167
  163.4 20.2 %collective-permute-start.26 = (bf16[2,4,32,896]{3,2,1,0:T(8,128)(2,1)S(1)}, bf16[2,4,32,896]{3,2,1,0:T(8,128)(2,1)S(1)}, u32[]{:S(2)}, u32[]{:S(2)}) collective-permute-start(bf16[2,4,32,896]{3,2,1,0:T(8,128)(2,1)S(1)} %pad_maximum_fusion.6.refs_0_), channel_id=1, source_target_pairs={{0,2},{1,5},{2,0},{3,7},{4,6},{5,1},{6,4},{7,3},{8,10},{9,13},{10,... | collective-permute-start | bytes 1376264 | tf_op jit(solution)/shard_map/ppermute | solution.py:167
  164.7 19.0 %collective-permute-start.27 = (bf16[2,4,32,896]{3,2,1,0:T(8,128)(2,1)S(1)}, bf16[2,4,32,896]{3,2,1,0:T(8,128)(2,1)S(1)}, u32[]{:S(2)}, u32[]{:S(2)}) collective-permute-start(bf16[2,4,32,896]{3,2,1,0:T(8,128)(2,1)S(1)} %pad_maximum_fusion.6.refs_0_), channel_id=1, source_target_pairs={{0,1},{1,0},{2,3},{3,2},{4,5},{5,4},{6,7},{7,6},{8,9},{9,8},{10,11... | collective-permute-start | bytes 1376264 | tf_op jit(solution)/shard_map/ppermute | solution.py:167
  184.6 22.8 %collective-permute-start.31 = (bf16[2,768,768]{2,1,0:T(8,128)(2,1)}, bf16[2,768,768]{2,1,0:T(8,128)(2,1)}, u32[]{:S(2)}, u32[]{:S(2)}) collective-permute-start(bf16[2,768,768]{2,1,0:T(8,128)(2,1)} %get-tuple-element.286), channel_id=1, source_target_pairs={{0,1},{1,0},{2,3},{3,2},{4,5},{5,4},{6,7},{7,6},{8,9},{9,8},{10,11... | collective-permute-start | bytes 7077896 | tf_op jit(solution)/shard_map/ppermute | solution.py:167
  186.5 20.8 %collective-permute-start.30 = (bf16[4,96,768]{2,1,0:T(8,128)(2,1)S(1)}, bf16[4,96,768]{2,1,0:T(8,128)(2,1)S(1)}, u32[]{:S(2)}, u32[]{:S(2)}) collective-permute-start(bf16[4,96,768]{2,1,0:T(8,128)(2,1)S(1)} %fusion.3), channel_id=1, source_target_pairs={{0,4},{1,3},{2,6},{3,1},{4,0},{5,7},{6,2},{7,5},{8,12},{9,11},{10,... | collective-permute-start | bytes 1769480 | tf_op jit(solution)/shard_map/ppermute | solution.py:167
  187.4 19.9 %collective-permute-start.29 = (bf16[2,4,32,896]{3,2,1,0:T(8,128)(2,1)S(1)}, bf16[2,4,32,896]{3,2,1,0:T(8,128)(2,1)S(1)}, u32[]{:S(2)}, u32[]{:S(2)}) collective-permute-start(bf16[2,4,32,896]{3,2,1,0:T(8,128)(2,1)S(1)} %copy-done.55), channel_id=1, source_target_pairs={{0,1},{1,0},{2,3},{3,2},{4,5},{5,4},{6,7},{7,6},{8,9},{9,8},{10,11... | collective-permute-start | bytes 1376264 | tf_op jit(solution)/shard_map/ppermute | solution.py:167
  210.8 18.6 %collective-permute-start.32 = (bf16[2,4,96,768]{3,2,1,0:T(8,128)(2,1)}, bf16[2,4,96,768]{3,2,1,0:T(8,128)(2,1)}, u32[]{:S(2)}, u32[]{:S(2)}) collective-permute-start(bf16[2,4,96,768]{3,2,1,0:T(8,128)(2,1)} %pad_maximum_fusion.4), channel_id=1, source_target_pairs={{0,2},{1,5},{2,0},{3,7},{4,6},{5,1},{6,4},{7,3},{8,10},{9,13},{10,... | collective-permute-start | bytes 3538952 | tf_op jit(solution)/shard_map/ppermute | solution.py:167
  216.0 13.3 %collective-permute-start.34 = (bf16[96,768]{1,0:T(8,128)(2,1)S(1)}, bf16[96,768]{1,0:T(8,128)(2,1)S(1)}, u32[]{:S(2)}, u32[]{:S(2)}) collective-permute-start(bf16[96,768]{1,0:T(8,128)(2,1)S(1)} %get-tuple-element.403), channel_id=1, source_target_pairs={{0,16},{1,17},{2,18},{3,19},{4,20},{5,21},{6,22},{7,23},{8,24},{9,... | collective-permute-start | bytes 442376 | tf_op jit(solution)/shard_map/ppermute | solution.py:167
  246.3 13.4 %collective-permute-start.39 = (bf16[96,768]{1,0:T(8,128)(2,1)S(1)}, bf16[96,768]{1,0:T(8,128)(2,1)S(1)}, u32[]{:S(2)}, u32[]{:S(2)}) collective-permute-start(bf16[96,768]{1,0:T(8,128)(2,1)S(1)} %get-tuple-element.401), channel_id=1, source_target_pairs={{0,8},{1,9},{2,10},{3,11},{4,12},{5,13},{6,14},{7,15},{8,16},{9,17... | collective-permute-start | bytes 442376 | tf_op jit(solution)/shard_map/ppermute | solution.py:167
  (107 other events, 875.8 us)

commit v6 on v5

--- a/solution.py
+++ b/solution.py
@@ -465,12 +465,20 @@
     stream_out_ref,
     rows_out_ref,
     sum_ref,
+    stream_here,
+    sem,
     *,
     order,
 ):
     step = pl.program_id(0)
     count, padded = present_ref.shape
     share = attended_ref.shape[2]
+
+    late = pltpu.make_async_copy(stream_ref, stream_here, sem.at[0])
+
+    @pl.when(step == 0)
+    def _():
+        late.start()
 
     group = own_group(place_ref, order)
     projected = dot(rows_ref[...], weight(0, 3 * share))
@@ -493,7 +501,7 @@
 
     @pl.when(step == 0)
     def _():
-        stream_out_ref[...] = stream_ref[...] + line(vectors_ref, ATTEND_BIAS) + part
+        stream_out_ref[...] = part
 
     @pl.when(step > 0)
     def _():
@@ -501,6 +509,8 @@
 
     @pl.when(step == pl.num_programs(0) - 1)
     def _():
+        late.wait()
+        stream_out_ref[...] += stream_here[...] + line(vectors_ref, ATTEND_BIAS)
         hat, _ = normal_parts(stream_out_ref[...])
         rows_two = hat * line(vectors_ref, GAIN_TWO) + line(vectors_ref, SHIFT_TWO)
         rows_out_ref[...] = rows_two.astype(bf16)
@@ -629,8 +639,17 @@
     d_low_ref,
     *refs,
 ):
-    grad_ref, bias_ref, d_rows_ref, d_projected, column_ref = refs[-5:]
     step = pl.program_id(0)
+    late = None
+    if len(refs) > 5:
+        late = pltpu.make_async_copy(refs[0], refs[-2], refs[-1].at[0])
+        given, refs = refs[-2], refs[1:-2]
+
+        @pl.when(step == 0)
+        def _():
+            late.start()
+
+    grad_ref, bias_ref, d_rows_ref, d_projected, column_ref = refs
     share = attended_ref.shape[2]
     count = bias_ref.shape[1] // 2
     padded = attended_ref.shape[1] // count
@@ -669,11 +688,18 @@
 
     @pl.when(step == 0)
     def _():
-        d_rows_ref[...] = part + refs[0][...] if len(refs) > 5 else part
+        d_rows_ref[...] = part
 
     @pl.when(step > 0)
     def _():
         d_rows_ref[...] += part
+
+    if late is not None:
+
+        @pl.when(step == pl.num_programs(0) - 1)
+        def _():
+            late.wait()
+            d_rows_ref[...] += given[...]
 
 
 def stem_back_kernel(
@@ -1459,7 +1485,7 @@
             (rows_one, False),
             (vector_lines, False),
             (present, False),
-            (stream_zero, False),
+            (stream_zero, "any"),
         ),
         (
             ((groups, 3, rows, head_share), bf16, "far"),
@@ -1468,6 +1494,7 @@
             ((rows, D), bf16, False),
             ((2 * count, D), f32, False),
         ),
+        scratch=(((rows, D), f32), ((1,), None)),
         flops=2 * rows * D * 4 * D,
         weights=attend_all,
     )
@@ -1571,13 +1598,14 @@
                 (present, False),
                 (d_attend_low, False),
             )
-            + tuple((value, False) for value in before),
+            + tuple((value, "any") for value in before),
             (
                 ((pair, D, D), bf16, lambda g: g),
                 ((pair, 2 * count, head_share), f32, lambda g: g),
                 ((rows, D), f32, False),
             ),
-            (((rows, 3 * head_share), bf16), ((rows, 1), f32)),
+            (((rows, 3 * head_share), bf16), ((rows, 1), f32))
+            + ((((rows, D), f32), ((1,), None)) if before else ()),
             flops=2 * rows * D * 4 * D,
             weights=attend_all,
         )

time: 320 us -> 318 us (level)
  no operation moved by 1% of the time
where the time goes in v6:
time: 318 us; the launch traced here: 314 us
  Pallas kernels  156 us (49%)
  waiting for transfers between devices  66.5 us (21%)
  starting transfers between devices  57.4 us (18%)
  other arithmetic  23.9 us (8%)
  local copies, waits for them, and re-layouts  8.6 us (3%)
    pallas_call x17, Pallas kernels, call(): pl.pallas_call(kernel, grid_spec=pltpu.PrefetchScalarGridSpec(num_scalar_...  145 us
    ppermute x58, waiting for transfers between devices, send(): return lax.ppermute(values, ALL, table)  66.5 us
    ppermute x58, starting transfers between devices, send(): return lax.ppermute(values, ALL, table)  57.4 us
    pallas_call x4, Pallas kernels, gather(): pl.pallas_call(column_kernel, in_specs=[pl.BlockSpec(memory_space=pltpu.S...  7.6 us
    unnamed x147, local copies, waits for them, and re-layouts  7.33 us
  transfers between devices with their start and end apart: 58, of which 25 were waited for; matrix products, arithmetic and copies ran while one was open for 5% of the time, Pallas kernels for 42%

profile of v6, /device:TPU:0, one launch (start us, length us, event | category | flops | bytes accessed | tf_op | source)
XLA Modules:
  0.0 314.5 jit_solution(7990843890213318462)
XLA Ops:
  4.2 5.0 %collective-permute-start = (bf16[96,768]{1,0:T(8,128)(2,1)}, bf16[96,768]{1,0:T(8,128)(2,1)S(1)}, u32[]{:S(2)}, u32[]{:S(2)}) collective-permute-start(bf16[96,768]{1,0:T(8,128)(2,1)} %get-tuple-element.210.refs_0_), channel_id=1, source_target_pairs={{0,24},{1,25},{2,26},{3,27},{4,28},{5,29},{6,30},{7,31},{8,0},{9,1... | collective-permute-start | bytes 442376 | tf_op jit(solution)/shard_map/ppermute | solution.py:167
  13.9 8.1 %collective-permute-done.1.refs_2_ = bf16[96,768]{1,0:T(8,128)(2,1)S(1)} collective-permute-done((bf16[96,768]{1,0:T(8,128)(2,1)}, bf16[96,768]{1,0:T(8,128)(2,1)S(1)}, u32[]{:S(2)}, u32[]{:S(2)}) %collective-permute-start.1) | collective-permute-done | bytes 147488 | tf_op jit(solution)/shard_map/ppermute | solution.py:167
  32.6 4.0 %shard_map.475 = (f32[832,768]{1,0:T(8,128)}, bf16[832,768]{1,0:T(8,128)(2,1)S(1)}, f32[4,208]{1,0:T(4,128)S(1)}, f32[8,128]{1,0:T(8,128)S(1)}) custom-call(s32[8]{0:T(128)S(1)} %copy-done.24, s32[4]{0:T(128)S(1)} %copy-done.45, bf16[832,768]{1,0:T(8,128)(2,1)S(1)} %bitcast.118, f32[768,768]{1,0:T(8,128)S(1)} %copy-done.4, f32[197,768]{1,0:T(8,128)S(1)} %copy-done.11, ...), custom_call_target="tpu_custom_call" | custom-call | flops 981467136 | bytes 16000000 | tf_op jit(solution)/shard_map/pallas_call | solution.py:1361
  36.6 4.7 %collective-permute-done.5.refs_2_ = bf16[96,768]{1,0:T(8,128)(2,1)S(1)} collective-permute-done((bf16[96,768]{1,0:T(8,128)(2,1)S(1)}, bf16[96,768]{1,0:T(8,128)(2,1)S(1)}, u32[]{:S(2)}, u32[]{:S(2)}) %collective-permute-start.5) | collective-permute-done | bytes 147488 | tf_op jit(solution)/shard_map/ppermute | solution.py:167
  48.4 6.3 %collective-permute-done.10.refs_1_ = bf16[96,768]{1,0:T(8,128)(2,1)S(1)} collective-permute-done((bf16[96,768]{1,0:T(8,128)(2,1)S(1)}, bf16[96,768]{1,0:T(8,128)(2,1)S(1)}, u32[]{:S(2)}, u32[]{:S(2)}) %collective-permute-start.10) | collective-permute-done | bytes 147488 | tf_op jit(solution)/shard_map/ppermute | solution.py:167
  55.9 6.2 %collective-permute-done.11.refs_2_ = bf16[96,768]{1,0:T(8,128)(2,1)S(1)} collective-permute-done((bf16[96,768]{1,0:T(8,128)(2,1)S(1)}, bf16[96,768]{1,0:T(8,128)(2,1)S(1)}, u32[]{:S(2)}, u32[]{:S(2)}) %collective-permute-start.11) | collective-permute-done | bytes 147488 | tf_op jit(solution)/shard_map/ppermute | solution.py:167
  62.4 3.8 %collective-permute-done.7.refs_1_ = bf16[2,4,96,768]{3,2,1,0:T(8,128)(2,1)} collective-permute-done((bf16[2,4,96,768]{3,2,1,0:T(8,128)(2,1)}, bf16[2,4,96,768]{3,2,1,0:T(8,128)(2,1)}, u32[]{:S(2)}, u32[]{:S(2)}) %collective-permute-start.7) | collective-permute-done | bytes 1179680 | tf_op jit(solution)/shard_map/ppermute | solution.py:167
  71.6 18.8 %shard_map.478 = (bf16[4,3,832,192]{3,2,1,0:T(8,128)(2,1)}, bf16[4,832,192]{2,1,0:T(8,128)(2,1)}, f32[832,768]{1,0:T(8,128)}, bf16[832,768]{1,0:T(8,128)(2,1)S(1)}, f32[8,768]{1,0:T(8,128)S(1)}) custom-call(s32[8]{0:T(128)S(1)} %copy-done.25, bf16[2,4,96,768]{3,2,1,0:T(8,128)(2,1)} %pad_maximum_fusion.refs_0_, ...), custom_call_target="tpu_custom_call" | custom-call | flops 3925868544 | bytes 16000000 | tf_op jit(solution)/shard_map/pallas_call | solution.py:1361
  93.6 12.6 %shard_map.479 = (f32[4,8,768]{2,1,0:T(8,128)S(1)}, bf16[4,832,768]{2,1,0:T(8,128)(2,1)}) custom-call(s32[8]{0:T(128)S(1)} %copy-done.25, bf16[2,4,96,768]{3,2,1,0:T(8,128)(2,1)} %pad_maximum_fusion.1.refs_0_, bf16[2,4,96,768]{3,2,1,0:T(8,128)(2,1)} %collective-permute-done.13.refs_1_, bf16[2,4,96,768]{3,2,1,0:T(8,128)(2,1)} %collective-permute-done.14.refs_2_, ...), custom_call_target="tpu_custom_call" | custom-call | flops 3925868544 | bytes 16000000 | tf_op jit(solution)/shard_map/pallas_call | solution.py:1361
  109.8 17.9 %shard_map.480 = (bf16[32,896]{1,0:T(8,128)(2,1)S(1)}, f32[8,768]{1,0:T(8,128)S(1)}, f32[4,8,768]{2,1,0:T(8,128)S(1)}) custom-call(s32[8]{0:T(128)S(1)} %copy-done.25, f32[4,8,768]{2,1,0:T(8,128)S(1)} %get-tuple-element.254.active_ref, f32[8,768]{1,0:T(8,128)S(1)} %get-tuple-element.255.sum_ref, f32[8,128]{1,0:T(8,128)S(1)} %get-tuple-element.256.facts_ref, ...), custom_call_target="tpu_custom_call" | custom-call | bytes 16000000 | tf_op jit(solution)/shard_map/pallas_call | solution.py:1361
  130.7 18.2 %shard_map.481 = (bf16[2,768,768]{2,1,0:T(8,128)(2,1)}, bf16[2,768,768]{2,1,0:T(8,128)(2,1)}, f32[4,1,768]{2,1,0:T(1,128)S(1)}, f32[832,768]{1,0:T(8,128)}) custom-call(s32[8]{0:T(128)S(1)} %copy-done.25, bf16[2,4,96,768]{3,2,1,0:T(8,128)(2,1)} %pad_maximum_fusion.1.refs_0_, bf16[2,4,96,768]{3,2,1,0:T(8,128)(2,1)} %collective-permute-done.13.refs_1_, ...), custom_call_target="tpu_custom_call" | custom-call | flops 7851737088 | bytes 16000000 | tf_op jit(solution)/shard_map/pallas_call | solution.py:1361
  152.4 5.4 %shard_map.483 = (f32[832,768]{1,0:T(8,128)S(1)}, bf16[832,768]{1,0:T(8,128)(2,1)S(1)}, f32[8,768]{1,0:T(8,128)S(1)}) custom-call(s32[8]{0:T(128)S(1)} %copy-done.26, f32[832,768]{1,0:T(8,128)} %get-tuple-element.271.d_rows_ref, f32[8,768]{1,0:T(8,128)S(1)} %get-tuple-element.272.d_row_ref, f32[4,208]{1,0:T(4,128)S(1)} %get-tuple-element.239.refs_6_.present_ref.refs_7_, ...), custom_call_target="tpu_custom_call" | custom-call | bytes 16000000 | tf_op jit(solution)/shard_map/pallas_call | solution.py:1361
  163.7 18.6 %shard_map.484 = (bf16[2,768,768]{2,1,0:T(8,128)(2,1)}, f32[2,8,192]{2,1,0:T(8,128)S(1)}, f32[832,768]{1,0:T(8,128)}) custom-call(s32[8]{0:T(128)S(1)} %copy-done.26, bf16[2,4,96,768]{3,2,1,0:T(8,128)(2,1)} %pad_maximum_fusion.refs_0_, bf16[2,4,96,768]{3,2,1,0:T(8,128)(2,1)} %collective-permute-done.7.refs_1_, ...), custom_call_target="tpu_custom_call" | custom-call | flops 3925868544 | bytes 16000000 | tf_op jit(solution)/shard_map/pallas_call | solution.py:1361
  186.6 19.2 %shard_map.485 = (bf16[2,768,768]{2,1,0:T(8,128)(2,1)}, f32[2,8,192]{2,1,0:T(8,128)S(1)}, f32[832,768]{1,0:T(8,128)}) custom-call(s32[8]{0:T(128)S(1)} %copy-done.26, bf16[2,4,96,768]{3,2,1,0:T(8,128)(2,1)} %pad_maximum_fusion.refs_0_, bf16[2,4,96,768]{3,2,1,0:T(8,128)(2,1)} %collective-permute-done.7.refs_1_, ...), custom_call_target="tpu_custom_call" | custom-call | flops 3925868544 | bytes 16000000 | tf_op jit(solution)/shard_map/pallas_call | solution.py:1361
  210.4 3.1 fusion.14
  218.7 7.2 %shard_map.486 = (bf16[4,128,768]{2,1,0:T(8,128)(2,1)}, bf16[4,128,768]{2,1,0:T(8,128)(2,1)S(1)}, f32[216,768]{1,0:T(8,128)S(1)}) custom-call(s32[8]{0:T(128)S(1)} %copy-done.26, f32[832,768]{1,0:T(8,128)S(1)} %copy-done.10, f32[832,768]{1,0:T(8,128)} %copy-done.9, f32[832,768]{1,0:T(8,128)} %get-tuple-element.240.refs_7_.stream_ref, ...), custom_call_target="tpu_custom_call" | custom-call | flops 981467136 | bytes 16000000 | tf_op jit(solution)/shard_map/pallas_call | solution.py:1361
  232.3 3.5 %shard_map.487 = bf16[4,4,2,32,896]{4,3,2,1,0:T(8,128)(2,1)} custom-call(s32[8]{0:T(128)} %stack.43.place_ref, bf16[2,4,32,896]{3,2,1,0:T(8,128)(2,1)} %copy-done.51, bf16[2,4,32,896]{3,2,1,0:T(8,128)(2,1)} %copy-done.54, bf16[2,4,32,896]{3,2,1,0:T(8,128)(2,1)} %copy-done.56, bf16[2,4,32,896]{3,2,1,0:T(8,128)(2,1)} %copy-done.57), custom_call_target="tpu_custom_call" | custom-call | tf_op jit(solution)/shard_map/pallas_call | solution.py:198
  235.8 4.7 %collective-permute-done.38 = bf16[4,96,768]{2,1,0:T(8,128)(2,1)} collective-permute-done((bf16[4,96,768]{2,1,0:T(8,128)(2,1)}, bf16[4,96,768]{2,1,0:T(8,128)(2,1)}, u32[]{:S(2)}, u32[]{:S(2)}) %collective-permute-start.38) | collective-permute-done | bytes 589856 | tf_op jit(solution)/shard_map/ppermute | solution.py:167
  244.7 3.2 %collective-permute-start.39 = (bf16[96,768]{1,0:T(8,128)(2,1)S(1)}, bf16[96,768]{1,0:T(8,128)(2,1)S(1)}, u32[]{:S(2)}, u32[]{:S(2)}) collective-permute-start(bf16[96,768]{1,0:T(8,128)(2,1)S(1)} %get-tuple-element.401), channel_id=1, source_target_pairs={{0,8},{1,9},{2,10},{3,11},{4,12},{5,13},{6,14},{7,15},{8,16},{9,17... | collective-permute-start | bytes 442376 | tf_op jit(solution)/shard_map/ppermute | solution.py:167
  250.6 5.3 %shard_map.488 = (f32[1000,768]{1,0:T(8,128)}, f32[96,768]{1,0:T(8,128)S(1)}, f32[8,768]{1,0:T(8,128)S(1)}, f32[8,1000]{1,0:T(8,128)S(1)}) custom-call(s32[8]{0:T(128)S(1)} %copy-done.27, bf16[1,32,32,896]{3,2,1,0:T(8,128)(2,1)S(1)} %bitcast.120, f32[24,768]{1,0:T(8,128)S(1)} %copy-done.8, bf16[1000,768]{1,0:T(8,128)(2,1)S(1)} %copy-done), custom_call_target="tpu_custom_call" | custom-call | bytes 16000000 | tf_op jit(solution)/shard_map/pallas_call | solution.py:1361
  267.0 3.8 %collective-permute-done.44 = f32[32,768]{1,0:T(8,128)S(1)} collective-permute-done((f32[32,768]{1,0:T(8,128)S(1)}, f32[32,768]{1,0:T(8,128)S(1)}, u32[]{:S(2)}, u32[]{:S(2)}) %collective-permute-start.44) | collective-permute-done | bytes 98336 | tf_op jit(solution)/shard_map/ppermute | solution.py:167
  277.4 5.0 %shard_map.490 = (f32[1000,768]{1,0:T(8,128)}, f32[768]{0:T(1024)}, f32[1000]{0:T(1024)}) custom-call(s32[8]{0:T(128)S(1)} %copy-done.27, f32[1000,768]{1,0:T(8,128)S(1)} %bitcast.117, f32[1000,768]{1,0:T(8,128)S(1)} %copy-done.7, f32[768]{0:T(1024)S(1)} %copy-done.33, f32[1000]{0:T(1024)S(1)} %copy-done.34), custom_call_target="tpu_custom_call" | custom-call | bytes 16000000 | tf_op jit(solution)/shard_map/pallas_call | solution.py:1361
  285.6 5.7 %collective-permute-done.49 = f32[32,768]{1,0:T(8,128)S(1)} collective-permute-done((f32[32,768]{1,0:T(8,128)S(1)}, f32[32,768]{1,0:T(8,128)S(1)}, u32[]{:S(2)}, u32[]{:S(2)}) %collective-permute-start.49) | collective-permute-done | bytes 98336 | tf_op jit(solution)/shard_map/ppermute | solution.py:167
  303.4 4.4 %shard_map.492 = (f32[768,768]{1,0:T(8,128)}, f32[768]{0:T(1024)}, f32[768]{0:T(1024)}, f32[197,768]{1,0:T(8,128)}, f32[197]{0:T(256)}, /*index=5*/f32[768]{0:T(1024)}) custom-call(s32[8]{0:T(128)S(1)} %copy-done.27, bf16[4,128,768]{2,1,0:T(8,128)(2,1)S(1)} %pad_maximum_fusion.5.near_ref, bf16[4,128,768]{2,1,0:T(8,128)(2,1)S(1)} %collective-permute-done.55.far_ref, ...), custom_call_target="tpu_custom_call" | custom-call | bytes 16000000 | tf_op jit(solution)/shard_map/pallas_call | solution.py:1361
  (298 shorter events, 118.2 us)
Async XLA Ops:
  9.3 12.7 %collective-permute-start.2 = (bf16[96,768]{1,0:T(8,128)(2,1)}, bf16[96,768]{1,0:T(8,128)(2,1)S(1)}, u32[]{:S(2)}, u32[]{:S(2)}) collective-permute-start(bf16[96,768]{1,0:T(8,128)(2,1)} %get-tuple-element.210.refs_0_), channel_id=1, source_target_pairs={{0,8},{1,9},{2,10},{3,11},{4,12},{5,13},{6,14},{7,15},{8,16},{9,17... | collective-permute-start | bytes 442376 | tf_op jit(solution)/shard_map/ppermute | solution.py:167
  24.7 16.7 %collective-permute-start.3 = (bf16[1,4,96,768]{3,2,1,0:T(8,128)(2,1)}, bf16[1,4,96,768]{3,2,1,0:T(8,128)(2,1)S(1)}, u32[]{:S(2)}, u32[]{:S(2)}) collective-permute-start(bf16[1,4,96,768]{3,2,1,0:T(8,128)(2,1)} %shard_map.474), channel_id=1, source_target_pairs={{0,4},{1,3},{2,6},{3,1},{4,0},{5,7},{6,2},{7,5},{8,12},{9,11},{10,... | collective-permute-start | bytes 1769480 | tf_op jit(solution)/shard_map/ppermute | solution.py:167
  27.6 13.8 %collective-permute-start.5 = (bf16[96,768]{1,0:T(8,128)(2,1)S(1)}, bf16[96,768]{1,0:T(8,128)(2,1)S(1)}, u32[]{:S(2)}, u32[]{:S(2)}) collective-permute-start(bf16[96,768]{1,0:T(8,128)(2,1)S(1)} %copy-done.60), channel_id=1, source_target_pairs={{0,16},{1,17},{2,18},{3,19},{4,20},{5,21},{6,22},{7,23},{8,24},{9,... | collective-permute-start | bytes 442376 | tf_op jit(solution)/shard_map/ppermute | solution.py:167
  43.3 22.8 %collective-permute-start.7 = (bf16[2,4,96,768]{3,2,1,0:T(8,128)(2,1)}, bf16[2,4,96,768]{3,2,1,0:T(8,128)(2,1)}, u32[]{:S(2)}, u32[]{:S(2)}) collective-permute-start(bf16[2,4,96,768]{3,2,1,0:T(8,128)(2,1)} %pad_maximum_fusion.refs_0_), channel_id=1, source_target_pairs={{0,2},{1,5},{2,0},{3,7},{4,6},{5,1},{6,4},{7,3},{8,10},{9,13},{10,... | collective-permute-start | bytes 3538952 | tf_op jit(solution)/shard_map/ppermute | solution.py:167
  43.9 22.3 %collective-permute-start.8 = (bf16[2,4,96,768]{3,2,1,0:T(8,128)(2,1)}, bf16[2,4,96,768]{3,2,1,0:T(8,128)(2,1)}, u32[]{:S(2)}, u32[]{:S(2)}) collective-permute-start(bf16[2,4,96,768]{3,2,1,0:T(8,128)(2,1)} %pad_maximum_fusion.refs_0_), channel_id=1, source_target_pairs={{0,1},{1,0},{2,3},{3,2},{4,5},{5,4},{6,7},{7,6},{8,9},{9,8},{10,11... | collective-permute-start | bytes 3538952 | tf_op jit(solution)/shard_map/ppermute | solution.py:167
  46.0 16.5 %collective-permute-start.9 = (bf16[1,4,96,768]{3,2,1,0:T(8,128)(2,1)}, bf16[1,4,96,768]{3,2,1,0:T(8,128)(2,1)S(1)}, u32[]{:S(2)}, u32[]{:S(2)}) collective-permute-start(bf16[1,4,96,768]{3,2,1,0:T(8,128)(2,1)} %shard_map.476), channel_id=1, source_target_pairs={{0,4},{1,3},{2,6},{3,1},{4,0},{5,7},{6,2},{7,5},{8,12},{9,11},{10,... | collective-permute-start | bytes 1769480 | tf_op jit(solution)/shard_map/ppermute | solution.py:167
  47.4 14.8 %collective-permute-start.11 = (bf16[96,768]{1,0:T(8,128)(2,1)S(1)}, bf16[96,768]{1,0:T(8,128)(2,1)S(1)}, u32[]{:S(2)}, u32[]{:S(2)}) collective-permute-start(bf16[96,768]{1,0:T(8,128)(2,1)S(1)} %copy-done.59), channel_id=1, source_target_pairs={{0,16},{1,17},{2,18},{3,19},{4,20},{5,21},{6,22},{7,23},{8,24},{9,... | collective-permute-start | bytes 442376 | tf_op jit(solution)/shard_map/ppermute | solution.py:167
  67.3 23.1 %collective-permute-start.13 = (bf16[2,4,96,768]{3,2,1,0:T(8,128)(2,1)}, bf16[2,4,96,768]{3,2,1,0:T(8,128)(2,1)}, u32[]{:S(2)}, u32[]{:S(2)}) collective-permute-start(bf16[2,4,96,768]{3,2,1,0:T(8,128)(2,1)} %pad_maximum_fusion.1.refs_0_), channel_id=1, source_target_pairs={{0,2},{1,5},{2,0},{3,7},{4,6},{5,1},{6,4},{7,3},{8,10},{9,13},{10,... | collective-permute-start | bytes 3538952 | tf_op jit(solution)/shard_map/ppermute | solution.py:167
  67.9 22.6 %collective-permute-start.14 = (bf16[2,4,96,768]{3,2,1,0:T(8,128)(2,1)}, bf16[2,4,96,768]{3,2,1,0:T(8,128)(2,1)}, u32[]{:S(2)}, u32[]{:S(2)}) collective-permute-start(bf16[2,4,96,768]{3,2,1,0:T(8,128)(2,1)} %pad_maximum_fusion.1.refs_0_), channel_id=1, source_target_pairs={{0,1},{1,0},{2,3},{3,2},{4,5},{5,4},{6,7},{7,6},{8,9},{9,8},{10,11... | collective-permute-start | bytes 3538952 | tf_op jit(solution)/shard_map/ppermute | solution.py:167
  71.1 19.4 %collective-permute-start.15 = (bf16[1,4,96,768]{3,2,1,0:T(8,128)(2,1)}, bf16[1,4,96,768]{3,2,1,0:T(8,128)(2,1)S(1)}, u32[]{:S(2)}, u32[]{:S(2)}) collective-permute-start(bf16[1,4,96,768]{3,2,1,0:T(8,128)(2,1)} %shard_map.477), channel_id=1, source_target_pairs={{0,4},{1,3},{2,6},{3,1},{4,0},{5,7},{6,2},{7,5},{8,12},{9,11},{10,... | collective-permute-start | bytes 1769480 | tf_op jit(solution)/shard_map/ppermute | solution.py:167
  90.6 16.3 %collective-permute-start.17 = (bf16[2,4,96,768]{3,2,1,0:T(8,128)(2,1)S(1)}, bf16[2,4,96,768]{3,2,1,0:T(8,128)(2,1)S(1)}, u32[]{:S(2)}, u32[]{:S(2)}) collective-permute-start(bf16[2,4,96,768]{3,2,1,0:T(8,128)(2,1)S(1)} %pad_maximum_fusion.2.refs_0_), channel_id=1, source_target_pairs={{0,2},{1,5},{2,0},{3,7},{4,6},{5,1},{6,4},{7,3},{8,10},{9,13},{10,... | collective-permute-start | bytes 3538952 | tf_op jit(solution)/shard_map/ppermute | solution.py:167
  92.0 14.9 %collective-permute-start.18 = (bf16[2,4,96,768]{3,2,1,0:T(8,128)(2,1)S(1)}, bf16[2,4,96,768]{3,2,1,0:T(8,128)(2,1)S(1)}, u32[]{:S(2)}, u32[]{:S(2)}) collective-permute-start(bf16[2,4,96,768]{3,2,1,0:T(8,128)(2,1)S(1)} %pad_maximum_fusion.2.refs_0_), channel_id=1, source_target_pairs={{0,1},{1,0},{2,3},{3,2},{4,5},{5,4},{6,7},{7,6},{8,9},{9,8},{10,11... | collective-permute-start | bytes 3538952 | tf_op jit(solution)/shard_map/ppermute | solution.py:167
  127.6 21.3 %collective-permute-start.21 = (bf16[32,896]{1,0:T(8,128)(2,1)S(1)}, bf16[32,896]{1,0:T(8,128)(2,1)S(1)}, u32[]{:S(2)}, u32[]{:S(2)}) collective-permute-start(bf16[32,896]{1,0:T(8,128)(2,1)S(1)} %get-tuple-element.260.refs_0_), channel_id=1, source_target_pairs={{0,24},{1,25},{2,26},{3,27},{4,28},{5,29},{6,30},{7,31},{8,0},{9,1... | collective-permute-start | bytes 172040 | tf_op jit(solution)/shard_map/ppermute | solution.py:167
  127.7 21.3 %collective-permute-start.22 = (bf16[32,896]{1,0:T(8,128)(2,1)S(1)}, bf16[32,896]{1,0:T(8,128)(2,1)S(1)}, u32[]{:S(2)}, u32[]{:S(2)}) collective-permute-start(bf16[32,896]{1,0:T(8,128)(2,1)S(1)} %get-tuple-element.260.refs_0_), channel_id=1, source_target_pairs={{0,16},{1,17},{2,18},{3,19},{4,20},{5,21},{6,22},{7,23},{8,24},{9,... | collective-permute-start | bytes 172040 | tf_op jit(solution)/shard_map/ppermute | solution.py:167
  128.8 20.2 %collective-permute-start.23 = (bf16[32,896]{1,0:T(8,128)(2,1)S(1)}, bf16[32,896]{1,0:T(8,128)(2,1)S(1)}, u32[]{:S(2)}, u32[]{:S(2)}) collective-permute-start(bf16[32,896]{1,0:T(8,128)(2,1)S(1)} %get-tuple-element.260.refs_0_), channel_id=1, source_target_pairs={{0,8},{1,9},{2,10},{3,11},{4,12},{5,13},{6,14},{7,15},{8,16},{9,17... | collective-permute-start | bytes 172040 | tf_op jit(solution)/shard_map/ppermute | solution.py:167
  161.5 21.2 %collective-permute-start.28 = (bf16[2,4,96,768]{3,2,1,0:T(8,128)(2,1)S(1)}, bf16[2,4,96,768]{3,2,1,0:T(8,128)(2,1)}, u32[]{:S(2)}, u32[]{:S(2)}) collective-permute-start(bf16[2,4,96,768]{3,2,1,0:T(8,128)(2,1)S(1)} %pad_maximum_fusion.3), channel_id=1, source_target_pairs={{0,2},{1,5},{2,0},{3,7},{4,6},{5,1},{6,4},{7,3},{8,10},{9,13},{10,... | collective-permute-start | bytes 3538952 | tf_op jit(solution)/shard_map/ppermute | solution.py:167
  162.4 20.2 %collective-permute-start.26 = (bf16[2,4,32,896]{3,2,1,0:T(8,128)(2,1)S(1)}, bf16[2,4,32,896]{3,2,1,0:T(8,128)(2,1)S(1)}, u32[]{:S(2)}, u32[]{:S(2)}) collective-permute-start(bf16[2,4,32,896]{3,2,1,0:T(8,128)(2,1)S(1)} %pad_maximum_fusion.6.refs_0_), channel_id=1, source_target_pairs={{0,2},{1,5},{2,0},{3,7},{4,6},{5,1},{6,4},{7,3},{8,10},{9,13},{10,... | collective-permute-start | bytes 1376264 | tf_op jit(solution)/shard_map/ppermute | solution.py:167
  163.7 19.0 %collective-permute-start.27 = (bf16[2,4,32,896]{3,2,1,0:T(8,128)(2,1)S(1)}, bf16[2,4,32,896]{3,2,1,0:T(8,128)(2,1)S(1)}, u32[]{:S(2)}, u32[]{:S(2)}) collective-permute-start(bf16[2,4,32,896]{3,2,1,0:T(8,128)(2,1)S(1)} %pad_maximum_fusion.6.refs_0_), channel_id=1, source_target_pairs={{0,1},{1,0},{2,3},{3,2},{4,5},{5,4},{6,7},{7,6},{8,9},{9,8},{10,11... | collective-permute-start | bytes 1376264 | tf_op jit(solution)/shard_map/ppermute | solution.py:167
  183.7 22.1 %collective-permute-start.31 = (bf16[2,768,768]{2,1,0:T(8,128)(2,1)}, bf16[2,768,768]{2,1,0:T(8,128)(2,1)}, u32[]{:S(2)}, u32[]{:S(2)}) collective-permute-start(bf16[2,768,768]{2,1,0:T(8,128)(2,1)} %get-tuple-element.286), channel_id=1, source_target_pairs={{0,1},{1,0},{2,3},{3,2},{4,5},{5,4},{6,7},{7,6},{8,9},{9,8},{10,11... | collective-permute-start | bytes 7077896 | tf_op jit(solution)/shard_map/ppermute | solution.py:167
  185.6 20.2 %collective-permute-start.30 = (bf16[4,96,768]{2,1,0:T(8,128)(2,1)S(1)}, bf16[4,96,768]{2,1,0:T(8,128)(2,1)S(1)}, u32[]{:S(2)}, u32[]{:S(2)}) collective-permute-start(bf16[4,96,768]{2,1,0:T(8,128)(2,1)S(1)} %fusion.3), channel_id=1, source_target_pairs={{0,4},{1,3},{2,6},{3,1},{4,0},{5,7},{6,2},{7,5},{8,12},{9,11},{10,... | collective-permute-start | bytes 1769480 | tf_op jit(solution)/shard_map/ppermute | solution.py:167
  186.5 19.2 %collective-permute-start.29 = (bf16[2,4,32,896]{3,2,1,0:T(8,128)(2,1)S(1)}, bf16[2,4,32,896]{3,2,1,0:T(8,128)(2,1)S(1)}, u32[]{:S(2)}, u32[]{:S(2)}) collective-permute-start(bf16[2,4,32,896]{3,2,1,0:T(8,128)(2,1)S(1)} %copy-done.55), channel_id=1, source_target_pairs={{0,1},{1,0},{2,3},{3,2},{4,5},{5,4},{6,7},{7,6},{8,9},{9,8},{10,11... | collective-permute-start | bytes 1376264 | tf_op jit(solution)/shard_map/ppermute | solution.py:167
  209.1 18.6 %collective-permute-start.32 = (bf16[2,4,96,768]{3,2,1,0:T(8,128)(2,1)}, bf16[2,4,96,768]{3,2,1,0:T(8,128)(2,1)}, u32[]{:S(2)}, u32[]{:S(2)}) collective-permute-start(bf16[2,4,96,768]{3,2,1,0:T(8,128)(2,1)} %pad_maximum_fusion.4), channel_id=1, source_target_pairs={{0,2},{1,5},{2,0},{3,7},{4,6},{5,1},{6,4},{7,3},{8,10},{9,13},{10,... | collective-permute-start | bytes 3538952 | tf_op jit(solution)/shard_map/ppermute | solution.py:167
  214.4 13.3 %collective-permute-start.34 = (bf16[96,768]{1,0:T(8,128)(2,1)S(1)}, bf16[96,768]{1,0:T(8,128)(2,1)S(1)}, u32[]{:S(2)}, u32[]{:S(2)}) collective-permute-start(bf16[96,768]{1,0:T(8,128)(2,1)S(1)} %get-tuple-element.403), channel_id=1, source_target_pairs={{0,16},{1,17},{2,18},{3,19},{4,20},{5,21},{6,22},{7,23},{8,24},{9,... | collective-permute-start | bytes 442376 | tf_op jit(solution)/shard_map/ppermute | solution.py:167
  244.7 13.3 %collective-permute-start.39 = (bf16[96,768]{1,0:T(8,128)(2,1)S(1)}, bf16[96,768]{1,0:T(8,128)(2,1)S(1)}, u32[]{:S(2)}, u32[]{:S(2)}) collective-permute-start(bf16[96,768]{1,0:T(8,128)(2,1)S(1)} %get-tuple-element.401), channel_id=1, source_target_pairs={{0,8},{1,9},{2,10},{3,11},{4,12},{5,13},{6,14},{7,15},{8,16},{9,17... | collective-permute-start | bytes 442376 | tf_op jit(solution)/shard_map/ppermute | solution.py:167
  (107 other events, 874.8 us)
